TPU v7x, 32 devices: a whole 2x2x4 slice. The times are simulated.
32 devices in a mesh: rep: 4 (over x, core), shard: 8 (over z, y).
Axes of the slice: x: 2, y: 2, z: 4, core: 2. Of those that a mesh axis runs over, the one named last changes fastest.
Arguments:
- hidden: bfloat16 [2048, 3584], P(('rep', 'shard')), may hold values from -6 to 6
- norm_gain: float32 [3584], replicated, may hold values from 0.5 to 1.5
- input_ids: int32 [2048], replicated, may hold values from 0 to 16383
- sampled_ids: int32 [2048], replicated, may hold values from 0 to 16383
- head_weight: bfloat16 [3584, 16384], P(None, 'shard'), as said below
- moment: bfloat16 [3584, 16384], P('rep', 'shard'), may hold values from -0.29882812 to 0.29882812
- curvature: bfloat16 [3584, 16384], P('rep', 'shard'), may hold values from 0.049804688 to 5
Outputs:
- moment_new: bfloat16 [3584, 16384], P('rep', 'shard')
- curvature_new: bfloat16 [3584, 16384], P('rep', 'shard')
- update_direction: bfloat16 [3584, 16384], P('rep', 'shard')
Inputs may be any that keep to these rules, and one draw needn't show every extreme that they name: Entries of head_weight are finite.
All inputs are finite; a program needn't handle non-finite values.
Results may differ from a plain program's by a relative error of at most 0.039.
Values may be sent and summed in bfloat16 or wider, within the bound.
No kernel may reach another device: no remote copies, remote signals or barrier semaphores. Data moves between devices by JAX's collectives and lax.ppermute only.
A program may use at most 192 MiB of HBM per device.

v0:
```python
import jax
import jax.numpy as jnp
from jax import lax
from jax.sharding import PartitionSpec as P

EPS_NORM = 1e-05
BETA_ONE = 0.96
BETA_TWO = 0.95
RHO_SCALE = 0.05


def normalize(hidden, norm_gain):
    values = hidden.astype(jnp.float32)
    row_scale = lax.rsqrt(jnp.mean(values * values, axis=-1, keepdims=True) + EPS_NORM)
    return (values * row_scale * norm_gain).astype(jnp.bfloat16)


def local_targets(token_ids, sample_ids, first_col, columns):
    row_count = token_ids.shape[0]
    position = jnp.arange(row_count)
    shifted = jnp.roll(token_ids, -1) - first_col
    usable = (position < row_count - 1) & (shifted >= 0) & (shifted < columns)
    true_slot = jnp.where(usable, shifted, columns)
    sample_local = sample_ids - first_col
    inside = (sample_local >= 0) & (sample_local < columns)
    sample_slot = jnp.where(inside, sample_local, columns)
    return (true_slot, sample_slot)


def group_partial(feature_rows, probabilities, true_slot, sample_slot, columns):
    shared = lax.dot_general(
        feature_rows, probabilities, (((0,), (0,)), ((), ())), preferred_element_type=jnp.float32
    )
    widened = feature_rows.astype(jnp.float32)
    true_sums = jax.ops.segment_sum(widened, true_slot, num_segments=columns + 1)[:columns]
    sample_sums = jax.ops.segment_sum(widened, sample_slot, num_segments=columns + 1)[:columns]
    true_part = (shared - true_sums.T).astype(jnp.bfloat16)
    sample_part = (shared - sample_sums.T).astype(jnp.bfloat16)
    return (true_part, sample_part)


def on_device(hidden, norm_gain, input_ids, sampled_ids, head_weight, moment, curvature):
    normed = normalize(hidden, norm_gain)
    gathered = lax.all_gather(normed, "shard", axis=0, tiled=True)
    group_len = gathered.shape[0]
    columns = head_weight.shape[1]
    first_col = lax.axis_index("shard") * columns
    logits = jnp.dot(gathered, head_weight, preferred_element_type=jnp.float32)
    local_peak = jnp.max(logits, axis=-1)
    row_peak = lax.pmax(local_peak, "shard")
    scaled_exp = jnp.exp(logits - row_peak[:, None])
    row_sum = lax.psum(jnp.sum(scaled_exp, axis=-1), "shard")
    probabilities = scaled_exp / row_sum[:, None]
    probabilities = probabilities.astype(jnp.bfloat16)
    group_start = lax.axis_index("rep") * group_len
    token_ids = lax.dynamic_slice_in_dim(input_ids, group_start, group_len, 0)
    sample_ids = lax.dynamic_slice_in_dim(sampled_ids, group_start, group_len, 0)
    true_slot, sample_slot = local_targets(token_ids, sample_ids, first_col, columns)
    true_part, sample_part = group_partial(gathered, probabilities, true_slot, sample_slot, columns)
    gradient, sample_grad = (
        lax.psum_scatter(true_part, "rep", scatter_dimension=0, tiled=True).astype(jnp.float32),
        lax.psum_scatter(sample_part, "rep", scatter_dimension=0, tiled=True).astype(jnp.float32),
    )
    moment_new = BETA_ONE * moment.astype(jnp.float32) + (1.0 - BETA_ONE) * gradient
    curvature_new = (
        BETA_TWO * curvature.astype(jnp.float32) + (1.0 - BETA_TWO) * sample_grad * sample_grad
    )
    update_direction = jnp.clip(moment_new / (RHO_SCALE * curvature_new), -1.0, 1.0)
    return (
        moment_new.astype(jnp.bfloat16),
        curvature_new.astype(jnp.bfloat16),
        update_direction.astype(jnp.bfloat16),
    )


def solution(mesh):
    in_specs = (
        P(("rep", "shard"), None),
        P(),
        P(),
        P(),
        P(None, "shard"),
        P("rep", "shard"),
        P("rep", "shard"),
    )
    out_specs = (P("rep", "shard"), P("rep", "shard"), P("rep", "shard"))
    return jax.shard_map(
        on_device, mesh=mesh, in_specs=in_specs, out_specs=out_specs, check_vma=False
    )
```

profile of v0, /device:TPU:0, one launch (start us, length us, event | category | flops | bytes accessed | tf_op | source)
XLA Modules:
  0.0 561.8 jit_solution(15523479421373400461)
XLA Ops:
  7.2 0.0 all-gather.2.cloned.1.call-start
  7.2 1.2 fusion.15
  8.4 2.0 fusion.17
  10.4 0.0 all-gather.2.cloned.1.call-update
  10.4 0.0 reduce-scatter.3.cloned.1.call-start
  10.5 0.8 dynamic_slice.6
  11.3 0.1 slice.14
  11.3 0.5 slice.15
  11.8 0.8 and_select_fusion.1
  12.6 0.7 and_select_fusion
  13.3 67.0 %all-gather.2.cloned.1.call-done = bf16[512,3584]{1,0:T(8,128)(2,1)} async-done(((bf16[64,3584]{1,0:T(8,128)(2,1)}), bf16[512,3584]{1,0:T(8,128)(2,1)}) %all-gather.2.cloned.1.call-update) | async-done | bytes 3670032 | tf_op jit(solution)/shard_map/all_gather | solution.py:44
  80.3 23.7 %scatter_custom_fusion = f32[2049,3584]{1,0:T(8,128)} fusion(s32[512]{0:T(512)S(1)} %bitcast.15, f32[]{:T(128)} %constant.17.clone.1, bf16[512,3584]{1,0:T(8,128)(2,1)} %all-gather.2.cloned.1.call-done), kind=kCustom, calls=%fused_computation.8 | custom fusion | flops 3670016 | bytes 33044484 | tf_op jit(solution)/shard_map/scatter-add | solution.py:35
  104.0 22.1 %slice.18 = f32[2048,3584]{1,0:T(8,128)} slice(f32[2049,3584]{1,0:T(8,128)} %scatter_custom_fusion), slice={[0:2048], [0:3584]} | slice | bytes 58720256 | tf_op jit(solution)/shard_map/slice | solution.py:35
  126.1 29.7 %copy.13 = f32[2048,3584]{0,1:T(8,128)} copy(f32[2048,3584]{1,0:T(8,128)} %slice.18) | data formatting | bytes 58720256
  155.8 23.6 %scatter_custom_fusion.1 = f32[2049,3584]{1,0:T(8,128)} fusion(s32[512]{0:T(512)S(1)} %and_select_fusion.1, f32[]{:T(128)} %constant.17.clone.1, bf16[512,3584]{1,0:T(8,128)(2,1)} %all-gather.2.cloned.1.call-done), kind=kCustom, calls=%fused_computation.6 | custom fusion | flops 3670016 | bytes 33044484 | tf_op jit(solution)/shard_map/scatter-add | solution.py:36
  179.4 22.1 %slice.19 = f32[2048,3584]{1,0:T(8,128)} slice(f32[2049,3584]{1,0:T(8,128)} %scatter_custom_fusion.1), slice={[0:2048], [0:3584]} | slice | bytes 58720256 | tf_op jit(solution)/shard_map/slice | solution.py:36
  201.5 29.7 %copy.14 = f32[2048,3584]{0,1:T(8,128)} copy(f32[2048,3584]{1,0:T(8,128)} %slice.19) | data formatting | bytes 58720256
  231.2 13.4 %fusion.18 = (f32[512]{0:T(512)S(1)}, f32[512,2048]{1,0:T(8,128)}) fusion(bf16[512,3584]{1,0:T(8,128)(2,1)} %all-gather.2.cloned.1.call-done, bf16[3584,2048]{1,0:T(8,128)(2,1)} %param.11), kind=kOutput, calls=%fused_computation.34 | convolution fusion | flops 7517240832 | bytes 22546432 | tf_op jit(solution)/shard_map/dot_general | solution.py:48
  244.6 18.9 %pmax.7 = f32[512]{0:T(512)S(1)} all-reduce(f32[512]{0:T(512)S(1)} %get-tuple-element.8), channel_id=1, replica_groups=mesh['rep'=4,'shard'=8] {'shard'}, use_global_device_ids=true, to_apply=%region_2.0 | all-reduce | flops 512 | bytes 4096 | tf_op jit(solution)/shard_map/pmax | solution.py:50
  263.5 2.9 fusion.11
  266.4 17.4 %psum.7 = f32[512]{0:T(512)S(1)} all-reduce(f32[512]{0:T(512)S(1)} %fusion.11), channel_id=1, replica_groups=mesh['rep'=4,'shard'=8] {'shard'}, use_global_device_ids=true, to_apply=%region_4.0 | all-reduce | flops 512 | bytes 4096 | tf_op jit(solution)/shard_map/psum | solution.py:52
  283.8 34.1 %fusion = (bf16[3584,2048]{1,0:T(8,128)(2,1)}, bf16[3584,2048]{1,0:T(8,128)(2,1)}) fusion(f32[2048,3584]{0,1:T(8,128)} %copy.14, f32[2048,3584]{0,1:T(8,128)} %copy.13, bf16[512,3584]{1,0:T(8,128)(2,1)} %all-gather.2.cloned.1.call-done, f32[512,2048]{1,0:T(8,128)} %get-tuple-element.9, f32[512]{0:T(512)S(1)} %psum.7, f32[512]{0:T(512)S(1)} %pmax.7), kind=kOutput, calls=%fused_computation.3 | convolution fusion | flops 7548698624 | bytes 95948800 | tf_op jit(solution)/shard_map/dot_general | solution.py:31
  317.9 0.0 reduce-scatter.3.cloned.1.call-update
  317.9 0.0 reduce-scatter.5.cloned.1.call-start
  317.9 0.7 reduce-scatter.5.cloned.1.call-update
  318.6 110.8 %reduce-scatter.3.cloned.1.call-done = bf16[896,2048]{1,0:T(8,128)(2,1)} async-done(((bf16[3584,2048]{1,0:T(8,128)(2,1)}), bf16[896,2048]{1,0:T(8,128)(2,1)}) %reduce-scatter.3.cloned.1.call-update) | async-done | bytes 3670032 | tf_op jit(solution)/shard_map/reduce_scatter | solution.py:61
  429.4 115.6 %reduce-scatter.5.cloned.1.call-done = bf16[896,2048]{1,0:T(8,128)(2,1)} async-done(((bf16[3584,2048]{1,0:T(8,128)(2,1)}), bf16[896,2048]{1,0:T(8,128)(2,1)}) %reduce-scatter.5.cloned.1.call-update) | async-done | bytes 3670032 | tf_op jit(solution)/shard_map/reduce_scatter | solution.py:62
  545.0 9.8 %clamp_convert_fusion = (bf16[896,2048]{1,0:T(8,128)(2,1)}, bf16[896,2048]{1,0:T(8,128)(2,1)}, bf16[896,2048]{1,0:T(8,128)(2,1)}) fusion(bf16[896,2048]{1,0:T(8,128)(2,1)} %reduce-scatter.3.cloned.1.call-done, bf16[896,2048]{1,0:T(8,128)(2,1)} %param.12, bf16[896,2048]{1,0:T(8,128)(2,1)} %reduce-scatter.5.cloned.1.call-done, bf16[896,2048]{1,0:T(8,128)(2,1)} %param.13), kind=kLoop, calls=%fused_computation.14 | loop fusion | flops 31195136 | bytes 25690112 | tf_op jit(solution)/shard_map/convert_element_type | solution.py:72
  (1 shorter events, 0.0 us)
Async XLA Ops:
  7.2 73.1 %all-gather.2.cloned.1.call-start = ((), (), s32[]{:S(2)}) async-start(), calls=%async_computation.2 | async-start | bytes 4128768 | tf_op jit(solution)/shard_map/all_gather | solution.py:44
  10.4 419.0 %reduce-scatter.3.cloned.1.call-start = ((), (), s32[]{:S(2)}) async-start(), calls=%async_computation.3 | async-start | bytes 18350080 | tf_op jit(solution)/shard_map/reduce_scatter | solution.py:61
  317.9 227.1 %reduce-scatter.5.cloned.1.call-start = ((), (), s32[]{:S(2)}) async-start(), calls=%async_computation.4 | async-start | bytes 18350080 | tf_op jit(solution)/shard_map/reduce_scatter | solution.py:62
Sparse Core Ops, SparseCore 0:
  10.8 69.5 all-gather.1
  318.0 111.3 reduce-scatter.2
  432.0 112.9 reduce-scatter.4
where the time goes:
time: 571 us; the launch traced here: 562 us
  waiting for transfers between devices  294 us (51%)
  local copies, waits for them, and re-layouts  105 us (18%)
  other arithmetic  64.7 us (11%)
  matrix products  47.6 us (8%)
  blocking collectives  36.2 us (6%)
  between operations  14.2 us (2%)
    reduce_scatter x1, waiting for transfers between devices, on_device(): lax.psum_scatter(sample_part, 'rep', scatter_dimension=0, tiled=True)  116 us
    reduce_scatter x1, waiting for transfers between devices, on_device(): lax.psum_scatter(true_part, 'rep', scatter_dimension=0, tiled=True)  111 us
    all_gather x1, waiting for transfers between devices, on_device(): gathered = lax.all_gather(normed, 'shard', axis=0, tiled=True)  67 us
    unnamed x2, local copies, waits for them, and re-layouts  59.4 us
    dot_general x1, matrix products, group_partial(): lax.dot_general(feature_rows, probabilities, (((0,), (0,)), ((), ())), pr...  34.1 us
    scatter-add x1, other arithmetic, group_partial(): jax.ops.segment_sum(widened, true_slot, num_segments=columns + 1)[:columns]  23.7 us
    scatter-add x1, other arithmetic, group_partial(): jax.ops.segment_sum(widened, sample_slot, num_segments=columns + 1)  23.6 us
    slice x1, local copies, waits for them, and re-layouts, group_partial(): jax.ops.segment_sum(widened, sample_slot, num_segments=columns + 1)  22.1 us
  transfers between devices with their start and end apart: 3, of which 3 were waited for; matrix products, arithmetic and copies ran while one was open for 1% of the time, Pallas kernels for 0%

commit v1 on v0

v1 whole, which is shorter than its diff:
```python
import functools

import jax
import jax.numpy as jnp
import numpy as np
from jax import lax
from jax.experimental import pallas as pl
from jax.experimental.pallas import tpu as pltpu
from jax.sharding import PartitionSpec as P

EPS_NORM = 1e-05
BETA_ONE = 0.96
BETA_TWO = 0.95
RHO_SCALE = 0.05
GATHER_BYTES = 32 * 1024 * 1024


def normalize(hidden, norm_gain):
    values = hidden.astype(jnp.float32)
    row_scale = lax.rsqrt(jnp.mean(values * values, axis=-1, keepdims=True) + EPS_NORM)
    return (values * row_scale * norm_gain).astype(jnp.bfloat16)


def refresh(gradient, sample_grad, moment, curvature):
    moment_new = BETA_ONE * moment.astype(jnp.float32) + (1.0 - BETA_ONE) * gradient
    curvature_new = (
        BETA_TWO * curvature.astype(jnp.float32) + (1.0 - BETA_TWO) * sample_grad * sample_grad
    )
    update_direction = jnp.clip(moment_new / (RHO_SCALE * curvature_new), -1.0, 1.0)
    return (
        moment_new.astype(jnp.bfloat16),
        curvature_new.astype(jnp.bfloat16),
        update_direction.astype(jnp.bfloat16),
    )


def by_groups(hidden, norm_gain, input_ids, sampled_ids, head_weight, moment, curvature):
    normed = normalize(hidden, norm_gain)
    gathered = lax.all_gather(normed, "shard", axis=0, tiled=True)
    group_len = gathered.shape[0]
    columns = head_weight.shape[1]
    first_col = lax.axis_index("shard") * columns
    logits = jnp.dot(gathered, head_weight, preferred_element_type=jnp.float32)
    row_peak = lax.pmax(jnp.max(logits, axis=-1), "shard")
    scaled_exp = jnp.exp(logits - row_peak[:, None])
    row_sum = lax.psum(jnp.sum(scaled_exp, axis=-1), "shard")
    probabilities = (scaled_exp / row_sum[:, None]).astype(jnp.bfloat16)
    group_start = lax.axis_index("rep") * group_len
    token_ids = lax.dynamic_slice_in_dim(input_ids, group_start, group_len, 0)
    sample_ids = lax.dynamic_slice_in_dim(sampled_ids, group_start, group_len, 0)
    position = jnp.arange(group_len)
    shifted = jnp.roll(token_ids, -1) - first_col
    usable = (position < group_len - 1) & (shifted >= 0) & (shifted < columns)
    true_slot = jnp.where(usable, shifted, columns)
    sample_local = sample_ids - first_col
    inside = (sample_local >= 0) & (sample_local < columns)
    sample_slot = jnp.where(inside, sample_local, columns)
    shared = lax.dot_general(
        gathered, probabilities, (((0,), (0,)), ((), ())), preferred_element_type=jnp.float32
    )
    widened = gathered.astype(jnp.float32)
    true_sums = jax.ops.segment_sum(widened, true_slot, num_segments=columns + 1)[:columns]
    sample_sums = jax.ops.segment_sum(widened, sample_slot, num_segments=columns + 1)[:columns]
    true_part = (shared - true_sums.T).astype(jnp.bfloat16)
    sample_part = (shared - sample_sums.T).astype(jnp.bfloat16)
    gradient = lax.psum_scatter(true_part, "rep", scatter_dimension=0, tiled=True)
    sample_grad = lax.psum_scatter(sample_part, "rep", scatter_dimension=0, tiled=True)
    return refresh(
        gradient.astype(jnp.float32), sample_grad.astype(jnp.float32), moment, curvature
    )


def swap_pairs(count, bit):
    return [(index, index ^ bit) for index in range(count)]


def shift_pairs(lines, along, across):
    pairs = []
    for place in range(lines):
        for side in range(2):
            source = 2 * place + side
            pairs.append((source, 2 * ((place + along) % lines) + (side ^ across)))
    return pairs


def logits_kernel(start, sizes, *refs):
    block_refs, refs = refs[:len(sizes)], refs[len(sizes):]
    weight_ref, before_ref, exp_ref, stats_ref, tokens, logits, highs, sums = refs
    step = pl.program_id(0)
    count, columns = logits.shape
    width = weight_ref.shape[1]
    shift = start % 128
    half = stats_ref.shape[0] // 2

    @pl.when(step == 0)
    def _():
        place = 0
        for size, ref in zip(sizes, block_refs):
            tokens[place:place + size] = ref[...]
            place += size
        highs[...] = jnp.full(highs.shape, -jnp.inf, jnp.float32)

    tile = jnp.dot(tokens[...], weight_ref[...], preferred_element_type=jnp.float32)
    logits[:, pl.ds(pl.multiple_of(step * width, 128), width)] = tile
    high = functools.reduce(
        jnp.maximum, [tile[:, lane:lane + 128] for lane in range(0, width, 128)]
    )
    highs[shift:shift + count] = jnp.maximum(highs[shift:shift + count], high)

    @pl.when(step == pl.num_programs(0) - 1)
    def _():
        highs[...] = jnp.broadcast_to(jnp.max(highs[...], axis=1, keepdims=True), highs.shape)
        chunk = 16

        def body(index, carry):
            place = pl.ds(pl.multiple_of(index * chunk, chunk), chunk)
            outer = pl.ds(pl.multiple_of(shift + index * chunk, chunk), chunk)
            peak = highs[outer, :]
            total = jnp.zeros((chunk, 128), jnp.float32)
            for lane in range(0, columns, 128):
                scaled = jnp.exp(logits[place, lane:lane + 128] - peak)
                exp_ref[place, lane:lane + 128] = scaled.astype(jnp.bfloat16)
                total += scaled
            sums[outer, :] = total
            return carry

        lax.fori_loop(0, count // chunk, body, 0, unroll=2)
        totals = jnp.broadcast_to(jnp.sum(sums[...], axis=1, keepdims=True), sums.shape)
        stats_ref[...] = before_ref[...]
        for base, rows in ((0, highs[...].T[0:1]), (half, totals.T[0:1])):
            for lane in range(shift, shift + count, 64):
                row = base + (start - shift + lane) // 128
                inner = lane % 128
                stats_ref[row:row + 1, inner:inner + 64] = rows[:, lane:lane + 64]


def round_logits(start, blocks, head_weight, before):
    depth, columns = head_weight.shape
    sizes = [block.shape[0] for block in blocks]
    count = sum(sizes)
    width = min(256, columns)
    spread = -(-(start % 128 + count) // 128) * 128
    whole = lambda array: pl.BlockSpec(array.shape, lambda step: (0, 0))
    return pl.pallas_call(
        functools.partial(logits_kernel, start, sizes),
        grid=(columns // width,),
        in_specs=[whole(block) for block in blocks]
        + [pl.BlockSpec((depth, width), lambda step: (0, step)), whole(before)],
        out_specs=[pl.BlockSpec((count, columns), lambda step: (0, 0)), whole(before)],
        out_shape=[
            jax.ShapeDtypeStruct((count, columns), jnp.bfloat16),
            jax.ShapeDtypeStruct(before.shape, jnp.float32),
        ],
        scratch_shapes=[
            pltpu.VMEM((count, depth), jnp.bfloat16),
            pltpu.VMEM((count, columns), jnp.float32),
            pltpu.VMEM((spread, 128), jnp.float32),
            pltpu.VMEM((spread, 128), jnp.float32),
        ],
        compiler_params=pltpu.CompilerParams(vmem_limit_bytes=40 * 1024 * 1024),
        cost_estimate=pl.CostEstimate(
            flops=2 * count * depth * columns,
            bytes_accessed=2 * depth * columns,
            transcendentals=count * columns,
        ),
        name="round_logits",
    )(*blocks, head_weight, before)


def turn_kernel(sizes, rep_ref, *refs):
    block_refs = refs[:len(sizes)]
    mine_ref, other_ref, tokens = refs[len(sizes):]
    step = pl.program_id(0)
    place = 0
    for size, ref in zip(sizes, block_refs):
        tokens[place:place + size] = ref[...]
        place += size
    turned = tokens[...].T

    @pl.when(step == 0)
    def _():
        mine_ref[...] = turned

    @pl.when(step == 1)
    def _():
        other_ref[...] = turned


def turned_features(rep, blocks, rows):
    sizes = [block.shape[0] for block in blocks]
    count = sum(sizes)
    whole = pl.BlockSpec((rows, count), lambda step, rep_ref: (0, 0))
    return pl.pallas_call(
        functools.partial(turn_kernel, sizes),
        grid_spec=pltpu.PrefetchScalarGridSpec(
            num_scalar_prefetch=1,
            grid=(2,),
            in_specs=[
                pl.BlockSpec((size, rows), lambda step, rep_ref: (0, rep_ref[0] ^ step))
                for size in sizes
            ],
            out_specs=[whole, whole],
            scratch_shapes=[pltpu.VMEM((count, rows), jnp.bfloat16)],
        ),
        out_shape=[jax.ShapeDtypeStruct((rows, count), jnp.bfloat16)] * 2,
        compiler_params=pltpu.CompilerParams(vmem_limit_bytes=24 * 1024 * 1024),
        cost_estimate=pl.CostEstimate(
            flops=0, bytes_accessed=8 * rows * count, transcendentals=0
        ),
        name="turned_features",
    )(rep, *blocks)


def one_hot_kernel(count, *refs):
    feature_refs, refs = refs[:count], refs[count:]
    (true_ref, sample_ref), refs = refs[:2], refs[2:]
    before_refs, refs = refs[:-3], refs[-3:]
    true_out, sample_out, features = refs
    step = pl.program_id(0)
    width = true_out.shape[1]
    part = feature_refs[0].shape[1]

    @pl.when(step == 0)
    def _():
        for index, ref in enumerate(feature_refs):
            features[:, index * part:(index + 1) * part] = ref[...]

    tokens = part * count
    columns = step * width + lax.broadcasted_iota(jnp.int32, (width, tokens), 0)
    for index, (ids_ref, out_ref) in enumerate(((true_ref, true_out), (sample_ref, sample_out))):
        hot = (columns == ids_ref[...]).astype(jnp.float32).astype(jnp.bfloat16)
        total = lax.dot_general(
            features[...], hot, (((1,), (1,)), ((), ())), preferred_element_type=jnp.float32
        )
        if before_refs:
            total += before_refs[index][...].astype(jnp.float32)
        out_ref[...] = total.astype(jnp.bfloat16)


def one_hot_sums(features, ids, columns, before=()):
    rows, part = features[0].shape
    tokens = part * len(features)
    width = min(256, columns)
    whole = lambda array: pl.BlockSpec(array.shape, lambda step: (0, 0))
    tile = pl.BlockSpec((rows, width), lambda step: (0, step))
    return pl.pallas_call(
        functools.partial(one_hot_kernel, len(features)),
        grid=(columns // width,),
        in_specs=[whole(array) for array in (*features, *ids)] + [tile] * len(before),
        out_specs=[tile, tile],
        out_shape=[jax.ShapeDtypeStruct((rows, columns), jnp.bfloat16)] * 2,
        scratch_shapes=[pltpu.VMEM((rows, tokens), jnp.bfloat16)],
        compiler_params=pltpu.CompilerParams(vmem_limit_bytes=24 * 1024 * 1024),
        cost_estimate=pl.CostEstimate(
            flops=4 * rows * tokens * columns,
            bytes_accessed=2 * rows * (tokens + 2 * columns),
            transcendentals=0,
        ),
        name="one_hot_sums",
    )(*features, *ids, *before)


def refresh_kernel(lines, counts, *refs):
    feature_refs, refs = refs[:counts[0]], refs[counts[0]:]
    exp_refs, refs = refs[:counts[1]], refs[counts[1]:]
    stats_refs, refs = refs[:lines], refs[lines:]
    (true_sum, sample_sum, moment_ref, curvature_ref,
     moment_out, curvature_out, update_out, scaled) = refs
    step = pl.program_id(0)
    part = feature_refs[0].shape[1]

    @pl.when(step == 0)
    def _():
        rows = 4 * lines
        peaks = [ref[0:rows] for ref in stats_refs]
        totals = [ref[rows:2 * rows] for ref in stats_refs]
        own_peaks = stats_refs[0][2 * rows:]
        for core in range(2):
            for turn in range(lines):
                for side in range(2):
                    row = (core * lines + turn) * 2 + side
                    away = [
                        (core * lines + (turn + along) % lines) * 2 + side for along in range(lines)
                    ]
                    near = [values[index:index + 1] for values, index in zip(peaks, away)]
                    parts = [values[index:index + 1] for values, index in zip(totals, away)]
                    peak = functools.reduce(jnp.maximum, near)
                    total = sum(t * jnp.exp(p - peak) for p, t in zip(near, parts))
                    factor = jnp.exp(own_peaks[row:row + 1] - peak) / total
                    place = row * 128
                    ref = feature_refs[place // part]
                    inner = place % part
                    values = ref[:, inner:inner + 128].astype(jnp.float32)
                    scaled[:, place:place + 128] = (values * factor).astype(jnp.bfloat16)

    exps = jnp.concatenate([ref[...] for ref in exp_refs], axis=0)
    shared = jnp.dot(scaled[...], exps, preferred_element_type=jnp.float32)
    moment_out[...], curvature_out[...], update_out[...] = refresh(
        shared - true_sum[...].astype(jnp.float32),
        shared - sample_sum[...].astype(jnp.float32),
        moment_ref[...],
        curvature_ref[...],
    )


def refresh_states(lines, features, exps, stats, sums, moment, curvature):
    rows, columns = moment.shape
    tokens = sum(array.shape[1] for array in features)
    width = min(256, columns)
    whole = lambda array: pl.BlockSpec(array.shape, lambda step: (0, 0))
    tile = pl.BlockSpec((rows, width), lambda step: (0, step))
    return pl.pallas_call(
        functools.partial(refresh_kernel, lines, (len(features), len(exps))),
        grid=(columns // width,),
        in_specs=[whole(array) for array in features]
        + [pl.BlockSpec((array.shape[0], width), lambda step: (0, step)) for array in exps]
        + [whole(array) for array in stats]
        + [tile] * 4,
        out_specs=[tile] * 3,
        out_shape=[jax.ShapeDtypeStruct((rows, columns), jnp.bfloat16)] * 3,
        scratch_shapes=[pltpu.VMEM((rows, tokens), jnp.bfloat16)],
        compiler_params=pltpu.CompilerParams(vmem_limit_bytes=32 * 1024 * 1024),
        cost_estimate=pl.CostEstimate(
            flops=2 * rows * columns * tokens,
            bytes_accessed=2 * (rows * tokens + tokens * columns + 7 * rows * columns),
            transcendentals=0,
        ),
        name="refresh_states",
    )(*features, *exps, *stats, *sums, moment, curvature)


def merge_kernel(own_ref, across_ref, core_ref, both_ref, merged_ref):
    rows = own_ref.shape[0] // 2
    for core, (near, far) in enumerate(((own_ref, across_ref), (core_ref, both_ref))):
        for row in range(rows):
            place = core * rows + row
            other = row ^ 1
            first, second = near[row:row + 1], far[other:other + 1]
            peak = jnp.maximum(first, second)
            total = near[rows + row:rows + row + 1] * jnp.exp(first - peak)
            total += far[rows + other:rows + other + 1] * jnp.exp(second - peak)
            merged_ref[place:place + 1] = peak
            merged_ref[2 * rows + place:2 * rows + place + 1] = total
            merged_ref[4 * rows + place:4 * rows + place + 1] = first


def merged_stats(own, across, core, both):
    rows, lanes = own.shape
    return pl.pallas_call(
        merge_kernel,
        out_shape=jax.ShapeDtypeStruct((3 * rows, lanes), jnp.float32),
        name="merged_stats",
    )(own, across, core, both)


def after(value, *others):
    return lax.optimization_barrier((value, *others))[0]


def all_tokens(reps, shards, hidden, norm_gain, input_ids, sampled_ids, head_weight, moment, curvature):
    lines = shards // 2
    length = hidden.shape[0]
    half = length // 2
    rows, columns = moment.shape
    rep = lax.axis_index("rep")
    shard = lax.axis_index("shard")
    first_col = shard * columns
    group_len = length * shards

    def to_x(values):
        return lax.ppermute(values, "rep", swap_pairs(reps, 2))

    def to_core(values):
        return lax.ppermute(values, "rep", swap_pairs(reps, 1))

    def to_y(values):
        return lax.ppermute(values, "shard", swap_pairs(shards, 1))

    def to_y_core(values):
        pairs = [
            (rep_at * shards + at, (rep_at ^ 1) * shards + (at ^ 1))
            for rep_at in range(reps) for at in range(shards)
        ]
        return lax.ppermute(values, ("rep", "shard"), pairs)

    normed = normalize(hidden, norm_gain)

    core, turn, side, across = np.meshgrid(
        np.arange(2), np.arange(lines), np.arange(2), np.arange(2), indexing="ij"
    )
    holder = (rep ^ (2 * across + core)).reshape(-1)
    place = (2 * ((shard // 2 - turn) % lines) + ((shard % 2) ^ side)).reshape(-1)
    order = holder * shards + place
    last = jnp.arange(input_ids.shape[0]) % group_len == group_len - 1
    targets = jnp.where(last, -1, jnp.roll(input_ids, -1) - first_col)
    ids = jnp.stack([targets, sampled_ids - first_col]).reshape(2, reps * shards, length)
    ids = jnp.take(ids, order, axis=1).reshape(2, 2, lines, 4 * length)
    split = lines // 2
    early_ids = ids[:, :, :split].reshape(2, 1, -1)
    late_ids = ids[:, :, split:].reshape(2, 1, -1)

    rep_scalar = rep.astype(jnp.int32).reshape(1)
    stats = jnp.zeros((4 * lines, 128), jnp.float32)
    block, waiting, start = normed, [], 0
    quads, exps, other_exps, early, sums = [], [], [], None, None
    for turn in range(lines):
        final = turn + 1 == lines
        if turn > 1:
            block = after(block, exps[turn - 2])
        from_x = to_x(block)
        from_y = to_y(block)
        following = None
        if not final:
            following = lax.ppermute(block, "shard", shift_pairs(lines, 1, 0))
        if exps:
            from_x, from_y = lax.optimization_barrier((from_x, from_y, exps[-1], *waiting))[:2]
        first = to_x(from_y[:half])
        second = to_y(from_x[half:])
        quads.append([block, from_x, from_y, first, second])
        blocks = waiting + [block, from_x, from_y]
        gates = [following]
        if final:
            blocks = blocks + [first, second]
            gates = [*sums, *other_exps]
        if turn == split:
            turns = sum(quads[:split], [])
            turns[0] = after(turns[0], exps[-1], following)
            early = turned_features(rep_scalar, turns, rows)
            gates.append(early[0])
        blocks[0] = after(blocks[0], *gates)
        exp, stats = round_logits(start, blocks, head_weight, stats)
        exps.append(exp)
        start += exp.shape[0]
        if turn == split:
            early = [early[0], to_core(early[1])]
            early_ids = [after(early_ids[0], exp), early_ids[1]]
            sums = one_hot_sums(early, early_ids, columns)
        if turn + 2 == lines:
            other_exps = [to_core(after(early_exp, exp)) for early_exp in exps[:-1]]
        waiting = [first, second]
        block = following

    across_stats, core_stats, both_stats = to_y(stats), to_core(stats), to_y_core(stats)
    late_blocks = sum(quads[split:], [])
    late_blocks[0] = after(late_blocks[0], stats)
    late = turned_features(rep_scalar, late_blocks, rows)
    merged = merged_stats(stats, across_stats, core_stats, both_stats)
    all_stats = [merged] + [
        lax.ppermute(merged, "shard", shift_pairs(lines, -along, 0)) for along in range(1, lines)
    ]
    late_exps = lax.optimization_barrier((late[1], *exps[-2:], merged))
    other_exps += [to_core(exp) for exp in late_exps[1:3]]
    late = [late[0], to_core(late_exps[0])]
    sums = one_hot_sums(late, late_ids, columns, sums)
    return tuple(refresh_states(
        lines, [early[0], late[0], early[1], late[1]], exps + other_exps,
        all_stats, sums, moment, curvature,
    ))


def solution(mesh):
    in_specs = (
        P(("rep", "shard"), None),
        P(),
        P(),
        P(),
        P(None, "shard"),
        P("rep", "shard"),
        P("rep", "shard"),
    )
    out_specs = (P("rep", "shard"), P("rep", "shard"), P("rep", "shard"))
    reps, shards = mesh.shape["rep"], mesh.shape["shard"]

    def whole(hidden, *others):
        tokens, depth = hidden.shape
        length = tokens // (reps * shards)
        fits = hidden.size * 2 <= GATHER_BYTES and reps == 4 and shards % 2 == 0
        if fits and length == 64 and (depth // reps) % 128 == 0:
            plan = functools.partial(all_tokens, reps, shards)
        else:
            plan = by_groups

        return jax.shard_map(
            plan, mesh=mesh, in_specs=in_specs, out_specs=out_specs, check_vma=False
        )(hidden, *others)

    return whole
```

time: 571 us -> 154 us (0.27); the launches traced: 562 us -> 153 us
  waiting for transfers between devices: 294 us -> 9.13 us
  Pallas kernels: 0 us -> 89 us
  local copies, waits for them, and re-layouts: 105 us -> 20.1 us
  other arithmetic: 64.7 us -> 4.65 us
  matrix products: 47.6 us -> 0 us
  blocking collectives: 36.2 us -> 0 us
  starting transfers between devices: 0.12 us -> 29.6 us
  between operations: 14.2 us -> 1.03 us
    reduce_scatter x2 -> x0, waiting for transfers between devices: 226 us -> none  [the longest x1 116 us: on_device(): lax.psum_scatter(sample_part, 'rep', scatter_dimension=0, tiled=True)]
    pallas_call x0 -> x10, Pallas kernels: none -> 89 us  [the longest x4 44.2 us: round_logits(): pl.pallas_call(functools.partial(logits_kernel, start, sizes), grid=(colu...]
    all_gather x1 -> x0, waiting for transfers between devices: 67 us -> none  [on_device(): gathered = lax.all_gather(normed, 'shard', axis=0, tiled=True)]
    dot_general x2 -> x0, matrix products: 47.6 us -> none  [the longest x1 34.1 us: group_partial(): lax.dot_general(feature_rows, probabilities, (((0,), (0,)), ((), ())), pr...]
    scatter-add x2 -> x0, other arithmetic: 47.3 us -> none  [the longest x1 23.7 us: group_partial(): jax.ops.segment_sum(widened, true_slot, num_segments=columns + 1)[:columns]]
    unnamed x2 -> x56, local copies, waits for them, and re-layouts: 59.4 us -> 16.6 us
    slice x4 -> x10, local copies, waits for them, and re-layouts: 44.7 us -> 2.1 us  [the longest x2 1.97 us: all_tokens(): targets = jnp.where(last, -1, jnp.roll(input_ids, -1) - first_col)]
    ppermute x0 -> x31, starting transfers between devices: none -> 29.6 us  [the longest x8 9.75 us: to_x(): return lax.ppermute(values, 'rep', swap_pairs(reps, 2))]
  transfers between devices with their start and end apart: 3 -> 31, of which waited for: 3 -> 5; matrix products, arithmetic and copies ran while one was open for 1% -> 4% of each run, Pallas kernels for 0% -> 38%
where the time goes in v1:
time: 154 us; the launch traced here: 153 us
  Pallas kernels  89 us (58%)
  starting transfers between devices  29.6 us (19%)
  local copies, waits for them, and re-layouts  20.1 us (13%)
  waiting for transfers between devices  9.13 us (6%)
  other arithmetic  4.65 us (3%)
    pallas_call x4, Pallas kernels, round_logits(): pl.pallas_call(functools.partial(logits_kernel, start, sizes), grid=(colu...  44.2 us
    pallas_call x2, Pallas kernels, one_hot_sums(): pl.pallas_call(functools.partial(one_hot_kernel, len(features)), grid=(co...  22.8 us
    pallas_call x1, Pallas kernels, refresh_states(): pl.pallas_call(functools.partial(refresh_kernel, lines, (len(features), l...  17.5 us
    unnamed x56, local copies, waits for them, and re-layouts  16.6 us
    ppermute x8, starting transfers between devices, to_x(): return lax.ppermute(values, 'rep', swap_pairs(reps, 2))  9.75 us
    ppermute x9, starting transfers between devices, to_y(): return lax.ppermute(values, 'shard', swap_pairs(shards, 1))  8.88 us
    ppermute x3, waiting for transfers between devices, all_tokens(): following = lax.ppermute(block, 'shard', shift_pairs(lines, 1, 0))  6.3 us
    ppermute x3, starting transfers between devices, all_tokens(): lax.ppermute(merged, 'shard', shift_pairs(lines, -along, 0))  6 us
  transfers between devices with their start and end apart: 31, of which 5 were waited for; matrix products, arithmetic and copies ran while one was open for 4% of the time, Pallas kernels for 38%

profile of v1, /device:TPU:0, one launch (start us, length us, event | category | flops | bytes accessed | tf_op | source)
XLA Modules:
  0.0 153.5 jit_solution(17274037971789311384)
XLA Ops:
  0.6 1.2 fusion
  1.9 1.2 fusion.2.refs_0_
  3.1 3.0 %collective-permute-start.4 = (bf16[64,3584]{1,0:T(8,128)(2,1)S(1)}, bf16[64,3584]{1,0:T(8,128)(2,1)S(1)}, u32[]{:S(2)}, u32[]{:S(2)}) collective-permute-start(bf16[64,3584]{1,0:T(8,128)(2,1)S(1)} %fusion.2.refs_0_), channel_id=1, source_target_pairs={{0,16},{8,24},{16,0},{24,8},{1,17},{9,25},{17,1},{25,9},{2,18},{10... | collective-permute-start | bytes 1376264 | tf_op jit(solution)/shard_map/ppermute | solution.py:371
  6.1 1.6 %collective-permute-start.2 = (bf16[64,3584]{1,0:T(8,128)(2,1)S(1)}, bf16[64,3584]{1,0:T(8,128)(2,1)S(1)}, u32[]{:S(2)}, u32[]{:S(2)}) collective-permute-start(bf16[64,3584]{1,0:T(8,128)(2,1)S(1)} %fusion.2.refs_0_), channel_id=1, source_target_pairs={{0,2},{1,3},{2,4},{3,5},{4,6},{5,7},{6,0},{7,1},{8,10},{9,11},{10,... | collective-permute-start | bytes 1376264 | tf_op jit(solution)/shard_map/ppermute | solution.py:414
  7.6 1.5 collective-permute-start
  9.2 0.7 broadcast_subtract_fusion
  9.9 0.7 fusion.8
  10.6 1.2 slice.54
  11.8 0.8 slice.53
  12.8 0.7 fusion.4
  13.6 6.3 %collective-permute-done.2.refs_2_.refs_5_ = bf16[64,3584]{1,0:T(8,128)(2,1)S(1)} collective-permute-done((bf16[64,3584]{1,0:T(8,128)(2,1)S(1)}, bf16[64,3584]{1,0:T(8,128)(2,1)S(1)}, u32[]{:S(2)}, u32[]{:S(2)}) %collective-permute-start.2) | collective-permute-done | bytes 458784 | tf_op jit(solution)/shard_map/ppermute | solution.py:414
  20.0 1.6 %collective-permute-start.5 = (bf16[32,3584]{1,0:T(8,128)(2,1)S(1)}, bf16[32,3584]{1,0:T(8,128)(2,1)S(1)}, u32[]{:S(2)}, u32[]{:S(2)}) collective-permute-start(bf16[32,3584]{1,0:T(8,128)(2,1)S(1)} %slice.63), channel_id=1, source_target_pairs={{0,1},{1,0},{2,3},{3,2},{4,5},{5,4},{6,7},{7,6},{8,9},{9,8},{10,11... | collective-permute-start | bytes 688136 | tf_op jit(solution)/shard_map/ppermute | solution.py:377
  22.7 1.5 collective-permute-start.6
  24.2 10.7 %round_logits.4 = (bf16[192,2048]{1,0:T(8,128)(2,1)}, f32[16,128]{1,0:T(8,128)S(1)}) custom-call(bf16[64,3584]{1,0:T(8,128)(2,1)S(1)} %fusion.2.refs_0_, bf16[64,3584]{1,0:T(8,128)(2,1)S(1)} %collective-permute-done.4.refs_1_, bf16[64,3584]{1,0:T(8,128)(2,1)S(1)} %collective-permute-done.refs_2_, bf16[3584,2048]{1,0:T(8,128)(2,1)} %refs_7_.1, ...), custom_call_target="tpu_custom_call" | custom-call | flops 2818572288 | bytes 14680064 | tf_op jit(solution)/shard_map/round_logits/pallas_call | solution.py:144
  34.9 1.3 collective-permute-start.8
  36.2 1.5 collective-permute-start.12
  38.3 1.6 %collective-permute-start.9 = (bf16[32,3584]{1,0:T(8,128)(2,1)S(1)}, bf16[32,3584]{1,0:T(8,128)(2,1)S(1)}, u32[]{:S(2)}, u32[]{:S(2)}) collective-permute-start(bf16[32,3584]{1,0:T(8,128)(2,1)S(1)} %slice.50), channel_id=1, source_target_pairs={{0,16},{8,24},{16,0},{24,8},{1,17},{9,25},{17,1},{25,9},{2,18},{10... | collective-permute-start | bytes 688136 | tf_op jit(solution)/shard_map/ppermute | solution.py:371
  40.4 11.6 %round_logits.5 = (bf16[256,2048]{1,0:T(8,128)(2,1)}, f32[16,128]{1,0:T(8,128)S(1)}) custom-call(bf16[32,3584]{1,0:T(8,128)(2,1)S(1)} %collective-permute-done.1.refs_0_.refs_3_, bf16[32,3584]{1,0:T(8,128)(2,1)S(1)} %collective-permute-done.5.refs_1_.refs_4_, bf16[64,3584]{1,0:T(8,128)(2,1)S(1)} %collective-permute-done.2.refs_2_.refs_5_, ...), custom_call_target="tpu_custom_call" | custom-call | flops 3758096384 | bytes 14680064 | tf_op jit(solution)/shard_map/round_logits/pallas_call | solution.py:144
  52.1 2.0 %turned_features.2 = (bf16[896,512]{1,0:T(8,128)(2,1)S(1)}, bf16[896,512]{1,0:T(8,128)(2,1)}) custom-call(s32[1]{0:T(128)} %bitcast.rep_ref, bf16[64,3584]{1,0:T(8,128)(2,1)S(1)} %fusion.2.refs_0_, bf16[64,3584]{1,0:T(8,128)(2,1)S(1)} %collective-permute-done.4.refs_1_, bf16[64,3584]{1,0:T(8,128)(2,1)S(1)} %collective-permute-done.refs_2_, ...), custom_call_target="tpu_custom_call" | custom-call | bytes 3670016 | tf_op jit(solution)/shard_map/turned_features/pallas_call | solution.py:193
  54.1 1.0 copy-done.14
  55.5 0.6 gather_fusion
  56.2 1.5 collective-permute-start.19
  58.3 0.6 collective-permute-start.17
  58.9 1.5 collective-permute-start.13
  60.4 0.9 copy-done.1
  61.3 10.6 %round_logits.6 = (bf16[256,2048]{1,0:T(8,128)(2,1)S(1)}, f32[16,128]{1,0:T(8,128)S(1)}) custom-call(bf16[32,3584]{1,0:T(8,128)(2,1)S(1)} %collective-permute-done.9.refs_8_.refs_0_, bf16[32,3584]{1,0:T(8,128)(2,1)S(1)} %copy-done.1, bf16[64,3584]{1,0:T(8,128)(2,1)S(1)} %collective-permute-done.3.refs_2_.refs_0_, ...), custom_call_target="tpu_custom_call" | custom-call | flops 3758096384 | bytes 14680064 | tf_op jit(solution)/shard_map/round_logits/pallas_call | solution.py:144
  71.9 1.0 copy-done.12
  72.9 1.4 collective-permute-done.17.refs_1_.refs_4_
  74.3 1.2 collective-permute-done.13.refs_0_.refs_3_
  77.2 1.2 copy-done.15
  78.4 11.4 %one_hot_sums.2 = (bf16[896,2048]{1,0:T(8,128)(2,1)S(1)}, bf16[896,2048]{1,0:T(8,128)(2,1)S(1)}) custom-call(bf16[896,512]{1,0:T(8,128)(2,1)S(1)} %copy-done.15, bf16[896,512]{1,0:T(8,128)(2,1)} %collective-permute-done.14.refs_1_.refs_2_, s32[1,1024]{1,0:T(1,128)S(1)} %squeeze.6.refs_2_, s32[1,1024]{1,0:T(1,128)S(1)} %squeeze.7.refs_3_), custom_call_target="tpu_custom_call" | custom-call | flops 7516192768 | bytes 9175040 | tf_op jit(solution)/shard_map/one_hot_sums/pallas_call | solution.py:246
  89.9 1.8 %copy-done.21 = bf16[896,2048]{1,0:T(8,128)(2,1)} copy-done((bf16[896,2048]{1,0:T(8,128)(2,1)}, bf16[896,2048]{1,0:T(8,128)(2,1)S(1)}, u32[]{:S(2)}) %copy-start.21) | copy-done | bytes 3670040
  91.7 1.8 %copy-done.23 = bf16[896,2048]{1,0:T(8,128)(2,1)} copy-done((bf16[896,2048]{1,0:T(8,128)(2,1)}, bf16[896,2048]{1,0:T(8,128)(2,1)S(1)}, u32[]{:S(2)}) %copy-start.23) | copy-done | bytes 3670040
  93.6 11.3 %round_logits.7 = (bf16[320,2048]{1,0:T(8,128)(2,1)S(1)}, f32[16,128]{1,0:T(8,128)S(1)}) custom-call(bf16[32,3584]{1,0:T(8,128)(2,1)S(1)} %copy-done.7, bf16[32,3584]{1,0:T(8,128)(2,1)S(1)} %copy-done.5, bf16[64,3584]{1,0:T(8,128)(2,1)S(1)} %copy-done.3, bf16[64,3584]{1,0:T(8,128)(2,1)S(1)} %collective-permute-done.18.refs_3_.refs_6_, ...), custom_call_target="tpu_custom_call" | custom-call | flops 4697620480 | bytes 14680064 | tf_op jit(solution)/shard_map/round_logits/pallas_call | solution.py:144
  104.9 0.6 collective-permute-start.24
  105.5 1.0 collective-permute-start.23
  107.1 1.1 turned_features.3
  108.2 0.9 copy-done.17
  109.2 0.9 copy-done.20
  111.3 1.4 merged_stats.1.refs_12_
  113.2 1.5 %collective-permute-start.30 = (f32[48,128]{1,0:T(8,128)}, f32[48,128]{1,0:T(8,128)S(1)}, u32[]{:S(2)}, u32[]{:S(2)}) collective-permute-start(f32[48,128]{1,0:T(8,128)} %merged_stats.1.refs_12_), channel_id=1, source_target_pairs={{0,2},{1,3},{2,4},{3,5},{4,6},{5,7},{6,0},{7,1},{8,10},{9,11},{10,... | collective-permute-start | bytes 73736 | tf_op jit(solution)/shard_map/ppermute | solution.py:449
  114.8 2.6 %collective-permute-start.29 = (f32[48,128]{1,0:T(8,128)}, f32[48,128]{1,0:T(8,128)S(1)}, u32[]{:S(2)}, u32[]{:S(2)}) collective-permute-start(f32[48,128]{1,0:T(8,128)} %merged_stats.1.refs_12_), channel_id=1, source_target_pairs={{0,4},{1,5},{2,6},{3,7},{4,0},{5,1},{6,2},{7,3},{8,12},{9,13},{10,... | collective-permute-start | bytes 73736 | tf_op jit(solution)/shard_map/ppermute | solution.py:449
  117.4 1.9 %collective-permute-start.28 = (f32[48,128]{1,0:T(8,128)}, f32[48,128]{1,0:T(8,128)S(1)}, u32[]{:S(2)}, u32[]{:S(2)}) collective-permute-start(f32[48,128]{1,0:T(8,128)} %merged_stats.1.refs_12_), channel_id=1, source_target_pairs={{0,6},{1,7},{2,0},{3,1},{4,2},{5,3},{6,4},{7,5},{8,14},{9,15},{10,... | collective-permute-start | bytes 73736 | tf_op jit(solution)/shard_map/ppermute | solution.py:449
  119.3 1.2 copy-done.18
  120.4 2.0 %copy-done.22 = bf16[896,2048]{1,0:T(8,128)(2,1)S(1)} copy-done((bf16[896,2048]{1,0:T(8,128)(2,1)S(1)}, bf16[896,2048]{1,0:T(8,128)(2,1)}, u32[]{:S(2)}) %copy-start.22) | copy-done | bytes 3670040
  122.5 2.0 %copy-done.24 = bf16[896,2048]{1,0:T(8,128)(2,1)S(1)} copy-done((bf16[896,2048]{1,0:T(8,128)(2,1)S(1)}, bf16[896,2048]{1,0:T(8,128)(2,1)}, u32[]{:S(2)}) %copy-start.24) | copy-done | bytes 3670040
  124.5 11.4 %one_hot_sums.3 = (bf16[896,2048]{1,0:T(8,128)(2,1)S(1)}, bf16[896,2048]{1,0:T(8,128)(2,1)S(1)}) custom-call(bf16[896,512]{1,0:T(8,128)(2,1)S(1)} %copy-done.18, bf16[896,512]{1,0:T(8,128)(2,1)S(1)} %collective-permute-done.25.refs_1_.refs_3_, s32[1,1024]{1,0:T(1,128)S(1)} %unstack.13.refs_2_, s32[1,1024]{1,0:T(1,128)S(1)} %unstack.15.refs_3_, ...), custom_call_target="tpu_custom_call" | custom-call | flops 7516192768 | bytes 9175040 | tf_op jit(solution)/shard_map/one_hot_sums/pallas_call | solution.py:246
  136.0 17.5 %refresh_states.1 = (bf16[896,2048]{1,0:T(8,128)(2,1)}, bf16[896,2048]{1,0:T(8,128)(2,1)}, bf16[896,2048]{1,0:T(8,128)(2,1)}) custom-call(bf16[896,512]{1,0:T(8,128)(2,1)S(1)} %copy-done.16, bf16[896,512]{1,0:T(8,128)(2,1)S(1)} %copy-done.19, bf16[896,512]{1,0:T(8,128)(2,1)} %collective-permute-done.14.refs_1_.refs_2_, ...), custom_call_target="tpu_custom_call" | custom-call | flops 7516192768 | bytes 37748736 | tf_op jit(solution)/shard_map/refresh_states/pallas_call | solution.py:312
  (118 shorter events, 7.9 us)
Async XLA Ops:
  3.1 16.9 %collective-permute-start.4 = (bf16[64,3584]{1,0:T(8,128)(2,1)S(1)}, bf16[64,3584]{1,0:T(8,128)(2,1)S(1)}, u32[]{:S(2)}, u32[]{:S(2)}) collective-permute-start(bf16[64,3584]{1,0:T(8,128)(2,1)S(1)} %fusion.2.refs_0_), channel_id=1, source_target_pairs={{0,16},{8,24},{16,0},{24,8},{1,17},{9,25},{17,1},{25,9},{2,18},{10... | collective-permute-start | bytes 1376264 | tf_op jit(solution)/shard_map/ppermute | solution.py:371
  6.1 13.8 %collective-permute-start.2 = (bf16[64,3584]{1,0:T(8,128)(2,1)S(1)}, bf16[64,3584]{1,0:T(8,128)(2,1)S(1)}, u32[]{:S(2)}, u32[]{:S(2)}) collective-permute-start(bf16[64,3584]{1,0:T(8,128)(2,1)S(1)} %fusion.2.refs_0_), channel_id=1, source_target_pairs={{0,2},{1,3},{2,4},{3,5},{4,6},{5,7},{6,0},{7,1},{8,10},{9,11},{10,... | collective-permute-start | bytes 1376264 | tf_op jit(solution)/shard_map/ppermute | solution.py:414
  7.6 13.9 %collective-permute-start = (bf16[64,3584]{1,0:T(8,128)(2,1)S(1)}, bf16[64,3584]{1,0:T(8,128)(2,1)S(1)}, u32[]{:S(2)}, u32[]{:S(2)}) collective-permute-start(bf16[64,3584]{1,0:T(8,128)(2,1)S(1)} %fusion.2.refs_0_), channel_id=1, source_target_pairs={{0,1},{1,0},{2,3},{3,2},{4,5},{5,4},{6,7},{7,6},{8,9},{9,8},{10,11... | collective-permute-start | bytes 1376264 | tf_op jit(solution)/shard_map/ppermute | solution.py:377
  19.9 15.0 %collective-permute-start.3 = (bf16[64,3584]{1,0:T(8,128)(2,1)S(1)}, bf16[64,3584]{1,0:T(8,128)(2,1)S(1)}, u32[]{:S(2)}, u32[]{:S(2)}) collective-permute-start(bf16[64,3584]{1,0:T(8,128)(2,1)S(1)} %collective-permute-done.2.refs_2_.refs_5_), channel_id=1, source_target_pairs={{0,2},{1,3},{2,4},{3,5},{4,6},{5,7},{6,0},{7,1},{8,10},{9,11},{10,... | collective-permute-start | bytes 1376264 | tf_op jit(solution)/shard_map/ppermute | solution.py:414
  20.0 17.8 %collective-permute-start.5 = (bf16[32,3584]{1,0:T(8,128)(2,1)S(1)}, bf16[32,3584]{1,0:T(8,128)(2,1)S(1)}, u32[]{:S(2)}, u32[]{:S(2)}) collective-permute-start(bf16[32,3584]{1,0:T(8,128)(2,1)S(1)} %slice.63), channel_id=1, source_target_pairs={{0,1},{1,0},{2,3},{3,2},{4,5},{5,4},{6,7},{7,6},{8,9},{9,8},{10,11... | collective-permute-start | bytes 688136 | tf_op jit(solution)/shard_map/ppermute | solution.py:377
  21.6 14.6 %collective-permute-start.1 = (bf16[32,3584]{1,0:T(8,128)(2,1)S(1)}, bf16[32,3584]{1,0:T(8,128)(2,1)S(1)}, u32[]{:S(2)}, u32[]{:S(2)}) collective-permute-start(bf16[32,3584]{1,0:T(8,128)(2,1)S(1)} %slice.62), channel_id=1, source_target_pairs={{0,16},{8,24},{16,0},{24,8},{1,17},{9,25},{17,1},{25,9},{2,18},{10... | collective-permute-start | bytes 688136 | tf_op jit(solution)/shard_map/ppermute | solution.py:371
  22.2 16.1 %collective-permute-start.7 = (bf16[64,3584]{1,0:T(8,128)(2,1)S(1)}, bf16[64,3584]{1,0:T(8,128)(2,1)S(1)}, u32[]{:S(2)}, u32[]{:S(2)}) collective-permute-start(bf16[64,3584]{1,0:T(8,128)(2,1)S(1)} %collective-permute-done.2.refs_2_.refs_5_), channel_id=1, source_target_pairs={{0,1},{1,0},{2,3},{3,2},{4,5},{5,4},{6,7},{7,6},{8,9},{9,8},{10,11... | collective-permute-start | bytes 1376264 | tf_op jit(solution)/shard_map/ppermute | solution.py:377
  22.7 15.6 %collective-permute-start.6 = (bf16[64,3584]{1,0:T(8,128)(2,1)S(1)}, bf16[64,3584]{1,0:T(8,128)(2,1)S(1)}, u32[]{:S(2)}, u32[]{:S(2)}) collective-permute-start(bf16[64,3584]{1,0:T(8,128)(2,1)S(1)} %collective-permute-done.2.refs_2_.refs_5_), channel_id=1, source_target_pairs={{0,16},{8,24},{16,0},{24,8},{1,17},{9,25},{17,1},{25,9},{2,18},{10... | collective-permute-start | bytes 1376264 | tf_op jit(solution)/shard_map/ppermute | solution.py:371
  34.9 17.1 %collective-permute-start.8 = (bf16[64,3584]{1,0:T(8,128)(2,1)S(1)}, bf16[64,3584]{1,0:T(8,128)(2,1)S(1)}, u32[]{:S(2)}, u32[]{:S(2)}) collective-permute-start(bf16[64,3584]{1,0:T(8,128)(2,1)S(1)} %collective-permute-done.3.refs_2_.refs_0_), channel_id=1, source_target_pairs={{0,2},{1,3},{2,4},{3,5},{4,6},{5,7},{6,0},{7,1},{8,10},{9,11},{10,... | collective-permute-start | bytes 1376264 | tf_op jit(solution)/shard_map/ppermute | solution.py:414
  36.2 22.0 %collective-permute-start.12 = (bf16[64,3584]{1,0:T(8,128)(2,1)S(1)}, bf16[64,3584]{1,0:T(8,128)(2,1)S(1)}, u32[]{:S(2)}, u32[]{:S(2)}) collective-permute-start(bf16[64,3584]{1,0:T(8,128)(2,1)S(1)} %collective-permute-done.3.refs_2_.refs_0_), channel_id=1, source_target_pairs={{0,1},{1,0},{2,3},{3,2},{4,5},{5,4},{6,7},{7,6},{8,9},{9,8},{10,11... | collective-permute-start | bytes 1376264 | tf_op jit(solution)/shard_map/ppermute | solution.py:377
  37.7 20.5 %collective-permute-start.11 = (bf16[64,3584]{1,0:T(8,128)(2,1)S(1)}, bf16[64,3584]{1,0:T(8,128)(2,1)S(1)}, u32[]{:S(2)}, u32[]{:S(2)}) collective-permute-start(bf16[64,3584]{1,0:T(8,128)(2,1)S(1)} %collective-permute-done.3.refs_2_.refs_0_), channel_id=1, source_target_pairs={{0,16},{8,24},{16,0},{24,8},{1,17},{9,25},{17,1},{25,9},{2,18},{10... | collective-permute-start | bytes 1376264 | tf_op jit(solution)/shard_map/ppermute | solution.py:371
  38.3 13.8 %collective-permute-start.9 = (bf16[32,3584]{1,0:T(8,128)(2,1)S(1)}, bf16[32,3584]{1,0:T(8,128)(2,1)S(1)}, u32[]{:S(2)}, u32[]{:S(2)}) collective-permute-start(bf16[32,3584]{1,0:T(8,128)(2,1)S(1)} %slice.50), channel_id=1, source_target_pairs={{0,16},{8,24},{16,0},{24,8},{1,17},{9,25},{17,1},{25,9},{2,18},{10... | collective-permute-start | bytes 688136 | tf_op jit(solution)/shard_map/ppermute | solution.py:371
  39.9 12.3 %collective-permute-start.10 = (bf16[32,3584]{1,0:T(8,128)(2,1)S(1)}, bf16[32,3584]{1,0:T(8,128)(2,1)S(1)}, u32[]{:S(2)}, u32[]{:S(2)}) collective-permute-start(bf16[32,3584]{1,0:T(8,128)(2,1)S(1)} %slice.51), channel_id=1, source_target_pairs={{0,1},{1,0},{2,3},{3,2},{4,5},{5,4},{6,7},{7,6},{8,9},{9,8},{10,11... | collective-permute-start | bytes 688136 | tf_op jit(solution)/shard_map/ppermute | solution.py:377
  52.0 3.1 %copy-start.2 = (bf16[64,3584]{1,0:T(8,128)(2,1)}, bf16[64,3584]{1,0:T(8,128)(2,1)S(1)}, u32[]{:S(2)}) copy-start(bf16[64,3584]{1,0:T(8,128)(2,1)S(1)} %collective-permute-done.8.refs_2_.refs_5_) | copy-start | bytes 1376260
  52.1 2.0 %copy-start = (bf16[32,3584]{1,0:T(8,128)(2,1)}, bf16[32,3584]{1,0:T(8,128)(2,1)S(1)}, u32[]{:S(2)}) copy-start(bf16[32,3584]{1,0:T(8,128)(2,1)S(1)} %collective-permute-done.10.refs_9_.refs_1_) | copy-start | bytes 688132
  55.1 22.2 %collective-permute-start.14 = (bf16[896,512]{1,0:T(8,128)(2,1)}, bf16[896,512]{1,0:T(8,128)(2,1)}, u32[]{:S(2)}, u32[]{:S(2)}) collective-permute-start(bf16[896,512]{1,0:T(8,128)(2,1)} %get-tuple-element.50), channel_id=1, source_target_pairs={{0,8},{8,0},{16,24},{24,16},{1,9},{9,1},{17,25},{25,17},{2,10},{10... | collective-permute-start | bytes 2752520 | tf_op jit(solution)/shard_map/ppermute | solution.py:374
  56.2 19.3 %collective-permute-start.19 = (bf16[64,3584]{1,0:T(8,128)(2,1)}, bf16[64,3584]{1,0:T(8,128)(2,1)S(1)}, u32[]{:S(2)}, u32[]{:S(2)}) collective-permute-start(bf16[64,3584]{1,0:T(8,128)(2,1)} %copy-done.2), channel_id=1, source_target_pairs={{0,1},{1,0},{2,3},{3,2},{4,5},{5,4},{6,7},{7,6},{8,9},{9,8},{10,11... | collective-permute-start | bytes 1376264 | tf_op jit(solution)/shard_map/ppermute | solution.py:377
  57.7 17.8 %collective-permute-start.18 = (bf16[64,3584]{1,0:T(8,128)(2,1)}, bf16[64,3584]{1,0:T(8,128)(2,1)S(1)}, u32[]{:S(2)}, u32[]{:S(2)}) collective-permute-start(bf16[64,3584]{1,0:T(8,128)(2,1)} %copy-done.2), channel_id=1, source_target_pairs={{0,16},{8,24},{16,0},{24,8},{1,17},{9,25},{17,1},{25,9},{2,18},{10... | collective-permute-start | bytes 1376264 | tf_op jit(solution)/shard_map/ppermute | solution.py:371
  58.3 16.0 %collective-permute-start.17 = (bf16[32,3584]{1,0:T(8,128)(2,1)S(1)}, bf16[32,3584]{1,0:T(8,128)(2,1)S(1)}, u32[]{:S(2)}, u32[]{:S(2)}) collective-permute-start(bf16[32,3584]{1,0:T(8,128)(2,1)S(1)} %slice.57), channel_id=1, source_target_pairs={{0,1},{1,0},{2,3},{3,2},{4,5},{5,4},{6,7},{7,6},{8,9},{9,8},{10,11... | collective-permute-start | bytes 688136 | tf_op jit(solution)/shard_map/ppermute | solution.py:377
  58.9 16.6 %collective-permute-start.13 = (bf16[32,3584]{1,0:T(8,128)(2,1)S(1)}, bf16[32,3584]{1,0:T(8,128)(2,1)S(1)}, u32[]{:S(2)}, u32[]{:S(2)}) collective-permute-start(bf16[32,3584]{1,0:T(8,128)(2,1)S(1)} %slice.52), channel_id=1, source_target_pairs={{0,16},{8,24},{16,0},{24,8},{1,17},{9,25},{17,1},{25,9},{2,18},{10... | collective-permute-start | bytes 688136 | tf_op jit(solution)/shard_map/ppermute | solution.py:371
  74.3 1.3 copy-start.4
  74.3 19.3 %collective-permute-start.16 = (bf16[256,2048]{1,0:T(8,128)(2,1)}, bf16[256,2048]{1,0:T(8,128)(2,1)}, u32[]{:S(2)}, u32[]{:S(2)}) collective-permute-start(bf16[256,2048]{1,0:T(8,128)(2,1)} %get-tuple-element.59.refs_5_), channel_id=1, source_target_pairs={{0,8},{8,0},{16,24},{24,16},{1,9},{9,1},{17,25},{25,17},{2,10},{10... | collective-permute-start | bytes 3145736 | tf_op jit(solution)/shard_map/ppermute | solution.py:374
  75.4 18.1 %collective-permute-start.15 = (bf16[192,2048]{1,0:T(8,128)(2,1)}, bf16[192,2048]{1,0:T(8,128)(2,1)}, u32[]{:S(2)}, u32[]{:S(2)}) collective-permute-start(bf16[192,2048]{1,0:T(8,128)(2,1)} %get-tuple-element.58.refs_4_), channel_id=1, source_target_pairs={{0,8},{8,0},{16,24},{24,16},{1,9},{9,1},{17,25},{25,17},{2,10},{10... | collective-permute-start | bytes 2359304 | tf_op jit(solution)/shard_map/ppermute | solution.py:374
  76.1 17.4 %copy-start.3 = (bf16[64,3584]{1,0:T(8,128)(2,1)S(1)}, bf16[64,3584]{1,0:T(8,128)(2,1)}, u32[]{:S(2)}) copy-start(bf16[64,3584]{1,0:T(8,128)(2,1)} %copy-done.2) | copy-start | bytes 1376260
  76.1 17.4 %copy-start.5 = (bf16[32,3584]{1,0:T(8,128)(2,1)S(1)}, bf16[32,3584]{1,0:T(8,128)(2,1)}, u32[]{:S(2)}) copy-start(bf16[32,3584]{1,0:T(8,128)(2,1)} %copy-done.4) | copy-start | bytes 688132
  76.1 17.4 %collective-permute-start.20 = (bf16[32,3584]{1,0:T(8,128)(2,1)S(1)}, bf16[32,3584]{1,0:T(8,128)(2,1)S(1)}, u32[]{:S(2)}, u32[]{:S(2)}) collective-permute-start(bf16[32,3584]{1,0:T(8,128)(2,1)S(1)} %slice.58), channel_id=1, source_target_pairs={{0,16},{8,24},{16,0},{24,8},{1,17},{9,25},{17,1},{25,9},{2,18},{10... | collective-permute-start | bytes 688136 | tf_op jit(solution)/shard_map/ppermute | solution.py:371
  76.7 16.9 %copy-start.7 = (bf16[32,3584]{1,0:T(8,128)(2,1)S(1)}, bf16[32,3584]{1,0:T(8,128)(2,1)}, u32[]{:S(2)}) copy-start(bf16[32,3584]{1,0:T(8,128)(2,1)} %copy-done.6) | copy-start | bytes 688132
  76.7 16.9 %collective-permute-start.21 = (bf16[32,3584]{1,0:T(8,128)(2,1)S(1)}, bf16[32,3584]{1,0:T(8,128)(2,1)S(1)}, u32[]{:S(2)}, u32[]{:S(2)}) collective-permute-start(bf16[32,3584]{1,0:T(8,128)(2,1)S(1)} %slice.59), channel_id=1, source_target_pairs={{0,1},{1,0},{2,3},{3,2},{4,5},{5,4},{6,7},{7,6},{8,9},{9,8},{10,11... | collective-permute-start | bytes 688136 | tf_op jit(solution)/shard_map/ppermute | solution.py:377
  89.9 1.8 %copy-start.21 = (bf16[896,2048]{1,0:T(8,128)(2,1)}, bf16[896,2048]{1,0:T(8,128)(2,1)S(1)}, u32[]{:S(2)}) copy-start(bf16[896,2048]{1,0:T(8,128)(2,1)S(1)} %get-tuple-element.56.refs_4_) | copy-start | bytes 11010052
  91.7 1.8 %copy-start.23 = (bf16[896,2048]{1,0:T(8,128)(2,1)}, bf16[896,2048]{1,0:T(8,128)(2,1)S(1)}, u32[]{:S(2)}) copy-start(bf16[896,2048]{1,0:T(8,128)(2,1)S(1)} %get-tuple-element.57.refs_5_) | copy-start | bytes 11010052
  104.9 5.2 %copy-start.10 = (bf16[320,2048]{1,0:T(8,128)(2,1)}, bf16[320,2048]{1,0:T(8,128)(2,1)S(1)}, u32[]{:S(2)}) copy-start(bf16[320,2048]{1,0:T(8,128)(2,1)S(1)} %get-tuple-element.72.refs_7_) | copy-start | bytes 3932164
  104.9 5.3 %copy-start.9 = (f32[16,128]{1,0:T(8,128)}, f32[16,128]{1,0:T(8,128)S(1)}, u32[]{:S(2)}) copy-start(f32[16,128]{1,0:T(8,128)S(1)} %get-tuple-element.65.own_ref) | copy-start | bytes 24580
  104.9 5.2 %collective-permute-start.24 = (f32[16,128]{1,0:T(8,128)S(1)}, f32[16,128]{1,0:T(8,128)S(1)}, u32[]{:S(2)}, u32[]{:S(2)}) collective-permute-start(f32[16,128]{1,0:T(8,128)S(1)} %get-tuple-element.65.own_ref), channel_id=1, source_target_pairs={{0,9},{1,8},{2,11},{3,10},{4,13},{5,12},{6,15},{7,14},{8,1},{9,0},... | collective-permute-start | bytes 24584 | tf_op jit(solution)/shard_map/ppermute | solution.py:384
  105.5 4.6 %collective-permute-start.23 = (f32[16,128]{1,0:T(8,128)S(1)}, f32[16,128]{1,0:T(8,128)S(1)}, u32[]{:S(2)}, u32[]{:S(2)}) collective-permute-start(f32[16,128]{1,0:T(8,128)S(1)} %get-tuple-element.65.own_ref), channel_id=1, source_target_pairs={{0,8},{8,0},{16,24},{24,16},{1,9},{9,1},{17,25},{25,17},{2,10},{10... | collective-permute-start | bytes 24584 | tf_op jit(solution)/shard_map/ppermute | solution.py:374
  106.6 3.7 %collective-permute-start.22 = (f32[16,128]{1,0:T(8,128)S(1)}, f32[16,128]{1,0:T(8,128)S(1)}, u32[]{:S(2)}, u32[]{:S(2)}) collective-permute-start(f32[16,128]{1,0:T(8,128)S(1)} %get-tuple-element.65.own_ref), channel_id=1, source_target_pairs={{0,1},{1,0},{2,3},{3,2},{4,5},{5,4},{6,7},{7,6},{8,9},{9,8},{10,11... | collective-permute-start | bytes 24584 | tf_op jit(solution)/shard_map/ppermute | solution.py:377
  112.7 4.7 %collective-permute-start.25 = (bf16[896,512]{1,0:T(8,128)(2,1)}, bf16[896,512]{1,0:T(8,128)(2,1)S(1)}, u32[]{:S(2)}, u32[]{:S(2)}) collective-permute-start(bf16[896,512]{1,0:T(8,128)(2,1)} %copy-done.20), channel_id=1, source_target_pairs={{0,8},{8,0},{16,24},{24,16},{1,9},{9,1},{17,25},{25,17},{2,10},{10... | collective-permute-start | bytes 2752520 | tf_op jit(solution)/shard_map/ppermute | solution.py:374
  112.7 23.3 %collective-permute-start.27 = (bf16[320,2048]{1,0:T(8,128)(2,1)}, bf16[320,2048]{1,0:T(8,128)(2,1)S(1)}, u32[]{:S(2)}, u32[]{:S(2)}) collective-permute-start(bf16[320,2048]{1,0:T(8,128)(2,1)} %copy-done.10), channel_id=1, source_target_pairs={{0,8},{8,0},{16,24},{24,16},{1,9},{9,1},{17,25},{25,17},{2,10},{10... | collective-permute-start | bytes 3932168 | tf_op jit(solution)/shard_map/ppermute | solution.py:374
  113.2 22.8 %collective-permute-start.26 = (bf16[256,2048]{1,0:T(8,128)(2,1)}, bf16[256,2048]{1,0:T(8,128)(2,1)S(1)}, u32[]{:S(2)}, u32[]{:S(2)}) collective-permute-start(bf16[256,2048]{1,0:T(8,128)(2,1)} %copy-done.12), channel_id=1, source_target_pairs={{0,8},{8,0},{16,24},{24,16},{1,9},{9,1},{17,25},{25,17},{2,10},{10... | collective-permute-start | bytes 3145736 | tf_op jit(solution)/shard_map/ppermute | solution.py:374
  113.2 22.7 %collective-permute-start.30 = (f32[48,128]{1,0:T(8,128)}, f32[48,128]{1,0:T(8,128)S(1)}, u32[]{:S(2)}, u32[]{:S(2)}) collective-permute-start(f32[48,128]{1,0:T(8,128)} %merged_stats.1.refs_12_), channel_id=1, source_target_pairs={{0,2},{1,3},{2,4},{3,5},{4,6},{5,7},{6,0},{7,1},{8,10},{9,11},{10,... | collective-permute-start | bytes 73736 | tf_op jit(solution)/shard_map/ppermute | solution.py:449
  114.8 21.2 %collective-permute-start.29 = (f32[48,128]{1,0:T(8,128)}, f32[48,128]{1,0:T(8,128)S(1)}, u32[]{:S(2)}, u32[]{:S(2)}) collective-permute-start(f32[48,128]{1,0:T(8,128)} %merged_stats.1.refs_12_), channel_id=1, source_target_pairs={{0,4},{1,5},{2,6},{3,7},{4,0},{5,1},{6,2},{7,3},{8,12},{9,13},{10,... | collective-permute-start | bytes 73736 | tf_op jit(solution)/shard_map/ppermute | solution.py:449
  117.4 18.6 %collective-permute-start.28 = (f32[48,128]{1,0:T(8,128)}, f32[48,128]{1,0:T(8,128)S(1)}, u32[]{:S(2)}, u32[]{:S(2)}) collective-permute-start(f32[48,128]{1,0:T(8,128)} %merged_stats.1.refs_12_), channel_id=1, source_target_pairs={{0,6},{1,7},{2,0},{3,1},{4,2},{5,3},{6,4},{7,5},{8,14},{9,15},{10,... | collective-permute-start | bytes 73736 | tf_op jit(solution)/shard_map/ppermute | solution.py:449
  120.4 2.0 %copy-start.22 = (bf16[896,2048]{1,0:T(8,128)(2,1)S(1)}, bf16[896,2048]{1,0:T(8,128)(2,1)}, u32[]{:S(2)}) copy-start(bf16[896,2048]{1,0:T(8,128)(2,1)} %copy-done.21) | copy-start | bytes 11010052
  122.5 2.0 %copy-start.24 = (bf16[896,2048]{1,0:T(8,128)(2,1)S(1)}, bf16[896,2048]{1,0:T(8,128)(2,1)}, u32[]{:S(2)}) copy-start(bf16[896,2048]{1,0:T(8,128)(2,1)} %copy-done.23) | copy-start | bytes 11010052
  124.5 11.5 %copy-start.8 = (f32[48,128]{1,0:T(8,128)S(1)}, f32[48,128]{1,0:T(8,128)}, u32[]{:S(2)}) copy-start(f32[48,128]{1,0:T(8,128)} %merged_stats.1.refs_12_) | copy-start | bytes 73732
  124.5 11.5 %copy-start.11 = (bf16[320,2048]{1,0:T(8,128)(2,1)S(1)}, bf16[320,2048]{1,0:T(8,128)(2,1)}, u32[]{:S(2)}) copy-start(bf16[320,2048]{1,0:T(8,128)(2,1)} %copy-done.10) | copy-start | bytes 3932164
  124.5 11.5 %copy-start.13 = (bf16[256,2048]{1,0:T(8,128)(2,1)S(1)}, bf16[256,2048]{1,0:T(8,128)(2,1)}, u32[]{:S(2)}) copy-start(bf16[256,2048]{1,0:T(8,128)(2,1)} %copy-done.12) | copy-start | bytes 3145732
  124.5 11.5 %copy-start.16 = (bf16[896,512]{1,0:T(8,128)(2,1)S(1)}, bf16[896,512]{1,0:T(8,128)(2,1)}, u32[]{:S(2)}) copy-start(bf16[896,512]{1,0:T(8,128)(2,1)} %copy-done.14) | copy-start | bytes 2752516
  124.5 11.5 %copy-start.19 = (bf16[896,512]{1,0:T(8,128)(2,1)S(1)}, bf16[896,512]{1,0:T(8,128)(2,1)}, u32[]{:S(2)}) copy-start(bf16[896,512]{1,0:T(8,128)(2,1)} %copy-done.17) | copy-start | bytes 2752516
  (11 other events, 9.6 us)

commit v2 on v1

--- a/solution.py
+++ b/solution.py
@@ -13,6 +13,8 @@
 BETA_TWO = 0.95
 RHO_SCALE = 0.05
 GATHER_BYTES = 32 * 1024 * 1024
+BANDS = 4
+BRIEF = pl.CostEstimate(flops=1024, bytes_accessed=1024, transcendentals=0)
 
 
 def normalize(hidden, norm_gain):
@@ -85,10 +87,11 @@
 
 def logits_kernel(start, sizes, *refs):
     block_refs, refs = refs[:len(sizes)], refs[len(sizes):]
-    weight_ref, before_ref, exp_ref, stats_ref, tokens, logits, highs, sums = refs
+    weight_refs, refs = refs[:BANDS], refs[BANDS:]
+    before_ref, exp_ref, stats_ref, tokens, logits, highs, sums = refs
     step = pl.program_id(0)
     count, columns = logits.shape
-    width = weight_ref.shape[1]
+    depth, width = weight_refs[0].shape
     shift = start % 128
     half = stats_ref.shape[0] // 2
 
@@ -100,7 +103,13 @@
             place += size
         highs[...] = jnp.full(highs.shape, -jnp.inf, jnp.float32)
 
-    tile = jnp.dot(tokens[...], weight_ref[...], preferred_element_type=jnp.float32)
+    tile = sum(
+        jnp.dot(
+            tokens[:, band * depth:(band + 1) * depth], ref[...],
+            preferred_element_type=jnp.float32,
+        )
+        for band, ref in enumerate(weight_refs)
+    )
     logits[:, pl.ds(pl.multiple_of(step * width, 128), width)] = tile
     high = functools.reduce(
         jnp.maximum, [tile[:, lane:lane + 128] for lane in range(0, width, 128)]
@@ -145,7 +154,11 @@
         functools.partial(logits_kernel, start, sizes),
         grid=(columns // width,),
         in_specs=[whole(block) for block in blocks]
-        + [pl.BlockSpec((depth, width), lambda step: (0, step)), whole(before)],
+        + [
+            pl.BlockSpec((depth // BANDS, width), lambda step, band=band: (band, step))
+            for band in range(BANDS)
+        ]
+        + [whole(before)],
         out_specs=[pl.BlockSpec((count, columns), lambda step: (0, 0)), whole(before)],
         out_shape=[
             jax.ShapeDtypeStruct((count, columns), jnp.bfloat16),
@@ -157,14 +170,10 @@
             pltpu.VMEM((spread, 128), jnp.float32),
             pltpu.VMEM((spread, 128), jnp.float32),
         ],
-        compiler_params=pltpu.CompilerParams(vmem_limit_bytes=40 * 1024 * 1024),
-        cost_estimate=pl.CostEstimate(
-            flops=2 * count * depth * columns,
-            bytes_accessed=2 * depth * columns,
-            transcendentals=count * columns,
-        ),
+        compiler_params=pltpu.CompilerParams(vmem_limit_bytes=26 * 1024 * 1024),
+        cost_estimate=BRIEF,
         name="round_logits",
-    )(*blocks, head_weight, before)
+    )(*blocks, *[head_weight] * BANDS, before)
 
 
 def turn_kernel(sizes, rep_ref, *refs):
@@ -204,9 +213,7 @@
         ),
         out_shape=[jax.ShapeDtypeStruct((rows, count), jnp.bfloat16)] * 2,
         compiler_params=pltpu.CompilerParams(vmem_limit_bytes=24 * 1024 * 1024),
-        cost_estimate=pl.CostEstimate(
-            flops=0, bytes_accessed=8 * rows * count, transcendentals=0
-        ),
+        cost_estimate=BRIEF,
         name="turned_features",
     )(rep, *blocks)
 
@@ -227,11 +234,13 @@
 
     tokens = part * count
     columns = step * width + lax.broadcasted_iota(jnp.int32, (width, tokens), 0)
-    for index, (ids_ref, out_ref) in enumerate(((true_ref, true_out), (sample_ref, sample_out))):
-        hot = (columns == ids_ref[...]).astype(jnp.float32).astype(jnp.bfloat16)
-        total = lax.dot_general(
-            features[...], hot, (((1,), (1,)), ((), ())), preferred_element_type=jnp.float32
-        )
+    hot = jnp.concatenate([columns == true_ref[...], columns == sample_ref[...]], axis=0)
+    totals = lax.dot_general(
+        features[...], hot.astype(jnp.float32).astype(jnp.bfloat16),
+        (((1,), (1,)), ((), ())), preferred_element_type=jnp.float32,
+    )
+    for index, out_ref in enumerate((true_out, sample_out)):
+        total = totals[:, index * width:(index + 1) * width]
         if before_refs:
             total += before_refs[index][...].astype(jnp.float32)
         out_ref[...] = total.astype(jnp.bfloat16)
@@ -251,11 +260,7 @@
         out_shape=[jax.ShapeDtypeStruct((rows, columns), jnp.bfloat16)] * 2,
         scratch_shapes=[pltpu.VMEM((rows, tokens), jnp.bfloat16)],
         compiler_params=pltpu.CompilerParams(vmem_limit_bytes=24 * 1024 * 1024),
-        cost_estimate=pl.CostEstimate(
-            flops=4 * rows * tokens * columns,
-            bytes_accessed=2 * rows * (tokens + 2 * columns),
-            transcendentals=0,
-        ),
+        cost_estimate=BRIEF,
         name="one_hot_sums",
     )(*features, *ids, *before)
 
@@ -320,11 +325,7 @@
         out_shape=[jax.ShapeDtypeStruct((rows, columns), jnp.bfloat16)] * 3,
         scratch_shapes=[pltpu.VMEM((rows, tokens), jnp.bfloat16)],
         compiler_params=pltpu.CompilerParams(vmem_limit_bytes=32 * 1024 * 1024),
-        cost_estimate=pl.CostEstimate(
-            flops=2 * rows * columns * tokens,
-            bytes_accessed=2 * (rows * tokens + tokens * columns + 7 * rows * columns),
-            transcendentals=0,
-        ),
+        cost_estimate=BRIEF,
         name="refresh_states",
     )(*features, *exps, *stats, *sums, moment, curvature)
 
@@ -400,58 +401,61 @@
     late_ids = ids[:, :, split:].reshape(2, 1, -1)
 
     rep_scalar = rep.astype(jnp.int32).reshape(1)
+    head_weight = pltpu.with_memory_space_constraint(head_weight, pltpu.HBM)
     stats = jnp.zeros((4 * lines, 128), jnp.float32)
-    block, waiting, start = normed, [], 0
-    quads, exps, other_exps, early, sums = [], [], [], None, None
+    block, start = normed, 0
+    quads, waiting, exps, done = [], [], [], []
     for turn in range(lines):
         final = turn + 1 == lines
-        if turn > 1:
-            block = after(block, exps[turn - 2])
         from_x = to_x(block)
         from_y = to_y(block)
         following = None
         if not final:
             following = lax.ppermute(block, "shard", shift_pairs(lines, 1, 0))
-        if exps:
-            from_x, from_y = lax.optimization_barrier((from_x, from_y, exps[-1], *waiting))[:2]
+        if turn > 0:
+            gates = (*done, *exps[-1:])
+            from_x, from_y = lax.optimization_barrier((from_x, from_y, *gates))[:2]
         first = to_x(from_y[:half])
         second = to_y(from_x[half:])
+        done = [first, second]
         quads.append([block, from_x, from_y, first, second])
-        blocks = waiting + [block, from_x, from_y]
-        gates = [following]
+        waiting = waiting + [block, from_x, from_y]
+        block = following
+        if turn + 1 < split:
+            waiting = waiting + done
+            continue
+        gates = [] if final else [following]
         if final:
-            blocks = blocks + [first, second]
-            gates = [*sums, *other_exps]
+            waiting = waiting + done
+            turns = sum(quads[split:], [])
+            turns[0] = after(turns[0], *sums)
+            late = turned_features(rep_scalar, turns, rows)
+            gates = [late[1]]
+            held = lax.optimization_barrier((*exps, late[0]))
+            other_exps = [to_core(exp) for exp in held[:-1]]
+            late = [late[0], to_core(late[1])]
         if turn == split:
-            turns = sum(quads[:split], [])
-            turns[0] = after(turns[0], exps[-1], following)
-            early = turned_features(rep_scalar, turns, rows)
-            gates.append(early[0])
-        blocks[0] = after(blocks[0], *gates)
-        exp, stats = round_logits(start, blocks, head_weight, stats)
+            early = turned_features(rep_scalar, sum(quads[:split], []), rows)
+            gates.append(early[1])
+        waiting[0] = after(waiting[0], *gates)
+        exp, stats = round_logits(start, waiting, head_weight, stats)
         exps.append(exp)
         start += exp.shape[0]
         if turn == split:
             early = [early[0], to_core(early[1])]
             early_ids = [after(early_ids[0], exp), early_ids[1]]
             sums = one_hot_sums(early, early_ids, columns)
-        if turn + 2 == lines:
-            other_exps = [to_core(after(early_exp, exp)) for early_exp in exps[:-1]]
-        waiting = [first, second]
-        block = following
-
+        waiting = done
+
+    stats = after(stats, late[1], *other_exps)
     across_stats, core_stats, both_stats = to_y(stats), to_core(stats), to_y_core(stats)
-    late_blocks = sum(quads[split:], [])
-    late_blocks[0] = after(late_blocks[0], stats)
-    late = turned_features(rep_scalar, late_blocks, rows)
     merged = merged_stats(stats, across_stats, core_stats, both_stats)
     all_stats = [merged] + [
         lax.ppermute(merged, "shard", shift_pairs(lines, -along, 0)) for along in range(1, lines)
     ]
-    late_exps = lax.optimization_barrier((late[1], *exps[-2:], merged))
-    other_exps += [to_core(exp) for exp in late_exps[1:3]]
-    late = [late[0], to_core(late_exps[0])]
-    sums = one_hot_sums(late, late_ids, columns, sums)
+    held = lax.optimization_barrier((late_ids[0], exps[-1], merged))
+    other_exps.append(to_core(held[1]))
+    sums = one_hot_sums(late, [held[0], late_ids[1]], columns, sums)
     return tuple(refresh_states(
         lines, [early[0], late[0], early[1], late[1]], exps + other_exps,
         all_stats, sums, moment, curvature,

time: 154 us -> 180 us (1.17)
  waiting for transfers between devices: 9.13 us -> 26.5 us
  local copies, waits for them, and re-layouts: 20.1 us -> 36.7 us
  Pallas kernels: 89 us -> 81.6 us
  starting transfers between devices: 29.6 us -> 27.5 us
    ppermute x3, waiting for transfers between devices: 6.3 us -> 18.3 us  [all_tokens(): following = lax.ppermute(block, 'shard', shift_pairs(lines, 1, 0))]
    unnamed x56 -> x80, local copies, waits for them, and re-layouts: 16.6 us -> 27.2 us
    pallas_call x4 -> x3, Pallas kernels: 44.2 us -> 36.5 us  [round_logits(): pl.pallas_call(functools.partial(logits_kernel, start, sizes), grid=(colu...]
    slice x4, local copies, waits for them, and re-layouts: 0.07 us -> 3.41 us  [all_tokens(): second = to_y(from_x[half:])]
    ppermute x8, waiting for transfers between devices: 1.31 us -> 4.22 us  [to_x(): return lax.ppermute(values, 'rep', swap_pairs(reps, 2))]
    slice x4, local copies, waits for them, and re-layouts: 0.07 us -> 2.63 us  [all_tokens(): first = to_x(from_y[:half])]
  transfers between devices with their start and end apart: 31 -> 30, of which waited for: 5 -> 7; matrix products, arithmetic and copies ran while one was open for 4% -> 7% of each run, Pallas kernels for 38% -> 34%
where the time goes in v2:
time: 180 us; the launch traced here: 178 us
  Pallas kernels  81.6 us (45%)
  local copies, waits for them, and re-layouts  36.7 us (20%)
  starting transfers between devices  27.5 us (15%)
  waiting for transfers between devices  26.5 us (15%)
  other arithmetic  4.7 us (3%)
    pallas_call x3, Pallas kernels, round_logits(): pl.pallas_call(functools.partial(logits_kernel, start, sizes), grid=(colu...  36.5 us
    unnamed x80, local copies, waits for them, and re-layouts  27.2 us
    pallas_call x2, Pallas kernels, one_hot_sums(): pl.pallas_call(functools.partial(one_hot_kernel, len(features)), grid=(co...  21.7 us
    ppermute x3, waiting for transfers between devices, all_tokens(): following = lax.ppermute(block, 'shard', shift_pairs(lines, 1, 0))  18.3 us
    pallas_call x1, Pallas kernels, refresh_states(): pl.pallas_call(functools.partial(refresh_kernel, lines, (len(features), l...  17.3 us
    ppermute x9, starting transfers between devices, to_y(): return lax.ppermute(values, 'shard', swap_pairs(shards, 1))  8.99 us
    ppermute x8, starting transfers between devices, to_x(): return lax.ppermute(values, 'rep', swap_pairs(reps, 2))  8.39 us
    ppermute x3, starting transfers between devices, all_tokens(): lax.ppermute(merged, 'shard', shift_pairs(lines, -along, 0))  4.87 us
  transfers between devices with their start and end apart: 30, of which 7 were waited for; matrix products, arithmetic and copies ran while one was open for 7% of the time, Pallas kernels for 34%

profile of v2, /device:TPU:0, one launch (start us, length us, event | category | flops | bytes accessed | tf_op | source)
XLA Modules:
  0.0 178.1 jit_solution(8070680965421493554)
XLA Ops:
  0.6 1.2 fusion
  1.9 1.2 fusion.2.refs_0_
  3.1 3.1 %collective-permute-start.4 = (bf16[64,3584]{1,0:T(8,128)(2,1)S(1)}, bf16[64,3584]{1,0:T(8,128)(2,1)S(1)}, u32[]{:S(2)}, u32[]{:S(2)}) collective-permute-start(bf16[64,3584]{1,0:T(8,128)(2,1)S(1)} %fusion.2.refs_0_), channel_id=1, source_target_pairs={{0,2},{1,3},{2,4},{3,5},{4,6},{5,7},{6,0},{7,1},{8,10},{9,11},{10,... | collective-permute-start | bytes 1376264 | tf_op jit(solution)/shard_map/ppermute | solution.py:414
  6.1 1.5 collective-permute-start.1
  7.7 1.5 collective-permute-start
  9.1 9.5 %collective-permute-done.4.refs_5_ = bf16[64,3584]{1,0:T(8,128)(2,1)S(1)} collective-permute-done((bf16[64,3584]{1,0:T(8,128)(2,1)S(1)}, bf16[64,3584]{1,0:T(8,128)(2,1)S(1)}, u32[]{:S(2)}, u32[]{:S(2)}) %collective-permute-start.4) | collective-permute-done | bytes 458784 | tf_op jit(solution)/shard_map/ppermute | solution.py:414
  18.7 1.5 collective-permute-start.6
  20.2 1.5 collective-permute-start.5
  23.5 8.8 %collective-permute-done.9.refs_2_.refs_0_ = bf16[64,3584]{1,0:T(8,128)(2,1)} collective-permute-done((bf16[64,3584]{1,0:T(8,128)(2,1)S(1)}, bf16[64,3584]{1,0:T(8,128)(2,1)}, u32[]{:S(2)}, u32[]{:S(2)}) %collective-permute-start.9) | collective-permute-done | bytes 458784 | tf_op jit(solution)/shard_map/ppermute | solution.py:414
  33.0 3.3 %collective-permute-done.2.refs_3_ = bf16[32,3584]{1,0:T(8,128)(2,1)S(1)} collective-permute-done((bf16[32,3584]{1,0:T(8,128)(2,1)S(1)}, bf16[32,3584]{1,0:T(8,128)(2,1)S(1)}, u32[]{:S(2)}, u32[]{:S(2)}) %collective-permute-start.2) | collective-permute-done | bytes 229408 | tf_op jit(solution)/shard_map/ppermute | solution.py:372
  37.8 1.5 collective-permute-start.7
  39.8 1.5 collective-permute-start.13
  42.6 1.3 slice.59
  47.2 1.0 collective-permute-done.8.refs_9_.refs_1_
  48.2 1.0 copy-done.12
  51.1 2.6 %turned_features.2 = (bf16[896,512]{1,0:T(8,128)(2,1)S(1)}, bf16[896,512]{1,0:T(8,128)(2,1)}) custom-call(s32[1]{0:T(128)} %bitcast.rep_ref, bf16[64,3584]{1,0:T(8,128)(2,1)S(1)} %fusion.2.refs_0_, bf16[64,3584]{1,0:T(8,128)(2,1)S(1)} %collective-permute-done.refs_1_, bf16[64,3584]{1,0:T(8,128)(2,1)S(1)} %collective-permute-done.1.refs_2_, ...), custom_call_target="tpu_custom_call" | custom-call | flops 1024 | bytes 1024 | tf_op jit(solution)/shard_map/turned_features/pallas_call | solution.py:202
  55.3 1.0 copy-done.8
  56.3 1.0 copy-done.10
  57.4 1.0 copy-done.13
  59.3 13.0 %round_logits.3 = (bf16[448,2048]{1,0:T(8,128)(2,1)S(1)}, f32[16,128]{1,0:T(8,128)S(1)}) custom-call(bf16[64,3584]{1,0:T(8,128)(2,1)S(1)} %fusion.2.refs_0_, bf16[64,3584]{1,0:T(8,128)(2,1)S(1)} %collective-permute-done.refs_1_, bf16[64,3584]{1,0:T(8,128)(2,1)S(1)} %collective-permute-done.1.refs_2_, bf16[32,3584]{1,0:T(8,128)(2,1)S(1)} %collective-permute-done.2.refs_3_, ...), custom_call_target="tpu_custom_call" | custom-call | flops 1024 | bytes 1024 | tf_op jit(solution)/shard_map/round_logits/pallas_call | solution.py:153
  72.3 1.2 copy-done.14
  73.6 1.0 slice.63
  74.5 1.0 slice.62
  75.5 1.3 collective-permute-start.14
  76.8 1.5 collective-permute-start.15
  79.4 0.9 copy-done.34
  80.4 11.4 %round_logits.4 = (bf16[256,2048]{1,0:T(8,128)(2,1)S(1)}, f32[16,128]{1,0:T(8,128)S(1)}) custom-call(bf16[32,3584]{1,0:T(8,128)(2,1)S(1)} %copy-done.34, bf16[32,3584]{1,0:T(8,128)(2,1)} %collective-permute-done.8.refs_9_.refs_1_, bf16[64,3584]{1,0:T(8,128)(2,1)} %collective-permute-done.9.refs_2_.refs_0_, ...), custom_call_target="tpu_custom_call" | custom-call | flops 1024 | bytes 1024 | tf_op jit(solution)/shard_map/round_logits/pallas_call | solution.py:153
  91.8 1.0 copy-done.21
  92.7 1.0 slice.65
  93.7 1.0 slice.64
  96.1 10.3 %one_hot_sums.2 = (bf16[896,2048]{1,0:T(8,128)(2,1)S(1)}, bf16[896,2048]{1,0:T(8,128)(2,1)S(1)}) custom-call(bf16[896,512]{1,0:T(8,128)(2,1)S(1)} %get-tuple-element.35.refs_0_, bf16[896,512]{1,0:T(8,128)(2,1)S(1)} %collective-permute-done.10.refs_1_.refs_2_, s32[1,1024]{1,0:T(1,128)S(1)} %squeeze.12.refs_2_, s32[1,1024]{1,0:T(1,128)S(1)} %squeeze.13.refs_3_), custom_call_target="tpu_custom_call" | custom-call | flops 1024 | bytes 1024 | tf_op jit(solution)/shard_map/one_hot_sums/pallas_call | solution.py:255
  106.4 1.8 %copy-done = bf16[896,2048]{1,0:T(8,128)(2,1)} copy-done((bf16[896,2048]{1,0:T(8,128)(2,1)}, bf16[896,2048]{1,0:T(8,128)(2,1)S(1)}, u32[]{:S(2)}) %copy-start) | copy-done | bytes 3670040
  108.2 1.8 %copy-done.2 = bf16[896,2048]{1,0:T(8,128)(2,1)} copy-done((bf16[896,2048]{1,0:T(8,128)(2,1)}, bf16[896,2048]{1,0:T(8,128)(2,1)S(1)}, u32[]{:S(2)}) %copy-start.2) | copy-done | bytes 3670040
  111.7 2.0 %turned_features.3 = (bf16[896,512]{1,0:T(8,128)(2,1)S(1)}, bf16[896,512]{1,0:T(8,128)(2,1)S(1)}) custom-call(s32[1]{0:T(128)} %bitcast.rep_ref, bf16[64,3584]{1,0:T(8,128)(2,1)} %collective-permute-done.9.refs_2_.refs_0_, bf16[64,3584]{1,0:T(8,128)(2,1)} %collective-permute-done.12.refs_3_.refs_1_, ...), custom_call_target="tpu_custom_call" | custom-call | flops 1024 | bytes 1024 | tf_op jit(solution)/shard_map/turned_features/pallas_call | solution.py:202
  115.4 12.2 %round_logits.5 = (bf16[320,2048]{1,0:T(8,128)(2,1)S(1)}, f32[16,128]{1,0:T(8,128)S(1)}) custom-call(bf16[32,3584]{1,0:T(8,128)(2,1)S(1)} %collective-permute-done.14.refs_3_.refs_0_, bf16[32,3584]{1,0:T(8,128)(2,1)S(1)} %collective-permute-done.15.refs_4_.refs_1_, bf16[64,3584]{1,0:T(8,128)(2,1)} %collective-permute-done.11.refs_5_.refs_2_, ...), custom_call_target="tpu_custom_call" | custom-call | flops 1024 | bytes 1024 | tf_op jit(solution)/shard_map/round_logits/pallas_call | solution.py:153
  127.6 1.1 copy-done.19
  128.6 1.0 copy-done.4
  129.6 1.0 copy-done.24
  130.6 1.3 copy-done.17
  131.9 1.4 collective-permute-start.25
  135.0 2.0 %collective-permute-done.23.across_ref = f32[16,128]{1,0:T(8,128)S(1)} collective-permute-done((f32[16,128]{1,0:T(8,128)S(1)}, f32[16,128]{1,0:T(8,128)S(1)}, u32[]{:S(2)}, u32[]{:S(2)}) %collective-permute-start.23) | collective-permute-done | bytes 8224 | tf_op jit(solution)/shard_map/ppermute | solution.py:378
  137.6 1.4 merged_stats.1.refs_10_
  139.9 3.2 %collective-permute-start.28 = (f32[48,128]{1,0:T(8,128)}, f32[48,128]{1,0:T(8,128)S(1)}, u32[]{:S(2)}, u32[]{:S(2)}) collective-permute-start(f32[48,128]{1,0:T(8,128)} %merged_stats.1.refs_10_), channel_id=1, source_target_pairs={{0,4},{1,5},{2,6},{3,7},{4,0},{5,1},{6,2},{7,3},{8,12},{9,13},{10,... | collective-permute-start | bytes 73736 | tf_op jit(solution)/shard_map/ppermute | solution.py:454
  143.9 2.0 %copy-done.1 = bf16[896,2048]{1,0:T(8,128)(2,1)S(1)} copy-done((bf16[896,2048]{1,0:T(8,128)(2,1)S(1)}, bf16[896,2048]{1,0:T(8,128)(2,1)}, u32[]{:S(2)}) %copy-start.1) | copy-done | bytes 3670040
  145.9 2.0 %copy-done.3 = bf16[896,2048]{1,0:T(8,128)(2,1)S(1)} copy-done((bf16[896,2048]{1,0:T(8,128)(2,1)S(1)}, bf16[896,2048]{1,0:T(8,128)(2,1)}, u32[]{:S(2)}) %copy-start.3) | copy-done | bytes 3670040
  148.0 1.2 copy-done.5
  149.2 11.4 %one_hot_sums.3 = (bf16[896,2048]{1,0:T(8,128)(2,1)S(1)}, bf16[896,2048]{1,0:T(8,128)(2,1)S(1)}) custom-call(bf16[896,512]{1,0:T(8,128)(2,1)S(1)} %get-tuple-element.50.refs_0_.refs_1_, bf16[896,512]{1,0:T(8,128)(2,1)S(1)} %copy-done.5, s32[1,1024]{1,0:T(1,128)S(1)} %squeeze.14.refs_2_, s32[1,1024]{1,0:T(1,128)S(1)} %squeeze.15.refs_3_, ...), custom_call_target="tpu_custom_call" | custom-call | flops 1024 | bytes 1024 | tf_op jit(solution)/shard_map/one_hot_sums/pallas_call | solution.py:255
  160.7 17.3 %refresh_states.1 = (bf16[896,2048]{1,0:T(8,128)(2,1)}, bf16[896,2048]{1,0:T(8,128)(2,1)}, bf16[896,2048]{1,0:T(8,128)(2,1)}) custom-call(bf16[896,512]{1,0:T(8,128)(2,1)S(1)} %get-tuple-element.35.refs_0_, bf16[896,512]{1,0:T(8,128)(2,1)S(1)} %get-tuple-element.50.refs_0_.refs_1_, bf16[896,512]{1,0:T(8,128)(2,1)S(1)} %collective-permute-done.10.refs_1_.refs_2_, ...), custom_call_target="tpu_custom_call" | custom-call | flops 1024 | bytes 1024 | tf_op jit(solution)/shard_map/refresh_states/pallas_call | solution.py:317
  (139 shorter events, 23.3 us)
Async XLA Ops:
  3.1 15.6 %collective-permute-start.4 = (bf16[64,3584]{1,0:T(8,128)(2,1)S(1)}, bf16[64,3584]{1,0:T(8,128)(2,1)S(1)}, u32[]{:S(2)}, u32[]{:S(2)}) collective-permute-start(bf16[64,3584]{1,0:T(8,128)(2,1)S(1)} %fusion.2.refs_0_), channel_id=1, source_target_pairs={{0,2},{1,3},{2,4},{3,5},{4,6},{5,7},{6,0},{7,1},{8,10},{9,11},{10,... | collective-permute-start | bytes 1376264 | tf_op jit(solution)/shard_map/ppermute | solution.py:414
  6.1 15.6 %collective-permute-start.1 = (bf16[64,3584]{1,0:T(8,128)(2,1)S(1)}, bf16[64,3584]{1,0:T(8,128)(2,1)S(1)}, u32[]{:S(2)}, u32[]{:S(2)}) collective-permute-start(bf16[64,3584]{1,0:T(8,128)(2,1)S(1)} %fusion.2.refs_0_), channel_id=1, source_target_pairs={{0,1},{1,0},{2,3},{3,2},{4,5},{5,4},{6,7},{7,6},{8,9},{9,8},{10,11... | collective-permute-start | bytes 1376264 | tf_op jit(solution)/shard_map/ppermute | solution.py:378
  7.7 14.7 %collective-permute-start = (bf16[64,3584]{1,0:T(8,128)(2,1)S(1)}, bf16[64,3584]{1,0:T(8,128)(2,1)S(1)}, u32[]{:S(2)}, u32[]{:S(2)}) collective-permute-start(bf16[64,3584]{1,0:T(8,128)(2,1)S(1)} %fusion.2.refs_0_), channel_id=1, source_target_pairs={{0,16},{8,24},{16,0},{24,8},{1,17},{9,25},{17,1},{25,9},{2,18},{10... | collective-permute-start | bytes 1376264 | tf_op jit(solution)/shard_map/ppermute | solution.py:372
  18.7 29.5 %copy-start.11 = (bf16[64,3584]{1,0:T(8,128)(2,1)}, bf16[64,3584]{1,0:T(8,128)(2,1)S(1)}, u32[]{:S(2)}) copy-start(bf16[64,3584]{1,0:T(8,128)(2,1)S(1)} %collective-permute-done.4.refs_5_) | copy-start | bytes 1376260
  18.7 13.6 %collective-permute-start.9 = (bf16[64,3584]{1,0:T(8,128)(2,1)S(1)}, bf16[64,3584]{1,0:T(8,128)(2,1)}, u32[]{:S(2)}, u32[]{:S(2)}) collective-permute-start(bf16[64,3584]{1,0:T(8,128)(2,1)S(1)} %collective-permute-done.4.refs_5_), channel_id=1, source_target_pairs={{0,2},{1,3},{2,4},{3,5},{4,6},{5,7},{6,0},{7,1},{8,10},{9,11},{10,... | collective-permute-start | bytes 1376264 | tf_op jit(solution)/shard_map/ppermute | solution.py:414
  18.7 17.6 %collective-permute-start.6 = (bf16[64,3584]{1,0:T(8,128)(2,1)S(1)}, bf16[64,3584]{1,0:T(8,128)(2,1)S(1)}, u32[]{:S(2)}, u32[]{:S(2)}) collective-permute-start(bf16[64,3584]{1,0:T(8,128)(2,1)S(1)} %collective-permute-done.4.refs_5_), channel_id=1, source_target_pairs={{0,1},{1,0},{2,3},{3,2},{4,5},{5,4},{6,7},{7,6},{8,9},{9,8},{10,11... | collective-permute-start | bytes 1376264 | tf_op jit(solution)/shard_map/ppermute | solution.py:378
  20.2 16.1 %collective-permute-start.5 = (bf16[64,3584]{1,0:T(8,128)(2,1)S(1)}, bf16[64,3584]{1,0:T(8,128)(2,1)S(1)}, u32[]{:S(2)}, u32[]{:S(2)}) collective-permute-start(bf16[64,3584]{1,0:T(8,128)(2,1)S(1)} %collective-permute-done.4.refs_5_), channel_id=1, source_target_pairs={{0,16},{8,24},{16,0},{24,8},{1,17},{9,25},{17,1},{25,9},{2,18},{10... | collective-permute-start | bytes 1376264 | tf_op jit(solution)/shard_map/ppermute | solution.py:372
  21.7 14.6 %collective-permute-start.2 = (bf16[32,3584]{1,0:T(8,128)(2,1)S(1)}, bf16[32,3584]{1,0:T(8,128)(2,1)S(1)}, u32[]{:S(2)}, u32[]{:S(2)}) collective-permute-start(bf16[32,3584]{1,0:T(8,128)(2,1)S(1)} %slice.70), channel_id=1, source_target_pairs={{0,16},{8,24},{16,0},{24,8},{1,17},{9,25},{17,1},{25,9},{2,18},{10... | collective-permute-start | bytes 688136 | tf_op jit(solution)/shard_map/ppermute | solution.py:372
  23.0 13.3 %collective-permute-start.3 = (bf16[32,3584]{1,0:T(8,128)(2,1)}, bf16[32,3584]{1,0:T(8,128)(2,1)S(1)}, u32[]{:S(2)}, u32[]{:S(2)}) collective-permute-start(bf16[32,3584]{1,0:T(8,128)(2,1)} %slice.71), channel_id=1, source_target_pairs={{0,1},{1,0},{2,3},{3,2},{4,5},{5,4},{6,7},{7,6},{8,9},{9,8},{10,11... | collective-permute-start | bytes 688136 | tf_op jit(solution)/shard_map/ppermute | solution.py:378
  32.3 21.4 %collective-permute-start.11 = (bf16[64,3584]{1,0:T(8,128)(2,1)}, bf16[64,3584]{1,0:T(8,128)(2,1)}, u32[]{:S(2)}, u32[]{:S(2)}) collective-permute-start(bf16[64,3584]{1,0:T(8,128)(2,1)} %collective-permute-done.9.refs_2_.refs_0_), channel_id=1, source_target_pairs={{0,2},{1,3},{2,4},{3,5},{4,6},{5,7},{6,0},{7,1},{8,10},{9,11},{10,... | collective-permute-start | bytes 1376264 | tf_op jit(solution)/shard_map/ppermute | solution.py:414
  36.3 11.9 %copy-start.26 = (bf16[32,3584]{1,0:T(8,128)(2,1)}, bf16[32,3584]{1,0:T(8,128)(2,1)S(1)}, u32[]{:S(2)}) copy-start(bf16[32,3584]{1,0:T(8,128)(2,1)S(1)} %collective-permute-done.3.refs_4_) | copy-start | bytes 688132
  36.3 17.4 %copy-start.7 = (bf16[64,3584]{1,0:T(8,128)(2,1)}, bf16[64,3584]{1,0:T(8,128)(2,1)S(1)}, u32[]{:S(2)}) copy-start(bf16[64,3584]{1,0:T(8,128)(2,1)S(1)} %collective-permute-done.6.refs_7_) | copy-start | bytes 1376260
  36.3 17.4 %copy-start.9 = (bf16[64,3584]{1,0:T(8,128)(2,1)}, bf16[64,3584]{1,0:T(8,128)(2,1)S(1)}, u32[]{:S(2)}) copy-start(bf16[64,3584]{1,0:T(8,128)(2,1)S(1)} %collective-permute-done.5.refs_6_) | copy-start | bytes 1376260
  37.8 8.6 %collective-permute-start.7 = (bf16[32,3584]{1,0:T(8,128)(2,1)}, bf16[32,3584]{1,0:T(8,128)(2,1)S(1)}, u32[]{:S(2)}, u32[]{:S(2)}) collective-permute-start(bf16[32,3584]{1,0:T(8,128)(2,1)} %slice.56), channel_id=1, source_target_pairs={{0,16},{8,24},{16,0},{24,8},{1,17},{9,25},{17,1},{25,9},{2,18},{10... | collective-permute-start | bytes 688136 | tf_op jit(solution)/shard_map/ppermute | solution.py:372
  39.3 8.9 %collective-permute-start.8 = (bf16[32,3584]{1,0:T(8,128)(2,1)}, bf16[32,3584]{1,0:T(8,128)(2,1)}, u32[]{:S(2)}, u32[]{:S(2)}) collective-permute-start(bf16[32,3584]{1,0:T(8,128)(2,1)} %slice.57), channel_id=1, source_target_pairs={{0,1},{1,0},{2,3},{3,2},{4,5},{5,4},{6,7},{7,6},{8,9},{9,8},{10,11... | collective-permute-start | bytes 688136 | tf_op jit(solution)/shard_map/ppermute | solution.py:378
  39.8 33.7 %collective-permute-start.13 = (bf16[64,3584]{1,0:T(8,128)(2,1)}, bf16[64,3584]{1,0:T(8,128)(2,1)}, u32[]{:S(2)}, u32[]{:S(2)}) collective-permute-start(bf16[64,3584]{1,0:T(8,128)(2,1)} %collective-permute-done.9.refs_2_.refs_0_), channel_id=1, source_target_pairs={{0,1},{1,0},{2,3},{3,2},{4,5},{5,4},{6,7},{7,6},{8,9},{9,8},{10,11... | collective-permute-start | bytes 1376264 | tf_op jit(solution)/shard_map/ppermute | solution.py:378
  41.4 32.2 %collective-permute-start.12 = (bf16[64,3584]{1,0:T(8,128)(2,1)}, bf16[64,3584]{1,0:T(8,128)(2,1)}, u32[]{:S(2)}, u32[]{:S(2)}) collective-permute-start(bf16[64,3584]{1,0:T(8,128)(2,1)} %collective-permute-done.9.refs_2_.refs_0_), channel_id=1, source_target_pairs={{0,16},{8,24},{16,0},{24,8},{1,17},{9,25},{17,1},{25,9},{2,18},{10... | collective-permute-start | bytes 1376264 | tf_op jit(solution)/shard_map/ppermute | solution.py:372
  53.7 42.4 %collective-permute-start.10 = (bf16[896,512]{1,0:T(8,128)(2,1)}, bf16[896,512]{1,0:T(8,128)(2,1)S(1)}, u32[]{:S(2)}, u32[]{:S(2)}) collective-permute-start(bf16[896,512]{1,0:T(8,128)(2,1)} %get-tuple-element.36), channel_id=1, source_target_pairs={{0,8},{8,0},{16,24},{24,16},{1,9},{9,1},{17,25},{25,17},{2,10},{10... | collective-permute-start | bytes 2752520 | tf_op jit(solution)/shard_map/ppermute | solution.py:375
  53.7 39.0 %collective-permute-start.17 = (bf16[64,3584]{1,0:T(8,128)(2,1)}, bf16[64,3584]{1,0:T(8,128)(2,1)}, u32[]{:S(2)}, u32[]{:S(2)}) collective-permute-start(bf16[64,3584]{1,0:T(8,128)(2,1)} %collective-permute-done.11.refs_5_.refs_2_), channel_id=1, source_target_pairs={{0,1},{1,0},{2,3},{3,2},{4,5},{5,4},{6,7},{7,6},{8,9},{9,8},{10,11... | collective-permute-start | bytes 1376264 | tf_op jit(solution)/shard_map/ppermute | solution.py:378
  54.3 38.4 %collective-permute-start.16 = (bf16[64,3584]{1,0:T(8,128)(2,1)}, bf16[64,3584]{1,0:T(8,128)(2,1)}, u32[]{:S(2)}, u32[]{:S(2)}) collective-permute-start(bf16[64,3584]{1,0:T(8,128)(2,1)} %collective-permute-done.11.refs_5_.refs_2_), channel_id=1, source_target_pairs={{0,16},{8,24},{16,0},{24,8},{1,17},{9,25},{17,1},{25,9},{2,18},{10... | collective-permute-start | bytes 1376264 | tf_op jit(solution)/shard_map/ppermute | solution.py:372
  75.5 17.2 %collective-permute-start.14 = (bf16[32,3584]{1,0:T(8,128)(2,1)S(1)}, bf16[32,3584]{1,0:T(8,128)(2,1)S(1)}, u32[]{:S(2)}, u32[]{:S(2)}) collective-permute-start(bf16[32,3584]{1,0:T(8,128)(2,1)S(1)} %slice.62), channel_id=1, source_target_pairs={{0,16},{8,24},{16,0},{24,8},{1,17},{9,25},{17,1},{25,9},{2,18},{10... | collective-permute-start | bytes 688136 | tf_op jit(solution)/shard_map/ppermute | solution.py:372
  76.8 15.9 %collective-permute-start.15 = (bf16[32,3584]{1,0:T(8,128)(2,1)S(1)}, bf16[32,3584]{1,0:T(8,128)(2,1)S(1)}, u32[]{:S(2)}, u32[]{:S(2)}) collective-permute-start(bf16[32,3584]{1,0:T(8,128)(2,1)S(1)} %slice.63), channel_id=1, source_target_pairs={{0,1},{1,0},{2,3},{3,2},{4,5},{5,4},{6,7},{7,6},{8,9},{9,8},{10,11... | collective-permute-start | bytes 688136 | tf_op jit(solution)/shard_map/ppermute | solution.py:378
  94.7 15.4 %collective-permute-start.18 = (bf16[32,3584]{1,0:T(8,128)(2,1)S(1)}, bf16[32,3584]{1,0:T(8,128)(2,1)S(1)}, u32[]{:S(2)}, u32[]{:S(2)}) collective-permute-start(bf16[32,3584]{1,0:T(8,128)(2,1)S(1)} %slice.64), channel_id=1, source_target_pairs={{0,16},{8,24},{16,0},{24,8},{1,17},{9,25},{17,1},{25,9},{2,18},{10... | collective-permute-start | bytes 688136 | tf_op jit(solution)/shard_map/ppermute | solution.py:372
  95.4 14.7 %collective-permute-start.19 = (bf16[32,3584]{1,0:T(8,128)(2,1)S(1)}, bf16[32,3584]{1,0:T(8,128)(2,1)S(1)}, u32[]{:S(2)}, u32[]{:S(2)}) collective-permute-start(bf16[32,3584]{1,0:T(8,128)(2,1)S(1)} %slice.65), channel_id=1, source_target_pairs={{0,1},{1,0},{2,3},{3,2},{4,5},{5,4},{6,7},{7,6},{8,9},{9,8},{10,11... | collective-permute-start | bytes 688136 | tf_op jit(solution)/shard_map/ppermute | solution.py:378
  96.1 17.7 %copy-start.15 = (bf16[448,2048]{1,0:T(8,128)(2,1)S(1)}, bf16[448,2048]{1,0:T(8,128)(2,1)}, u32[]{:S(2)}) copy-start(bf16[448,2048]{1,0:T(8,128)(2,1)} %copy-done.14) | copy-start | bytes 5505028
  96.1 17.8 %copy-start.22 = (bf16[256,2048]{1,0:T(8,128)(2,1)S(1)}, bf16[256,2048]{1,0:T(8,128)(2,1)}, u32[]{:S(2)}) copy-start(bf16[256,2048]{1,0:T(8,128)(2,1)} %copy-done.21) | copy-start | bytes 3145732
  113.8 16.8 %collective-permute-start.21 = (bf16[448,2048]{1,0:T(8,128)(2,1)S(1)}, bf16[448,2048]{1,0:T(8,128)(2,1)S(1)}, u32[]{:S(2)}, u32[]{:S(2)}) collective-permute-start(bf16[448,2048]{1,0:T(8,128)(2,1)S(1)} %copy-done.15), channel_id=1, source_target_pairs={{0,8},{8,0},{16,24},{24,16},{1,9},{9,1},{17,25},{25,17},{2,10},{10... | collective-permute-start | bytes 5505032 | tf_op jit(solution)/shard_map/ppermute | solution.py:375
  113.9 15.8 %collective-permute-start.22 = (bf16[256,2048]{1,0:T(8,128)(2,1)S(1)}, bf16[256,2048]{1,0:T(8,128)(2,1)S(1)}, u32[]{:S(2)}, u32[]{:S(2)}) collective-permute-start(bf16[256,2048]{1,0:T(8,128)(2,1)S(1)} %copy-done.22), channel_id=1, source_target_pairs={{0,8},{8,0},{16,24},{24,16},{1,9},{9,1},{17,25},{25,17},{2,10},{10... | collective-permute-start | bytes 3145736 | tf_op jit(solution)/shard_map/ppermute | solution.py:375
  114.3 14.3 %collective-permute-start.20 = (bf16[896,512]{1,0:T(8,128)(2,1)S(1)}, bf16[896,512]{1,0:T(8,128)(2,1)S(1)}, u32[]{:S(2)}, u32[]{:S(2)}) collective-permute-start(bf16[896,512]{1,0:T(8,128)(2,1)S(1)} %get-tuple-element.51), channel_id=1, source_target_pairs={{0,8},{8,0},{16,24},{24,16},{1,9},{9,1},{17,25},{25,17},{2,10},{10... | collective-permute-start | bytes 2752520 | tf_op jit(solution)/shard_map/ppermute | solution.py:375
  128.6 8.4 %copy-start.36 = (f32[16,128]{1,0:T(8,128)}, f32[16,128]{1,0:T(8,128)S(1)}, u32[]{:S(2)}) copy-start(f32[16,128]{1,0:T(8,128)S(1)} %get-tuple-element.58.own_ref) | copy-start | bytes 24580
  131.9 3.1 %collective-permute-start.25 = (f32[16,128]{1,0:T(8,128)S(1)}, f32[16,128]{1,0:T(8,128)S(1)}, u32[]{:S(2)}, u32[]{:S(2)}) collective-permute-start(f32[16,128]{1,0:T(8,128)S(1)} %get-tuple-element.58.own_ref), channel_id=1, source_target_pairs={{0,9},{1,8},{2,11},{3,10},{4,13},{5,12},{6,15},{7,14},{8,1},{9,0},... | collective-permute-start | bytes 24584 | tf_op jit(solution)/shard_map/ppermute | solution.py:385
  133.3 1.7 collective-permute-start.24
  133.4 3.7 %collective-permute-start.23 = (f32[16,128]{1,0:T(8,128)S(1)}, f32[16,128]{1,0:T(8,128)S(1)}, u32[]{:S(2)}, u32[]{:S(2)}) collective-permute-start(f32[16,128]{1,0:T(8,128)S(1)} %get-tuple-element.58.own_ref), channel_id=1, source_target_pairs={{0,1},{1,0},{2,3},{3,2},{4,5},{5,4},{6,7},{7,6},{8,9},{9,8},{10,11... | collective-permute-start | bytes 24584 | tf_op jit(solution)/shard_map/ppermute | solution.py:378
  135.0 2.1 %copy-start.37 = (f32[16,128]{1,0:T(8,128)}, f32[16,128]{1,0:T(8,128)S(1)}, u32[]{:S(2)}) copy-start(f32[16,128]{1,0:T(8,128)S(1)} %collective-permute-done.25.both_ref) | copy-start | bytes 24580
  135.0 2.0 %copy-start.38 = (f32[16,128]{1,0:T(8,128)}, f32[16,128]{1,0:T(8,128)S(1)}, u32[]{:S(2)}) copy-start(f32[16,128]{1,0:T(8,128)S(1)} %collective-permute-done.24.core_ref) | copy-start | bytes 24580
  139.0 21.6 %collective-permute-start.26 = (bf16[320,2048]{1,0:T(8,128)(2,1)}, bf16[320,2048]{1,0:T(8,128)(2,1)}, u32[]{:S(2)}, u32[]{:S(2)}) collective-permute-start(bf16[320,2048]{1,0:T(8,128)(2,1)} %copy-done.19), channel_id=1, source_target_pairs={{0,8},{8,0},{16,24},{24,16},{1,9},{9,1},{17,25},{25,17},{2,10},{10... | collective-permute-start | bytes 3932168 | tf_op jit(solution)/shard_map/ppermute | solution.py:375
  139.0 21.6 %collective-permute-start.29 = (f32[48,128]{1,0:T(8,128)}, f32[48,128]{1,0:T(8,128)S(1)}, u32[]{:S(2)}, u32[]{:S(2)}) collective-permute-start(f32[48,128]{1,0:T(8,128)} %merged_stats.1.refs_10_), channel_id=1, source_target_pairs={{0,2},{1,3},{2,4},{3,5},{4,6},{5,7},{6,0},{7,1},{8,10},{9,11},{10,... | collective-permute-start | bytes 73736 | tf_op jit(solution)/shard_map/ppermute | solution.py:454
  139.9 20.7 %collective-permute-start.28 = (f32[48,128]{1,0:T(8,128)}, f32[48,128]{1,0:T(8,128)S(1)}, u32[]{:S(2)}, u32[]{:S(2)}) collective-permute-start(f32[48,128]{1,0:T(8,128)} %merged_stats.1.refs_10_), channel_id=1, source_target_pairs={{0,4},{1,5},{2,6},{3,7},{4,0},{5,1},{6,2},{7,3},{8,12},{9,13},{10,... | collective-permute-start | bytes 73736 | tf_op jit(solution)/shard_map/ppermute | solution.py:454
  143.1 17.5 %collective-permute-start.27 = (f32[48,128]{1,0:T(8,128)}, f32[48,128]{1,0:T(8,128)S(1)}, u32[]{:S(2)}, u32[]{:S(2)}) collective-permute-start(f32[48,128]{1,0:T(8,128)} %merged_stats.1.refs_10_), channel_id=1, source_target_pairs={{0,6},{1,7},{2,0},{3,1},{4,2},{5,3},{6,4},{7,5},{8,14},{9,15},{10,... | collective-permute-start | bytes 73736 | tf_op jit(solution)/shard_map/ppermute | solution.py:454
  143.9 2.0 %copy-start.1 = (bf16[896,2048]{1,0:T(8,128)(2,1)S(1)}, bf16[896,2048]{1,0:T(8,128)(2,1)}, u32[]{:S(2)}) copy-start(bf16[896,2048]{1,0:T(8,128)(2,1)} %copy-done) | copy-start | bytes 11010052
  145.9 2.0 %copy-start.3 = (bf16[896,2048]{1,0:T(8,128)(2,1)S(1)}, bf16[896,2048]{1,0:T(8,128)(2,1)}, u32[]{:S(2)}) copy-start(bf16[896,2048]{1,0:T(8,128)(2,1)} %copy-done.2) | copy-start | bytes 11010052
  149.2 11.5 %copy-start.6 = (bf16[896,512]{1,0:T(8,128)(2,1)S(1)}, bf16[896,512]{1,0:T(8,128)(2,1)}, u32[]{:S(2)}) copy-start(bf16[896,512]{1,0:T(8,128)(2,1)} %copy-done.4) | copy-start | bytes 2752516
  149.2 11.5 %copy-start.16 = (bf16[448,2048]{1,0:T(8,128)(2,1)S(1)}, bf16[448,2048]{1,0:T(8,128)(2,1)}, u32[]{:S(2)}) copy-start(bf16[448,2048]{1,0:T(8,128)(2,1)} %copy-done.14) | copy-start | bytes 5505028
  149.2 11.5 %copy-start.18 = (bf16[448,2048]{1,0:T(8,128)(2,1)S(1)}, bf16[448,2048]{1,0:T(8,128)(2,1)}, u32[]{:S(2)}) copy-start(bf16[448,2048]{1,0:T(8,128)(2,1)} %copy-done.17) | copy-start | bytes 5505028
  149.2 11.5 %copy-start.20 = (bf16[320,2048]{1,0:T(8,128)(2,1)S(1)}, bf16[320,2048]{1,0:T(8,128)(2,1)}, u32[]{:S(2)}) copy-start(bf16[320,2048]{1,0:T(8,128)(2,1)} %copy-done.19) | copy-start | bytes 3932164
  149.2 11.5 %copy-start.23 = (bf16[256,2048]{1,0:T(8,128)(2,1)S(1)}, bf16[256,2048]{1,0:T(8,128)(2,1)}, u32[]{:S(2)}) copy-start(bf16[256,2048]{1,0:T(8,128)(2,1)} %copy-done.21) | copy-start | bytes 3145732
  149.2 11.5 %copy-start.25 = (bf16[256,2048]{1,0:T(8,128)(2,1)S(1)}, bf16[256,2048]{1,0:T(8,128)(2,1)}, u32[]{:S(2)}) copy-start(bf16[256,2048]{1,0:T(8,128)(2,1)} %copy-done.24) | copy-start | bytes 3145732
  149.2 11.5 %copy-start.35 = (f32[48,128]{1,0:T(8,128)S(1)}, f32[48,128]{1,0:T(8,128)}, u32[]{:S(2)}) copy-start(f32[48,128]{1,0:T(8,128)} %merged_stats.1.refs_10_) | copy-start | bytes 73732
  (22 other events, 23.1 us)

commit v3 on v0

v3 whole, which is shorter than its diff:
```python
import functools

import jax
import jax.numpy as jnp
import numpy as np
from jax import lax
from jax.experimental import pallas as pl
from jax.experimental.pallas import tpu as pltpu
from jax.sharding import PartitionSpec as P

EPS_NORM = 1e-05
BETA_ONE = 0.96
BETA_TWO = 0.95
RHO_SCALE = 0.05
GATHER_BYTES = 32 * 1024 * 1024
BRIEF = pl.CostEstimate(flops=1024, bytes_accessed=1024, transcendentals=0)


def normalize(hidden, norm_gain):
    values = hidden.astype(jnp.float32)
    row_scale = lax.rsqrt(jnp.mean(values * values, axis=-1, keepdims=True) + EPS_NORM)
    return (values * row_scale * norm_gain).astype(jnp.bfloat16)


def refresh(gradient, sample_grad, moment, curvature):
    moment_new = BETA_ONE * moment.astype(jnp.float32) + (1.0 - BETA_ONE) * gradient
    curvature_new = (
        BETA_TWO * curvature.astype(jnp.float32) + (1.0 - BETA_TWO) * sample_grad * sample_grad
    )
    update_direction = jnp.clip(moment_new / (RHO_SCALE * curvature_new), -1.0, 1.0)
    return (
        moment_new.astype(jnp.bfloat16),
        curvature_new.astype(jnp.bfloat16),
        update_direction.astype(jnp.bfloat16),
    )


def by_groups(hidden, norm_gain, input_ids, sampled_ids, head_weight, moment, curvature):
    normed = normalize(hidden, norm_gain)
    gathered = lax.all_gather(normed, "shard", axis=0, tiled=True)
    group_len = gathered.shape[0]
    columns = head_weight.shape[1]
    first_col = lax.axis_index("shard") * columns
    logits = jnp.dot(gathered, head_weight, preferred_element_type=jnp.float32)
    row_peak = lax.pmax(jnp.max(logits, axis=-1), "shard")
    scaled_exp = jnp.exp(logits - row_peak[:, None])
    row_sum = lax.psum(jnp.sum(scaled_exp, axis=-1), "shard")
    probabilities = (scaled_exp / row_sum[:, None]).astype(jnp.bfloat16)
    group_start = lax.axis_index("rep") * group_len
    token_ids = lax.dynamic_slice_in_dim(input_ids, group_start, group_len, 0)
    sample_ids = lax.dynamic_slice_in_dim(sampled_ids, group_start, group_len, 0)
    position = jnp.arange(group_len)
    shifted = jnp.roll(token_ids, -1) - first_col
    usable = (position < group_len - 1) & (shifted >= 0) & (shifted < columns)
    true_slot = jnp.where(usable, shifted, columns)
    sample_local = sample_ids - first_col
    inside = (sample_local >= 0) & (sample_local < columns)
    sample_slot = jnp.where(inside, sample_local, columns)
    shared = lax.dot_general(
        gathered, probabilities, (((0,), (0,)), ((), ())), preferred_element_type=jnp.float32
    )
    widened = gathered.astype(jnp.float32)
    true_sums = jax.ops.segment_sum(widened, true_slot, num_segments=columns + 1)[:columns]
    sample_sums = jax.ops.segment_sum(widened, sample_slot, num_segments=columns + 1)[:columns]
    true_part = (shared - true_sums.T).astype(jnp.bfloat16)
    sample_part = (shared - sample_sums.T).astype(jnp.bfloat16)
    gradient = lax.psum_scatter(true_part, "rep", scatter_dimension=0, tiled=True)
    sample_grad = lax.psum_scatter(sample_part, "rep", scatter_dimension=0, tiled=True)
    return refresh(
        gradient.astype(jnp.float32), sample_grad.astype(jnp.float32), moment, curvature
    )


def swap_pairs(count, bit):
    return [(index, index ^ bit) for index in range(count)]


def shift_pairs(lines, along, across):
    pairs = []
    for place in range(lines):
        for side in range(2):
            source = 2 * place + side
            pairs.append((source, 2 * ((place + along) % lines) + (side ^ across)))
    return pairs


def logits_kernel(stat_rows, *refs):
    count = len(stat_rows)
    block_refs, refs = refs[:count], refs[count:]
    weight_ref, before_ref, exp_ref, stats_ref, logits, highs, sums = refs
    step = pl.program_id(0)
    tokens, columns = logits.shape
    length = tokens // count
    half = stats_ref.shape[0] // 2
    rows = jnp.concatenate([ref[...] for ref in block_refs], axis=0)
    width = min(512, columns)
    for lane in range(0, columns, width):
        part = jnp.dot(
            rows, weight_ref[:, lane:lane + width], preferred_element_type=jnp.float32
        )
        held = logits[:, lane:lane + width]
        logits[:, lane:lane + width] = jnp.where(step == 0, 0.0, held) + part

    @pl.when(step == pl.num_programs(0) - 1)
    def _():
        chunk = 16

        def peaks(index, carry):
            place = pl.ds(pl.multiple_of(index * chunk, chunk), chunk)
            highs[place, :] = functools.reduce(
                jnp.maximum, [logits[place, lane:lane + 128] for lane in range(0, columns, 128)]
            )
            return carry

        lax.fori_loop(0, tokens // chunk, peaks, 0, unroll=2)
        highs[...] = jnp.broadcast_to(jnp.max(highs[...], axis=1, keepdims=True), highs.shape)

        def scale(index, carry):
            place = pl.ds(pl.multiple_of(index * chunk, chunk), chunk)
            peak = highs[place, :]
            total = jnp.zeros((chunk, 128), jnp.float32)
            for lane in range(0, columns, 128):
                scaled = jnp.exp(logits[place, lane:lane + 128] - peak)
                exp_ref[place, lane:lane + 128] = scaled.astype(jnp.bfloat16)
                total += scaled
            sums[place, :] = total
            return carry

        lax.fori_loop(0, tokens // chunk, scale, 0, unroll=2)
        totals = jnp.broadcast_to(jnp.sum(sums[...], axis=1, keepdims=True), sums.shape)
        stats_ref[...] = before_ref[...]
        for base, values in ((0, highs[...].T[0:1]), (half, totals.T[0:1])):
            for index, row in enumerate(stat_rows):
                stats_ref[base + row:base + row + 1, :length] = (
                    values[:, index * length:(index + 1) * length]
                )


def round_logits(blocks, stat_rows, head_weight, before):
    depth, columns = head_weight.shape
    length = blocks[0].shape[0]
    tokens = length * len(blocks)
    band = 512
    whole = lambda shape: pl.BlockSpec(shape, lambda step: (0, 0))
    return pl.pallas_call(
        functools.partial(logits_kernel, stat_rows),
        grid=(depth // band,),
        in_specs=[pl.BlockSpec((length, band), lambda step: (0, step))] * len(blocks)
        + [pl.BlockSpec((band, columns), lambda step: (step, 0)), whole(before.shape)],
        out_specs=[whole((tokens, columns)), whole(before.shape)],
        out_shape=[
            jax.ShapeDtypeStruct((tokens, columns), jnp.bfloat16),
            jax.ShapeDtypeStruct(before.shape, jnp.float32),
        ],
        scratch_shapes=[
            pltpu.VMEM((tokens, columns), jnp.float32),
            pltpu.VMEM((tokens, 128), jnp.float32),
            pltpu.VMEM((tokens, 128), jnp.float32),
        ],
        compiler_params=pltpu.CompilerParams(vmem_limit_bytes=24 * 1024 * 1024),
        cost_estimate=BRIEF,
        name="round_logits",
    )(*blocks, head_weight, before)


def turn_kernel(count, rep_ref, *refs):
    mine_ref, other_ref = refs[count:]
    step = pl.program_id(0)
    turned = jnp.concatenate([ref[...] for ref in refs[:count]], axis=0).T

    @pl.when(step == 0)
    def _():
        mine_ref[...] = turned

    @pl.when(step == 1)
    def _():
        other_ref[...] = turned


def turned_features(rep, blocks, rows):
    length = blocks[0].shape[0]
    tokens = length * len(blocks)
    whole = pl.BlockSpec((rows, tokens), lambda step, rep_ref: (0, 0))
    block = pl.BlockSpec((length, rows), lambda step, rep_ref: (0, rep_ref[0] ^ step))
    return pl.pallas_call(
        functools.partial(turn_kernel, len(blocks)),
        grid_spec=pltpu.PrefetchScalarGridSpec(
            num_scalar_prefetch=1,
            grid=(2,),
            in_specs=[block] * len(blocks),
            out_specs=[whole, whole],
        ),
        out_shape=[jax.ShapeDtypeStruct((rows, tokens), jnp.bfloat16)] * 2,
        compiler_params=pltpu.CompilerParams(vmem_limit_bytes=20 * 1024 * 1024),
        cost_estimate=BRIEF,
        name="turned_features",
    )(rep, *blocks)


def one_hot_kernel(count, *refs):
    feature_refs, refs = refs[:count], refs[count:]
    true_ref, sample_ref, true_out, sample_out = refs
    width = true_out.shape[1]
    features = jnp.concatenate([ref[...] for ref in feature_refs], axis=1)
    columns = pl.program_id(0) * width + lax.broadcasted_iota(
        jnp.int32, (width, features.shape[1]), 0
    )
    hot = jnp.concatenate([columns == true_ref[...], columns == sample_ref[...]], axis=0)
    totals = lax.dot_general(
        features, hot.astype(jnp.float32).astype(jnp.bfloat16),
        (((1,), (1,)), ((), ())), preferred_element_type=jnp.float32,
    )
    true_out[...] = totals[:, :width].astype(jnp.bfloat16)
    sample_out[...] = totals[:, width:].astype(jnp.bfloat16)


def one_hot_sums(features, ids, columns):
    rows = features[0].shape[0]
    width = min(256, columns)
    whole = lambda array: pl.BlockSpec(array.shape, lambda step: (0, 0))
    tile = pl.BlockSpec((rows, width), lambda step: (0, step))
    return pl.pallas_call(
        functools.partial(one_hot_kernel, len(features)),
        grid=(columns // width,),
        in_specs=[whole(array) for array in (*features, *ids)],
        out_specs=[tile, tile],
        out_shape=[jax.ShapeDtypeStruct((rows, columns), jnp.bfloat16)] * 2,
        compiler_params=pltpu.CompilerParams(vmem_limit_bytes=24 * 1024 * 1024),
        cost_estimate=BRIEF,
        name="one_hot_sums",
    )(*features, *ids)


def merge_kernel(own_ref, across_ref, core_ref, both_ref, merged_ref, first_ref):
    rows = own_ref.shape[0] // 2
    side = rows // 2
    for core, (near, far) in enumerate(((own_ref, across_ref), (core_ref, both_ref))):
        place = core * rows
        first, total = near[:rows], near[rows:]
        second = jnp.concatenate([far[side:rows], far[:side]], axis=0)
        other = jnp.concatenate([far[rows + side:], far[rows:rows + side]], axis=0)
        peak = jnp.maximum(first, second)
        merged_ref[place:place + rows] = peak
        merged_ref[2 * rows + place:3 * rows + place] = (
            total * jnp.exp(first - peak) + other * jnp.exp(second - peak)
        )
        first_ref[place:place + rows] = first


def merged_stats(own, across, core, both):
    rows, lanes = own.shape
    return pl.pallas_call(
        merge_kernel,
        out_shape=[
            jax.ShapeDtypeStruct((2 * rows, lanes), jnp.float32),
            jax.ShapeDtypeStruct((rows, lanes), jnp.float32),
        ],
        compiler_params=pltpu.CompilerParams(vmem_limit_bytes=4 * 1024 * 1024),
        cost_estimate=BRIEF,
        name="merged_stats",
    )(own, across, core, both)


def refresh_kernel(lines, length, early_rows, late_rows, *refs):
    early_refs, late_refs, refs = refs[:2], refs[2:4], refs[4:]
    exp_refs, refs = refs[:6], refs[6:]
    stats_refs, refs = refs[:lines], refs[lines:]
    (first_ref, true_ids, sample_ids, true_sum, sample_sum, moment_ref, curvature_ref,
     moment_out, curvature_out, update_out, scaled, factors, true_at, sample_at) = refs
    step = pl.program_id(0)
    width = moment_out.shape[1]
    early = len(early_rows) * length
    late = len(late_rows) * length

    @pl.when(step == 0)
    def _():
        rows = first_ref.shape[0]

        def turned(values, along):
            return jnp.concatenate([
                values[group + (turn + along) % lines:group + (turn + along) % lines + 1]
                for group in range(0, rows, lines) for turn in range(lines)
            ], axis=0) if along else values

        peaks = [turned(ref[:rows], along) for along, ref in enumerate(stats_refs)]
        totals = [turned(ref[rows:], along) for along, ref in enumerate(stats_refs)]
        peak = functools.reduce(jnp.maximum, peaks)
        total = sum(t * jnp.exp(p - peak) for p, t in zip(peaks, totals))
        factor = jnp.exp(first_ref[...] - peak) / total
        per_core = rows // 2
        for core in range(2):
            for index in range(0, len(early_rows), 2):
                pair = jnp.concatenate([
                    factor[core * per_core + row:core * per_core + row + 1, :length]
                    for row in early_rows[index:index + 2]
                ], axis=1)
                place = index * length
                values = early_refs[core][:, place:place + 2 * length].astype(jnp.float32)
                place += core * early
                scaled[:, place:place + 2 * length] = (values * pair).astype(jnp.bfloat16)
        full = jnp.concatenate([factor, jnp.zeros((128 - rows, 128), jnp.float32)], axis=0).T
        for core in range(2):
            for index, row in enumerate(late_rows):
                place = core * late + index * length
                at = core * per_core + row
                factors[place:place + length] = jnp.broadcast_to(
                    full[:length, at:at + 1], (length, 128)
                )
        lanes = lax.broadcasted_iota(jnp.int32, true_at.shape, 1)
        true_at[...] = true_ids[...] - lanes
        sample_at[...] = sample_ids[...] - lanes

    shared = jnp.dot(
        scaled[...], jnp.concatenate([exp_refs[0][...], exp_refs[3][...]], axis=0),
        preferred_element_type=jnp.float32,
    )
    gradient = shared - true_sum[...].astype(jnp.float32)
    sample_grad = shared - sample_sum[...].astype(jnp.float32)
    for core in range(2):
        place = slice(core * late, (core + 1) * late)
        exps = jnp.concatenate([ref[...] for ref in exp_refs[3 * core + 1:3 * core + 3]], axis=0)
        true_parts, sample_parts = [], []
        for lane in range(0, width, 128):
            probs = exps[:, lane:lane + 128].astype(jnp.float32) * factors[place]
            at = step * width + lane
            true_parts.append(
                (probs - jnp.where(true_at[place] == at, 1.0, 0.0)).astype(jnp.bfloat16)
            )
            sample_parts.append(
                (probs - jnp.where(sample_at[place] == at, 1.0, 0.0)).astype(jnp.bfloat16)
            )
        features = late_refs[core][...]
        gradient += jnp.dot(
            features, jnp.concatenate(true_parts, axis=1), preferred_element_type=jnp.float32
        )
        sample_grad += jnp.dot(
            features, jnp.concatenate(sample_parts, axis=1), preferred_element_type=jnp.float32
        )
    moment_out[...], curvature_out[...], update_out[...] = refresh(
        gradient, sample_grad, moment_ref[...], curvature_ref[...]
    )


def refresh_states(lines, length, early_rows, late_rows, early, late, exps, stats, first,
                   late_ids, sums, moment, curvature):
    rows, columns = moment.shape
    width = min(256, columns)
    late_tokens = 2 * late[0].shape[1]
    whole = lambda array: pl.BlockSpec(array.shape, lambda step: (0, 0))
    tile = pl.BlockSpec((rows, width), lambda step: (0, step))
    return pl.pallas_call(
        functools.partial(refresh_kernel, lines, length, early_rows, late_rows),
        grid=(columns // width,),
        in_specs=[whole(array) for array in (*early, *late)]
        + [pl.BlockSpec((array.shape[0], width), lambda step: (0, step)) for array in exps]
        + [whole(array) for array in (*stats, first, *late_ids)]
        + [tile] * 4,
        out_specs=[tile] * 3,
        out_shape=[jax.ShapeDtypeStruct((rows, columns), jnp.bfloat16)] * 3,
        scratch_shapes=[
            pltpu.VMEM((rows, 2 * early[0].shape[1]), jnp.bfloat16),
            pltpu.VMEM((late_tokens, 128), jnp.float32),
            pltpu.VMEM((late_tokens, 128), jnp.int32),
            pltpu.VMEM((late_tokens, 128), jnp.int32),
        ],
        compiler_params=pltpu.CompilerParams(vmem_limit_bytes=36 * 1024 * 1024),
        cost_estimate=BRIEF,
        name="refresh_states",
    )(*early, *late, *exps, *stats, first, *late_ids, *sums, moment, curvature)


def after(value, *others):
    return lax.optimization_barrier((value, *others))[0]


def all_tokens(reps, shards, hidden, norm_gain, input_ids, sampled_ids, head_weight, moment, curvature):
    lines = shards // 2
    length = hidden.shape[0]
    rows, columns = moment.shape
    rep = lax.axis_index("rep")
    shard = lax.axis_index("shard")
    first_col = shard * columns
    group_len = length * shards

    def to_x(values):
        return lax.ppermute(values, "rep", swap_pairs(reps, 2))

    def to_core(values):
        return lax.ppermute(values, "rep", swap_pairs(reps, 1))

    def to_y(values):
        return lax.ppermute(values, "shard", swap_pairs(shards, 1))

    def to_y_core(values):
        pairs = [
            (rep_at * shards + at, (rep_at ^ 1) * shards + (at ^ 1))
            for rep_at in range(reps) for at in range(shards)
        ]
        return lax.ppermute(values, ("rep", "shard"), pairs)

    def to_z(values, along):
        return lax.ppermute(values, "shard", shift_pairs(lines, along, 0))

    split = lines // 2
    plain = [(0, 0), (0, 1), (1, 0)]
    early_blocks = [(*kind, turn) for turn in range(split) for kind in plain]
    middle_blocks = [(*kind, turn) for turn in range(split, lines) for kind in plain]
    middle_blocks += [(1, 1, turn) for turn in range(split)]
    last_blocks = [(1, 1, turn) for turn in range(split, lines)]
    groups = [early_blocks, middle_blocks, last_blocks]

    def stat_row(block):
        return (2 * block[0] + block[1]) * lines + block[2]

    normed = normalize(hidden, norm_gain)

    last = jnp.arange(input_ids.shape[0]) % group_len == group_len - 1
    targets = jnp.where(last, -1, jnp.roll(input_ids, -1) - first_col)
    ids = jnp.stack([targets, sampled_ids - first_col]).reshape(2, reps * shards, length)
    side, across, turn = (np.array(values) for values in zip(*sum(groups, [])))
    holder = (rep ^ (2 * across[None] + np.arange(2)[:, None])).reshape(-1)
    place = 2 * ((shard // 2 - turn) % lines) + ((shard % 2) ^ side)
    ids = jnp.take(ids, holder * shards + jnp.tile(place, 2), axis=1)
    ids = ids.reshape(2, 2, len(side), length)
    early_ids = ids[:, :, :len(early_blocks)].reshape(2, 1, -1)
    late_ids = ids[:, :, len(early_blocks):].reshape(2, -1, 1)
    early_ids, late_ids = [early_ids[0], early_ids[1]], [late_ids[0], late_ids[1]]
    rep_scalar = rep.astype(jnp.int32).reshape(1)
    head_weight = pltpu.with_memory_space_constraint(head_weight, pltpu.HBM)
    stats = jnp.zeros((8 * lines, 128), jnp.float32)

    held = {(0, 0, 0): normed}
    exps = []

    def logits(group, stats, *gates):
        blocks = [held[block] for block in group]
        blocks[0] = after(blocks[0], *gates)
        exp, stats = round_logits(blocks, [stat_row(block) for block in group], head_weight, stats)
        exps.append(exp)
        return stats

    def diagonal(turn, *gates):
        if turn % 2 == 0:
            return to_x(after(held[1, 0, turn], *gates) if gates else held[1, 0, turn])
        return to_y(after(held[0, 1, turn], *gates) if gates else held[0, 1, turn])

    for turn in range(lines):
        block = held[0, 0, turn]
        held[0, 1, turn] = to_x(block)
        held[1, 0, turn] = to_y(block)
        if turn + 1 < lines:
            arrived = [to_z(block, 1), held[0, 1, turn], held[1, 0, turn]]
            if turn == 0:
                arrived += [*early_ids, *late_ids, rep_scalar, stats]
            arrived = lax.optimization_barrier((*arrived, *exps[-1:]))
            held[0, 0, turn + 1], held[0, 1, turn], held[1, 0, turn] = arrived[:3]
            if turn == 0:
                early_ids, late_ids = list(arrived[3:5]), list(arrived[5:7])
                rep_scalar, stats = arrived[7:]
            if turn + 1 == split:
                stats = logits(early_blocks, stats, held[0, 0, split])
        if turn < split:
            held[1, 1, turn] = diagonal(turn)

    early = [held[block] for block in early_blocks]
    early[0] = after(early[0], held[0, 0, lines - 1], held[1, 1, 0])
    early = turned_features(rep_scalar, early, rows)
    early = [early[0], to_core(early[1])]
    early_ids[0] = after(early_ids[0], held[0, 0, lines - 1])
    sums = one_hot_sums(early, early_ids, columns)
    for turn in range(split, lines):
        held[1, 1, turn] = diagonal(turn, early[0] if turn % 2 == 0 else sums[0])
    other_exps = [to_core(after(exps[0], early[0]))]
    stats = logits(middle_blocks, stats, *sums, other_exps[0])
    stats = logits(last_blocks, stats)
    other_exps.append(to_core(after(exps[1], stats)))
    across_stats, core_stats, both_stats = to_y(stats), to_core(stats), to_y_core(stats)
    late_held = [held[block] for block in middle_blocks + last_blocks]
    late_held[0] = after(late_held[0], stats)
    late = turned_features(rep_scalar, late_held, rows)
    merged, first = merged_stats(
        after(stats, *other_exps), across_stats, core_stats, both_stats
    )
    all_stats = [merged] + [to_z(merged, -along) for along in range(1, lines)]
    other_exps.append(to_core(after(exps[-1], merged)))
    late = [late[0], to_core(late[1])]
    return tuple(refresh_states(
        lines, length, [stat_row(block) for block in early_blocks],
        [stat_row(block) for block in middle_blocks + last_blocks], early, late,
        exps + other_exps, all_stats, first, late_ids, sums, moment, curvature,
    ))


def solution(mesh):
    in_specs = (
        P(("rep", "shard"), None),
        P(),
        P(),
        P(),
        P(None, "shard"),
        P("rep", "shard"),
        P("rep", "shard"),
    )
    out_specs = (P("rep", "shard"), P("rep", "shard"), P("rep", "shard"))
    reps, shards = mesh.shape["rep"], mesh.shape["shard"]

    def whole(hidden, *others):
        tokens, depth = hidden.shape
        length = tokens // (reps * shards)
        fits = hidden.size * 2 <= GATHER_BYTES and reps == 4 and shards % 2 == 0
        if fits and length == 64 and (depth // reps) % 128 == 0:
            plan = functools.partial(all_tokens, reps, shards)
        else:
            plan = by_groups

        return jax.shard_map(
            plan, mesh=mesh, in_specs=in_specs, out_specs=out_specs, check_vma=False
        )(hidden, *others)

    return whole
```

time: 571 us -> 153 us (0.27); the launches traced: 562 us -> 152 us
  waiting for transfers between devices: 294 us -> 33.1 us
  local copies, waits for them, and re-layouts: 105 us -> 19 us
  Pallas kernels: 0 us -> 70.4 us
  other arithmetic: 64.7 us -> 6.04 us
  matrix products: 47.6 us -> 0 us
  blocking collectives: 36.2 us -> 0 us
  starting transfers between devices: 0.12 us -> 22.6 us
  between operations: 14.2 us -> 0.83 us
    reduce_scatter x2 -> x0, waiting for transfers between devices: 226 us -> none  [the longest x1 116 us: on_device(): lax.psum_scatter(sample_part, 'rep', scatter_dimension=0, tiled=True)]
    pallas_call x0 -> x8, Pallas kernels: none -> 70.4 us  [the longest x3 35.9 us: round_logits(): pl.pallas_call(functools.partial(logits_kernel, stat_rows), grid=(depth /...]
    all_gather x1 -> x0, waiting for transfers between devices: 67 us -> none  [on_device(): gathered = lax.all_gather(normed, 'shard', axis=0, tiled=True)]
    dot_general x2 -> x0, matrix products: 47.6 us -> none  [the longest x1 34.1 us: group_partial(): lax.dot_general(feature_rows, probabilities, (((0,), (0,)), ((), ())), pr...]
    scatter-add x2 -> x0, other arithmetic: 47.3 us -> none  [the longest x1 23.7 us: group_partial(): jax.ops.segment_sum(widened, true_slot, num_segments=columns + 1)[:columns]]
    unnamed x2 -> x26, local copies, waits for them, and re-layouts: 59.4 us -> 15.4 us
    slice x4, local copies, waits for them, and re-layouts: 44.7 us -> 1.98 us  [the longest x2 1.96 us: all_tokens(): targets = jnp.where(last, -1, jnp.roll(input_ids, -1) - first_col)]
    ppermute x0 -> x26, waiting for transfers between devices: none -> 33.1 us  [the longest x7 13.7 us: to_y(): return lax.ppermute(values, 'shard', swap_pairs(shards, 1))]
  transfers between devices with their start and end apart: 3 -> 26, of which waited for: 3 -> 13; matrix products, arithmetic and copies ran while one was open for 1% -> 5% of each run, Pallas kernels for 0% -> 24%
where the time goes in v3:
time: 153 us; the launch traced here: 152 us
  Pallas kernels  70.4 us (46%)
  waiting for transfers between devices  33.1 us (22%)
  starting transfers between devices  22.6 us (15%)
  local copies, waits for them, and re-layouts  19 us (12%)
  other arithmetic  6.04 us (4%)
    pallas_call x3, Pallas kernels, round_logits(): pl.pallas_call(functools.partial(logits_kernel, stat_rows), grid=(depth /...  35.9 us
    pallas_call x1, Pallas kernels, refresh_states(): pl.pallas_call(functools.partial(refresh_kernel, lines, length, early_row...  23.1 us
    unnamed x26, local copies, waits for them, and re-layouts  15.4 us
    ppermute x7, waiting for transfers between devices, to_y(): return lax.ppermute(values, 'shard', swap_pairs(shards, 1))  13.7 us
    ppermute x6, waiting for transfers between devices, to_x(): return lax.ppermute(values, 'rep', swap_pairs(reps, 2))  11.2 us
    ppermute x7, starting transfers between devices, to_y(): return lax.ppermute(values, 'shard', swap_pairs(shards, 1))  8.88 us
    pallas_call x1, Pallas kernels, one_hot_sums(): pl.pallas_call(functools.partial(one_hot_kernel, len(features)), grid=(co...  8.23 us
    ppermute x6, waiting for transfers between devices, to_z(): return lax.ppermute(values, 'shard', shift_pairs(lines, along, 0))  7.3 us
  transfers between devices with their start and end apart: 26, of which 13 were waited for; matrix products, arithmetic and copies ran while one was open for 5% of the time, Pallas kernels for 24%

profile of v3, /device:TPU:0, one launch (start us, length us, event | category | flops | bytes accessed | tf_op | source)
XLA Modules:
  0.0 152.1 jit_solution(5964752240210360856)
XLA Ops:
  0.6 1.2 fusion
  1.9 1.2 fusion.2.refs_0_
  3.1 3.0 %collective-permute-start.2 = (bf16[64,3584]{1,0:T(8,128)(2,1)S(1)}, bf16[64,3584]{1,0:T(8,128)(2,1)S(1)}, u32[]{:S(2)}, u32[]{:S(2)}) collective-permute-start(bf16[64,3584]{1,0:T(8,128)(2,1)S(1)} %fusion.2.refs_0_), channel_id=1, source_target_pairs={{0,1},{1,0},{2,3},{3,2},{4,5},{5,4},{6,7},{7,6},{8,9},{9,8},{10,11... | collective-permute-start | bytes 1376264 | tf_op jit(solution)/shard_map/ppermute | solution.py:392
  6.1 1.5 collective-permute-start.1
  7.6 1.6 %collective-permute-start = (bf16[64,3584]{1,0:T(8,128)(2,1)S(1)}, bf16[64,3584]{1,0:T(8,128)(2,1)S(1)}, u32[]{:S(2)}, u32[]{:S(2)}) collective-permute-start(bf16[64,3584]{1,0:T(8,128)(2,1)S(1)} %fusion.2.refs_0_), channel_id=1, source_target_pairs={{0,2},{1,3},{2,4},{3,5},{4,6},{5,7},{6,0},{7,1},{8,10},{9,11},{10,... | collective-permute-start | bytes 1376264 | tf_op jit(solution)/shard_map/ppermute | solution.py:402
  9.2 0.7 fusion.7
  9.8 0.7 compare_and_fusion
  10.5 0.7 multiply_add_fusion
  11.2 1.2 slice.31
  12.4 0.8 slice.30
  13.3 0.7 broadcast_subtract_fusion
  14.1 0.7 fusion.4
  16.0 0.7 collective-permute-done.2.refs_2_
  16.6 1.5 collective-permute-done.1.refs_1_
  18.1 3.1 %collective-permute-done.refs_3_ = bf16[64,3584]{1,0:T(8,128)(2,1)S(1)} collective-permute-done((bf16[64,3584]{1,0:T(8,128)(2,1)S(1)}, bf16[64,3584]{1,0:T(8,128)(2,1)S(1)}, u32[]{:S(2)}, u32[]{:S(2)}) %collective-permute-start) | collective-permute-done | bytes 458784 | tf_op jit(solution)/shard_map/ppermute | solution.py:402
  22.2 9.8 %collective-permute-done.5.refs_5_ = bf16[64,3584]{1,0:T(8,128)(2,1)S(1)} collective-permute-done((bf16[64,3584]{1,0:T(8,128)(2,1)S(1)}, bf16[64,3584]{1,0:T(8,128)(2,1)S(1)}, u32[]{:S(2)}, u32[]{:S(2)}) %collective-permute-start.5) | collective-permute-done | bytes 458784 | tf_op jit(solution)/shard_map/ppermute | solution.py:392
  32.2 2.3 %collective-permute-done.3.refs_0_ = bf16[64,3584]{1,0:T(8,128)(2,1)S(1)} collective-permute-done((bf16[64,3584]{1,0:T(8,128)(2,1)S(1)}, bf16[64,3584]{1,0:T(8,128)(2,1)S(1)}, u32[]{:S(2)}, u32[]{:S(2)}) %collective-permute-start.3) | collective-permute-done | bytes 458784 | tf_op jit(solution)/shard_map/ppermute | solution.py:402
  34.5 1.3 collective-permute-start.8
  35.8 1.5 collective-permute-start.7
  37.8 11.9 %round_logits.3 = (bf16[384,2048]{1,0:T(8,128)(2,1)S(1)}, f32[32,128]{1,0:T(8,128)S(1)}) custom-call(bf16[64,3584]{1,0:T(8,128)(2,1)S(1)} %fusion.2.refs_0_, bf16[64,3584]{1,0:T(8,128)(2,1)S(1)} %collective-permute-done.1.refs_1_, bf16[64,3584]{1,0:T(8,128)(2,1)S(1)} %collective-permute-done.2.refs_2_, bf16[64,3584]{1,0:T(8,128)(2,1)S(1)} %collective-permute-done.refs_3_, ...), custom_call_target="tpu_custom_call" | custom-call | flops 1024 | bytes 1024 | tf_op jit(solution)/shard_map/round_logits/pallas_call | solution.py:145
  49.8 4.9 %collective-permute-done.9.refs_6_ = bf16[64,3584]{1,0:T(8,128)(2,1)S(1)} collective-permute-done((bf16[64,3584]{1,0:T(8,128)(2,1)S(1)}, bf16[64,3584]{1,0:T(8,128)(2,1)S(1)}, u32[]{:S(2)}, u32[]{:S(2)}) %collective-permute-start.9) | collective-permute-done | bytes 458784 | tf_op jit(solution)/shard_map/ppermute | solution.py:386
  54.7 0.9 turned_features.2
  56.1 1.5 collective-permute-start.12
  58.1 1.0 collective-permute-start.11
  59.1 0.9 collective-permute-done.10.refs_1_
  60.0 1.0 collective-permute-start.15
  61.0 8.2 %one_hot_sums.1 = (bf16[896,2048]{1,0:T(8,128)(2,1)S(1)}, bf16[896,2048]{1,0:T(8,128)(2,1)S(1)}) custom-call(bf16[896,384]{1,0:T(8,128)(2,1)S(1)} %get-tuple-element.55.refs_0_, bf16[896,384]{1,0:T(8,128)(2,1)S(1)} %collective-permute-done.10.refs_1_, s32[1,768]{1,0:T(1,128)S(1)} %squeeze.12.refs_2_, s32[1,768]{1,0:T(1,128)S(1)} %squeeze.13.refs_3_), custom_call_target="tpu_custom_call" | custom-call | flops 1024 | bytes 1024 | tf_op jit(solution)/shard_map/one_hot_sums/pallas_call | solution.py:222
  69.2 1.8 %copy-done = bf16[896,2048]{1,0:T(8,128)(2,1)} copy-done((bf16[896,2048]{1,0:T(8,128)(2,1)}, bf16[896,2048]{1,0:T(8,128)(2,1)S(1)}, u32[]{:S(2)}) %copy-start) | copy-done | bytes 3670040
  71.1 1.8 %copy-done.2 = bf16[896,2048]{1,0:T(8,128)(2,1)} copy-done((bf16[896,2048]{1,0:T(8,128)(2,1)}, bf16[896,2048]{1,0:T(8,128)(2,1)S(1)}, u32[]{:S(2)}) %copy-start.2) | copy-done | bytes 3670040
  72.9 1.1 collective-permute-start.13
  73.9 4.5 %collective-permute-done.11.refs_0_.refs_8_ = bf16[64,3584]{1,0:T(8,128)(2,1)S(1)} collective-permute-done((bf16[64,3584]{1,0:T(8,128)(2,1)S(1)}, bf16[64,3584]{1,0:T(8,128)(2,1)S(1)}, u32[]{:S(2)}, u32[]{:S(2)}) %collective-permute-start.11) | collective-permute-done | bytes 458784 | tf_op jit(solution)/shard_map/ppermute | solution.py:386
  78.5 2.4 %collective-permute-done.15.refs_5_ = bf16[64,3584]{1,0:T(8,128)(2,1)S(1)} collective-permute-done((bf16[64,3584]{1,0:T(8,128)(2,1)S(1)}, bf16[64,3584]{1,0:T(8,128)(2,1)S(1)}, u32[]{:S(2)}, u32[]{:S(2)}) %collective-permute-start.15) | collective-permute-done | bytes 458784 | tf_op jit(solution)/shard_map/ppermute | solution.py:392
  80.9 13.4 %round_logits.4 = (bf16[512,2048]{1,0:T(8,128)(2,1)S(1)}, f32[32,128]{1,0:T(8,128)S(1)}) custom-call(bf16[64,3584]{1,0:T(8,128)(2,1)S(1)} %collective-permute-done.3.refs_0_, bf16[64,3584]{1,0:T(8,128)(2,1)S(1)} %collective-permute-done.7.refs_1_, bf16[64,3584]{1,0:T(8,128)(2,1)S(1)} %collective-permute-done.8.refs_2_, ...), custom_call_target="tpu_custom_call" | custom-call | flops 1024 | bytes 1024 | tf_op jit(solution)/shard_map/round_logits/pallas_call | solution.py:145
  94.3 10.6 %round_logits.5 = (bf16[128,2048]{1,0:T(8,128)(2,1)}, f32[32,128]{1,0:T(8,128)S(1)}) custom-call(bf16[64,3584]{1,0:T(8,128)(2,1)S(1)} %collective-permute-done.11.refs_0_.refs_8_, bf16[64,3584]{1,0:T(8,128)(2,1)S(1)} %collective-permute-done.13.refs_1_.refs_9_, bf16[3584,2048]{1,0:T(8,128)(2,1)} %refs_2_.1, f32[32,128]{1,0:T(8,128)S(1)} %get-tuple-element.69.refs_3_), custom_call_target="tpu_custom_call" | custom-call | flops 1024 | bytes 1024 | tf_op jit(solution)/shard_map/round_logits/pallas_call | solution.py:145
  105.0 2.3 %turned_features.3 = (bf16[896,640]{1,0:T(8,128)(2,1)S(1)}, bf16[896,640]{1,0:T(8,128)(2,1)}) custom-call(s32[1]{0:T(128)} %bitcast.5.rep_ref, bf16[64,3584]{1,0:T(8,128)(2,1)S(1)} %collective-permute-done.3.refs_0_, bf16[64,3584]{1,0:T(8,128)(2,1)S(1)} %collective-permute-done.7.refs_1_, bf16[64,3584]{1,0:T(8,128)(2,1)S(1)} %collective-permute-done.8.refs_2_, ...), custom_call_target="tpu_custom_call" | custom-call | flops 1024 | bytes 1024 | tf_op jit(solution)/shard_map/turned_features/pallas_call | solution.py:185
  107.3 1.1 copy-done.11
  109.5 1.5 collective-permute-start.19
  111.0 1.3 copy-done.5
  112.4 0.9 collective-permute-done.19.across_ref
  113.8 3.5 %collective-permute-start.23 = (f32[64,128]{1,0:T(8,128)S(1)}, f32[64,128]{1,0:T(8,128)S(1)}, u32[]{:S(2)}, u32[]{:S(2)}) collective-permute-start(f32[64,128]{1,0:T(8,128)S(1)} %get-tuple-element.78.refs_10_), channel_id=1, source_target_pairs={{0,6},{1,7},{2,0},{3,1},{4,2},{5,3},{6,4},{7,5},{8,14},{9,15},{10,... | collective-permute-start | bytes 98312 | tf_op jit(solution)/shard_map/ppermute | solution.py:402
  117.8 1.6 %collective-permute-done.25.refs_13_ = f32[64,128]{1,0:T(8,128)S(1)} collective-permute-done((f32[64,128]{1,0:T(8,128)S(1)}, f32[64,128]{1,0:T(8,128)S(1)}, u32[]{:S(2)}, u32[]{:S(2)}) %collective-permute-start.25) | collective-permute-done | bytes 32800 | tf_op jit(solution)/shard_map/ppermute | solution.py:402
  119.7 2.0 %copy-done.1 = bf16[896,2048]{1,0:T(8,128)(2,1)S(1)} copy-done((bf16[896,2048]{1,0:T(8,128)(2,1)S(1)}, bf16[896,2048]{1,0:T(8,128)(2,1)}, u32[]{:S(2)}) %copy-start.1) | copy-done | bytes 3670040
  121.8 1.6 %copy-done.4 = bf16[512,2048]{1,0:T(8,128)(2,1)S(1)} copy-done((bf16[512,2048]{1,0:T(8,128)(2,1)S(1)}, bf16[512,2048]{1,0:T(8,128)(2,1)}, u32[]{:S(2)}) %copy-start.4) | copy-done | bytes 2097176
  123.3 1.6 %copy-done.6 = bf16[512,2048]{1,0:T(8,128)(2,1)S(1)} copy-done((bf16[512,2048]{1,0:T(8,128)(2,1)S(1)}, bf16[512,2048]{1,0:T(8,128)(2,1)}, u32[]{:S(2)}) %copy-start.6) | copy-done | bytes 2097176
  124.9 1.4 copy-done.8
  126.3 1.4 copy-done.10
  127.8 1.3 copy-done.12
  129.0 23.1 %refresh_states.1 = (bf16[896,2048]{1,0:T(8,128)(2,1)}, bf16[896,2048]{1,0:T(8,128)(2,1)}, bf16[896,2048]{1,0:T(8,128)(2,1)}) custom-call(bf16[896,384]{1,0:T(8,128)(2,1)S(1)} %get-tuple-element.55.refs_0_, bf16[896,384]{1,0:T(8,128)(2,1)S(1)} %collective-permute-done.10.refs_1_, bf16[896,640]{1,0:T(8,128)(2,1)S(1)} %copy-done.12, ...), custom_call_target="tpu_custom_call" | custom-call | flops 1024 | bytes 1024 | tf_op jit(solution)/shard_map/refresh_states/pallas_call | solution.py:351
  (66 shorter events, 6.8 us)
Async XLA Ops:
  3.1 13.6 %collective-permute-start.2 = (bf16[64,3584]{1,0:T(8,128)(2,1)S(1)}, bf16[64,3584]{1,0:T(8,128)(2,1)S(1)}, u32[]{:S(2)}, u32[]{:S(2)}) collective-permute-start(bf16[64,3584]{1,0:T(8,128)(2,1)S(1)} %fusion.2.refs_0_), channel_id=1, source_target_pairs={{0,1},{1,0},{2,3},{3,2},{4,5},{5,4},{6,7},{7,6},{8,9},{9,8},{10,11... | collective-permute-start | bytes 1376264 | tf_op jit(solution)/shard_map/ppermute | solution.py:392
  6.1 12.0 %collective-permute-start.1 = (bf16[64,3584]{1,0:T(8,128)(2,1)S(1)}, bf16[64,3584]{1,0:T(8,128)(2,1)S(1)}, u32[]{:S(2)}, u32[]{:S(2)}) collective-permute-start(bf16[64,3584]{1,0:T(8,128)(2,1)S(1)} %fusion.2.refs_0_), channel_id=1, source_target_pairs={{0,16},{8,24},{16,0},{24,8},{1,17},{9,25},{17,1},{25,9},{2,18},{10... | collective-permute-start | bytes 1376264 | tf_op jit(solution)/shard_map/ppermute | solution.py:386
  7.6 13.6 %collective-permute-start = (bf16[64,3584]{1,0:T(8,128)(2,1)S(1)}, bf16[64,3584]{1,0:T(8,128)(2,1)S(1)}, u32[]{:S(2)}, u32[]{:S(2)}) collective-permute-start(bf16[64,3584]{1,0:T(8,128)(2,1)S(1)} %fusion.2.refs_0_), channel_id=1, source_target_pairs={{0,2},{1,3},{2,4},{3,5},{4,6},{5,7},{6,0},{7,1},{8,10},{9,11},{10,... | collective-permute-start | bytes 1376264 | tf_op jit(solution)/shard_map/ppermute | solution.py:402
  21.1 10.8 %collective-permute-start.5 = (bf16[64,3584]{1,0:T(8,128)(2,1)S(1)}, bf16[64,3584]{1,0:T(8,128)(2,1)S(1)}, u32[]{:S(2)}, u32[]{:S(2)}) collective-permute-start(bf16[64,3584]{1,0:T(8,128)(2,1)S(1)} %collective-permute-done.refs_3_), channel_id=1, source_target_pairs={{0,1},{1,0},{2,3},{3,2},{4,5},{5,4},{6,7},{7,6},{8,9},{9,8},{10,11... | collective-permute-start | bytes 1376264 | tf_op jit(solution)/shard_map/ppermute | solution.py:392
  21.6 10.6 %collective-permute-start.4 = (bf16[64,3584]{1,0:T(8,128)(2,1)S(1)}, bf16[64,3584]{1,0:T(8,128)(2,1)S(1)}, u32[]{:S(2)}, u32[]{:S(2)}) collective-permute-start(bf16[64,3584]{1,0:T(8,128)(2,1)S(1)} %collective-permute-done.refs_3_), channel_id=1, source_target_pairs={{0,16},{8,24},{16,0},{24,8},{1,17},{9,25},{17,1},{25,9},{2,18},{10... | collective-permute-start | bytes 1376264 | tf_op jit(solution)/shard_map/ppermute | solution.py:386
  22.2 12.3 %collective-permute-start.3 = (bf16[64,3584]{1,0:T(8,128)(2,1)S(1)}, bf16[64,3584]{1,0:T(8,128)(2,1)S(1)}, u32[]{:S(2)}, u32[]{:S(2)}) collective-permute-start(bf16[64,3584]{1,0:T(8,128)(2,1)S(1)} %collective-permute-done.refs_3_), channel_id=1, source_target_pairs={{0,2},{1,3},{2,4},{3,5},{4,6},{5,7},{6,0},{7,1},{8,10},{9,11},{10,... | collective-permute-start | bytes 1376264 | tf_op jit(solution)/shard_map/ppermute | solution.py:402
  34.5 15.2 %collective-permute-start.8 = (bf16[64,3584]{1,0:T(8,128)(2,1)S(1)}, bf16[64,3584]{1,0:T(8,128)(2,1)S(1)}, u32[]{:S(2)}, u32[]{:S(2)}) collective-permute-start(bf16[64,3584]{1,0:T(8,128)(2,1)S(1)} %collective-permute-done.3.refs_0_), channel_id=1, source_target_pairs={{0,1},{1,0},{2,3},{3,2},{4,5},{5,4},{6,7},{7,6},{8,9},{9,8},{10,11... | collective-permute-start | bytes 1376264 | tf_op jit(solution)/shard_map/ppermute | solution.py:392
  35.8 14.0 %collective-permute-start.7 = (bf16[64,3584]{1,0:T(8,128)(2,1)S(1)}, bf16[64,3584]{1,0:T(8,128)(2,1)S(1)}, u32[]{:S(2)}, u32[]{:S(2)}) collective-permute-start(bf16[64,3584]{1,0:T(8,128)(2,1)S(1)} %collective-permute-done.3.refs_0_), channel_id=1, source_target_pairs={{0,16},{8,24},{16,0},{24,8},{1,17},{9,25},{17,1},{25,9},{2,18},{10... | collective-permute-start | bytes 1376264 | tf_op jit(solution)/shard_map/ppermute | solution.py:386
  37.3 12.5 %collective-permute-start.6 = (bf16[64,3584]{1,0:T(8,128)(2,1)S(1)}, bf16[64,3584]{1,0:T(8,128)(2,1)S(1)}, u32[]{:S(2)}, u32[]{:S(2)}) collective-permute-start(bf16[64,3584]{1,0:T(8,128)(2,1)S(1)} %collective-permute-done.3.refs_0_), channel_id=1, source_target_pairs={{0,2},{1,3},{2,4},{3,5},{4,6},{5,7},{6,0},{7,1},{8,10},{9,11},{10,... | collective-permute-start | bytes 1376264 | tf_op jit(solution)/shard_map/ppermute | solution.py:402
  37.3 17.4 %collective-permute-start.9 = (bf16[64,3584]{1,0:T(8,128)(2,1)S(1)}, bf16[64,3584]{1,0:T(8,128)(2,1)S(1)}, u32[]{:S(2)}, u32[]{:S(2)}) collective-permute-start(bf16[64,3584]{1,0:T(8,128)(2,1)S(1)} %collective-permute-done.2.refs_2_), channel_id=1, source_target_pairs={{0,16},{8,24},{16,0},{24,8},{1,17},{9,25},{17,1},{25,9},{2,18},{10... | collective-permute-start | bytes 1376264 | tf_op jit(solution)/shard_map/ppermute | solution.py:386
  49.7 44.6 %copy-start.7 = (bf16[384,2048]{1,0:T(8,128)(2,1)}, bf16[384,2048]{1,0:T(8,128)(2,1)S(1)}, u32[]{:S(2)}) copy-start(bf16[384,2048]{1,0:T(8,128)(2,1)S(1)} %get-tuple-element.65.refs_4_) | copy-start | bytes 4718596
  55.6 22.9 %collective-permute-start.14 = (bf16[384,2048]{1,0:T(8,128)(2,1)S(1)}, bf16[384,2048]{1,0:T(8,128)(2,1)S(1)}, u32[]{:S(2)}, u32[]{:S(2)}) collective-permute-start(bf16[384,2048]{1,0:T(8,128)(2,1)S(1)} %get-tuple-element.65.refs_4_), channel_id=1, source_target_pairs={{0,8},{8,0},{16,24},{24,16},{1,9},{9,1},{17,25},{25,17},{2,10},{10... | collective-permute-start | bytes 4718600 | tf_op jit(solution)/shard_map/ppermute | solution.py:389
  55.6 4.4 %collective-permute-start.10 = (bf16[896,384]{1,0:T(8,128)(2,1)S(1)}, bf16[896,384]{1,0:T(8,128)(2,1)S(1)}, u32[]{:S(2)}, u32[]{:S(2)}) collective-permute-start(bf16[896,384]{1,0:T(8,128)(2,1)S(1)} %get-tuple-element.56), channel_id=1, source_target_pairs={{0,8},{8,0},{16,24},{24,16},{1,9},{9,1},{17,25},{25,17},{2,10},{10... | collective-permute-start | bytes 2064392 | tf_op jit(solution)/shard_map/ppermute | solution.py:389
  56.1 16.7 %collective-permute-start.12 = (bf16[64,3584]{1,0:T(8,128)(2,1)S(1)}, bf16[64,3584]{1,0:T(8,128)(2,1)S(1)}, u32[]{:S(2)}, u32[]{:S(2)}) collective-permute-start(bf16[64,3584]{1,0:T(8,128)(2,1)S(1)} %collective-permute-done.6.refs_3_), channel_id=1, source_target_pairs={{0,16},{8,24},{16,0},{24,8},{1,17},{9,25},{17,1},{25,9},{2,18},{10... | collective-permute-start | bytes 1376264 | tf_op jit(solution)/shard_map/ppermute | solution.py:386
  57.6 20.9 %collective-permute-start.16 = (bf16[64,3584]{1,0:T(8,128)(2,1)S(1)}, bf16[64,3584]{1,0:T(8,128)(2,1)S(1)}, u32[]{:S(2)}, u32[]{:S(2)}) collective-permute-start(bf16[64,3584]{1,0:T(8,128)(2,1)S(1)} %collective-permute-done.4.refs_4_), channel_id=1, source_target_pairs={{0,1},{1,0},{2,3},{3,2},{4,5},{5,4},{6,7},{7,6},{8,9},{9,8},{10,11... | collective-permute-start | bytes 1376264 | tf_op jit(solution)/shard_map/ppermute | solution.py:392
  58.1 20.3 %collective-permute-start.11 = (bf16[64,3584]{1,0:T(8,128)(2,1)S(1)}, bf16[64,3584]{1,0:T(8,128)(2,1)S(1)}, u32[]{:S(2)}, u32[]{:S(2)}) collective-permute-start(bf16[64,3584]{1,0:T(8,128)(2,1)S(1)} %collective-permute-done.8.refs_2_), channel_id=1, source_target_pairs={{0,16},{8,24},{16,0},{24,8},{1,17},{9,25},{17,1},{25,9},{2,18},{10... | collective-permute-start | bytes 1376264 | tf_op jit(solution)/shard_map/ppermute | solution.py:386
  60.0 20.9 %collective-permute-start.15 = (bf16[64,3584]{1,0:T(8,128)(2,1)S(1)}, bf16[64,3584]{1,0:T(8,128)(2,1)S(1)}, u32[]{:S(2)}, u32[]{:S(2)}) collective-permute-start(bf16[64,3584]{1,0:T(8,128)(2,1)S(1)} %collective-permute-done.6.refs_3_), channel_id=1, source_target_pairs={{0,1},{1,0},{2,3},{3,2},{4,5},{5,4},{6,7},{7,6},{8,9},{9,8},{10,11... | collective-permute-start | bytes 1376264 | tf_op jit(solution)/shard_map/ppermute | solution.py:392
  69.2 1.8 %copy-start = (bf16[896,2048]{1,0:T(8,128)(2,1)}, bf16[896,2048]{1,0:T(8,128)(2,1)S(1)}, u32[]{:S(2)}) copy-start(bf16[896,2048]{1,0:T(8,128)(2,1)S(1)} %get-tuple-element.62.refs_17_) | copy-start | bytes 11010052
  71.1 1.8 %copy-start.2 = (bf16[896,2048]{1,0:T(8,128)(2,1)}, bf16[896,2048]{1,0:T(8,128)(2,1)S(1)}, u32[]{:S(2)}) copy-start(bf16[896,2048]{1,0:T(8,128)(2,1)S(1)} %get-tuple-element.64.refs_18_) | copy-start | bytes 11010052
  72.9 21.5 %collective-permute-start.13 = (bf16[64,3584]{1,0:T(8,128)(2,1)S(1)}, bf16[64,3584]{1,0:T(8,128)(2,1)S(1)}, u32[]{:S(2)}, u32[]{:S(2)}) collective-permute-start(bf16[64,3584]{1,0:T(8,128)(2,1)S(1)} %collective-permute-done.12.refs_4_), channel_id=1, source_target_pairs={{0,1},{1,0},{2,3},{3,2},{4,5},{5,4},{6,7},{7,6},{8,9},{9,8},{10,11... | collective-permute-start | bytes 1376264 | tf_op jit(solution)/shard_map/ppermute | solution.py:392
  78.5 15.8 %copy-start.9 = (bf16[384,2048]{1,0:T(8,128)(2,1)}, bf16[384,2048]{1,0:T(8,128)(2,1)S(1)}, u32[]{:S(2)}) copy-start(bf16[384,2048]{1,0:T(8,128)(2,1)S(1)} %collective-permute-done.14.refs_7_) | copy-start | bytes 4718596
  94.3 10.7 %copy-start.3 = (bf16[512,2048]{1,0:T(8,128)(2,1)}, bf16[512,2048]{1,0:T(8,128)(2,1)S(1)}, u32[]{:S(2)}) copy-start(bf16[512,2048]{1,0:T(8,128)(2,1)S(1)} %get-tuple-element.76.refs_5_) | copy-start | bytes 6291460
  105.0 6.1 %collective-permute-start.18 = (bf16[512,2048]{1,0:T(8,128)(2,1)S(1)}, bf16[512,2048]{1,0:T(8,128)(2,1)S(1)}, u32[]{:S(2)}, u32[]{:S(2)}) collective-permute-start(bf16[512,2048]{1,0:T(8,128)(2,1)S(1)} %get-tuple-element.76.refs_5_), channel_id=1, source_target_pairs={{0,8},{8,0},{16,24},{24,16},{1,9},{9,1},{17,25},{25,17},{2,10},{10... | collective-permute-start | bytes 6291464 | tf_op jit(solution)/shard_map/ppermute | solution.py:389
  107.3 1.1 copy-start.11
  108.4 9.4 %collective-permute-start.17 = (bf16[896,640]{1,0:T(8,128)(2,1)}, bf16[896,640]{1,0:T(8,128)(2,1)}, u32[]{:S(2)}, u32[]{:S(2)}) collective-permute-start(bf16[896,640]{1,0:T(8,128)(2,1)} %get-tuple-element.73), channel_id=1, source_target_pairs={{0,8},{8,0},{16,24},{24,16},{1,9},{9,1},{17,25},{25,17},{2,10},{10... | collective-permute-start | bytes 3440648 | tf_op jit(solution)/shard_map/ppermute | solution.py:389
  108.9 3.5 %collective-permute-start.21 = (f32[32,128]{1,0:T(8,128)S(1)}, f32[32,128]{1,0:T(8,128)S(1)}, u32[]{:S(2)}, u32[]{:S(2)}) collective-permute-start(f32[32,128]{1,0:T(8,128)S(1)} %get-tuple-element.77.own_ref), channel_id=1, source_target_pairs={{0,9},{1,8},{2,11},{3,10},{4,13},{5,12},{6,15},{7,14},{8,1},{9,0},... | collective-permute-start | bytes 49160 | tf_op jit(solution)/shard_map/ppermute | solution.py:399
  109.0 3.4 %collective-permute-start.20 = (f32[32,128]{1,0:T(8,128)S(1)}, f32[32,128]{1,0:T(8,128)S(1)}, u32[]{:S(2)}, u32[]{:S(2)}) collective-permute-start(f32[32,128]{1,0:T(8,128)S(1)} %get-tuple-element.77.own_ref), channel_id=1, source_target_pairs={{0,8},{8,0},{16,24},{24,16},{1,9},{9,1},{17,25},{25,17},{2,10},{10... | collective-permute-start | bytes 49160 | tf_op jit(solution)/shard_map/ppermute | solution.py:389
  109.5 3.7 %collective-permute-start.19 = (f32[32,128]{1,0:T(8,128)S(1)}, f32[32,128]{1,0:T(8,128)S(1)}, u32[]{:S(2)}, u32[]{:S(2)}) collective-permute-start(f32[32,128]{1,0:T(8,128)S(1)} %get-tuple-element.77.own_ref), channel_id=1, source_target_pairs={{0,1},{1,0},{2,3},{3,2},{4,5},{5,4},{6,7},{7,6},{8,9},{9,8},{10,11... | collective-permute-start | bytes 49160 | tf_op jit(solution)/shard_map/ppermute | solution.py:392
  111.0 1.3 copy-start.5
  113.3 6.5 %collective-permute-start.22 = (bf16[128,2048]{1,0:T(8,128)(2,1)}, bf16[128,2048]{1,0:T(8,128)(2,1)}, u32[]{:S(2)}, u32[]{:S(2)}) collective-permute-start(bf16[128,2048]{1,0:T(8,128)(2,1)} %get-tuple-element.79.refs_6_), channel_id=1, source_target_pairs={{0,8},{8,0},{16,24},{24,16},{1,9},{9,1},{17,25},{25,17},{2,10},{10... | collective-permute-start | bytes 1572872 | tf_op jit(solution)/shard_map/ppermute | solution.py:389
  113.3 6.0 %collective-permute-start.25 = (f32[64,128]{1,0:T(8,128)S(1)}, f32[64,128]{1,0:T(8,128)S(1)}, u32[]{:S(2)}, u32[]{:S(2)}) collective-permute-start(f32[64,128]{1,0:T(8,128)S(1)} %get-tuple-element.78.refs_10_), channel_id=1, source_target_pairs={{0,2},{1,3},{2,4},{3,5},{4,6},{5,7},{6,0},{7,1},{8,10},{9,11},{10,... | collective-permute-start | bytes 98312 | tf_op jit(solution)/shard_map/ppermute | solution.py:402
  113.4 6.0 %collective-permute-start.24 = (f32[64,128]{1,0:T(8,128)S(1)}, f32[64,128]{1,0:T(8,128)S(1)}, u32[]{:S(2)}, u32[]{:S(2)}) collective-permute-start(f32[64,128]{1,0:T(8,128)S(1)} %get-tuple-element.78.refs_10_), channel_id=1, source_target_pairs={{0,4},{1,5},{2,6},{3,7},{4,0},{5,1},{6,2},{7,3},{8,12},{9,13},{10,... | collective-permute-start | bytes 98312 | tf_op jit(solution)/shard_map/ppermute | solution.py:402
  113.8 5.9 %collective-permute-start.23 = (f32[64,128]{1,0:T(8,128)S(1)}, f32[64,128]{1,0:T(8,128)S(1)}, u32[]{:S(2)}, u32[]{:S(2)}) collective-permute-start(f32[64,128]{1,0:T(8,128)S(1)} %get-tuple-element.78.refs_10_), channel_id=1, source_target_pairs={{0,6},{1,7},{2,0},{3,1},{4,2},{5,3},{6,4},{7,5},{8,14},{9,15},{10,... | collective-permute-start | bytes 98312 | tf_op jit(solution)/shard_map/ppermute | solution.py:402
  119.7 2.0 %copy-start.1 = (bf16[896,2048]{1,0:T(8,128)(2,1)S(1)}, bf16[896,2048]{1,0:T(8,128)(2,1)}, u32[]{:S(2)}) copy-start(bf16[896,2048]{1,0:T(8,128)(2,1)} %copy-done) | copy-start | bytes 11010052
  121.8 1.6 %copy-start.4 = (bf16[512,2048]{1,0:T(8,128)(2,1)S(1)}, bf16[512,2048]{1,0:T(8,128)(2,1)}, u32[]{:S(2)}) copy-start(bf16[512,2048]{1,0:T(8,128)(2,1)} %copy-done.3) | copy-start | bytes 6291460
  123.3 1.6 %copy-start.6 = (bf16[512,2048]{1,0:T(8,128)(2,1)S(1)}, bf16[512,2048]{1,0:T(8,128)(2,1)}, u32[]{:S(2)}) copy-start(bf16[512,2048]{1,0:T(8,128)(2,1)} %copy-done.5) | copy-start | bytes 6291460
  124.9 1.4 copy-start.8
  126.3 1.4 copy-start.10
  127.8 1.3 copy-start.12

commit v4 on v3

--- a/solution.py
+++ b/solution.py
@@ -13,6 +13,7 @@
 BETA_TWO = 0.95
 RHO_SCALE = 0.05
 GATHER_BYTES = 32 * 1024 * 1024
+LOGITS_VMEM = 20 * 1024 * 1024
 BRIEF = pl.CostEstimate(flops=1024, bytes_accessed=1024, transcendentals=0)
 
 
@@ -84,83 +85,125 @@
     return pairs
 
 
+def prepare_kernel(weight_ref, true_ids, sample_ids, *refs):
+    held_ref, true_at, sample_at, arrived = refs[-4:]
+    count = arrived.shape[0]
+    band = weight_ref.shape[0] // count
+    copies = [
+        pltpu.make_async_copy(
+            weight_ref.at[pl.ds(index * band, band)], held_ref.at[pl.ds(index * band, band)],
+            arrived.at[index],
+        )
+        for index in range(count)
+    ]
+    for copy in copies:
+        copy.start()
+    lanes = lax.broadcasted_iota(jnp.int32, (128, 128), 1)
+    for ids_ref, out_ref in ((true_ids, true_at), (sample_ids, sample_at)):
+        for place in range(0, out_ref.shape[0], 128):
+            ids = jnp.broadcast_to(ids_ref[:, place:place + 128], (128, 128)).T
+            out_ref[place:place + 128] = ids - lanes
+    for copy in copies:
+        copy.wait()
+
+
+def prepared(weight, true_ids, sample_ids, *earlier):
+    near = pl.BlockSpec(memory_space=pltpu.VMEM)
+    late = jax.ShapeDtypeStruct((true_ids.shape[1], 128), jnp.int32)
+    return pl.pallas_call(
+        prepare_kernel,
+        in_specs=[pl.BlockSpec(memory_space=pltpu.HBM)] + [near] * (2 + len(earlier)),
+        out_specs=[near] * 3,
+        out_shape=[pltpu.VMEM(weight.shape, weight.dtype), late, late],
+        scratch_shapes=[pltpu.SemaphoreType.DMA((4,))],
+        compiler_params=pltpu.CompilerParams(vmem_limit_bytes=8 * 1024 * 1024),
+        cost_estimate=BRIEF,
+        name="prepared",
+    )(pltpu.with_memory_space_constraint(weight, pltpu.HBM), true_ids, sample_ids, *earlier)
+
+
 def logits_kernel(stat_rows, *refs):
     count = len(stat_rows)
     block_refs, refs = refs[:count], refs[count:]
-    weight_ref, before_ref, exp_ref, stats_ref, logits, highs, sums = refs
-    step = pl.program_id(0)
+    weight_ref, before_ref, exp_ref, stats_ref, rows, logits, scaled_exp, highs, sums, sent = refs
     tokens, columns = logits.shape
     length = tokens // count
     half = stats_ref.shape[0] // 2
-    rows = jnp.concatenate([ref[...] for ref in block_refs], axis=0)
-    width = min(512, columns)
-    for lane in range(0, columns, width):
-        part = jnp.dot(
-            rows, weight_ref[:, lane:lane + width], preferred_element_type=jnp.float32
+    for index, ref in enumerate(block_refs):
+        rows[index * length:(index + 1) * length] = ref[...]
+    highs[...] = jnp.full(highs.shape, -jnp.inf, jnp.float32)
+    width = min(256, columns)
+
+    def multiply(index, carry):
+        place = pl.ds(pl.multiple_of(index * width, width), width)
+        part = jnp.dot(rows[...], weight_ref[:, place], preferred_element_type=jnp.float32)
+        logits[:, place] = part
+        high = functools.reduce(
+            jnp.maximum, [part[:, lane:lane + 128] for lane in range(0, width, 128)]
         )
-        held = logits[:, lane:lane + width]
-        logits[:, lane:lane + width] = jnp.where(step == 0, 0.0, held) + part
-
-    @pl.when(step == pl.num_programs(0) - 1)
-    def _():
-        chunk = 16
-
-        def peaks(index, carry):
-            place = pl.ds(pl.multiple_of(index * chunk, chunk), chunk)
-            highs[place, :] = functools.reduce(
-                jnp.maximum, [logits[place, lane:lane + 128] for lane in range(0, columns, 128)]
-            )
-            return carry
-
-        lax.fori_loop(0, tokens // chunk, peaks, 0, unroll=2)
-        highs[...] = jnp.broadcast_to(jnp.max(highs[...], axis=1, keepdims=True), highs.shape)
-
-        def scale(index, carry):
-            place = pl.ds(pl.multiple_of(index * chunk, chunk), chunk)
+        highs[...] = jnp.maximum(highs[...], high)
+        return carry
+
+    lax.fori_loop(0, columns // width, multiply, 0)
+    highs[...] = jnp.broadcast_to(jnp.max(highs[...], axis=1, keepdims=True), highs.shape)
+    chunk = 16
+    copies = []
+    for block in range(count):
+
+        def scale(index, carry, block=block):
+            place = pl.ds(pl.multiple_of(block * length + index * chunk, chunk), chunk)
             peak = highs[place, :]
             total = jnp.zeros((chunk, 128), jnp.float32)
             for lane in range(0, columns, 128):
                 scaled = jnp.exp(logits[place, lane:lane + 128] - peak)
-                exp_ref[place, lane:lane + 128] = scaled.astype(jnp.bfloat16)
+                scaled_exp[place, lane:lane + 128] = scaled.astype(jnp.bfloat16)
                 total += scaled
             sums[place, :] = total
             return carry
 
-        lax.fori_loop(0, tokens // chunk, scale, 0, unroll=2)
-        totals = jnp.broadcast_to(jnp.sum(sums[...], axis=1, keepdims=True), sums.shape)
-        stats_ref[...] = before_ref[...]
-        for base, values in ((0, highs[...].T[0:1]), (half, totals.T[0:1])):
-            for index, row in enumerate(stat_rows):
-                stats_ref[base + row:base + row + 1, :length] = (
-                    values[:, index * length:(index + 1) * length]
-                )
-
-
-def round_logits(blocks, stat_rows, head_weight, before):
-    depth, columns = head_weight.shape
+        lax.fori_loop(0, length // chunk, scale, 0, unroll=2)
+        place = pl.ds(block * length, length)
+        copies.append(
+            pltpu.make_async_copy(scaled_exp.at[place], exp_ref.at[place], sent.at[block])
+        )
+        copies[-1].start()
+    totals = jnp.broadcast_to(jnp.sum(sums[...], axis=1, keepdims=True), sums.shape)
+    stats_ref[...] = before_ref[...]
+    for base, values in ((0, highs[...].T[0:1]), (half, totals.T[0:1])):
+        for index, row in enumerate(stat_rows):
+            stats_ref[base + row:base + row + 1, :length] = (
+                values[:, index * length:(index + 1) * length]
+            )
+    for copy in copies:
+        copy.wait()
+
+
+def round_logits(blocks, stat_rows, held_weight, before):
+    depth, columns = held_weight.shape
     length = blocks[0].shape[0]
     tokens = length * len(blocks)
-    band = 512
-    whole = lambda shape: pl.BlockSpec(shape, lambda step: (0, 0))
+    near = pl.BlockSpec(memory_space=pltpu.VMEM)
+    held_weight = pltpu.with_memory_space_constraint(held_weight, pltpu.VMEM)
     return pl.pallas_call(
         functools.partial(logits_kernel, stat_rows),
-        grid=(depth // band,),
-        in_specs=[pl.BlockSpec((length, band), lambda step: (0, step))] * len(blocks)
-        + [pl.BlockSpec((band, columns), lambda step: (step, 0)), whole(before.shape)],
-        out_specs=[whole((tokens, columns)), whole(before.shape)],
+        in_specs=[near] * (len(blocks) + 2),
+        out_specs=[pl.BlockSpec(memory_space=pltpu.HBM), near],
         out_shape=[
-            jax.ShapeDtypeStruct((tokens, columns), jnp.bfloat16),
+            pltpu.HBM((tokens, columns), jnp.bfloat16),
             jax.ShapeDtypeStruct(before.shape, jnp.float32),
         ],
         scratch_shapes=[
+            pltpu.VMEM((tokens, depth), jnp.bfloat16),
             pltpu.VMEM((tokens, columns), jnp.float32),
+            pltpu.VMEM((tokens, columns), jnp.bfloat16),
             pltpu.VMEM((tokens, 128), jnp.float32),
             pltpu.VMEM((tokens, 128), jnp.float32),
+            pltpu.SemaphoreType.DMA((len(blocks),)),
         ],
-        compiler_params=pltpu.CompilerParams(vmem_limit_bytes=24 * 1024 * 1024),
+        compiler_params=pltpu.CompilerParams(vmem_limit_bytes=LOGITS_VMEM),
         cost_estimate=BRIEF,
         name="round_logits",
-    )(*blocks, head_weight, before)
+    )(*blocks, held_weight, before)
 
 
 def turn_kernel(count, rep_ref, *refs):
@@ -224,7 +267,7 @@
         grid=(columns // width,),
         in_specs=[whole(array) for array in (*features, *ids)],
         out_specs=[tile, tile],
-        out_shape=[jax.ShapeDtypeStruct((rows, columns), jnp.bfloat16)] * 2,
+        out_shape=[pltpu.HBM((rows, columns), jnp.bfloat16)] * 2,
         compiler_params=pltpu.CompilerParams(vmem_limit_bytes=24 * 1024 * 1024),
         cost_estimate=BRIEF,
         name="one_hot_sums",
@@ -265,8 +308,8 @@
     early_refs, late_refs, refs = refs[:2], refs[2:4], refs[4:]
     exp_refs, refs = refs[:6], refs[6:]
     stats_refs, refs = refs[:lines], refs[lines:]
-    (first_ref, true_ids, sample_ids, true_sum, sample_sum, moment_ref, curvature_ref,
-     moment_out, curvature_out, update_out, scaled, factors, true_at, sample_at) = refs
+    (first_ref, true_at, sample_at, true_sum, sample_sum, moment_ref, curvature_ref,
+     moment_out, curvature_out, update_out, scaled, factors) = refs
     step = pl.program_id(0)
     width = moment_out.shape[1]
     early = len(early_rows) * length
@@ -306,9 +349,6 @@
                 factors[place:place + length] = jnp.broadcast_to(
                     full[:length, at:at + 1], (length, 128)
                 )
-        lanes = lax.broadcasted_iota(jnp.int32, true_at.shape, 1)
-        true_at[...] = true_ids[...] - lanes
-        sample_at[...] = sample_ids[...] - lanes
 
     shared = jnp.dot(
         scaled[...], jnp.concatenate([exp_refs[0][...], exp_refs[3][...]], axis=0),
@@ -360,13 +400,18 @@
         scratch_shapes=[
             pltpu.VMEM((rows, 2 * early[0].shape[1]), jnp.bfloat16),
             pltpu.VMEM((late_tokens, 128), jnp.float32),
-            pltpu.VMEM((late_tokens, 128), jnp.int32),
-            pltpu.VMEM((late_tokens, 128), jnp.int32),
         ],
         compiler_params=pltpu.CompilerParams(vmem_limit_bytes=36 * 1024 * 1024),
         cost_estimate=BRIEF,
         name="refresh_states",
-    )(*early, *late, *exps, *stats, first, *late_ids, *sums, moment, curvature)
+    )(
+        *early, *late, *in_hbm(exps[:3]), *exps[3:], *stats, first, *late_ids,
+        *in_hbm(sums, [moment, curvature])
+    )
+
+
+def in_hbm(*lists):
+    return [pltpu.with_memory_space_constraint(array, pltpu.HBM) for array in sum(map(list, lists), [])]
 
 
 def after(value, *others):
@@ -423,10 +468,9 @@
     ids = jnp.take(ids, holder * shards + jnp.tile(place, 2), axis=1)
     ids = ids.reshape(2, 2, len(side), length)
     early_ids = ids[:, :, :len(early_blocks)].reshape(2, 1, -1)
-    late_ids = ids[:, :, len(early_blocks):].reshape(2, -1, 1)
+    late_ids = ids[:, :, len(early_blocks):].reshape(2, 1, -1)
     early_ids, late_ids = [early_ids[0], early_ids[1]], [late_ids[0], late_ids[1]]
     rep_scalar = rep.astype(jnp.int32).reshape(1)
-    head_weight = pltpu.with_memory_space_constraint(head_weight, pltpu.HBM)
     stats = jnp.zeros((8 * lines, 128), jnp.float32)
 
     held = {(0, 0, 0): normed}
@@ -451,12 +495,13 @@
         if turn + 1 < lines:
             arrived = [to_z(block, 1), held[0, 1, turn], held[1, 0, turn]]
             if turn == 0:
-                arrived += [*early_ids, *late_ids, rep_scalar, stats]
+                head_weight, *late_ids = prepared(head_weight, *late_ids, *early_ids, stats)
+                arrived += [*early_ids, *late_ids, rep_scalar, stats, head_weight]
             arrived = lax.optimization_barrier((*arrived, *exps[-1:]))
             held[0, 0, turn + 1], held[0, 1, turn], held[1, 0, turn] = arrived[:3]
             if turn == 0:
                 early_ids, late_ids = list(arrived[3:5]), list(arrived[5:7])
-                rep_scalar, stats = arrived[7:]
+                rep_scalar, stats, head_weight = arrived[7:]
             if turn + 1 == split:
                 stats = logits(early_blocks, stats, held[0, 0, split])
         if turn < split:

time: 153 us -> 134 us (0.88)
  local copies, waits for them, and re-layouts: 19 us -> 3.16 us
  Pallas kernels: 70.4 us -> 63.3 us
  waiting for transfers between devices: 33.1 us -> 36.3 us
    unnamed x26 -> x4, local copies, waits for them, and re-layouts: 15.4 us -> 0.01 us
    ppermute x6, waiting for transfers between devices: 11.2 us -> 17.4 us  [to_x(): return lax.ppermute(values, 'rep', swap_pairs(reps, 2))]
    pallas_call x3 -> x4, Pallas kernels: 35.9 us -> 30.6 us  [the longest x3 25.1 us: round_logits(): pl.pallas_call(functools.partial(logits_kernel, stat_rows), in_specs=[nea...]
    ppermute x6, waiting for transfers between devices: 7.3 us -> 4.54 us  [to_z(): return lax.ppermute(values, 'shard', shift_pairs(lines, along, 0))]
    ppermute x7, waiting for transfers between devices: 13.7 us -> 11.6 us  [to_y(): return lax.ppermute(values, 'shard', swap_pairs(shards, 1))]
    ppermute x6, starting transfers between devices: 5.45 us -> 7.03 us  [to_z(): return lax.ppermute(values, 'shard', shift_pairs(lines, along, 0))]
  transfers between devices with their start and end apart: 26 -> 26, of which waited for: 13 -> 15; matrix products, arithmetic and copies ran while one was open for 5% -> 5% of each run, Pallas kernels for 24% -> 27%
where the time goes in v4:
time: 134 us; the launch traced here: 133 us
  Pallas kernels  63.3 us (47%)
  waiting for transfers between devices  36.3 us (27%)
  starting transfers between devices  23.5 us (18%)
  other arithmetic  6.04 us (5%)
  local copies, waits for them, and re-layouts  3.16 us (2%)
    pallas_call x3, Pallas kernels, round_logits(): pl.pallas_call(functools.partial(logits_kernel, stat_rows), in_specs=[nea...  25.1 us
    pallas_call x1, Pallas kernels, refresh_states(): pl.pallas_call(functools.partial(refresh_kernel, lines, length, early_row...  21.8 us
    ppermute x6, waiting for transfers between devices, to_x(): return lax.ppermute(values, 'rep', swap_pairs(reps, 2))  17.4 us
    ppermute x7, waiting for transfers between devices, to_y(): return lax.ppermute(values, 'shard', swap_pairs(shards, 1))  11.6 us
    pallas_call x1, Pallas kernels, one_hot_sums(): pl.pallas_call(functools.partial(one_hot_kernel, len(features)), grid=(co...  8.67 us
    ppermute x7, starting transfers between devices, to_y(): return lax.ppermute(values, 'shard', swap_pairs(shards, 1))  8.55 us
    ppermute x6, starting transfers between devices, to_z(): return lax.ppermute(values, 'shard', shift_pairs(lines, along, 0))  7.03 us
    ppermute x6, starting transfers between devices, to_x(): return lax.ppermute(values, 'rep', swap_pairs(reps, 2))  6.08 us
  transfers between devices with their start and end apart: 26, of which 15 were waited for; matrix products, arithmetic and copies ran while one was open for 5% of the time, Pallas kernels for 27%

profile of v4, /device:TPU:0, one launch (start us, length us, event | category | flops | bytes accessed | tf_op | source)
XLA Modules:
  0.0 133.1 jit_solution(1232453698320510776)
XLA Ops:
  0.6 1.2 fusion
  1.9 1.2 fusion.2.refs_0_
  3.1 3.0 %collective-permute-start.2 = (bf16[64,3584]{1,0:T(8,128)(2,1)S(1)}, bf16[64,3584]{1,0:T(8,128)(2,1)S(1)}, u32[]{:S(2)}, u32[]{:S(2)}) collective-permute-start(bf16[64,3584]{1,0:T(8,128)(2,1)S(1)} %fusion.2.refs_0_), channel_id=1, source_target_pairs={{0,1},{1,0},{2,3},{3,2},{4,5},{5,4},{6,7},{7,6},{8,9},{9,8},{10,11... | collective-permute-start | bytes 1376264 | tf_op jit(solution)/shard_map/ppermute | solution.py:437
  6.1 1.5 %collective-permute-start.1 = (bf16[64,3584]{1,0:T(8,128)(2,1)S(1)}, bf16[64,3584]{1,0:T(8,128)(2,1)S(1)}, u32[]{:S(2)}, u32[]{:S(2)}) collective-permute-start(bf16[64,3584]{1,0:T(8,128)(2,1)S(1)} %fusion.2.refs_0_), channel_id=1, source_target_pairs={{0,16},{8,24},{16,0},{24,8},{1,17},{9,25},{17,1},{25,9},{2,18},{10... | collective-permute-start | bytes 1376264 | tf_op jit(solution)/shard_map/ppermute | solution.py:431
  7.6 1.6 %collective-permute-start = (bf16[64,3584]{1,0:T(8,128)(2,1)S(1)}, bf16[64,3584]{1,0:T(8,128)(2,1)S(1)}, u32[]{:S(2)}, u32[]{:S(2)}) collective-permute-start(bf16[64,3584]{1,0:T(8,128)(2,1)S(1)} %fusion.2.refs_0_), channel_id=1, source_target_pairs={{0,2},{1,3},{2,4},{3,5},{4,6},{5,7},{6,0},{7,1},{8,10},{9,11},{10,... | collective-permute-start | bytes 1376264 | tf_op jit(solution)/shard_map/ppermute | solution.py:447
  9.2 0.7 fusion.7
  9.8 0.7 compare_and_fusion
  10.5 0.7 multiply_add_fusion
  11.2 1.2 slice.31
  12.4 0.8 slice.30
  13.3 0.7 broadcast_subtract_fusion
  14.1 0.7 fusion.4
  14.9 0.6 gather_fusion
  16.0 5.5 %prepared.1 = (bf16[3584,2048]{1,0:T(8,128)(2,1)S(1)}, s32[1280,128]{1,0:T(8,128)S(1)}, s32[1280,128]{1,0:T(8,128)S(1)}) custom-call(bf16[3584,2048]{1,0:T(8,128)(2,1)} %weight_ref.1, s32[1,1280]{1,0:T(1,128)S(1)} %squeeze.14.true_ids, s32[1,1280]{1,0:T(1,128)S(1)} %squeeze.15.sample_ids, s32[1,768]{1,0:T(1,128)S(1)} %squeeze.12.refs_0_.refs_2_, ...), custom_call_target="tpu_custom_call" | custom-call | flops 1024 | bytes 1024 | tf_op jit(solution)/shard_map/prepared/pallas_call | solution.py:113
  21.5 0.6 collective-permute-start.5
  22.1 0.5 collective-permute-start.4
  22.6 1.6 %collective-permute-start.3 = (bf16[64,3584]{1,0:T(8,128)(2,1)S(1)}, bf16[64,3584]{1,0:T(8,128)(2,1)S(1)}, u32[]{:S(2)}, u32[]{:S(2)}) collective-permute-start(bf16[64,3584]{1,0:T(8,128)(2,1)S(1)} %collective-permute-done.refs_3_), channel_id=1, source_target_pairs={{0,2},{1,3},{2,4},{3,5},{4,6},{5,7},{6,0},{7,1},{8,10},{9,11},{10,... | collective-permute-start | bytes 1376264 | tf_op jit(solution)/shard_map/ppermute | solution.py:447
  24.2 8.8 %collective-permute-done.5.refs_5_ = bf16[64,3584]{1,0:T(8,128)(2,1)S(1)} collective-permute-done((bf16[64,3584]{1,0:T(8,128)(2,1)S(1)}, bf16[64,3584]{1,0:T(8,128)(2,1)S(1)}, u32[]{:S(2)}, u32[]{:S(2)}) %collective-permute-start.5) | collective-permute-done | bytes 458784 | tf_op jit(solution)/shard_map/ppermute | solution.py:437
  33.2 2.1 %collective-permute-done.3.refs_0_ = bf16[64,3584]{1,0:T(8,128)(2,1)S(1)} collective-permute-done((bf16[64,3584]{1,0:T(8,128)(2,1)S(1)}, bf16[64,3584]{1,0:T(8,128)(2,1)S(1)}, u32[]{:S(2)}, u32[]{:S(2)}) %collective-permute-start.3) | collective-permute-done | bytes 458784 | tf_op jit(solution)/shard_map/ppermute | solution.py:447
  35.3 1.5 %collective-permute-start.8 = (bf16[64,3584]{1,0:T(8,128)(2,1)S(1)}, bf16[64,3584]{1,0:T(8,128)(2,1)S(1)}, u32[]{:S(2)}, u32[]{:S(2)}) collective-permute-start(bf16[64,3584]{1,0:T(8,128)(2,1)S(1)} %collective-permute-done.3.refs_0_), channel_id=1, source_target_pairs={{0,1},{1,0},{2,3},{3,2},{4,5},{5,4},{6,7},{7,6},{8,9},{9,8},{10,11... | collective-permute-start | bytes 1376264 | tf_op jit(solution)/shard_map/ppermute | solution.py:437
  36.8 1.5 %collective-permute-start.7 = (bf16[64,3584]{1,0:T(8,128)(2,1)S(1)}, bf16[64,3584]{1,0:T(8,128)(2,1)S(1)}, u32[]{:S(2)}, u32[]{:S(2)}) collective-permute-start(bf16[64,3584]{1,0:T(8,128)(2,1)S(1)} %collective-permute-done.3.refs_0_), channel_id=1, source_target_pairs={{0,16},{8,24},{16,0},{24,8},{1,17},{9,25},{17,1},{25,9},{2,18},{10... | collective-permute-start | bytes 1376264 | tf_op jit(solution)/shard_map/ppermute | solution.py:431
  38.3 0.5 collective-permute-start.9
  38.8 9.0 %round_logits.3 = (bf16[384,2048]{1,0:T(8,128)(2,1)}, f32[32,128]{1,0:T(8,128)S(1)}) custom-call(bf16[64,3584]{1,0:T(8,128)(2,1)S(1)} %fusion.2.refs_0_, bf16[64,3584]{1,0:T(8,128)(2,1)S(1)} %collective-permute-done.1.refs_1_, bf16[64,3584]{1,0:T(8,128)(2,1)S(1)} %collective-permute-done.2.refs_2_, bf16[64,3584]{1,0:T(8,128)(2,1)S(1)} %collective-permute-done.refs_3_, ...), custom_call_target="tpu_custom_call" | custom-call | flops 1024 | bytes 1024 | tf_op jit(solution)/shard_map/round_logits/pallas_call | solution.py:187
  47.9 2.4 %collective-permute-done.7.refs_1_ = bf16[64,3584]{1,0:T(8,128)(2,1)S(1)} collective-permute-done((bf16[64,3584]{1,0:T(8,128)(2,1)S(1)}, bf16[64,3584]{1,0:T(8,128)(2,1)S(1)}, u32[]{:S(2)}, u32[]{:S(2)}) %collective-permute-start.7) | collective-permute-done | bytes 458784 | tf_op jit(solution)/shard_map/ppermute | solution.py:431
  50.3 6.0 %collective-permute-done.9.refs_6_ = bf16[64,3584]{1,0:T(8,128)(2,1)S(1)} collective-permute-done((bf16[64,3584]{1,0:T(8,128)(2,1)S(1)}, bf16[64,3584]{1,0:T(8,128)(2,1)S(1)}, u32[]{:S(2)}, u32[]{:S(2)}) %collective-permute-start.9) | collective-permute-done | bytes 458784 | tf_op jit(solution)/shard_map/ppermute | solution.py:431
  56.3 0.9 turned_features.2
  57.2 0.5 collective-permute-start.10
  57.7 1.5 %collective-permute-start.12 = (bf16[64,3584]{1,0:T(8,128)(2,1)S(1)}, bf16[64,3584]{1,0:T(8,128)(2,1)S(1)}, u32[]{:S(2)}, u32[]{:S(2)}) collective-permute-start(bf16[64,3584]{1,0:T(8,128)(2,1)S(1)} %collective-permute-done.6.refs_3_), channel_id=1, source_target_pairs={{0,16},{8,24},{16,0},{24,8},{1,17},{9,25},{17,1},{25,9},{2,18},{10... | collective-permute-start | bytes 1376264 | tf_op jit(solution)/shard_map/ppermute | solution.py:431
  59.2 0.5 collective-permute-start.16
  59.7 0.5 collective-permute-start.11
  60.3 1.0 collective-permute-done.10.refs_1_
  61.2 0.5 collective-permute-start.15
  61.8 8.7 %one_hot_sums.1 = (bf16[896,2048]{1,0:T(8,128)(2,1)}, bf16[896,2048]{1,0:T(8,128)(2,1)}) custom-call(bf16[896,384]{1,0:T(8,128)(2,1)S(1)} %get-tuple-element.63.refs_0_, bf16[896,384]{1,0:T(8,128)(2,1)S(1)} %collective-permute-done.10.refs_1_, s32[1,768]{1,0:T(1,128)S(1)} %squeeze.12.refs_0_.refs_2_, s32[1,768]{1,0:T(1,128)S(1)} %squeeze.13.refs_1_.refs_3_), custom_call_target="tpu_custom_call" | custom-call | flops 1024 | bytes 1024 | tf_op jit(solution)/shard_map/one_hot_sums/pallas_call | solution.py:265
  70.5 0.6 collective-permute-done.12.refs_4_
  71.1 0.9 collective-permute-start.13
  72.0 8.1 %collective-permute-done.11.refs_0_.refs_8_ = bf16[64,3584]{1,0:T(8,128)(2,1)S(1)} collective-permute-done((bf16[64,3584]{1,0:T(8,128)(2,1)S(1)}, bf16[64,3584]{1,0:T(8,128)(2,1)S(1)}, u32[]{:S(2)}, u32[]{:S(2)}) %collective-permute-start.11) | collective-permute-done | bytes 458784 | tf_op jit(solution)/shard_map/ppermute | solution.py:431
  80.1 2.4 %collective-permute-done.15.refs_5_ = bf16[64,3584]{1,0:T(8,128)(2,1)S(1)} collective-permute-done((bf16[64,3584]{1,0:T(8,128)(2,1)S(1)}, bf16[64,3584]{1,0:T(8,128)(2,1)S(1)}, u32[]{:S(2)}, u32[]{:S(2)}) %collective-permute-start.15) | collective-permute-done | bytes 458784 | tf_op jit(solution)/shard_map/ppermute | solution.py:437
  82.5 11.3 %round_logits.4 = (bf16[512,2048]{1,0:T(8,128)(2,1)}, f32[32,128]{1,0:T(8,128)S(1)}) custom-call(bf16[64,3584]{1,0:T(8,128)(2,1)S(1)} %collective-permute-done.3.refs_0_, bf16[64,3584]{1,0:T(8,128)(2,1)S(1)} %collective-permute-done.7.refs_1_, bf16[64,3584]{1,0:T(8,128)(2,1)S(1)} %collective-permute-done.8.refs_2_, ...), custom_call_target="tpu_custom_call" | custom-call | flops 1024 | bytes 1024 | tf_op jit(solution)/shard_map/round_logits/pallas_call | solution.py:187
  93.8 4.7 %round_logits.5 = (bf16[128,2048]{1,0:T(8,128)(2,1)}, f32[32,128]{1,0:T(8,128)S(1)}) custom-call(bf16[64,3584]{1,0:T(8,128)(2,1)S(1)} %collective-permute-done.11.refs_0_.refs_8_, bf16[64,3584]{1,0:T(8,128)(2,1)S(1)} %collective-permute-done.13.refs_1_.refs_9_, bf16[3584,2048]{1,0:T(8,128)(2,1)S(1)} %get-tuple-element.58.refs_6_.refs_8_.refs_2_, ...), custom_call_target="tpu_custom_call" | custom-call | flops 1024 | bytes 1024 | tf_op jit(solution)/shard_map/round_logits/pallas_call | solution.py:187
  98.6 1.4 %turned_features.3 = (bf16[896,640]{1,0:T(8,128)(2,1)S(1)}, bf16[896,640]{1,0:T(8,128)(2,1)S(1)}) custom-call(s32[1]{0:T(128)} %bitcast.5.rep_ref, bf16[64,3584]{1,0:T(8,128)(2,1)S(1)} %collective-permute-done.3.refs_0_, bf16[64,3584]{1,0:T(8,128)(2,1)S(1)} %collective-permute-done.7.refs_1_, bf16[64,3584]{1,0:T(8,128)(2,1)S(1)} %collective-permute-done.8.refs_2_, ...), custom_call_target="tpu_custom_call" | custom-call | flops 1024 | bytes 1024 | tf_op jit(solution)/shard_map/turned_features/pallas_call | solution.py:228
  100.0 0.5 collective-permute-start.17
  101.1 1.5 %collective-permute-start.19 = (f32[32,128]{1,0:T(8,128)S(1)}, f32[32,128]{1,0:T(8,128)S(1)}, u32[]{:S(2)}, u32[]{:S(2)}) collective-permute-start(f32[32,128]{1,0:T(8,128)S(1)} %get-tuple-element.85.own_ref), channel_id=1, source_target_pairs={{0,1},{1,0},{2,3},{3,2},{4,5},{5,4},{6,7},{7,6},{8,9},{9,8},{10,11... | collective-permute-start | bytes 49160 | tf_op jit(solution)/shard_map/ppermute | solution.py:437
  102.8 0.9 collective-permute-done.21.both_ref
  103.7 0.8 collective-permute-done.20.core_ref
  105.0 1.1 collective-permute-start.24
  106.2 2.7 %collective-permute-start.23 = (f32[64,128]{1,0:T(8,128)S(1)}, f32[64,128]{1,0:T(8,128)S(1)}, u32[]{:S(2)}, u32[]{:S(2)}) collective-permute-start(f32[64,128]{1,0:T(8,128)S(1)} %get-tuple-element.86.refs_10_), channel_id=1, source_target_pairs={{0,6},{1,7},{2,0},{3,1},{4,2},{5,3},{6,4},{7,5},{8,14},{9,15},{10,... | collective-permute-start | bytes 98312 | tf_op jit(solution)/shard_map/ppermute | solution.py:447
  108.8 2.2 %collective-permute-done.25.refs_13_ = f32[64,128]{1,0:T(8,128)S(1)} collective-permute-done((f32[64,128]{1,0:T(8,128)S(1)}, f32[64,128]{1,0:T(8,128)S(1)}, u32[]{:S(2)}, u32[]{:S(2)}) %collective-permute-start.25) | collective-permute-done | bytes 32800 | tf_op jit(solution)/shard_map/ppermute | solution.py:447
  111.3 21.8 %refresh_states.1 = (bf16[896,2048]{1,0:T(8,128)(2,1)}, bf16[896,2048]{1,0:T(8,128)(2,1)}, bf16[896,2048]{1,0:T(8,128)(2,1)}) custom-call(bf16[896,384]{1,0:T(8,128)(2,1)S(1)} %get-tuple-element.63.refs_0_, bf16[896,384]{1,0:T(8,128)(2,1)S(1)} %collective-permute-done.10.refs_1_, bf16[896,640]{1,0:T(8,128)(2,1)S(1)} %get-tuple-element.80.refs_2_, ...), custom_call_target="tpu_custom_call" | custom-call | flops 1024 | bytes 1024 | tf_op jit(solution)/shard_map/refresh_states/pallas_call | solution.py:391
  (43 shorter events, 2.8 us)
Async XLA Ops:
  3.1 18.4 %collective-permute-start.2 = (bf16[64,3584]{1,0:T(8,128)(2,1)S(1)}, bf16[64,3584]{1,0:T(8,128)(2,1)S(1)}, u32[]{:S(2)}, u32[]{:S(2)}) collective-permute-start(bf16[64,3584]{1,0:T(8,128)(2,1)S(1)} %fusion.2.refs_0_), channel_id=1, source_target_pairs={{0,1},{1,0},{2,3},{3,2},{4,5},{5,4},{6,7},{7,6},{8,9},{9,8},{10,11... | collective-permute-start | bytes 1376264 | tf_op jit(solution)/shard_map/ppermute | solution.py:437
  6.1 15.4 %collective-permute-start.1 = (bf16[64,3584]{1,0:T(8,128)(2,1)S(1)}, bf16[64,3584]{1,0:T(8,128)(2,1)S(1)}, u32[]{:S(2)}, u32[]{:S(2)}) collective-permute-start(bf16[64,3584]{1,0:T(8,128)(2,1)S(1)} %fusion.2.refs_0_), channel_id=1, source_target_pairs={{0,16},{8,24},{16,0},{24,8},{1,17},{9,25},{17,1},{25,9},{2,18},{10... | collective-permute-start | bytes 1376264 | tf_op jit(solution)/shard_map/ppermute | solution.py:431
  7.6 13.9 %collective-permute-start = (bf16[64,3584]{1,0:T(8,128)(2,1)S(1)}, bf16[64,3584]{1,0:T(8,128)(2,1)S(1)}, u32[]{:S(2)}, u32[]{:S(2)}) collective-permute-start(bf16[64,3584]{1,0:T(8,128)(2,1)S(1)} %fusion.2.refs_0_), channel_id=1, source_target_pairs={{0,2},{1,3},{2,4},{3,5},{4,6},{5,7},{6,0},{7,1},{8,10},{9,11},{10,... | collective-permute-start | bytes 1376264 | tf_op jit(solution)/shard_map/ppermute | solution.py:447
  21.5 11.5 %collective-permute-start.5 = (bf16[64,3584]{1,0:T(8,128)(2,1)S(1)}, bf16[64,3584]{1,0:T(8,128)(2,1)S(1)}, u32[]{:S(2)}, u32[]{:S(2)}) collective-permute-start(bf16[64,3584]{1,0:T(8,128)(2,1)S(1)} %collective-permute-done.refs_3_), channel_id=1, source_target_pairs={{0,1},{1,0},{2,3},{3,2},{4,5},{5,4},{6,7},{7,6},{8,9},{9,8},{10,11... | collective-permute-start | bytes 1376264 | tf_op jit(solution)/shard_map/ppermute | solution.py:437
  22.1 11.1 %collective-permute-start.4 = (bf16[64,3584]{1,0:T(8,128)(2,1)S(1)}, bf16[64,3584]{1,0:T(8,128)(2,1)S(1)}, u32[]{:S(2)}, u32[]{:S(2)}) collective-permute-start(bf16[64,3584]{1,0:T(8,128)(2,1)S(1)} %collective-permute-done.refs_3_), channel_id=1, source_target_pairs={{0,16},{8,24},{16,0},{24,8},{1,17},{9,25},{17,1},{25,9},{2,18},{10... | collective-permute-start | bytes 1376264 | tf_op jit(solution)/shard_map/ppermute | solution.py:431
  22.6 12.7 %collective-permute-start.3 = (bf16[64,3584]{1,0:T(8,128)(2,1)S(1)}, bf16[64,3584]{1,0:T(8,128)(2,1)S(1)}, u32[]{:S(2)}, u32[]{:S(2)}) collective-permute-start(bf16[64,3584]{1,0:T(8,128)(2,1)S(1)} %collective-permute-done.refs_3_), channel_id=1, source_target_pairs={{0,2},{1,3},{2,4},{3,5},{4,6},{5,7},{6,0},{7,1},{8,10},{9,11},{10,... | collective-permute-start | bytes 1376264 | tf_op jit(solution)/shard_map/ppermute | solution.py:447
  35.3 12.6 %collective-permute-start.8 = (bf16[64,3584]{1,0:T(8,128)(2,1)S(1)}, bf16[64,3584]{1,0:T(8,128)(2,1)S(1)}, u32[]{:S(2)}, u32[]{:S(2)}) collective-permute-start(bf16[64,3584]{1,0:T(8,128)(2,1)S(1)} %collective-permute-done.3.refs_0_), channel_id=1, source_target_pairs={{0,1},{1,0},{2,3},{3,2},{4,5},{5,4},{6,7},{7,6},{8,9},{9,8},{10,11... | collective-permute-start | bytes 1376264 | tf_op jit(solution)/shard_map/ppermute | solution.py:437
  36.8 13.5 %collective-permute-start.7 = (bf16[64,3584]{1,0:T(8,128)(2,1)S(1)}, bf16[64,3584]{1,0:T(8,128)(2,1)S(1)}, u32[]{:S(2)}, u32[]{:S(2)}) collective-permute-start(bf16[64,3584]{1,0:T(8,128)(2,1)S(1)} %collective-permute-done.3.refs_0_), channel_id=1, source_target_pairs={{0,16},{8,24},{16,0},{24,8},{1,17},{9,25},{17,1},{25,9},{2,18},{10... | collective-permute-start | bytes 1376264 | tf_op jit(solution)/shard_map/ppermute | solution.py:431
  38.3 12.0 %collective-permute-start.6 = (bf16[64,3584]{1,0:T(8,128)(2,1)S(1)}, bf16[64,3584]{1,0:T(8,128)(2,1)S(1)}, u32[]{:S(2)}, u32[]{:S(2)}) collective-permute-start(bf16[64,3584]{1,0:T(8,128)(2,1)S(1)} %collective-permute-done.3.refs_0_), channel_id=1, source_target_pairs={{0,2},{1,3},{2,4},{3,5},{4,6},{5,7},{6,0},{7,1},{8,10},{9,11},{10,... | collective-permute-start | bytes 1376264 | tf_op jit(solution)/shard_map/ppermute | solution.py:447
  38.3 18.0 %collective-permute-start.9 = (bf16[64,3584]{1,0:T(8,128)(2,1)S(1)}, bf16[64,3584]{1,0:T(8,128)(2,1)S(1)}, u32[]{:S(2)}, u32[]{:S(2)}) collective-permute-start(bf16[64,3584]{1,0:T(8,128)(2,1)S(1)} %collective-permute-done.2.refs_2_), channel_id=1, source_target_pairs={{0,16},{8,24},{16,0},{24,8},{1,17},{9,25},{17,1},{25,9},{2,18},{10... | collective-permute-start | bytes 1376264 | tf_op jit(solution)/shard_map/ppermute | solution.py:431
  57.2 22.9 %collective-permute-start.14 = (bf16[384,2048]{1,0:T(8,128)(2,1)}, bf16[384,2048]{1,0:T(8,128)(2,1)S(1)}, u32[]{:S(2)}, u32[]{:S(2)}) collective-permute-start(bf16[384,2048]{1,0:T(8,128)(2,1)} %get-tuple-element.73.refs_4_), channel_id=1, source_target_pairs={{0,8},{8,0},{16,24},{24,16},{1,9},{9,1},{17,25},{25,17},{2,10},{10... | collective-permute-start | bytes 4718600 | tf_op jit(solution)/shard_map/ppermute | solution.py:434
  57.2 4.0 %collective-permute-start.10 = (bf16[896,384]{1,0:T(8,128)(2,1)S(1)}, bf16[896,384]{1,0:T(8,128)(2,1)S(1)}, u32[]{:S(2)}, u32[]{:S(2)}) collective-permute-start(bf16[896,384]{1,0:T(8,128)(2,1)S(1)} %get-tuple-element.64), channel_id=1, source_target_pairs={{0,8},{8,0},{16,24},{24,16},{1,9},{9,1},{17,25},{25,17},{2,10},{10... | collective-permute-start | bytes 2064392 | tf_op jit(solution)/shard_map/ppermute | solution.py:434
  57.7 13.4 %collective-permute-start.12 = (bf16[64,3584]{1,0:T(8,128)(2,1)S(1)}, bf16[64,3584]{1,0:T(8,128)(2,1)S(1)}, u32[]{:S(2)}, u32[]{:S(2)}) collective-permute-start(bf16[64,3584]{1,0:T(8,128)(2,1)S(1)} %collective-permute-done.6.refs_3_), channel_id=1, source_target_pairs={{0,16},{8,24},{16,0},{24,8},{1,17},{9,25},{17,1},{25,9},{2,18},{10... | collective-permute-start | bytes 1376264 | tf_op jit(solution)/shard_map/ppermute | solution.py:431
  59.2 20.8 %collective-permute-start.16 = (bf16[64,3584]{1,0:T(8,128)(2,1)S(1)}, bf16[64,3584]{1,0:T(8,128)(2,1)S(1)}, u32[]{:S(2)}, u32[]{:S(2)}) collective-permute-start(bf16[64,3584]{1,0:T(8,128)(2,1)S(1)} %collective-permute-done.4.refs_4_), channel_id=1, source_target_pairs={{0,1},{1,0},{2,3},{3,2},{4,5},{5,4},{6,7},{7,6},{8,9},{9,8},{10,11... | collective-permute-start | bytes 1376264 | tf_op jit(solution)/shard_map/ppermute | solution.py:437
  59.7 20.3 %collective-permute-start.11 = (bf16[64,3584]{1,0:T(8,128)(2,1)S(1)}, bf16[64,3584]{1,0:T(8,128)(2,1)S(1)}, u32[]{:S(2)}, u32[]{:S(2)}) collective-permute-start(bf16[64,3584]{1,0:T(8,128)(2,1)S(1)} %collective-permute-done.8.refs_2_), channel_id=1, source_target_pairs={{0,16},{8,24},{16,0},{24,8},{1,17},{9,25},{17,1},{25,9},{2,18},{10... | collective-permute-start | bytes 1376264 | tf_op jit(solution)/shard_map/ppermute | solution.py:431
  61.2 21.2 %collective-permute-start.15 = (bf16[64,3584]{1,0:T(8,128)(2,1)S(1)}, bf16[64,3584]{1,0:T(8,128)(2,1)S(1)}, u32[]{:S(2)}, u32[]{:S(2)}) collective-permute-start(bf16[64,3584]{1,0:T(8,128)(2,1)S(1)} %collective-permute-done.6.refs_3_), channel_id=1, source_target_pairs={{0,1},{1,0},{2,3},{3,2},{4,5},{5,4},{6,7},{7,6},{8,9},{9,8},{10,11... | collective-permute-start | bytes 1376264 | tf_op jit(solution)/shard_map/ppermute | solution.py:437
  71.1 22.6 %collective-permute-start.13 = (bf16[64,3584]{1,0:T(8,128)(2,1)S(1)}, bf16[64,3584]{1,0:T(8,128)(2,1)S(1)}, u32[]{:S(2)}, u32[]{:S(2)}) collective-permute-start(bf16[64,3584]{1,0:T(8,128)(2,1)S(1)} %collective-permute-done.12.refs_4_), channel_id=1, source_target_pairs={{0,1},{1,0},{2,3},{3,2},{4,5},{5,4},{6,7},{7,6},{8,9},{9,8},{10,11... | collective-permute-start | bytes 1376264 | tf_op jit(solution)/shard_map/ppermute | solution.py:437
  93.8 4.8 %copy-start = (bf16[512,2048]{1,0:T(8,128)(2,1)S(1)}, bf16[512,2048]{1,0:T(8,128)(2,1)}, u32[]{:S(2)}) copy-start(bf16[512,2048]{1,0:T(8,128)(2,1)} %get-tuple-element.84.refs_5_) | copy-start | bytes 6291460
  98.5 6.4 %copy-start.1 = (bf16[128,2048]{1,0:T(8,128)(2,1)S(1)}, bf16[128,2048]{1,0:T(8,128)(2,1)}, u32[]{:S(2)}) copy-start(bf16[128,2048]{1,0:T(8,128)(2,1)} %get-tuple-element.87.refs_6_) | copy-start | bytes 1572868
  98.5 4.2 %collective-permute-start.18 = (bf16[512,2048]{1,0:T(8,128)(2,1)S(1)}, bf16[512,2048]{1,0:T(8,128)(2,1)S(1)}, u32[]{:S(2)}, u32[]{:S(2)}) collective-permute-start(bf16[512,2048]{1,0:T(8,128)(2,1)S(1)} %copy-done), channel_id=1, source_target_pairs={{0,8},{8,0},{16,24},{24,16},{1,9},{9,1},{17,25},{25,17},{2,10},{10... | collective-permute-start | bytes 6291464 | tf_op jit(solution)/shard_map/ppermute | solution.py:434
  100.0 8.9 %collective-permute-start.17 = (bf16[896,640]{1,0:T(8,128)(2,1)S(1)}, bf16[896,640]{1,0:T(8,128)(2,1)S(1)}, u32[]{:S(2)}, u32[]{:S(2)}) collective-permute-start(bf16[896,640]{1,0:T(8,128)(2,1)S(1)} %get-tuple-element.81), channel_id=1, source_target_pairs={{0,8},{8,0},{16,24},{24,16},{1,9},{9,1},{17,25},{25,17},{2,10},{10... | collective-permute-start | bytes 3440648 | tf_op jit(solution)/shard_map/ppermute | solution.py:434
  100.5 3.2 %collective-permute-start.21 = (f32[32,128]{1,0:T(8,128)S(1)}, f32[32,128]{1,0:T(8,128)S(1)}, u32[]{:S(2)}, u32[]{:S(2)}) collective-permute-start(f32[32,128]{1,0:T(8,128)S(1)} %get-tuple-element.85.own_ref), channel_id=1, source_target_pairs={{0,9},{1,8},{2,11},{3,10},{4,13},{5,12},{6,15},{7,14},{8,1},{9,0},... | collective-permute-start | bytes 49160 | tf_op jit(solution)/shard_map/ppermute | solution.py:444
  100.7 3.7 %collective-permute-start.20 = (f32[32,128]{1,0:T(8,128)S(1)}, f32[32,128]{1,0:T(8,128)S(1)}, u32[]{:S(2)}, u32[]{:S(2)}) collective-permute-start(f32[32,128]{1,0:T(8,128)S(1)} %get-tuple-element.85.own_ref), channel_id=1, source_target_pairs={{0,8},{8,0},{16,24},{24,16},{1,9},{9,1},{17,25},{25,17},{2,10},{10... | collective-permute-start | bytes 49160 | tf_op jit(solution)/shard_map/ppermute | solution.py:434
  101.1 3.7 %collective-permute-start.19 = (f32[32,128]{1,0:T(8,128)S(1)}, f32[32,128]{1,0:T(8,128)S(1)}, u32[]{:S(2)}, u32[]{:S(2)}) collective-permute-start(f32[32,128]{1,0:T(8,128)S(1)} %get-tuple-element.85.own_ref), channel_id=1, source_target_pairs={{0,1},{1,0},{2,3},{3,2},{4,5},{5,4},{6,7},{7,6},{8,9},{9,8},{10,11... | collective-permute-start | bytes 49160 | tf_op jit(solution)/shard_map/ppermute | solution.py:437
  104.9 6.4 %collective-permute-start.22 = (bf16[128,2048]{1,0:T(8,128)(2,1)S(1)}, bf16[128,2048]{1,0:T(8,128)(2,1)S(1)}, u32[]{:S(2)}, u32[]{:S(2)}) collective-permute-start(bf16[128,2048]{1,0:T(8,128)(2,1)S(1)} %copy-done.1), channel_id=1, source_target_pairs={{0,8},{8,0},{16,24},{24,16},{1,9},{9,1},{17,25},{25,17},{2,10},{10... | collective-permute-start | bytes 1572872 | tf_op jit(solution)/shard_map/ppermute | solution.py:434
  105.0 6.0 %collective-permute-start.25 = (f32[64,128]{1,0:T(8,128)S(1)}, f32[64,128]{1,0:T(8,128)S(1)}, u32[]{:S(2)}, u32[]{:S(2)}) collective-permute-start(f32[64,128]{1,0:T(8,128)S(1)} %get-tuple-element.86.refs_10_), channel_id=1, source_target_pairs={{0,2},{1,3},{2,4},{3,5},{4,6},{5,7},{6,0},{7,1},{8,10},{9,11},{10,... | collective-permute-start | bytes 98312 | tf_op jit(solution)/shard_map/ppermute | solution.py:447
  105.0 6.0 %collective-permute-start.24 = (f32[64,128]{1,0:T(8,128)S(1)}, f32[64,128]{1,0:T(8,128)S(1)}, u32[]{:S(2)}, u32[]{:S(2)}) collective-permute-start(f32[64,128]{1,0:T(8,128)S(1)} %get-tuple-element.86.refs_10_), channel_id=1, source_target_pairs={{0,4},{1,5},{2,6},{3,7},{4,0},{5,1},{6,2},{7,3},{8,12},{9,13},{10,... | collective-permute-start | bytes 98312 | tf_op jit(solution)/shard_map/ppermute | solution.py:447
  106.2 5.2 %collective-permute-start.23 = (f32[64,128]{1,0:T(8,128)S(1)}, f32[64,128]{1,0:T(8,128)S(1)}, u32[]{:S(2)}, u32[]{:S(2)}) collective-permute-start(f32[64,128]{1,0:T(8,128)S(1)} %get-tuple-element.86.refs_10_), channel_id=1, source_target_pairs={{0,6},{1,7},{2,0},{3,1},{4,2},{5,3},{6,4},{7,5},{8,14},{9,15},{10,... | collective-permute-start | bytes 98312 | tf_op jit(solution)/shard_map/ppermute | solution.py:447

commit v5 on v4

--- a/solution.py
+++ b/solution.py
@@ -306,7 +306,7 @@
 
 def refresh_kernel(lines, length, early_rows, late_rows, *refs):
     early_refs, late_refs, refs = refs[:2], refs[2:4], refs[4:]
-    exp_refs, refs = refs[:6], refs[6:]
+    exp_refs, refs = refs[:8], refs[8:]
     stats_refs, refs = refs[:lines], refs[lines:]
     (first_ref, true_at, sample_at, true_sum, sample_sum, moment_ref, curvature_ref,
      moment_out, curvature_out, update_out, scaled, factors) = refs
@@ -351,14 +351,15 @@
                 )
 
     shared = jnp.dot(
-        scaled[...], jnp.concatenate([exp_refs[0][...], exp_refs[3][...]], axis=0),
+        scaled[...],
+        jnp.concatenate([ref[...] for ref in exp_refs[:2] + exp_refs[4:6]], axis=0),
         preferred_element_type=jnp.float32,
     )
     gradient = shared - true_sum[...].astype(jnp.float32)
     sample_grad = shared - sample_sum[...].astype(jnp.float32)
     for core in range(2):
         place = slice(core * late, (core + 1) * late)
-        exps = jnp.concatenate([ref[...] for ref in exp_refs[3 * core + 1:3 * core + 3]], axis=0)
+        exps = jnp.concatenate([ref[...] for ref in exp_refs[4 * core + 2:4 * core + 4]], axis=0)
         true_parts, sample_parts = [], []
         for lane in range(0, width, 128):
             probs = exps[:, lane:lane + 128].astype(jnp.float32) * factors[place]
@@ -405,7 +406,7 @@
         cost_estimate=BRIEF,
         name="refresh_states",
     )(
-        *early, *late, *in_hbm(exps[:3]), *exps[3:], *stats, first, *late_ids,
+        *early, *late, *in_hbm(exps[:4]), *exps[4:], *stats, first, *late_ids,
         *in_hbm(sums, [moment, curvature])
     )
 
@@ -448,11 +449,12 @@
 
     split = lines // 2
     plain = [(0, 0), (0, 1), (1, 0)]
-    early_blocks = [(*kind, turn) for turn in range(split) for kind in plain]
-    middle_blocks = [(*kind, turn) for turn in range(split, lines) for kind in plain]
-    middle_blocks += [(1, 1, turn) for turn in range(split)]
-    last_blocks = [(1, 1, turn) for turn in range(split, lines)]
-    groups = [early_blocks, middle_blocks, last_blocks]
+    groups = [[(*kind, turn) for kind in plain] for turn in range(split)]
+    groups += [[(*kind, turn) for turn in range(split, lines - 1) for kind in plain]]
+    groups[-1] += [(0, 0, lines - 1)]
+    groups += [[(0, 1, lines - 1), (1, 0, lines - 1)]]
+    groups[-1] += [(1, 1, turn) for turn in range(lines)]
+    early_blocks, late_blocks = sum(groups[:split], []), sum(groups[split:], [])
 
     def stat_row(block):
         return (2 * block[0] + block[1]) * lines + block[2]
@@ -462,7 +464,7 @@
     last = jnp.arange(input_ids.shape[0]) % group_len == group_len - 1
     targets = jnp.where(last, -1, jnp.roll(input_ids, -1) - first_col)
     ids = jnp.stack([targets, sampled_ids - first_col]).reshape(2, reps * shards, length)
-    side, across, turn = (np.array(values) for values in zip(*sum(groups, [])))
+    side, across, turn = (np.array(values) for values in zip(*(early_blocks + late_blocks)))
     holder = (rep ^ (2 * across[None] + np.arange(2)[:, None])).reshape(-1)
     place = 2 * ((shard // 2 - turn) % lines) + ((shard % 2) ^ side)
     ids = jnp.take(ids, holder * shards + jnp.tile(place, 2), axis=1)
@@ -483,10 +485,10 @@
         exps.append(exp)
         return stats
 
-    def diagonal(turn, *gates):
+    def diagonal(turn):
         if turn % 2 == 0:
-            return to_x(after(held[1, 0, turn], *gates) if gates else held[1, 0, turn])
-        return to_y(after(held[0, 1, turn], *gates) if gates else held[0, 1, turn])
+            return to_x(held[1, 0, turn])
+        return to_y(held[0, 1, turn])
 
     for turn in range(lines):
         block = held[0, 0, turn]
@@ -495,34 +497,39 @@
         if turn + 1 < lines:
             arrived = [to_z(block, 1), held[0, 1, turn], held[1, 0, turn]]
             if turn == 0:
-                head_weight, *late_ids = prepared(head_weight, *late_ids, *early_ids, stats)
-                arrived += [*early_ids, *late_ids, rep_scalar, stats, head_weight]
-            arrived = lax.optimization_barrier((*arrived, *exps[-1:]))
+                arrived += [*early_ids, *late_ids, rep_scalar, stats]
+            else:
+                arrived += exps
+            arrived = lax.optimization_barrier(tuple(arrived))
             held[0, 0, turn + 1], held[0, 1, turn], held[1, 0, turn] = arrived[:3]
             if turn == 0:
                 early_ids, late_ids = list(arrived[3:5]), list(arrived[5:7])
-                rep_scalar, stats, head_weight = arrived[7:]
-            if turn + 1 == split:
-                stats = logits(early_blocks, stats, held[0, 0, split])
+                rep_scalar, stats = arrived[7:]
+                head_weight, *late_ids = prepared(head_weight, *late_ids, stats)
+            early_exps = arrived[3:]
+        if turn + 1 < lines:
+            held[1, 1, turn] = diagonal(turn)
         if turn < split:
-            held[1, 1, turn] = diagonal(turn)
+            stats = logits(groups[turn], stats, held[0, 0, turn + 1])
 
     early = [held[block] for block in early_blocks]
-    early[0] = after(early[0], held[0, 0, lines - 1], held[1, 1, 0])
+    early[0] = after(early[0], held[0, 0, split])
     early = turned_features(rep_scalar, early, rows)
     early = [early[0], to_core(early[1])]
-    early_ids[0] = after(early_ids[0], held[0, 0, lines - 1])
+    stats = logits(groups[split], stats, held[0, 0, lines - 1], early[1])
+    held[0, 1, lines - 1] = after(held[0, 1, lines - 1], exps[split])
+    held[1, 1, lines - 1] = diagonal(lines - 1)
+    early_exps = lax.optimization_barrier((*early_exps, early[1]))[:split]
+    other_exps = [to_core(exp) for exp in early_exps]
+    early_ids[0] = after(early_ids[0], exps[split], held[0, 1, lines - 1], *other_exps)
     sums = one_hot_sums(early, early_ids, columns)
-    for turn in range(split, lines):
-        held[1, 1, turn] = diagonal(turn, early[0] if turn % 2 == 0 else sums[0])
-    other_exps = [to_core(after(exps[0], early[0]))]
-    stats = logits(middle_blocks, stats, *sums, other_exps[0])
-    stats = logits(last_blocks, stats)
-    other_exps.append(to_core(after(exps[1], stats)))
+    stats = logits(groups[-1], stats, *sums)
+    stats = after(stats, *other_exps)
+    other_exps.append(to_core(after(exps[split], stats)))
     across_stats, core_stats, both_stats = to_y(stats), to_core(stats), to_y_core(stats)
-    late_held = [held[block] for block in middle_blocks + last_blocks]
-    late_held[0] = after(late_held[0], stats)
-    late = turned_features(rep_scalar, late_held, rows)
+    late = [held[block] for block in late_blocks]
+    late[0] = after(late[0], stats)
+    late = turned_features(rep_scalar, late, rows)
     merged, first = merged_stats(
         after(stats, *other_exps), across_stats, core_stats, both_stats
     )
@@ -531,7 +538,7 @@
     late = [late[0], to_core(late[1])]
     return tuple(refresh_states(
         lines, length, [stat_row(block) for block in early_blocks],
-        [stat_row(block) for block in middle_blocks + last_blocks], early, late,
+        [stat_row(block) for block in late_blocks], early, late,
         exps + other_exps, all_stats, first, late_ids, sums, moment, curvature,
     ))
 
@@ -552,7 +559,7 @@
     def whole(hidden, *others):
         tokens, depth = hidden.shape
         length = tokens // (reps * shards)
-        fits = hidden.size * 2 <= GATHER_BYTES and reps == 4 and shards % 2 == 0
+        fits = hidden.size * 2 <= GATHER_BYTES and reps == 4 and shards == 8
         if fits and length == 64 and (depth // reps) % 128 == 0:
             plan = functools.partial(all_tokens, reps, shards)
         else:

time: 134 us -> 132 us (0.985)
  waiting for transfers between devices: 36.3 us -> 32.5 us
  Pallas kernels: 63.3 us -> 65.8 us
    ppermute x6, waiting for transfers between devices: 4.54 us -> 9.55 us  [to_z(): return lax.ppermute(values, 'shard', shift_pairs(lines, along, 0))]
    ppermute x7, waiting for transfers between devices: 11.6 us -> 7.93 us  [to_y(): return lax.ppermute(values, 'shard', swap_pairs(shards, 1))]
    ppermute x6, waiting for transfers between devices: 17.4 us -> 14 us  [to_x(): return lax.ppermute(values, 'rep', swap_pairs(reps, 2))]
    pallas_call x3 -> x4, Pallas kernels: 25.1 us -> 27.4 us  [round_logits(): pl.pallas_call(functools.partial(logits_kernel, stat_rows), in_specs=[nea...]
    ppermute x6 -> x7, waiting for transfers between devices: 1.86 us -> 0.45 us  [to_core(): return lax.ppermute(values, 'rep', swap_pairs(reps, 1))]
  transfers between devices with their start and end apart: 26 -> 27, of which waited for: 15 -> 15; matrix products, arithmetic and copies ran while one was open for 5% -> 5% of each run, Pallas kernels for 27% -> 26%
where the time goes in v5:
time: 132 us; the launch traced here: 131 us
  Pallas kernels  65.8 us (50%)
  waiting for transfers between devices  32.5 us (25%)
  starting transfers between devices  22.9 us (17%)
  other arithmetic  6.04 us (5%)
  local copies, waits for them, and re-layouts  3.16 us (2%)
    pallas_call x4, Pallas kernels, round_logits(): pl.pallas_call(functools.partial(logits_kernel, stat_rows), in_specs=[nea...  27.4 us
    pallas_call x1, Pallas kernels, refresh_states(): pl.pallas_call(functools.partial(refresh_kernel, lines, length, early_row...  21.9 us
    ppermute x6, waiting for transfers between devices, to_x(): return lax.ppermute(values, 'rep', swap_pairs(reps, 2))  14 us
    ppermute x6, waiting for transfers between devices, to_z(): return lax.ppermute(values, 'shard', shift_pairs(lines, along, 0))  9.55 us
    ppermute x7, starting transfers between devices, to_y(): return lax.ppermute(values, 'shard', swap_pairs(shards, 1))  8.72 us
    pallas_call x1, Pallas kernels, one_hot_sums(): pl.pallas_call(functools.partial(one_hot_kernel, len(features)), grid=(co...  8.67 us
    ppermute x7, waiting for transfers between devices, to_y(): return lax.ppermute(values, 'shard', swap_pairs(shards, 1))  7.93 us
    ppermute x6, starting transfers between devices, to_x(): return lax.ppermute(values, 'rep', swap_pairs(reps, 2))  6.08 us
  transfers between devices with their start and end apart: 27, of which 15 were waited for; matrix products, arithmetic and copies ran while one was open for 5% of the time, Pallas kernels for 26%

profile of v5, /device:TPU:0, one launch (start us, length us, event | category | flops | bytes accessed | tf_op | source)
XLA Modules:
  0.0 131.2 jit_solution(10607943090751819967)
XLA Ops:
  0.6 1.2 fusion
  1.9 1.2 fusion.2.refs_0_
  3.1 3.0 %collective-permute-start.2 = (bf16[64,3584]{1,0:T(8,128)(2,1)S(1)}, bf16[64,3584]{1,0:T(8,128)(2,1)S(1)}, u32[]{:S(2)}, u32[]{:S(2)}) collective-permute-start(bf16[64,3584]{1,0:T(8,128)(2,1)S(1)} %fusion.2.refs_0_), channel_id=1, source_target_pairs={{0,1},{1,0},{2,3},{3,2},{4,5},{5,4},{6,7},{7,6},{8,9},{9,8},{10,11... | collective-permute-start | bytes 1376264 | tf_op jit(solution)/shard_map/ppermute | solution.py:438
  6.1 1.5 %collective-permute-start.1 = (bf16[64,3584]{1,0:T(8,128)(2,1)S(1)}, bf16[64,3584]{1,0:T(8,128)(2,1)S(1)}, u32[]{:S(2)}, u32[]{:S(2)}) collective-permute-start(bf16[64,3584]{1,0:T(8,128)(2,1)S(1)} %fusion.2.refs_0_), channel_id=1, source_target_pairs={{0,16},{8,24},{16,0},{24,8},{1,17},{9,25},{17,1},{25,9},{2,18},{10... | collective-permute-start | bytes 1376264 | tf_op jit(solution)/shard_map/ppermute | solution.py:432
  7.6 1.6 %collective-permute-start = (bf16[64,3584]{1,0:T(8,128)(2,1)S(1)}, bf16[64,3584]{1,0:T(8,128)(2,1)S(1)}, u32[]{:S(2)}, u32[]{:S(2)}) collective-permute-start(bf16[64,3584]{1,0:T(8,128)(2,1)S(1)} %fusion.2.refs_0_), channel_id=1, source_target_pairs={{0,2},{1,3},{2,4},{3,5},{4,6},{5,7},{6,0},{7,1},{8,10},{9,11},{10,... | collective-permute-start | bytes 1376264 | tf_op jit(solution)/shard_map/ppermute | solution.py:448
  9.2 0.7 fusion.7
  9.8 0.7 compare_and_fusion
  10.5 0.7 multiply_add_fusion
  11.2 1.2 slice.31
  12.4 0.8 slice.30
  13.3 0.7 broadcast_subtract_fusion
  14.1 0.7 fusion.4
  14.9 0.6 gather_fusion
  16.0 0.7 collective-permute-done.2.refs_2_
  16.6 1.5 %collective-permute-done.1.refs_1_ = bf16[64,3584]{1,0:T(8,128)(2,1)S(1)} collective-permute-done((bf16[64,3584]{1,0:T(8,128)(2,1)S(1)}, bf16[64,3584]{1,0:T(8,128)(2,1)S(1)}, u32[]{:S(2)}, u32[]{:S(2)}) %collective-permute-start.1) | collective-permute-done | bytes 458784 | tf_op jit(solution)/shard_map/ppermute | solution.py:432
  18.1 3.1 %collective-permute-done.refs_3_.refs_0_ = bf16[64,3584]{1,0:T(8,128)(2,1)S(1)} collective-permute-done((bf16[64,3584]{1,0:T(8,128)(2,1)S(1)}, bf16[64,3584]{1,0:T(8,128)(2,1)S(1)}, u32[]{:S(2)}, u32[]{:S(2)}) %collective-permute-start) | collective-permute-done | bytes 458784 | tf_op jit(solution)/shard_map/ppermute | solution.py:448
  21.6 0.5 collective-permute-start.4
  22.2 5.5 %prepared.1 = (bf16[3584,2048]{1,0:T(8,128)(2,1)S(1)}, s32[1280,128]{1,0:T(8,128)S(1)}, s32[1280,128]{1,0:T(8,128)S(1)}) custom-call(bf16[3584,2048]{1,0:T(8,128)(2,1)} %weight_ref.1, s32[1,1280]{1,0:T(1,128)S(1)} %squeeze.14.true_ids, s32[1,1280]{1,0:T(1,128)S(1)} %squeeze.15.sample_ids, f32[32,128]{1,0:T(8,128)S(1)} %broadcast_in_dim.22.refs_0_.refs_4_), custom_call_target="tpu_custom_call" | custom-call | flops 1024 | bytes 1024 | tf_op jit(solution)/shard_map/prepared/pallas_call | solution.py:113
  27.7 5.7 %round_logits.4 = (bf16[192,2048]{1,0:T(8,128)(2,1)}, f32[32,128]{1,0:T(8,128)S(1)}) custom-call(bf16[64,3584]{1,0:T(8,128)(2,1)S(1)} %fusion.2.refs_0_, bf16[64,3584]{1,0:T(8,128)(2,1)S(1)} %collective-permute-done.1.refs_1_, bf16[64,3584]{1,0:T(8,128)(2,1)S(1)} %collective-permute-done.2.refs_2_, ...), custom_call_target="tpu_custom_call" | custom-call | flops 1024 | bytes 1024 | tf_op jit(solution)/shard_map/round_logits/pallas_call | solution.py:187
  33.5 1.0 collective-permute-done.3.refs_0_
  34.5 0.9 turned_features.2
  35.4 1.4 %collective-permute-start.9 = (bf16[64,3584]{1,0:T(8,128)(2,1)S(1)}, bf16[64,3584]{1,0:T(8,128)(2,1)S(1)}, u32[]{:S(2)}, u32[]{:S(2)}) collective-permute-start(bf16[64,3584]{1,0:T(8,128)(2,1)S(1)} %collective-permute-done.3.refs_0_), channel_id=1, source_target_pairs={{0,1},{1,0},{2,3},{3,2},{4,5},{5,4},{6,7},{7,6},{8,9},{9,8},{10,11... | collective-permute-start | bytes 1376264 | tf_op jit(solution)/shard_map/ppermute | solution.py:438
  36.8 1.5 %collective-permute-start.8 = (bf16[64,3584]{1,0:T(8,128)(2,1)S(1)}, bf16[64,3584]{1,0:T(8,128)(2,1)S(1)}, u32[]{:S(2)}, u32[]{:S(2)}) collective-permute-start(bf16[64,3584]{1,0:T(8,128)(2,1)S(1)} %collective-permute-done.3.refs_0_), channel_id=1, source_target_pairs={{0,16},{8,24},{16,0},{24,8},{1,17},{9,25},{17,1},{25,9},{2,18},{10... | collective-permute-start | bytes 1376264 | tf_op jit(solution)/shard_map/ppermute | solution.py:432
  38.3 0.6 collective-permute-start.7
  38.8 5.8 %round_logits.5 = (bf16[192,2048]{1,0:T(8,128)(2,1)}, f32[32,128]{1,0:T(8,128)S(1)}) custom-call(bf16[64,3584]{1,0:T(8,128)(2,1)S(1)} %collective-permute-done.refs_3_.refs_0_, bf16[64,3584]{1,0:T(8,128)(2,1)S(1)} %collective-permute-done.4.refs_4_.refs_1_, bf16[64,3584]{1,0:T(8,128)(2,1)S(1)} %collective-permute-done.5.refs_5_.refs_2_, ...), custom_call_target="tpu_custom_call" | custom-call | flops 1024 | bytes 1024 | tf_op jit(solution)/shard_map/round_logits/pallas_call | solution.py:187
  44.6 3.8 %collective-permute-done.9.refs_2_ = bf16[64,3584]{1,0:T(8,128)(2,1)S(1)} collective-permute-done((bf16[64,3584]{1,0:T(8,128)(2,1)S(1)}, bf16[64,3584]{1,0:T(8,128)(2,1)S(1)}, u32[]{:S(2)}, u32[]{:S(2)}) %collective-permute-start.9) | collective-permute-done | bytes 458784 | tf_op jit(solution)/shard_map/ppermute | solution.py:438
  48.4 1.0 collective-permute-done.8.refs_1_
  49.4 3.0 %collective-permute-done.7.refs_3_ = bf16[64,3584]{1,0:T(8,128)(2,1)S(1)} collective-permute-done((bf16[64,3584]{1,0:T(8,128)(2,1)S(1)}, bf16[64,3584]{1,0:T(8,128)(2,1)S(1)}, u32[]{:S(2)}, u32[]{:S(2)}) %collective-permute-start.7) | collective-permute-done | bytes 458784 | tf_op jit(solution)/shard_map/ppermute | solution.py:448
  52.9 0.5 collective-permute-start.10
  53.4 1.5 %collective-permute-start.14 = (bf16[64,3584]{1,0:T(8,128)(2,1)S(1)}, bf16[64,3584]{1,0:T(8,128)(2,1)S(1)}, u32[]{:S(2)}, u32[]{:S(2)}) collective-permute-start(bf16[64,3584]{1,0:T(8,128)(2,1)S(1)} %collective-permute-done.2.refs_2_), channel_id=1, source_target_pairs={{0,16},{8,24},{16,0},{24,8},{1,17},{9,25},{17,1},{25,9},{2,18},{10... | collective-permute-start | bytes 1376264 | tf_op jit(solution)/shard_map/ppermute | solution.py:432
  55.4 6.8 %round_logits.6 = (bf16[256,2048]{1,0:T(8,128)(2,1)}, f32[32,128]{1,0:T(8,128)S(1)}) custom-call(bf16[64,3584]{1,0:T(8,128)(2,1)S(1)} %collective-permute-done.3.refs_0_, bf16[64,3584]{1,0:T(8,128)(2,1)S(1)} %collective-permute-done.8.refs_1_, bf16[64,3584]{1,0:T(8,128)(2,1)S(1)} %collective-permute-done.9.refs_2_, ...), custom_call_target="tpu_custom_call" | custom-call | flops 1024 | bytes 1024 | tf_op jit(solution)/shard_map/round_logits/pallas_call | solution.py:187
  62.3 4.0 %collective-permute-done.10.refs_0_.refs_4_ = bf16[64,3584]{1,0:T(8,128)(2,1)S(1)} collective-permute-done((bf16[64,3584]{1,0:T(8,128)(2,1)S(1)}, bf16[64,3584]{1,0:T(8,128)(2,1)S(1)}, u32[]{:S(2)}, u32[]{:S(2)}) %collective-permute-start.10) | collective-permute-done | bytes 458784 | tf_op jit(solution)/shard_map/ppermute | solution.py:432
  66.3 0.5 collective-permute-start.16
  66.8 0.7 collective-permute-start.13
  67.6 1.3 collective-permute-start.17
  68.9 8.7 %one_hot_sums.1 = (bf16[896,2048]{1,0:T(8,128)(2,1)}, bf16[896,2048]{1,0:T(8,128)(2,1)}) custom-call(bf16[896,384]{1,0:T(8,128)(2,1)S(1)} %get-tuple-element.67.refs_0_, bf16[896,384]{1,0:T(8,128)(2,1)S(1)} %collective-permute-done.6.refs_1_, s32[1,768]{1,0:T(1,128)S(1)} %squeeze.12.refs_2_, s32[1,768]{1,0:T(1,128)S(1)} %squeeze.13.refs_3_), custom_call_target="tpu_custom_call" | custom-call | flops 1024 | bytes 1024 | tf_op jit(solution)/shard_map/one_hot_sums/pallas_call | solution.py:265
  77.5 7.5 %collective-permute-done.16.refs_4_.refs_8_ = bf16[64,3584]{1,0:T(8,128)(2,1)S(1)} collective-permute-done((bf16[64,3584]{1,0:T(8,128)(2,1)S(1)}, bf16[64,3584]{1,0:T(8,128)(2,1)S(1)}, u32[]{:S(2)}, u32[]{:S(2)}) %collective-permute-start.16) | collective-permute-done | bytes 458784 | tf_op jit(solution)/shard_map/ppermute | solution.py:432
  85.1 2.1 %collective-permute-done.17.refs_5_.refs_9_ = bf16[64,3584]{1,0:T(8,128)(2,1)S(1)} collective-permute-done((bf16[64,3584]{1,0:T(8,128)(2,1)S(1)}, bf16[64,3584]{1,0:T(8,128)(2,1)S(1)}, u32[]{:S(2)}, u32[]{:S(2)}) %collective-permute-start.17) | collective-permute-done | bytes 458784 | tf_op jit(solution)/shard_map/ppermute | solution.py:438
  87.2 9.1 %round_logits.7 = (bf16[384,2048]{1,0:T(8,128)(2,1)}, f32[32,128]{1,0:T(8,128)S(1)}) custom-call(bf16[64,3584]{1,0:T(8,128)(2,1)S(1)} %collective-permute-done.10.refs_0_.refs_4_, bf16[64,3584]{1,0:T(8,128)(2,1)S(1)} %collective-permute-done.13.refs_1_.refs_5_, bf16[64,3584]{1,0:T(8,128)(2,1)S(1)} %collective-permute-done.14.refs_2_.refs_6_, ...), custom_call_target="tpu_custom_call" | custom-call | flops 1024 | bytes 1024 | tf_op jit(solution)/shard_map/round_logits/pallas_call | solution.py:187
  96.3 0.9 collective-permute-start.22
  97.3 1.3 collective-permute-start.20
  99.0 0.6 collective-permute-done.22.both_ref
  99.6 1.4 %collective-permute-done.20.across_ref = f32[32,128]{1,0:T(8,128)S(1)} collective-permute-done((f32[32,128]{1,0:T(8,128)S(1)}, f32[32,128]{1,0:T(8,128)S(1)}, u32[]{:S(2)}, u32[]{:S(2)}) %collective-permute-start.20) | collective-permute-done | bytes 16416 | tf_op jit(solution)/shard_map/ppermute | solution.py:438
  101.1 1.4 %turned_features.3 = (bf16[896,640]{1,0:T(8,128)(2,1)S(1)}, bf16[896,640]{1,0:T(8,128)(2,1)S(1)}) custom-call(s32[1]{0:T(128)} %bitcast.5.rep_ref, bf16[64,3584]{1,0:T(8,128)(2,1)S(1)} %collective-permute-done.3.refs_0_, bf16[64,3584]{1,0:T(8,128)(2,1)S(1)} %collective-permute-done.8.refs_1_, bf16[64,3584]{1,0:T(8,128)(2,1)S(1)} %collective-permute-done.9.refs_2_, ...), custom_call_target="tpu_custom_call" | custom-call | flops 1024 | bytes 1024 | tf_op jit(solution)/shard_map/turned_features/pallas_call | solution.py:228
  103.0 1.6 %collective-permute-start.25 = (f32[64,128]{1,0:T(8,128)S(1)}, f32[64,128]{1,0:T(8,128)S(1)}, u32[]{:S(2)}, u32[]{:S(2)}) collective-permute-start(f32[64,128]{1,0:T(8,128)S(1)} %get-tuple-element.98.refs_12_), channel_id=1, source_target_pairs={{0,4},{1,5},{2,6},{3,7},{4,0},{5,1},{6,2},{7,3},{8,12},{9,13},{10,... | collective-permute-start | bytes 98312 | tf_op jit(solution)/shard_map/ppermute | solution.py:448
  104.6 2.2 %collective-permute-start.24 = (f32[64,128]{1,0:T(8,128)S(1)}, f32[64,128]{1,0:T(8,128)S(1)}, u32[]{:S(2)}, u32[]{:S(2)}) collective-permute-start(f32[64,128]{1,0:T(8,128)S(1)} %get-tuple-element.98.refs_12_), channel_id=1, source_target_pairs={{0,6},{1,7},{2,0},{3,1},{4,2},{5,3},{6,4},{7,5},{8,14},{9,15},{10,... | collective-permute-start | bytes 98312 | tf_op jit(solution)/shard_map/ppermute | solution.py:448
  106.8 2.0 %collective-permute-done.26.refs_15_ = f32[64,128]{1,0:T(8,128)S(1)} collective-permute-done((f32[64,128]{1,0:T(8,128)S(1)}, f32[64,128]{1,0:T(8,128)S(1)}, u32[]{:S(2)}, u32[]{:S(2)}) %collective-permute-start.26) | collective-permute-done | bytes 32800 | tf_op jit(solution)/shard_map/ppermute | solution.py:448
  109.3 21.9 %refresh_states.1 = (bf16[896,2048]{1,0:T(8,128)(2,1)}, bf16[896,2048]{1,0:T(8,128)(2,1)}, bf16[896,2048]{1,0:T(8,128)(2,1)}) custom-call(bf16[896,384]{1,0:T(8,128)(2,1)S(1)} %get-tuple-element.67.refs_0_, bf16[896,384]{1,0:T(8,128)(2,1)S(1)} %collective-permute-done.6.refs_1_, bf16[896,640]{1,0:T(8,128)(2,1)S(1)} %get-tuple-element.93.refs_2_, ...), custom_call_target="tpu_custom_call" | custom-call | flops 1024 | bytes 1024 | tf_op jit(solution)/shard_map/refresh_states/pallas_call | solution.py:392
  (46 shorter events, 3.9 us)
Async XLA Ops:
  3.1 13.6 %collective-permute-start.2 = (bf16[64,3584]{1,0:T(8,128)(2,1)S(1)}, bf16[64,3584]{1,0:T(8,128)(2,1)S(1)}, u32[]{:S(2)}, u32[]{:S(2)}) collective-permute-start(bf16[64,3584]{1,0:T(8,128)(2,1)S(1)} %fusion.2.refs_0_), channel_id=1, source_target_pairs={{0,1},{1,0},{2,3},{3,2},{4,5},{5,4},{6,7},{7,6},{8,9},{9,8},{10,11... | collective-permute-start | bytes 1376264 | tf_op jit(solution)/shard_map/ppermute | solution.py:438
  6.1 12.0 %collective-permute-start.1 = (bf16[64,3584]{1,0:T(8,128)(2,1)S(1)}, bf16[64,3584]{1,0:T(8,128)(2,1)S(1)}, u32[]{:S(2)}, u32[]{:S(2)}) collective-permute-start(bf16[64,3584]{1,0:T(8,128)(2,1)S(1)} %fusion.2.refs_0_), channel_id=1, source_target_pairs={{0,16},{8,24},{16,0},{24,8},{1,17},{9,25},{17,1},{25,9},{2,18},{10... | collective-permute-start | bytes 1376264 | tf_op jit(solution)/shard_map/ppermute | solution.py:432
  7.6 13.6 %collective-permute-start = (bf16[64,3584]{1,0:T(8,128)(2,1)S(1)}, bf16[64,3584]{1,0:T(8,128)(2,1)S(1)}, u32[]{:S(2)}, u32[]{:S(2)}) collective-permute-start(bf16[64,3584]{1,0:T(8,128)(2,1)S(1)} %fusion.2.refs_0_), channel_id=1, source_target_pairs={{0,2},{1,3},{2,4},{3,5},{4,6},{5,7},{6,0},{7,1},{8,10},{9,11},{10,... | collective-permute-start | bytes 1376264 | tf_op jit(solution)/shard_map/ppermute | solution.py:448
  21.1 12.3 %collective-permute-start.5 = (bf16[64,3584]{1,0:T(8,128)(2,1)S(1)}, bf16[64,3584]{1,0:T(8,128)(2,1)S(1)}, u32[]{:S(2)}, u32[]{:S(2)}) collective-permute-start(bf16[64,3584]{1,0:T(8,128)(2,1)S(1)} %collective-permute-done.refs_3_.refs_0_), channel_id=1, source_target_pairs={{0,1},{1,0},{2,3},{3,2},{4,5},{5,4},{6,7},{7,6},{8,9},{9,8},{10,11... | collective-permute-start | bytes 1376264 | tf_op jit(solution)/shard_map/ppermute | solution.py:438
  21.6 11.8 %collective-permute-start.4 = (bf16[64,3584]{1,0:T(8,128)(2,1)S(1)}, bf16[64,3584]{1,0:T(8,128)(2,1)S(1)}, u32[]{:S(2)}, u32[]{:S(2)}) collective-permute-start(bf16[64,3584]{1,0:T(8,128)(2,1)S(1)} %collective-permute-done.refs_3_.refs_0_), channel_id=1, source_target_pairs={{0,16},{8,24},{16,0},{24,8},{1,17},{9,25},{17,1},{25,9},{2,18},{10... | collective-permute-start | bytes 1376264 | tf_op jit(solution)/shard_map/ppermute | solution.py:432
  22.2 12.3 %collective-permute-start.3 = (bf16[64,3584]{1,0:T(8,128)(2,1)S(1)}, bf16[64,3584]{1,0:T(8,128)(2,1)S(1)}, u32[]{:S(2)}, u32[]{:S(2)}) collective-permute-start(bf16[64,3584]{1,0:T(8,128)(2,1)S(1)} %collective-permute-done.refs_3_.refs_0_), channel_id=1, source_target_pairs={{0,2},{1,3},{2,4},{3,5},{4,6},{5,7},{6,0},{7,1},{8,10},{9,11},{10,... | collective-permute-start | bytes 1376264 | tf_op jit(solution)/shard_map/ppermute | solution.py:448
  35.4 17.0 %collective-permute-start.6 = (bf16[896,384]{1,0:T(8,128)(2,1)S(1)}, bf16[896,384]{1,0:T(8,128)(2,1)S(1)}, u32[]{:S(2)}, u32[]{:S(2)}) collective-permute-start(bf16[896,384]{1,0:T(8,128)(2,1)S(1)} %get-tuple-element.68), channel_id=1, source_target_pairs={{0,8},{8,0},{16,24},{24,16},{1,9},{9,1},{17,25},{25,17},{2,10},{10... | collective-permute-start | bytes 2064392 | tf_op jit(solution)/shard_map/ppermute | solution.py:435
  35.4 12.9 %collective-permute-start.9 = (bf16[64,3584]{1,0:T(8,128)(2,1)S(1)}, bf16[64,3584]{1,0:T(8,128)(2,1)S(1)}, u32[]{:S(2)}, u32[]{:S(2)}) collective-permute-start(bf16[64,3584]{1,0:T(8,128)(2,1)S(1)} %collective-permute-done.3.refs_0_), channel_id=1, source_target_pairs={{0,1},{1,0},{2,3},{3,2},{4,5},{5,4},{6,7},{7,6},{8,9},{9,8},{10,11... | collective-permute-start | bytes 1376264 | tf_op jit(solution)/shard_map/ppermute | solution.py:438
  36.8 12.6 %collective-permute-start.8 = (bf16[64,3584]{1,0:T(8,128)(2,1)S(1)}, bf16[64,3584]{1,0:T(8,128)(2,1)S(1)}, u32[]{:S(2)}, u32[]{:S(2)}) collective-permute-start(bf16[64,3584]{1,0:T(8,128)(2,1)S(1)} %collective-permute-done.3.refs_0_), channel_id=1, source_target_pairs={{0,16},{8,24},{16,0},{24,8},{1,17},{9,25},{17,1},{25,9},{2,18},{10... | collective-permute-start | bytes 1376264 | tf_op jit(solution)/shard_map/ppermute | solution.py:432
  38.3 14.1 %collective-permute-start.7 = (bf16[64,3584]{1,0:T(8,128)(2,1)S(1)}, bf16[64,3584]{1,0:T(8,128)(2,1)S(1)}, u32[]{:S(2)}, u32[]{:S(2)}) collective-permute-start(bf16[64,3584]{1,0:T(8,128)(2,1)S(1)} %collective-permute-done.3.refs_0_), channel_id=1, source_target_pairs={{0,2},{1,3},{2,4},{3,5},{4,6},{5,7},{6,0},{7,1},{8,10},{9,11},{10,... | collective-permute-start | bytes 1376264 | tf_op jit(solution)/shard_map/ppermute | solution.py:448
  38.8 13.6 %copy-start.1 = (bf16[192,2048]{1,0:T(8,128)(2,1)S(1)}, bf16[192,2048]{1,0:T(8,128)(2,1)}, u32[]{:S(2)}) copy-start(bf16[192,2048]{1,0:T(8,128)(2,1)} %get-tuple-element.82.refs_4_) | copy-start | bytes 2359300
  52.4 14.4 %collective-permute-start.11 = (bf16[192,2048]{1,0:T(8,128)(2,1)S(1)}, bf16[192,2048]{1,0:T(8,128)(2,1)S(1)}, u32[]{:S(2)}, u32[]{:S(2)}) collective-permute-start(bf16[192,2048]{1,0:T(8,128)(2,1)S(1)} %copy-done.1), channel_id=1, source_target_pairs={{0,8},{8,0},{16,24},{24,16},{1,9},{9,1},{17,25},{25,17},{2,10},{10... | collective-permute-start | bytes 2359304 | tf_op jit(solution)/shard_map/ppermute | solution.py:435
  52.4 15.2 %collective-permute-start.12 = (bf16[192,2048]{1,0:T(8,128)(2,1)}, bf16[192,2048]{1,0:T(8,128)(2,1)S(1)}, u32[]{:S(2)}, u32[]{:S(2)}) collective-permute-start(bf16[192,2048]{1,0:T(8,128)(2,1)} %get-tuple-element.83.refs_5_), channel_id=1, source_target_pairs={{0,8},{8,0},{16,24},{24,16},{1,9},{9,1},{17,25},{25,17},{2,10},{10... | collective-permute-start | bytes 2359304 | tf_op jit(solution)/shard_map/ppermute | solution.py:435
  52.9 13.4 %collective-permute-start.10 = (bf16[64,3584]{1,0:T(8,128)(2,1)S(1)}, bf16[64,3584]{1,0:T(8,128)(2,1)S(1)}, u32[]{:S(2)}, u32[]{:S(2)}) collective-permute-start(bf16[64,3584]{1,0:T(8,128)(2,1)S(1)} %collective-permute-done.7.refs_3_), channel_id=1, source_target_pairs={{0,16},{8,24},{16,0},{24,8},{1,17},{9,25},{17,1},{25,9},{2,18},{10... | collective-permute-start | bytes 1376264 | tf_op jit(solution)/shard_map/ppermute | solution.py:432
  53.4 24.1 %collective-permute-start.14 = (bf16[64,3584]{1,0:T(8,128)(2,1)S(1)}, bf16[64,3584]{1,0:T(8,128)(2,1)S(1)}, u32[]{:S(2)}, u32[]{:S(2)}) collective-permute-start(bf16[64,3584]{1,0:T(8,128)(2,1)S(1)} %collective-permute-done.2.refs_2_), channel_id=1, source_target_pairs={{0,16},{8,24},{16,0},{24,8},{1,17},{9,25},{17,1},{25,9},{2,18},{10... | collective-permute-start | bytes 1376264 | tf_op jit(solution)/shard_map/ppermute | solution.py:432
  54.9 22.6 %collective-permute-start.15 = (bf16[64,3584]{1,0:T(8,128)(2,1)S(1)}, bf16[64,3584]{1,0:T(8,128)(2,1)S(1)}, u32[]{:S(2)}, u32[]{:S(2)}) collective-permute-start(bf16[64,3584]{1,0:T(8,128)(2,1)S(1)} %collective-permute-done.4.refs_4_.refs_1_), channel_id=1, source_target_pairs={{0,1},{1,0},{2,3},{3,2},{4,5},{5,4},{6,7},{7,6},{8,9},{9,8},{10,11... | collective-permute-start | bytes 1376264 | tf_op jit(solution)/shard_map/ppermute | solution.py:438
  66.3 18.8 %collective-permute-start.16 = (bf16[64,3584]{1,0:T(8,128)(2,1)S(1)}, bf16[64,3584]{1,0:T(8,128)(2,1)S(1)}, u32[]{:S(2)}, u32[]{:S(2)}) collective-permute-start(bf16[64,3584]{1,0:T(8,128)(2,1)S(1)} %collective-permute-done.9.refs_2_), channel_id=1, source_target_pairs={{0,16},{8,24},{16,0},{24,8},{1,17},{9,25},{17,1},{25,9},{2,18},{10... | collective-permute-start | bytes 1376264 | tf_op jit(solution)/shard_map/ppermute | solution.py:432
  66.8 18.2 %collective-permute-start.13 = (bf16[64,3584]{1,0:T(8,128)(2,1)S(1)}, bf16[64,3584]{1,0:T(8,128)(2,1)S(1)}, u32[]{:S(2)}, u32[]{:S(2)}) collective-permute-start(bf16[64,3584]{1,0:T(8,128)(2,1)S(1)} %collective-permute-done.7.refs_3_), channel_id=1, source_target_pairs={{0,1},{1,0},{2,3},{3,2},{4,5},{5,4},{6,7},{7,6},{8,9},{9,8},{10,11... | collective-permute-start | bytes 1376264 | tf_op jit(solution)/shard_map/ppermute | solution.py:438
  67.6 19.6 %collective-permute-start.17 = (bf16[64,3584]{1,0:T(8,128)(2,1)S(1)}, bf16[64,3584]{1,0:T(8,128)(2,1)S(1)}, u32[]{:S(2)}, u32[]{:S(2)}) collective-permute-start(bf16[64,3584]{1,0:T(8,128)(2,1)S(1)} %collective-permute-done.10.refs_0_.refs_4_), channel_id=1, source_target_pairs={{0,1},{1,0},{2,3},{3,2},{4,5},{5,4},{6,7},{7,6},{8,9},{9,8},{10,11... | collective-permute-start | bytes 1376264 | tf_op jit(solution)/shard_map/ppermute | solution.py:438
  87.2 9.1 %copy-start = (bf16[256,2048]{1,0:T(8,128)(2,1)S(1)}, bf16[256,2048]{1,0:T(8,128)(2,1)}, u32[]{:S(2)}) copy-start(bf16[256,2048]{1,0:T(8,128)(2,1)} %get-tuple-element.96.refs_6_) | copy-start | bytes 3145732
  96.3 2.7 %collective-permute-start.19 = (bf16[256,2048]{1,0:T(8,128)(2,1)S(1)}, bf16[256,2048]{1,0:T(8,128)(2,1)S(1)}, u32[]{:S(2)}, u32[]{:S(2)}) collective-permute-start(bf16[256,2048]{1,0:T(8,128)(2,1)S(1)} %copy-done), channel_id=1, source_target_pairs={{0,8},{8,0},{16,24},{24,16},{1,9},{9,1},{17,25},{25,17},{2,10},{10... | collective-permute-start | bytes 3145736 | tf_op jit(solution)/shard_map/ppermute | solution.py:435
  96.3 3.2 %collective-permute-start.22 = (f32[32,128]{1,0:T(8,128)S(1)}, f32[32,128]{1,0:T(8,128)S(1)}, u32[]{:S(2)}, u32[]{:S(2)}) collective-permute-start(f32[32,128]{1,0:T(8,128)S(1)} %get-tuple-element.97.own_ref), channel_id=1, source_target_pairs={{0,9},{1,8},{2,11},{3,10},{4,13},{5,12},{6,15},{7,14},{8,1},{9,0},... | collective-permute-start | bytes 49160 | tf_op jit(solution)/shard_map/ppermute | solution.py:445
  97.2 2.4 %collective-permute-start.21 = (f32[32,128]{1,0:T(8,128)S(1)}, f32[32,128]{1,0:T(8,128)S(1)}, u32[]{:S(2)}, u32[]{:S(2)}) collective-permute-start(f32[32,128]{1,0:T(8,128)S(1)} %get-tuple-element.97.own_ref), channel_id=1, source_target_pairs={{0,8},{8,0},{16,24},{24,16},{1,9},{9,1},{17,25},{25,17},{2,10},{10... | collective-permute-start | bytes 49160 | tf_op jit(solution)/shard_map/ppermute | solution.py:435
  97.3 3.7 %collective-permute-start.20 = (f32[32,128]{1,0:T(8,128)S(1)}, f32[32,128]{1,0:T(8,128)S(1)}, u32[]{:S(2)}, u32[]{:S(2)}) collective-permute-start(f32[32,128]{1,0:T(8,128)S(1)} %get-tuple-element.97.own_ref), channel_id=1, source_target_pairs={{0,1},{1,0},{2,3},{3,2},{4,5},{5,4},{6,7},{7,6},{8,9},{9,8},{10,11... | collective-permute-start | bytes 49160 | tf_op jit(solution)/shard_map/ppermute | solution.py:438
  101.0 8.3 %collective-permute-start.23 = (bf16[384,2048]{1,0:T(8,128)(2,1)}, bf16[384,2048]{1,0:T(8,128)(2,1)S(1)}, u32[]{:S(2)}, u32[]{:S(2)}) collective-permute-start(bf16[384,2048]{1,0:T(8,128)(2,1)} %get-tuple-element.99.refs_7_), channel_id=1, source_target_pairs={{0,8},{8,0},{16,24},{24,16},{1,9},{9,1},{17,25},{25,17},{2,10},{10... | collective-permute-start | bytes 4718600 | tf_op jit(solution)/shard_map/ppermute | solution.py:435
  102.5 6.8 %collective-permute-start.18 = (bf16[896,640]{1,0:T(8,128)(2,1)S(1)}, bf16[896,640]{1,0:T(8,128)(2,1)S(1)}, u32[]{:S(2)}, u32[]{:S(2)}) collective-permute-start(bf16[896,640]{1,0:T(8,128)(2,1)S(1)} %get-tuple-element.94), channel_id=1, source_target_pairs={{0,8},{8,0},{16,24},{24,16},{1,9},{9,1},{17,25},{25,17},{2,10},{10... | collective-permute-start | bytes 3440648 | tf_op jit(solution)/shard_map/ppermute | solution.py:435
  103.0 5.9 %collective-permute-start.26 = (f32[64,128]{1,0:T(8,128)S(1)}, f32[64,128]{1,0:T(8,128)S(1)}, u32[]{:S(2)}, u32[]{:S(2)}) collective-permute-start(f32[64,128]{1,0:T(8,128)S(1)} %get-tuple-element.98.refs_12_), channel_id=1, source_target_pairs={{0,2},{1,3},{2,4},{3,5},{4,6},{5,7},{6,0},{7,1},{8,10},{9,11},{10,... | collective-permute-start | bytes 98312 | tf_op jit(solution)/shard_map/ppermute | solution.py:448
  103.0 5.9 %collective-permute-start.25 = (f32[64,128]{1,0:T(8,128)S(1)}, f32[64,128]{1,0:T(8,128)S(1)}, u32[]{:S(2)}, u32[]{:S(2)}) collective-permute-start(f32[64,128]{1,0:T(8,128)S(1)} %get-tuple-element.98.refs_12_), channel_id=1, source_target_pairs={{0,4},{1,5},{2,6},{3,7},{4,0},{5,1},{6,2},{7,3},{8,12},{9,13},{10,... | collective-permute-start | bytes 98312 | tf_op jit(solution)/shard_map/ppermute | solution.py:448
  104.6 4.7 %collective-permute-start.24 = (f32[64,128]{1,0:T(8,128)S(1)}, f32[64,128]{1,0:T(8,128)S(1)}, u32[]{:S(2)}, u32[]{:S(2)}) collective-permute-start(f32[64,128]{1,0:T(8,128)S(1)} %get-tuple-element.98.refs_12_), channel_id=1, source_target_pairs={{0,6},{1,7},{2,0},{3,1},{4,2},{5,3},{6,4},{7,5},{8,14},{9,15},{10,... | collective-permute-start | bytes 98312 | tf_op jit(solution)/shard_map/ppermute | solution.py:448

commit v6 on v5

--- a/solution.py
+++ b/solution.py
@@ -122,9 +122,11 @@
     )(pltpu.with_memory_space_constraint(weight, pltpu.HBM), true_ids, sample_ids, *earlier)
 
 
-def logits_kernel(stat_rows, *refs):
+def logits_kernel(stat_rows, first_row, joins, *refs):
     count = len(stat_rows)
     block_refs, refs = refs[:count], refs[count:]
+    if joins:
+        refs = refs[:2] + refs[3:]
     weight_ref, before_ref, exp_ref, stats_ref, rows, logits, scaled_exp, highs, sums, sent = refs
     tokens, columns = logits.shape
     length = tokens // count
@@ -163,8 +165,9 @@
 
         lax.fori_loop(0, length // chunk, scale, 0, unroll=2)
         place = pl.ds(block * length, length)
+        target = pl.ds(first_row + block * length, length)
         copies.append(
-            pltpu.make_async_copy(scaled_exp.at[place], exp_ref.at[place], sent.at[block])
+            pltpu.make_async_copy(scaled_exp.at[place], exp_ref.at[target], sent.at[block])
         )
         copies[-1].start()
     totals = jnp.broadcast_to(jnp.sum(sums[...], axis=1, keepdims=True), sums.shape)
@@ -178,18 +181,21 @@
         copy.wait()
 
 
-def round_logits(blocks, stat_rows, held_weight, before):
+def round_logits(blocks, stat_rows, held_weight, before, first_row, exp_rows, into):
     depth, columns = held_weight.shape
     length = blocks[0].shape[0]
     tokens = length * len(blocks)
     near = pl.BlockSpec(memory_space=pltpu.VMEM)
     held_weight = pltpu.with_memory_space_constraint(held_weight, pltpu.VMEM)
+    far = pl.BlockSpec(memory_space=pltpu.HBM)
+    joins = [] if into is None else [pltpu.with_memory_space_constraint(into, pltpu.HBM)]
     return pl.pallas_call(
-        functools.partial(logits_kernel, stat_rows),
-        in_specs=[near] * (len(blocks) + 2),
-        out_specs=[pl.BlockSpec(memory_space=pltpu.HBM), near],
+        functools.partial(logits_kernel, stat_rows, first_row, len(joins)),
+        in_specs=[near] * (len(blocks) + 2) + [far] * len(joins),
+        input_output_aliases={len(blocks) + 2: 0} if joins else {},
+        out_specs=[far, near],
         out_shape=[
-            pltpu.HBM((tokens, columns), jnp.bfloat16),
+            pltpu.HBM((exp_rows, columns), jnp.bfloat16),
             jax.ShapeDtypeStruct(before.shape, jnp.float32),
         ],
         scratch_shapes=[
@@ -203,7 +209,7 @@
         compiler_params=pltpu.CompilerParams(vmem_limit_bytes=LOGITS_VMEM),
         cost_estimate=BRIEF,
         name="round_logits",
-    )(*blocks, held_weight, before)
+    )(*blocks, held_weight, before, *joins)
 
 
 def turn_kernel(count, rep_ref, *refs):
@@ -306,7 +312,7 @@
 
 def refresh_kernel(lines, length, early_rows, late_rows, *refs):
     early_refs, late_refs, refs = refs[:2], refs[2:4], refs[4:]
-    exp_refs, refs = refs[:8], refs[8:]
+    exp_refs, refs = refs[:6], refs[6:]
     stats_refs, refs = refs[:lines], refs[lines:]
     (first_ref, true_at, sample_at, true_sum, sample_sum, moment_ref, curvature_ref,
      moment_out, curvature_out, update_out, scaled, factors) = refs
@@ -352,14 +358,14 @@
 
     shared = jnp.dot(
         scaled[...],
-        jnp.concatenate([ref[...] for ref in exp_refs[:2] + exp_refs[4:6]], axis=0),
+        jnp.concatenate([exp_refs[0][...], exp_refs[3][...]], axis=0),
         preferred_element_type=jnp.float32,
     )
     gradient = shared - true_sum[...].astype(jnp.float32)
     sample_grad = shared - sample_sum[...].astype(jnp.float32)
     for core in range(2):
         place = slice(core * late, (core + 1) * late)
-        exps = jnp.concatenate([ref[...] for ref in exp_refs[4 * core + 2:4 * core + 4]], axis=0)
+        exps = jnp.concatenate([ref[...] for ref in exp_refs[3 * core + 1:3 * core + 3]], axis=0)
         true_parts, sample_parts = [], []
         for lane in range(0, width, 128):
             probs = exps[:, lane:lane + 128].astype(jnp.float32) * factors[place]
@@ -406,7 +412,7 @@
         cost_estimate=BRIEF,
         name="refresh_states",
     )(
-        *early, *late, *in_hbm(exps[:4]), *exps[4:], *stats, first, *late_ids,
+        *early, *late, *in_hbm(exps[:3]), *exps[3:], *stats, first, *late_ids,
         *in_hbm(sums, [moment, curvature])
     )
 
@@ -451,9 +457,9 @@
     plain = [(0, 0), (0, 1), (1, 0)]
     groups = [[(*kind, turn) for kind in plain] for turn in range(split)]
     groups += [[(*kind, turn) for turn in range(split, lines - 1) for kind in plain]]
-    groups[-1] += [(0, 0, lines - 1)]
+    groups[-1] += [(0, 0, lines - 1)] + [(1, 1, turn) for turn in range(split)]
     groups += [[(0, 1, lines - 1), (1, 0, lines - 1)]]
-    groups[-1] += [(1, 1, turn) for turn in range(lines)]
+    groups[-1] += [(1, 1, turn) for turn in range(split, lines)]
     early_blocks, late_blocks = sum(groups[:split], []), sum(groups[split:], [])
 
     def stat_row(block):
@@ -476,14 +482,14 @@
     stats = jnp.zeros((8 * lines, 128), jnp.float32)
 
     held = {(0, 0, 0): normed}
-    exps = []
-
-    def logits(group, stats, *gates):
+    early_exp = None
+
+    def logits(group, stats, *gates, first_row=0, exp_rows=None, into=None):
         blocks = [held[block] for block in group]
         blocks[0] = after(blocks[0], *gates)
-        exp, stats = round_logits(blocks, [stat_row(block) for block in group], head_weight, stats)
-        exps.append(exp)
-        return stats
+        rows = [stat_row(block) for block in group]
+        exp_rows = exp_rows or len(group) * length
+        return round_logits(blocks, rows, head_weight, stats, first_row, exp_rows, into)
 
     def diagonal(turn):
         if turn % 2 == 0:
@@ -498,34 +504,41 @@
             arrived = [to_z(block, 1), held[0, 1, turn], held[1, 0, turn]]
             if turn == 0:
                 arrived += [*early_ids, *late_ids, rep_scalar, stats]
+            elif turn < split:
+                arrived += [early_exp]
             else:
-                arrived += exps
+                arrived += [early_exp] + [held[1, 1, past] for past in range(split)]
             arrived = lax.optimization_barrier(tuple(arrived))
             held[0, 0, turn + 1], held[0, 1, turn], held[1, 0, turn] = arrived[:3]
             if turn == 0:
                 early_ids, late_ids = list(arrived[3:5]), list(arrived[5:7])
                 rep_scalar, stats = arrived[7:]
                 head_weight, *late_ids = prepared(head_weight, *late_ids, stats)
-            early_exps = arrived[3:]
-        if turn + 1 < lines:
+            else:
+                early_exp = arrived[3]
+                held.update({(1, 1, past): got for past, got in enumerate(arrived[4:])})
             held[1, 1, turn] = diagonal(turn)
         if turn < split:
-            stats = logits(groups[turn], stats, held[0, 0, turn + 1])
+            size = len(groups[turn]) * length
+            early_exp, stats = logits(
+                groups[turn], stats, held[0, 0, turn + 1],
+                first_row=turn * size, exp_rows=split * size, into=early_exp,
+            )
 
     early = [held[block] for block in early_blocks]
-    early[0] = after(early[0], held[0, 0, split])
+    early[0] = after(early[0], held[0, 0, lines - 1])
     early = turned_features(rep_scalar, early, rows)
     early = [early[0], to_core(early[1])]
-    stats = logits(groups[split], stats, held[0, 0, lines - 1], early[1])
-    held[0, 1, lines - 1] = after(held[0, 1, lines - 1], exps[split])
+    other_exps = [to_core(early_exp)]
+    middle_exp, stats = logits(groups[split], stats, held[0, 0, lines - 1])
+    held[0, 1, lines - 1] = after(held[0, 1, lines - 1], middle_exp)
     held[1, 1, lines - 1] = diagonal(lines - 1)
-    early_exps = lax.optimization_barrier((*early_exps, early[1]))[:split]
-    other_exps = [to_core(exp) for exp in early_exps]
-    early_ids[0] = after(early_ids[0], exps[split], held[0, 1, lines - 1], *other_exps)
+    early_ids[0] = after(early_ids[0], middle_exp, held[0, 1, lines - 1], *other_exps)
     sums = one_hot_sums(early, early_ids, columns)
-    stats = logits(groups[-1], stats, *sums)
+    last_exp, stats = logits(groups[-1], stats, *sums)
+    exps = [early_exp, middle_exp, last_exp]
     stats = after(stats, *other_exps)
-    other_exps.append(to_core(after(exps[split], stats)))
+    other_exps.append(to_core(after(middle_exp, stats)))
     across_stats, core_stats, both_stats = to_y(stats), to_core(stats), to_y_core(stats)
     late = [held[block] for block in late_blocks]
     late[0] = after(late[0], stats)
@@ -534,7 +547,7 @@
         after(stats, *other_exps), across_stats, core_stats, both_stats
     )
     all_stats = [merged] + [to_z(merged, -along) for along in range(1, lines)]
-    other_exps.append(to_core(after(exps[-1], merged)))
+    other_exps.append(to_core(after(last_exp, merged)))
     late = [late[0], to_core(late[1])]
     return tuple(refresh_states(
         lines, length, [stat_row(block) for block in early_blocks],

time: 132 us -> 125 us (0.947)
  waiting for transfers between devices: 32.5 us -> 23.4 us
  starting transfers between devices: 22.9 us -> 25.1 us
    ppermute x6, waiting for transfers between devices: 14 us -> 1.84 us  [to_x(): return lax.ppermute(values, 'rep', swap_pairs(reps, 2))]
    ppermute x7, waiting for transfers between devices: 7.93 us -> 14.3 us  [to_y(): return lax.ppermute(values, 'shard', swap_pairs(shards, 1))]
    ppermute x6, waiting for transfers between devices: 9.55 us -> 6.21 us  [to_z(): return lax.ppermute(values, 'shard', shift_pairs(lines, along, 0))]
    ppermute x6, starting transfers between devices: 5.96 us -> 7.65 us  [to_z(): return lax.ppermute(values, 'shard', shift_pairs(lines, along, 0))]
  transfers between devices with their start and end apart: 27 -> 26, of which waited for: 15 -> 13; matrix products, arithmetic and copies ran while one was open for 5% -> 5% of each run, Pallas kernels for 26% -> 30%
where the time goes in v6:
time: 125 us; the launch traced here: 124 us
  Pallas kernels  65.7 us (53%)
  starting transfers between devices  25.1 us (20%)
  waiting for transfers between devices  23.4 us (19%)
  other arithmetic  6.04 us (5%)
  local copies, waits for them, and re-layouts  3.16 us (3%)
    pallas_call x4, Pallas kernels, round_logits(): pl.pallas_call(functools.partial(logits_kernel, stat_rows, first_row, len...  27.4 us
    pallas_call x1, Pallas kernels, refresh_states(): pl.pallas_call(functools.partial(refresh_kernel, lines, length, early_row...  21.9 us
    ppermute x7, waiting for transfers between devices, to_y(): return lax.ppermute(values, 'shard', swap_pairs(shards, 1))  14.3 us
    ppermute x7, starting transfers between devices, to_y(): return lax.ppermute(values, 'shard', swap_pairs(shards, 1))  9.51 us
    pallas_call x1, Pallas kernels, one_hot_sums(): pl.pallas_call(functools.partial(one_hot_kernel, len(features)), grid=(co...  8.65 us
    ppermute x6, starting transfers between devices, to_z(): return lax.ppermute(values, 'shard', shift_pairs(lines, along, 0))  7.65 us
    ppermute x6, starting transfers between devices, to_x(): return lax.ppermute(values, 'rep', swap_pairs(reps, 2))  6.51 us
    ppermute x6, waiting for transfers between devices, to_z(): return lax.ppermute(values, 'shard', shift_pairs(lines, along, 0))  6.21 us
  transfers between devices with their start and end apart: 26, of which 13 were waited for; matrix products, arithmetic and copies ran while one was open for 5% of the time, Pallas kernels for 30%

profile of v6, /device:TPU:0, one launch (start us, length us, event | category | flops | bytes accessed | tf_op | source)
XLA Modules:
  0.0 124.2 jit_solution(3994006179785616430)
XLA Ops:
  0.6 1.2 fusion
  1.9 1.2 fusion.2.refs_0_
  3.1 3.0 %collective-permute-start.2 = (bf16[64,3584]{1,0:T(8,128)(2,1)S(1)}, bf16[64,3584]{1,0:T(8,128)(2,1)S(1)}, u32[]{:S(2)}, u32[]{:S(2)}) collective-permute-start(bf16[64,3584]{1,0:T(8,128)(2,1)S(1)} %fusion.2.refs_0_), channel_id=1, source_target_pairs={{0,1},{1,0},{2,3},{3,2},{4,5},{5,4},{6,7},{7,6},{8,9},{9,8},{10,11... | collective-permute-start | bytes 1376264 | tf_op jit(solution)/shard_map/ppermute | solution.py:444
  6.1 1.5 %collective-permute-start.1 = (bf16[64,3584]{1,0:T(8,128)(2,1)S(1)}, bf16[64,3584]{1,0:T(8,128)(2,1)S(1)}, u32[]{:S(2)}, u32[]{:S(2)}) collective-permute-start(bf16[64,3584]{1,0:T(8,128)(2,1)S(1)} %fusion.2.refs_0_), channel_id=1, source_target_pairs={{0,16},{8,24},{16,0},{24,8},{1,17},{9,25},{17,1},{25,9},{2,18},{10... | collective-permute-start | bytes 1376264 | tf_op jit(solution)/shard_map/ppermute | solution.py:438
  7.6 1.6 %collective-permute-start = (bf16[64,3584]{1,0:T(8,128)(2,1)S(1)}, bf16[64,3584]{1,0:T(8,128)(2,1)S(1)}, u32[]{:S(2)}, u32[]{:S(2)}) collective-permute-start(bf16[64,3584]{1,0:T(8,128)(2,1)S(1)} %fusion.2.refs_0_), channel_id=1, source_target_pairs={{0,2},{1,3},{2,4},{3,5},{4,6},{5,7},{6,0},{7,1},{8,10},{9,11},{10,... | collective-permute-start | bytes 1376264 | tf_op jit(solution)/shard_map/ppermute | solution.py:454
  9.2 0.7 fusion.7
  9.8 0.7 compare_and_fusion
  10.5 0.7 multiply_add_fusion
  11.2 1.2 slice.31
  12.4 0.8 slice.30
  13.3 0.7 broadcast_subtract_fusion
  14.1 0.7 fusion.4
  14.9 0.6 gather_fusion
  16.0 0.7 collective-permute-done.2.refs_2_
  16.6 1.5 %collective-permute-done.1.refs_1_ = bf16[64,3584]{1,0:T(8,128)(2,1)S(1)} collective-permute-done((bf16[64,3584]{1,0:T(8,128)(2,1)S(1)}, bf16[64,3584]{1,0:T(8,128)(2,1)S(1)}, u32[]{:S(2)}, u32[]{:S(2)}) %collective-permute-start.1) | collective-permute-done | bytes 458784 | tf_op jit(solution)/shard_map/ppermute | solution.py:438
  18.1 3.1 %collective-permute-done.refs_0_.refs_3_ = bf16[64,3584]{1,0:T(8,128)(2,1)S(1)} collective-permute-done((bf16[64,3584]{1,0:T(8,128)(2,1)S(1)}, bf16[64,3584]{1,0:T(8,128)(2,1)S(1)}, u32[]{:S(2)}, u32[]{:S(2)}) %collective-permute-start) | collective-permute-done | bytes 458784 | tf_op jit(solution)/shard_map/ppermute | solution.py:454
  21.1 0.5 collective-permute-start.5
  21.6 0.5 collective-permute-start.4
  22.2 1.5 %collective-permute-start.9 = (bf16[64,3584]{1,0:T(8,128)(2,1)S(1)}, bf16[64,3584]{1,0:T(8,128)(2,1)S(1)}, u32[]{:S(2)}, u32[]{:S(2)}) collective-permute-start(bf16[64,3584]{1,0:T(8,128)(2,1)S(1)} %collective-permute-done.2.refs_2_), channel_id=1, source_target_pairs={{0,16},{8,24},{16,0},{24,8},{1,17},{9,25},{17,1},{25,9},{2,18},{10... | collective-permute-start | bytes 1376264 | tf_op jit(solution)/shard_map/ppermute | solution.py:438
  23.7 5.5 %prepared.1 = (bf16[3584,2048]{1,0:T(8,128)(2,1)S(1)}, s32[1280,128]{1,0:T(8,128)S(1)}, s32[1280,128]{1,0:T(8,128)S(1)}) custom-call(bf16[3584,2048]{1,0:T(8,128)(2,1)} %weight_ref.1, s32[1,1280]{1,0:T(1,128)S(1)} %squeeze.14.true_ids, s32[1,1280]{1,0:T(1,128)S(1)} %squeeze.15.sample_ids, f32[32,128]{1,0:T(8,128)S(1)} %broadcast_in_dim.22.refs_0_.refs_4_), custom_call_target="tpu_custom_call" | custom-call | flops 1024 | bytes 1024 | tf_op jit(solution)/shard_map/prepared/pallas_call | solution.py:113
  29.2 5.8 %round_logits.4 = (bf16[384,2048]{1,0:T(8,128)(2,1)}, f32[32,128]{1,0:T(8,128)S(1)}) custom-call(bf16[64,3584]{1,0:T(8,128)(2,1)S(1)} %fusion.2.refs_0_, bf16[64,3584]{1,0:T(8,128)(2,1)S(1)} %collective-permute-done.1.refs_1_, bf16[64,3584]{1,0:T(8,128)(2,1)S(1)} %collective-permute-done.2.refs_2_, ...), custom_call_target="tpu_custom_call" | custom-call | flops 1024 | bytes 1024 | tf_op jit(solution)/shard_map/round_logits/pallas_call | solution.py:192
  35.1 1.5 %collective-permute-start.10 = (bf16[64,3584]{1,0:T(8,128)(2,1)S(1)}, bf16[64,3584]{1,0:T(8,128)(2,1)S(1)}, u32[]{:S(2)}, u32[]{:S(2)}) collective-permute-start(bf16[64,3584]{1,0:T(8,128)(2,1)S(1)} %collective-permute-done.4.refs_1_.refs_4_), channel_id=1, source_target_pairs={{0,1},{1,0},{2,3},{3,2},{4,5},{5,4},{6,7},{7,6},{8,9},{9,8},{10,11... | collective-permute-start | bytes 1376264 | tf_op jit(solution)/shard_map/ppermute | solution.py:444
  37.1 0.6 collective-permute-start.7
  37.8 1.1 collective-permute-start.6
  38.9 5.8 %round_logits.5 = (bf16[384,2048]{1,0:T(8,128)(2,1)}, f32[32,128]{1,0:T(8,128)S(1)}) custom-call(bf16[64,3584]{1,0:T(8,128)(2,1)S(1)} %collective-permute-done.refs_0_.refs_3_, bf16[64,3584]{1,0:T(8,128)(2,1)S(1)} %collective-permute-done.4.refs_1_.refs_4_, ...), custom_call_target="tpu_custom_call", output_to_operand_aliasing={{0}: (5, {})} | custom-call | flops 1024 | bytes 1024 | tf_op jit(solution)/shard_map/round_logits/pallas_call | solution.py:192
  44.9 3.6 %collective-permute-done.10.refs_5_ = bf16[64,3584]{1,0:T(8,128)(2,1)S(1)} collective-permute-done((bf16[64,3584]{1,0:T(8,128)(2,1)S(1)}, bf16[64,3584]{1,0:T(8,128)(2,1)S(1)}, u32[]{:S(2)}, u32[]{:S(2)}) %collective-permute-start.10) | collective-permute-done | bytes 458784 | tf_op jit(solution)/shard_map/ppermute | solution.py:444
  48.6 6.3 %collective-permute-done.8.refs_2_ = bf16[64,3584]{1,0:T(8,128)(2,1)S(1)} collective-permute-done((bf16[64,3584]{1,0:T(8,128)(2,1)S(1)}, bf16[64,3584]{1,0:T(8,128)(2,1)S(1)}, u32[]{:S(2)}, u32[]{:S(2)}) %collective-permute-start.8) | collective-permute-done | bytes 458784 | tf_op jit(solution)/shard_map/ppermute | solution.py:444
  54.9 0.8 collective-permute-start.12
  55.7 0.9 turned_features.2
  56.8 1.3 %collective-permute-start.14 = (bf16[64,3584]{1,0:T(8,128)(2,1)S(1)}, bf16[64,3584]{1,0:T(8,128)(2,1)S(1)}, u32[]{:S(2)}, u32[]{:S(2)}) collective-permute-start(bf16[64,3584]{1,0:T(8,128)(2,1)S(1)} %collective-permute-done.6.refs_3_), channel_id=1, source_target_pairs={{0,1},{1,0},{2,3},{3,2},{4,5},{5,4},{6,7},{7,6},{8,9},{9,8},{10,11... | collective-permute-start | bytes 1376264 | tf_op jit(solution)/shard_map/ppermute | solution.py:444
  58.1 1.5 %collective-permute-start.15 = (bf16[64,3584]{1,0:T(8,128)(2,1)S(1)}, bf16[64,3584]{1,0:T(8,128)(2,1)S(1)}, u32[]{:S(2)}, u32[]{:S(2)}) collective-permute-start(bf16[64,3584]{1,0:T(8,128)(2,1)S(1)} %collective-permute-done.8.refs_2_), channel_id=1, source_target_pairs={{0,16},{8,24},{16,0},{24,8},{1,17},{9,25},{17,1},{25,9},{2,18},{10... | collective-permute-start | bytes 1376264 | tf_op jit(solution)/shard_map/ppermute | solution.py:438
  59.6 9.1 %round_logits.6 = (bf16[384,2048]{1,0:T(8,128)(2,1)}, f32[32,128]{1,0:T(8,128)S(1)}) custom-call(bf16[64,3584]{1,0:T(8,128)(2,1)S(1)} %collective-permute-done.3.refs_0_, bf16[64,3584]{1,0:T(8,128)(2,1)S(1)} %collective-permute-done.7.refs_1_, bf16[64,3584]{1,0:T(8,128)(2,1)S(1)} %collective-permute-done.8.refs_2_, ...), custom_call_target="tpu_custom_call" | custom-call | flops 1024 | bytes 1024 | tf_op jit(solution)/shard_map/round_logits/pallas_call | solution.py:192
  68.7 1.1 collective-permute-start.16
  69.8 8.7 %one_hot_sums.1 = (bf16[896,2048]{1,0:T(8,128)(2,1)}, bf16[896,2048]{1,0:T(8,128)(2,1)}) custom-call(bf16[896,384]{1,0:T(8,128)(2,1)S(1)} %get-tuple-element.72.refs_0_, bf16[896,384]{1,0:T(8,128)(2,1)S(1)} %collective-permute-done.11.refs_1_, s32[1,768]{1,0:T(1,128)S(1)} %squeeze.12.refs_2_, s32[1,768]{1,0:T(1,128)S(1)} %squeeze.13.refs_3_), custom_call_target="tpu_custom_call" | custom-call | flops 1024 | bytes 1024 | tf_op jit(solution)/shard_map/one_hot_sums/pallas_call | solution.py:271
  78.5 2.5 %collective-permute-done.16.refs_3_.refs_9_ = bf16[64,3584]{1,0:T(8,128)(2,1)S(1)} collective-permute-done((bf16[64,3584]{1,0:T(8,128)(2,1)S(1)}, bf16[64,3584]{1,0:T(8,128)(2,1)S(1)}, u32[]{:S(2)}, u32[]{:S(2)}) %collective-permute-start.16) | collective-permute-done | bytes 458784 | tf_op jit(solution)/shard_map/ppermute | solution.py:444
  81.0 6.8 %round_logits.7 = (bf16[256,2048]{1,0:T(8,128)(2,1)}, f32[32,128]{1,0:T(8,128)S(1)}) custom-call(bf16[64,3584]{1,0:T(8,128)(2,1)S(1)} %collective-permute-done.12.refs_0_.refs_6_, bf16[64,3584]{1,0:T(8,128)(2,1)S(1)} %collective-permute-done.14.refs_1_.refs_7_, bf16[64,3584]{1,0:T(8,128)(2,1)S(1)} %collective-permute-done.15.refs_2_.refs_8_, ...), custom_call_target="tpu_custom_call" | custom-call | flops 1024 | bytes 1024 | tf_op jit(solution)/shard_map/round_logits/pallas_call | solution.py:192
  87.9 1.4 %turned_features.3 = (bf16[896,640]{1,0:T(8,128)(2,1)S(1)}, bf16[896,640]{1,0:T(8,128)(2,1)S(1)}) custom-call(s32[1]{0:T(128)} %bitcast.5.rep_ref, bf16[64,3584]{1,0:T(8,128)(2,1)S(1)} %collective-permute-done.3.refs_0_, bf16[64,3584]{1,0:T(8,128)(2,1)S(1)} %collective-permute-done.7.refs_1_, bf16[64,3584]{1,0:T(8,128)(2,1)S(1)} %collective-permute-done.8.refs_2_, ...), custom_call_target="tpu_custom_call" | custom-call | flops 1024 | bytes 1024 | tf_op jit(solution)/shard_map/turned_features/pallas_call | solution.py:234
  89.3 0.5 collective-permute-start.17
  90.4 1.5 %collective-permute-start.19 = (f32[32,128]{1,0:T(8,128)S(1)}, f32[32,128]{1,0:T(8,128)S(1)}, u32[]{:S(2)}, u32[]{:S(2)}) collective-permute-start(f32[32,128]{1,0:T(8,128)S(1)} %get-tuple-element.97.own_ref), channel_id=1, source_target_pairs={{0,1},{1,0},{2,3},{3,2},{4,5},{5,4},{6,7},{7,6},{8,9},{9,8},{10,11... | collective-permute-start | bytes 49160 | tf_op jit(solution)/shard_map/ppermute | solution.py:444
  92.0 1.0 collective-permute-done.21.both_ref
  93.0 1.2 collective-permute-done.19.across_ref
  94.3 1.0 collective-permute-start.25
  95.3 3.2 %collective-permute-start.24 = (f32[64,128]{1,0:T(8,128)S(1)}, f32[64,128]{1,0:T(8,128)S(1)}, u32[]{:S(2)}, u32[]{:S(2)}) collective-permute-start(f32[64,128]{1,0:T(8,128)S(1)} %get-tuple-element.98.refs_10_), channel_id=1, source_target_pairs={{0,4},{1,5},{2,6},{3,7},{4,0},{5,1},{6,2},{7,3},{8,12},{9,13},{10,... | collective-permute-start | bytes 98312 | tf_op jit(solution)/shard_map/ppermute | solution.py:454
  98.4 0.8 collective-permute-start.23
  99.2 0.9 collective-permute-done.25.refs_13_
  100.1 1.3 %collective-permute-done.24.refs_12_ = f32[64,128]{1,0:T(8,128)S(1)} collective-permute-done((f32[64,128]{1,0:T(8,128)S(1)}, f32[64,128]{1,0:T(8,128)S(1)}, u32[]{:S(2)}, u32[]{:S(2)}) %collective-permute-start.24) | collective-permute-done | bytes 32800 | tf_op jit(solution)/shard_map/ppermute | solution.py:454
  101.4 0.9 collective-permute-done.23.refs_11_
  102.4 21.9 %refresh_states.1 = (bf16[896,2048]{1,0:T(8,128)(2,1)}, bf16[896,2048]{1,0:T(8,128)(2,1)}, bf16[896,2048]{1,0:T(8,128)(2,1)}) custom-call(bf16[896,384]{1,0:T(8,128)(2,1)S(1)} %get-tuple-element.72.refs_0_, bf16[896,384]{1,0:T(8,128)(2,1)S(1)} %collective-permute-done.11.refs_1_, bf16[896,640]{1,0:T(8,128)(2,1)S(1)} %get-tuple-element.93.refs_2_, ...), custom_call_target="tpu_custom_call" | custom-call | flops 1024 | bytes 1024 | tf_op jit(solution)/shard_map/refresh_states/pallas_call | solution.py:398
  (44 shorter events, 2.6 us)
Async XLA Ops:
  3.1 13.6 %collective-permute-start.2 = (bf16[64,3584]{1,0:T(8,128)(2,1)S(1)}, bf16[64,3584]{1,0:T(8,128)(2,1)S(1)}, u32[]{:S(2)}, u32[]{:S(2)}) collective-permute-start(bf16[64,3584]{1,0:T(8,128)(2,1)S(1)} %fusion.2.refs_0_), channel_id=1, source_target_pairs={{0,1},{1,0},{2,3},{3,2},{4,5},{5,4},{6,7},{7,6},{8,9},{9,8},{10,11... | collective-permute-start | bytes 1376264 | tf_op jit(solution)/shard_map/ppermute | solution.py:444
  6.1 12.0 %collective-permute-start.1 = (bf16[64,3584]{1,0:T(8,128)(2,1)S(1)}, bf16[64,3584]{1,0:T(8,128)(2,1)S(1)}, u32[]{:S(2)}, u32[]{:S(2)}) collective-permute-start(bf16[64,3584]{1,0:T(8,128)(2,1)S(1)} %fusion.2.refs_0_), channel_id=1, source_target_pairs={{0,16},{8,24},{16,0},{24,8},{1,17},{9,25},{17,1},{25,9},{2,18},{10... | collective-permute-start | bytes 1376264 | tf_op jit(solution)/shard_map/ppermute | solution.py:438
  7.6 13.6 %collective-permute-start = (bf16[64,3584]{1,0:T(8,128)(2,1)S(1)}, bf16[64,3584]{1,0:T(8,128)(2,1)S(1)}, u32[]{:S(2)}, u32[]{:S(2)}) collective-permute-start(bf16[64,3584]{1,0:T(8,128)(2,1)S(1)} %fusion.2.refs_0_), channel_id=1, source_target_pairs={{0,2},{1,3},{2,4},{3,5},{4,6},{5,7},{6,0},{7,1},{8,10},{9,11},{10,... | collective-permute-start | bytes 1376264 | tf_op jit(solution)/shard_map/ppermute | solution.py:454
  21.1 13.8 %collective-permute-start.5 = (bf16[64,3584]{1,0:T(8,128)(2,1)S(1)}, bf16[64,3584]{1,0:T(8,128)(2,1)S(1)}, u32[]{:S(2)}, u32[]{:S(2)}) collective-permute-start(bf16[64,3584]{1,0:T(8,128)(2,1)S(1)} %collective-permute-done.refs_0_.refs_3_), channel_id=1, source_target_pairs={{0,1},{1,0},{2,3},{3,2},{4,5},{5,4},{6,7},{7,6},{8,9},{9,8},{10,11... | collective-permute-start | bytes 1376264 | tf_op jit(solution)/shard_map/ppermute | solution.py:444
  21.6 13.5 %collective-permute-start.4 = (bf16[64,3584]{1,0:T(8,128)(2,1)S(1)}, bf16[64,3584]{1,0:T(8,128)(2,1)S(1)}, u32[]{:S(2)}, u32[]{:S(2)}) collective-permute-start(bf16[64,3584]{1,0:T(8,128)(2,1)S(1)} %collective-permute-done.refs_0_.refs_3_), channel_id=1, source_target_pairs={{0,16},{8,24},{16,0},{24,8},{1,17},{9,25},{17,1},{25,9},{2,18},{10... | collective-permute-start | bytes 1376264 | tf_op jit(solution)/shard_map/ppermute | solution.py:438
  22.2 12.9 %collective-permute-start.3 = (bf16[64,3584]{1,0:T(8,128)(2,1)S(1)}, bf16[64,3584]{1,0:T(8,128)(2,1)S(1)}, u32[]{:S(2)}, u32[]{:S(2)}) collective-permute-start(bf16[64,3584]{1,0:T(8,128)(2,1)S(1)} %collective-permute-done.refs_0_.refs_3_), channel_id=1, source_target_pairs={{0,2},{1,3},{2,4},{3,5},{4,6},{5,7},{6,0},{7,1},{8,10},{9,11},{10,... | collective-permute-start | bytes 1376264 | tf_op jit(solution)/shard_map/ppermute | solution.py:454
  22.2 22.7 %collective-permute-start.9 = (bf16[64,3584]{1,0:T(8,128)(2,1)S(1)}, bf16[64,3584]{1,0:T(8,128)(2,1)S(1)}, u32[]{:S(2)}, u32[]{:S(2)}) collective-permute-start(bf16[64,3584]{1,0:T(8,128)(2,1)S(1)} %collective-permute-done.2.refs_2_), channel_id=1, source_target_pairs={{0,16},{8,24},{16,0},{24,8},{1,17},{9,25},{17,1},{25,9},{2,18},{10... | collective-permute-start | bytes 1376264 | tf_op jit(solution)/shard_map/ppermute | solution.py:438
  35.1 13.5 %collective-permute-start.10 = (bf16[64,3584]{1,0:T(8,128)(2,1)S(1)}, bf16[64,3584]{1,0:T(8,128)(2,1)S(1)}, u32[]{:S(2)}, u32[]{:S(2)}) collective-permute-start(bf16[64,3584]{1,0:T(8,128)(2,1)S(1)} %collective-permute-done.4.refs_1_.refs_4_), channel_id=1, source_target_pairs={{0,1},{1,0},{2,3},{3,2},{4,5},{5,4},{6,7},{7,6},{8,9},{9,8},{10,11... | collective-permute-start | bytes 1376264 | tf_op jit(solution)/shard_map/ppermute | solution.py:444
  36.6 18.3 %collective-permute-start.8 = (bf16[64,3584]{1,0:T(8,128)(2,1)S(1)}, bf16[64,3584]{1,0:T(8,128)(2,1)S(1)}, u32[]{:S(2)}, u32[]{:S(2)}) collective-permute-start(bf16[64,3584]{1,0:T(8,128)(2,1)S(1)} %collective-permute-done.3.refs_0_), channel_id=1, source_target_pairs={{0,1},{1,0},{2,3},{3,2},{4,5},{5,4},{6,7},{7,6},{8,9},{9,8},{10,11... | collective-permute-start | bytes 1376264 | tf_op jit(solution)/shard_map/ppermute | solution.py:444
  37.1 17.7 %collective-permute-start.7 = (bf16[64,3584]{1,0:T(8,128)(2,1)S(1)}, bf16[64,3584]{1,0:T(8,128)(2,1)S(1)}, u32[]{:S(2)}, u32[]{:S(2)}) collective-permute-start(bf16[64,3584]{1,0:T(8,128)(2,1)S(1)} %collective-permute-done.3.refs_0_), channel_id=1, source_target_pairs={{0,16},{8,24},{16,0},{24,8},{1,17},{9,25},{17,1},{25,9},{2,18},{10... | collective-permute-start | bytes 1376264 | tf_op jit(solution)/shard_map/ppermute | solution.py:438
  37.8 17.1 %collective-permute-start.6 = (bf16[64,3584]{1,0:T(8,128)(2,1)S(1)}, bf16[64,3584]{1,0:T(8,128)(2,1)S(1)}, u32[]{:S(2)}, u32[]{:S(2)}) collective-permute-start(bf16[64,3584]{1,0:T(8,128)(2,1)S(1)} %collective-permute-done.3.refs_0_), channel_id=1, source_target_pairs={{0,2},{1,3},{2,4},{3,5},{4,6},{5,7},{6,0},{7,1},{8,10},{9,11},{10,... | collective-permute-start | bytes 1376264 | tf_op jit(solution)/shard_map/ppermute | solution.py:454
  54.9 14.9 %collective-permute-start.13 = (bf16[384,2048]{1,0:T(8,128)(2,1)}, bf16[384,2048]{1,0:T(8,128)(2,1)S(1)}, u32[]{:S(2)}, u32[]{:S(2)}) collective-permute-start(bf16[384,2048]{1,0:T(8,128)(2,1)} %get-tuple-element.83.refs_4_), channel_id=1, source_target_pairs={{0,8},{8,0},{16,24},{24,16},{1,9},{9,1},{17,25},{25,17},{2,10},{10... | collective-permute-start | bytes 4718600 | tf_op jit(solution)/shard_map/ppermute | solution.py:441
  54.9 13.8 %collective-permute-start.12 = (bf16[64,3584]{1,0:T(8,128)(2,1)S(1)}, bf16[64,3584]{1,0:T(8,128)(2,1)S(1)}, u32[]{:S(2)}, u32[]{:S(2)}) collective-permute-start(bf16[64,3584]{1,0:T(8,128)(2,1)S(1)} %collective-permute-done.6.refs_3_), channel_id=1, source_target_pairs={{0,16},{8,24},{16,0},{24,8},{1,17},{9,25},{17,1},{25,9},{2,18},{10... | collective-permute-start | bytes 1376264 | tf_op jit(solution)/shard_map/ppermute | solution.py:438
  56.6 13.2 %collective-permute-start.11 = (bf16[896,384]{1,0:T(8,128)(2,1)S(1)}, bf16[896,384]{1,0:T(8,128)(2,1)S(1)}, u32[]{:S(2)}, u32[]{:S(2)}) collective-permute-start(bf16[896,384]{1,0:T(8,128)(2,1)S(1)} %get-tuple-element.73), channel_id=1, source_target_pairs={{0,8},{8,0},{16,24},{24,16},{1,9},{9,1},{17,25},{25,17},{2,10},{10... | collective-permute-start | bytes 2064392 | tf_op jit(solution)/shard_map/ppermute | solution.py:441
  56.8 21.7 %collective-permute-start.14 = (bf16[64,3584]{1,0:T(8,128)(2,1)S(1)}, bf16[64,3584]{1,0:T(8,128)(2,1)S(1)}, u32[]{:S(2)}, u32[]{:S(2)}) collective-permute-start(bf16[64,3584]{1,0:T(8,128)(2,1)S(1)} %collective-permute-done.6.refs_3_), channel_id=1, source_target_pairs={{0,1},{1,0},{2,3},{3,2},{4,5},{5,4},{6,7},{7,6},{8,9},{9,8},{10,11... | collective-permute-start | bytes 1376264 | tf_op jit(solution)/shard_map/ppermute | solution.py:444
  58.1 20.4 %collective-permute-start.15 = (bf16[64,3584]{1,0:T(8,128)(2,1)S(1)}, bf16[64,3584]{1,0:T(8,128)(2,1)S(1)}, u32[]{:S(2)}, u32[]{:S(2)}) collective-permute-start(bf16[64,3584]{1,0:T(8,128)(2,1)S(1)} %collective-permute-done.8.refs_2_), channel_id=1, source_target_pairs={{0,16},{8,24},{16,0},{24,8},{1,17},{9,25},{17,1},{25,9},{2,18},{10... | collective-permute-start | bytes 1376264 | tf_op jit(solution)/shard_map/ppermute | solution.py:438
  68.7 12.3 %collective-permute-start.16 = (bf16[64,3584]{1,0:T(8,128)(2,1)S(1)}, bf16[64,3584]{1,0:T(8,128)(2,1)S(1)}, u32[]{:S(2)}, u32[]{:S(2)}) collective-permute-start(bf16[64,3584]{1,0:T(8,128)(2,1)S(1)} %collective-permute-done.12.refs_0_.refs_6_), channel_id=1, source_target_pairs={{0,1},{1,0},{2,3},{3,2},{4,5},{5,4},{6,7},{7,6},{8,9},{9,8},{10,11... | collective-permute-start | bytes 1376264 | tf_op jit(solution)/shard_map/ppermute | solution.py:444
  81.0 6.9 %copy-start = (bf16[384,2048]{1,0:T(8,128)(2,1)S(1)}, bf16[384,2048]{1,0:T(8,128)(2,1)}, u32[]{:S(2)}) copy-start(bf16[384,2048]{1,0:T(8,128)(2,1)} %get-tuple-element.96.refs_5_) | copy-start | bytes 4718596
  87.8 6.3 %copy-start.1 = (bf16[256,2048]{1,0:T(8,128)(2,1)S(1)}, bf16[256,2048]{1,0:T(8,128)(2,1)}, u32[]{:S(2)}) copy-start(bf16[256,2048]{1,0:T(8,128)(2,1)} %get-tuple-element.99.refs_6_) | copy-start | bytes 3145732
  87.9 4.1 %collective-permute-start.18 = (bf16[384,2048]{1,0:T(8,128)(2,1)S(1)}, bf16[384,2048]{1,0:T(8,128)(2,1)S(1)}, u32[]{:S(2)}, u32[]{:S(2)}) collective-permute-start(bf16[384,2048]{1,0:T(8,128)(2,1)S(1)} %copy-done), channel_id=1, source_target_pairs={{0,8},{8,0},{16,24},{24,16},{1,9},{9,1},{17,25},{25,17},{2,10},{10... | collective-permute-start | bytes 4718600 | tf_op jit(solution)/shard_map/ppermute | solution.py:441
  89.3 9.9 %collective-permute-start.17 = (bf16[896,640]{1,0:T(8,128)(2,1)S(1)}, bf16[896,640]{1,0:T(8,128)(2,1)S(1)}, u32[]{:S(2)}, u32[]{:S(2)}) collective-permute-start(bf16[896,640]{1,0:T(8,128)(2,1)S(1)} %get-tuple-element.94), channel_id=1, source_target_pairs={{0,8},{8,0},{16,24},{24,16},{1,9},{9,1},{17,25},{25,17},{2,10},{10... | collective-permute-start | bytes 3440648 | tf_op jit(solution)/shard_map/ppermute | solution.py:441
  89.8 3.2 %collective-permute-start.21 = (f32[32,128]{1,0:T(8,128)S(1)}, f32[32,128]{1,0:T(8,128)S(1)}, u32[]{:S(2)}, u32[]{:S(2)}) collective-permute-start(f32[32,128]{1,0:T(8,128)S(1)} %get-tuple-element.97.own_ref), channel_id=1, source_target_pairs={{0,9},{1,8},{2,11},{3,10},{4,13},{5,12},{6,15},{7,14},{8,1},{9,0},... | collective-permute-start | bytes 49160 | tf_op jit(solution)/shard_map/ppermute | solution.py:451
  90.0 3.0 %collective-permute-start.20 = (f32[32,128]{1,0:T(8,128)S(1)}, f32[32,128]{1,0:T(8,128)S(1)}, u32[]{:S(2)}, u32[]{:S(2)}) collective-permute-start(f32[32,128]{1,0:T(8,128)S(1)} %get-tuple-element.97.own_ref), channel_id=1, source_target_pairs={{0,8},{8,0},{16,24},{24,16},{1,9},{9,1},{17,25},{25,17},{2,10},{10... | collective-permute-start | bytes 49160 | tf_op jit(solution)/shard_map/ppermute | solution.py:441
  90.4 3.7 %collective-permute-start.19 = (f32[32,128]{1,0:T(8,128)S(1)}, f32[32,128]{1,0:T(8,128)S(1)}, u32[]{:S(2)}, u32[]{:S(2)}) collective-permute-start(f32[32,128]{1,0:T(8,128)S(1)} %get-tuple-element.97.own_ref), channel_id=1, source_target_pairs={{0,1},{1,0},{2,3},{3,2},{4,5},{5,4},{6,7},{7,6},{8,9},{9,8},{10,11... | collective-permute-start | bytes 49160 | tf_op jit(solution)/shard_map/ppermute | solution.py:444
  94.2 8.2 %collective-permute-start.22 = (bf16[256,2048]{1,0:T(8,128)(2,1)S(1)}, bf16[256,2048]{1,0:T(8,128)(2,1)S(1)}, u32[]{:S(2)}, u32[]{:S(2)}) collective-permute-start(bf16[256,2048]{1,0:T(8,128)(2,1)S(1)} %copy-done.1), channel_id=1, source_target_pairs={{0,8},{8,0},{16,24},{24,16},{1,9},{9,1},{17,25},{25,17},{2,10},{10... | collective-permute-start | bytes 3145736 | tf_op jit(solution)/shard_map/ppermute | solution.py:441
  94.3 5.9 %collective-permute-start.25 = (f32[64,128]{1,0:T(8,128)S(1)}, f32[64,128]{1,0:T(8,128)S(1)}, u32[]{:S(2)}, u32[]{:S(2)}) collective-permute-start(f32[64,128]{1,0:T(8,128)S(1)} %get-tuple-element.98.refs_10_), channel_id=1, source_target_pairs={{0,2},{1,3},{2,4},{3,5},{4,6},{5,7},{6,0},{7,1},{8,10},{9,11},{10,... | collective-permute-start | bytes 98312 | tf_op jit(solution)/shard_map/ppermute | solution.py:454
  95.3 6.2 %collective-permute-start.24 = (f32[64,128]{1,0:T(8,128)S(1)}, f32[64,128]{1,0:T(8,128)S(1)}, u32[]{:S(2)}, u32[]{:S(2)}) collective-permute-start(f32[64,128]{1,0:T(8,128)S(1)} %get-tuple-element.98.refs_10_), channel_id=1, source_target_pairs={{0,4},{1,5},{2,6},{3,7},{4,0},{5,1},{6,2},{7,3},{8,12},{9,13},{10,... | collective-permute-start | bytes 98312 | tf_op jit(solution)/shard_map/ppermute | solution.py:454
  98.4 3.9 %collective-permute-start.23 = (f32[64,128]{1,0:T(8,128)S(1)}, f32[64,128]{1,0:T(8,128)S(1)}, u32[]{:S(2)}, u32[]{:S(2)}) collective-permute-start(f32[64,128]{1,0:T(8,128)S(1)} %get-tuple-element.98.refs_10_), channel_id=1, source_target_pairs={{0,6},{1,7},{2,0},{3,1},{4,2},{5,3},{6,4},{7,5},{8,14},{9,15},{10,... | collective-permute-start | bytes 98312 | tf_op jit(solution)/shard_map/ppermute | solution.py:454

commit v7 on v6

--- a/solution.py
+++ b/solution.py
@@ -310,16 +310,16 @@
     )(own, across, core, both)
 
 
-def refresh_kernel(lines, length, early_rows, late_rows, *refs):
+def refresh_kernel(lines, length, block_rows, *refs):
     early_refs, late_refs, refs = refs[:2], refs[2:4], refs[4:]
     exp_refs, refs = refs[:6], refs[6:]
     stats_refs, refs = refs[:lines], refs[lines:]
     (first_ref, true_at, sample_at, true_sum, sample_sum, moment_ref, curvature_ref,
-     moment_out, curvature_out, update_out, scaled, factors) = refs
+     moment_out, curvature_out, update_out, factors) = refs
     step = pl.program_id(0)
     width = moment_out.shape[1]
-    early = len(early_rows) * length
-    late = len(late_rows) * length
+    early = early_refs[0].shape[1]
+    late = late_refs[0].shape[1]
 
     @pl.when(step == 0)
     def _():
@@ -337,66 +337,68 @@
         total = sum(t * jnp.exp(p - peak) for p, t in zip(peaks, totals))
         factor = jnp.exp(first_ref[...] - peak) / total
         per_core = rows // 2
-        for core in range(2):
-            for index in range(0, len(early_rows), 2):
-                pair = jnp.concatenate([
-                    factor[core * per_core + row:core * per_core + row + 1, :length]
-                    for row in early_rows[index:index + 2]
-                ], axis=1)
-                place = index * length
-                values = early_refs[core][:, place:place + 2 * length].astype(jnp.float32)
-                place += core * early
-                scaled[:, place:place + 2 * length] = (values * pair).astype(jnp.bfloat16)
         full = jnp.concatenate([factor, jnp.zeros((128 - rows, 128), jnp.float32)], axis=0).T
         for core in range(2):
-            for index, row in enumerate(late_rows):
-                place = core * late + index * length
+            for index, row in enumerate(block_rows):
+                place = (core * len(block_rows) + index) * length
                 at = core * per_core + row
                 factors[place:place + length] = jnp.broadcast_to(
                     full[:length, at:at + 1], (length, 128)
                 )
 
-    shared = jnp.dot(
-        scaled[...],
-        jnp.concatenate([exp_refs[0][...], exp_refs[3][...]], axis=0),
-        preferred_element_type=jnp.float32,
-    )
-    gradient = shared - true_sum[...].astype(jnp.float32)
-    sample_grad = shared - sample_sum[...].astype(jnp.float32)
+    def probs(ref, place, lane):
+        scale = factors[place:place + ref.shape[0]]
+        return ref[:, lane:lane + 128].astype(jnp.float32) * scale
+
+    early_sides, true_sides, sample_sides = [], [], []
     for core in range(2):
-        place = slice(core * late, (core + 1) * late)
-        exps = jnp.concatenate([ref[...] for ref in exp_refs[3 * core + 1:3 * core + 3]], axis=0)
-        true_parts, sample_parts = [], []
-        for lane in range(0, width, 128):
-            probs = exps[:, lane:lane + 128].astype(jnp.float32) * factors[place]
-            at = step * width + lane
-            true_parts.append(
-                (probs - jnp.where(true_at[place] == at, 1.0, 0.0)).astype(jnp.bfloat16)
-            )
-            sample_parts.append(
-                (probs - jnp.where(sample_at[place] == at, 1.0, 0.0)).astype(jnp.bfloat16)
-            )
-        features = late_refs[core][...]
-        gradient += jnp.dot(
-            features, jnp.concatenate(true_parts, axis=1), preferred_element_type=jnp.float32
+        first_exp, *late_exps = exp_refs[3 * core:3 * core + 3]
+        place = core * (early + late)
+        early_sides.append(jnp.concatenate([
+            probs(first_exp, place, lane).astype(jnp.bfloat16) for lane in range(0, width, 128)
+        ], axis=1))
+        place += early
+        at = core * late
+        for ref in late_exps:
+            rows = slice(at, at + ref.shape[0])
+            true_parts, sample_parts = [], []
+            for lane in range(0, width, 128):
+                prob = probs(ref, place, lane)
+                column = step * width + lane
+                true_hot = jnp.where(true_at[rows] == column, 1.0, 0.0)
+                sample_hot = jnp.where(sample_at[rows] == column, 1.0, 0.0)
+                true_parts.append((prob - true_hot).astype(jnp.bfloat16))
+                sample_parts.append((prob - sample_hot).astype(jnp.bfloat16))
+            true_sides.append(jnp.concatenate(true_parts, axis=1))
+            sample_sides.append(jnp.concatenate(sample_parts, axis=1))
+            place += ref.shape[0]
+            at += ref.shape[0]
+    early_features = jnp.concatenate([ref[...] for ref in early_refs], axis=1)
+    late_features = jnp.concatenate([ref[...] for ref in late_refs], axis=1)
+
+    def product(features, sides):
+        return jnp.dot(
+            features, jnp.concatenate(sides, axis=0), preferred_element_type=jnp.float32
         )
-        sample_grad += jnp.dot(
-            features, jnp.concatenate(sample_parts, axis=1), preferred_element_type=jnp.float32
-        )
+
+    shared = product(early_features, early_sides)
+    gradient = product(late_features, true_sides) + (shared - true_sum[...].astype(jnp.float32))
+    sample_grad = product(late_features, sample_sides) + (
+        shared - sample_sum[...].astype(jnp.float32)
+    )
     moment_out[...], curvature_out[...], update_out[...] = refresh(
         gradient, sample_grad, moment_ref[...], curvature_ref[...]
     )
 
 
-def refresh_states(lines, length, early_rows, late_rows, early, late, exps, stats, first,
+def refresh_states(lines, length, block_rows, early, late, exps, stats, first,
                    late_ids, sums, moment, curvature):
     rows, columns = moment.shape
     width = min(256, columns)
-    late_tokens = 2 * late[0].shape[1]
     whole = lambda array: pl.BlockSpec(array.shape, lambda step: (0, 0))
     tile = pl.BlockSpec((rows, width), lambda step: (0, step))
     return pl.pallas_call(
-        functools.partial(refresh_kernel, lines, length, early_rows, late_rows),
+        functools.partial(refresh_kernel, lines, length, block_rows),
         grid=(columns // width,),
         in_specs=[whole(array) for array in (*early, *late)]
         + [pl.BlockSpec((array.shape[0], width), lambda step: (0, step)) for array in exps]
@@ -404,10 +406,7 @@
         + [tile] * 4,
         out_specs=[tile] * 3,
         out_shape=[jax.ShapeDtypeStruct((rows, columns), jnp.bfloat16)] * 3,
-        scratch_shapes=[
-            pltpu.VMEM((rows, 2 * early[0].shape[1]), jnp.bfloat16),
-            pltpu.VMEM((late_tokens, 128), jnp.float32),
-        ],
+        scratch_shapes=[pltpu.VMEM((2 * length * len(block_rows), 128), jnp.float32)],
         compiler_params=pltpu.CompilerParams(vmem_limit_bytes=36 * 1024 * 1024),
         cost_estimate=BRIEF,
         name="refresh_states",
@@ -456,10 +455,11 @@
     split = lines // 2
     plain = [(0, 0), (0, 1), (1, 0)]
     groups = [[(*kind, turn) for kind in plain] for turn in range(split)]
-    groups += [[(*kind, turn) for turn in range(split, lines - 1) for kind in plain]]
-    groups[-1] += [(0, 0, lines - 1)] + [(1, 1, turn) for turn in range(split)]
-    groups += [[(0, 1, lines - 1), (1, 0, lines - 1)]]
-    groups[-1] += [(1, 1, turn) for turn in range(split, lines)]
+    groups += [
+        [(0, 0, split), (0, 1, split), (0, 0, split + 1), (1, 1, 0)],
+        [(1, 0, split), (1, 1, 1)],
+        [(0, 1, split + 1), (1, 0, split + 1), (1, 1, split), (1, 1, split + 1)],
+    ]
     early_blocks, late_blocks = sum(groups[:split], []), sum(groups[split:], [])
 
     def stat_row(block):
@@ -503,20 +503,26 @@
         if turn + 1 < lines:
             arrived = [to_z(block, 1), held[0, 1, turn], held[1, 0, turn]]
             if turn == 0:
-                arrived += [*early_ids, *late_ids, rep_scalar, stats]
+                head_weight, *late_ids = prepared(head_weight, *late_ids, *early_ids, stats)
+                arrived += [*early_ids, *late_ids, rep_scalar, stats, head_weight]
             elif turn < split:
                 arrived += [early_exp]
             else:
+                held[0, 0, turn + 1], held[0, 1, turn] = arrived[0], arrived[1]
+                middle_exp, stats = logits(
+                    groups[split], stats, exp_rows=6 * length
+                )
                 arrived += [early_exp] + [held[1, 1, past] for past in range(split)]
+                arrived += [middle_exp]
             arrived = lax.optimization_barrier(tuple(arrived))
             held[0, 0, turn + 1], held[0, 1, turn], held[1, 0, turn] = arrived[:3]
             if turn == 0:
                 early_ids, late_ids = list(arrived[3:5]), list(arrived[5:7])
-                rep_scalar, stats = arrived[7:]
-                head_weight, *late_ids = prepared(head_weight, *late_ids, stats)
+                rep_scalar, stats, head_weight = arrived[7:]
             else:
                 early_exp = arrived[3]
-                held.update({(1, 1, past): got for past, got in enumerate(arrived[4:])})
+                if turn == split:
+                    held[1, 1, 0], held[1, 1, 1], middle_exp = arrived[4:]
             held[1, 1, turn] = diagonal(turn)
         if turn < split:
             size = len(groups[turn]) * length
@@ -530,7 +536,10 @@
     early = turned_features(rep_scalar, early, rows)
     early = [early[0], to_core(early[1])]
     other_exps = [to_core(early_exp)]
-    middle_exp, stats = logits(groups[split], stats, held[0, 0, lines - 1])
+    middle_exp, stats = logits(
+        groups[split + 1], stats, held[0, 0, lines - 1],
+        first_row=4 * length, exp_rows=6 * length, into=middle_exp,
+    )
     held[0, 1, lines - 1] = after(held[0, 1, lines - 1], middle_exp)
     held[1, 1, lines - 1] = diagonal(lines - 1)
     early_ids[0] = after(early_ids[0], middle_exp, held[0, 1, lines - 1], *other_exps)
@@ -550,8 +559,7 @@
     other_exps.append(to_core(after(last_exp, merged)))
     late = [late[0], to_core(late[1])]
     return tuple(refresh_states(
-        lines, length, [stat_row(block) for block in early_blocks],
-        [stat_row(block) for block in late_blocks], early, late,
+        lines, length, [stat_row(block) for block in early_blocks + late_blocks], early, late,
         exps + other_exps, all_stats, first, late_ids, sums, moment, curvature,
     ))
 

time: 125 us -> 127 us (1.016)
  starting transfers between devices: 25.1 us -> 28.2 us
    ppermute x6, waiting for transfers between devices: 1.84 us -> 13.9 us  [to_x(): return lax.ppermute(values, 'rep', swap_pairs(reps, 2))]
    ppermute x7, waiting for transfers between devices: 14.3 us -> 5.67 us  [to_y(): return lax.ppermute(values, 'shard', swap_pairs(shards, 1))]
    ppermute x6, waiting for transfers between devices: 6.21 us -> 1.6 us  [to_z(): return lax.ppermute(values, 'shard', shift_pairs(lines, along, 0))]
    pallas_call x4 -> x5, Pallas kernels: 27.4 us -> 30 us  [round_logits(): pl.pallas_call(functools.partial(logits_kernel, stat_rows, first_row, len...]
    ppermute x6, starting transfers between devices: 7.65 us -> 9.6 us  [to_z(): return lax.ppermute(values, 'shard', shift_pairs(lines, along, 0))]
    pallas_call x1, Pallas kernels: 21.9 us -> 20 us  [refresh_states(): pl.pallas_call(functools.partial(refresh_kernel, lines, length, block_row...]
  transfers between devices with their start and end apart: 26 -> 26, of which waited for: 13 -> 10; matrix products, arithmetic and copies ran while one was open for 5% -> 5% of each run, Pallas kernels for 30% -> 31%
where the time goes in v7:
time: 127 us
  Pallas kernels  66.4 us (52%)
  starting transfers between devices  28.2 us (22%)
  waiting for transfers between devices  22.2 us (17%)
  other arithmetic  6.04 us (5%)
  local copies, waits for them, and re-layouts  3.16 us (2%)
    pallas_call x5, Pallas kernels, round_logits(): pl.pallas_call(functools.partial(logits_kernel, stat_rows, first_row, len...  30 us
    pallas_call x1, Pallas kernels, refresh_states(): pl.pallas_call(functools.partial(refresh_kernel, lines, length, block_row...  20 us
    ppermute x6, waiting for transfers between devices, to_x(): return lax.ppermute(values, 'rep', swap_pairs(reps, 2))  13.9 us
    ppermute x6, starting transfers between devices, to_z(): return lax.ppermute(values, 'shard', shift_pairs(lines, along, 0))  9.6 us
    ppermute x7, starting transfers between devices, to_y(): return lax.ppermute(values, 'shard', swap_pairs(shards, 1))  9.18 us
    pallas_call x1, Pallas kernels, one_hot_sums(): pl.pallas_call(functools.partial(one_hot_kernel, len(features)), grid=(co...  8.65 us
    ppermute x6, starting transfers between devices, to_x(): return lax.ppermute(values, 'rep', swap_pairs(reps, 2))  6.83 us
    ppermute x7, waiting for transfers between devices, to_y(): return lax.ppermute(values, 'shard', swap_pairs(shards, 1))  5.67 us
  transfers between devices with their start and end apart: 26, of which 10 were waited for; matrix products, arithmetic and copies ran while one was open for 5% of the time, Pallas kernels for 31%

profile of v7, /device:TPU:0, one launch (start us, length us, event | category | flops | bytes accessed | tf_op | source)
XLA Modules:
  0.0 126.8 jit_solution(11547153478165166351)
XLA Ops:
  0.6 1.2 fusion
  1.9 1.2 fusion.2.refs_0_
  3.1 3.0 %collective-permute-start.2 = (bf16[64,3584]{1,0:T(8,128)(2,1)S(1)}, bf16[64,3584]{1,0:T(8,128)(2,1)S(1)}, u32[]{:S(2)}, u32[]{:S(2)}) collective-permute-start(bf16[64,3584]{1,0:T(8,128)(2,1)S(1)} %fusion.2.refs_0_), channel_id=1, source_target_pairs={{0,1},{1,0},{2,3},{3,2},{4,5},{5,4},{6,7},{7,6},{8,9},{9,8},{10,11... | collective-permute-start | bytes 1376264 | tf_op jit(solution)/shard_map/ppermute | solution.py:443
  6.1 1.5 %collective-permute-start.1 = (bf16[64,3584]{1,0:T(8,128)(2,1)S(1)}, bf16[64,3584]{1,0:T(8,128)(2,1)S(1)}, u32[]{:S(2)}, u32[]{:S(2)}) collective-permute-start(bf16[64,3584]{1,0:T(8,128)(2,1)S(1)} %fusion.2.refs_0_), channel_id=1, source_target_pairs={{0,16},{8,24},{16,0},{24,8},{1,17},{9,25},{17,1},{25,9},{2,18},{10... | collective-permute-start | bytes 1376264 | tf_op jit(solution)/shard_map/ppermute | solution.py:437
  7.6 1.6 %collective-permute-start = (bf16[64,3584]{1,0:T(8,128)(2,1)S(1)}, bf16[64,3584]{1,0:T(8,128)(2,1)S(1)}, u32[]{:S(2)}, u32[]{:S(2)}) collective-permute-start(bf16[64,3584]{1,0:T(8,128)(2,1)S(1)} %fusion.2.refs_0_), channel_id=1, source_target_pairs={{0,2},{1,3},{2,4},{3,5},{4,6},{5,7},{6,0},{7,1},{8,10},{9,11},{10,... | collective-permute-start | bytes 1376264 | tf_op jit(solution)/shard_map/ppermute | solution.py:453
  9.2 0.7 fusion.7
  9.8 0.7 compare_and_fusion
  10.5 0.7 multiply_add_fusion
  11.2 1.2 slice.31
  12.4 0.8 slice.30
  13.3 0.7 broadcast_subtract_fusion
  14.1 0.7 fusion.4
  14.9 0.6 gather_fusion
  16.0 5.5 %prepared.1 = (bf16[3584,2048]{1,0:T(8,128)(2,1)S(1)}, s32[1280,128]{1,0:T(8,128)S(1)}, s32[1280,128]{1,0:T(8,128)S(1)}) custom-call(bf16[3584,2048]{1,0:T(8,128)(2,1)} %weight_ref.1, s32[1,1280]{1,0:T(1,128)S(1)} %squeeze.14.true_ids, s32[1,1280]{1,0:T(1,128)S(1)} %squeeze.15.sample_ids, s32[1,768]{1,0:T(1,128)S(1)} %squeeze.12.refs_0_.refs_2_, ...), custom_call_target="tpu_custom_call" | custom-call | flops 1024 | bytes 1024 | tf_op jit(solution)/shard_map/prepared/pallas_call | solution.py:113
  21.5 0.6 collective-permute-start.5
  22.1 0.5 collective-permute-start.4
  22.6 1.6 %collective-permute-start.3 = (bf16[64,3584]{1,0:T(8,128)(2,1)S(1)}, bf16[64,3584]{1,0:T(8,128)(2,1)S(1)}, u32[]{:S(2)}, u32[]{:S(2)}) collective-permute-start(bf16[64,3584]{1,0:T(8,128)(2,1)S(1)} %collective-permute-done.refs_0_.refs_3_), channel_id=1, source_target_pairs={{0,2},{1,3},{2,4},{3,5},{4,6},{5,7},{6,0},{7,1},{8,10},{9,11},{10,... | collective-permute-start | bytes 1376264 | tf_op jit(solution)/shard_map/ppermute | solution.py:453
  24.2 1.5 %collective-permute-start.9 = (bf16[64,3584]{1,0:T(8,128)(2,1)S(1)}, bf16[64,3584]{1,0:T(8,128)(2,1)S(1)}, u32[]{:S(2)}, u32[]{:S(2)}) collective-permute-start(bf16[64,3584]{1,0:T(8,128)(2,1)S(1)} %collective-permute-done.2.refs_2_), channel_id=1, source_target_pairs={{0,16},{8,24},{16,0},{24,8},{1,17},{9,25},{17,1},{25,9},{2,18},{10... | collective-permute-start | bytes 1376264 | tf_op jit(solution)/shard_map/ppermute | solution.py:437
  25.7 5.8 %round_logits.5 = (bf16[384,2048]{1,0:T(8,128)(2,1)}, f32[32,128]{1,0:T(8,128)S(1)}) custom-call(bf16[64,3584]{1,0:T(8,128)(2,1)S(1)} %fusion.2.refs_0_, bf16[64,3584]{1,0:T(8,128)(2,1)S(1)} %collective-permute-done.1.refs_1_, bf16[64,3584]{1,0:T(8,128)(2,1)S(1)} %collective-permute-done.2.refs_2_, ...), custom_call_target="tpu_custom_call" | custom-call | flops 1024 | bytes 1024 | tf_op jit(solution)/shard_map/round_logits/pallas_call | solution.py:192
  31.5 1.5 %collective-permute-done.5.refs_2_.refs_5_ = bf16[64,3584]{1,0:T(8,128)(2,1)S(1)} collective-permute-done((bf16[64,3584]{1,0:T(8,128)(2,1)S(1)}, bf16[64,3584]{1,0:T(8,128)(2,1)S(1)}, u32[]{:S(2)}, u32[]{:S(2)}) %collective-permute-start.5) | collective-permute-done | bytes 458784 | tf_op jit(solution)/shard_map/ppermute | solution.py:443
  33.0 2.5 %collective-permute-done.4.refs_1_.refs_4_ = bf16[64,3584]{1,0:T(8,128)(2,1)S(1)} collective-permute-done((bf16[64,3584]{1,0:T(8,128)(2,1)S(1)}, bf16[64,3584]{1,0:T(8,128)(2,1)S(1)}, u32[]{:S(2)}, u32[]{:S(2)}) %collective-permute-start.4) | collective-permute-done | bytes 458784 | tf_op jit(solution)/shard_map/ppermute | solution.py:437
  35.5 1.2 collective-permute-start.7
  36.8 0.9 collective-permute-start.6
  37.7 1.5 %collective-permute-start.10 = (bf16[64,3584]{1,0:T(8,128)(2,1)S(1)}, bf16[64,3584]{1,0:T(8,128)(2,1)S(1)}, u32[]{:S(2)}, u32[]{:S(2)}) collective-permute-start(bf16[64,3584]{1,0:T(8,128)(2,1)S(1)} %collective-permute-done.4.refs_1_.refs_4_), channel_id=1, source_target_pairs={{0,1},{1,0},{2,3},{3,2},{4,5},{5,4},{6,7},{7,6},{8,9},{9,8},{10,11... | collective-permute-start | bytes 1376264 | tf_op jit(solution)/shard_map/ppermute | solution.py:443
  39.2 0.5 collective-permute-start.8
  39.7 5.8 %round_logits.6 = (bf16[384,2048]{1,0:T(8,128)(2,1)}, f32[32,128]{1,0:T(8,128)S(1)}) custom-call(bf16[64,3584]{1,0:T(8,128)(2,1)S(1)} %collective-permute-done.refs_0_.refs_3_, bf16[64,3584]{1,0:T(8,128)(2,1)S(1)} %collective-permute-done.4.refs_1_.refs_4_, ...), custom_call_target="tpu_custom_call", output_to_operand_aliasing={{0}: (5, {})} | custom-call | flops 1024 | bytes 1024 | tf_op jit(solution)/shard_map/round_logits/pallas_call | solution.py:192
  45.5 7.4 %collective-permute-done.7.refs_1_ = bf16[64,3584]{1,0:T(8,128)(2,1)S(1)} collective-permute-done((bf16[64,3584]{1,0:T(8,128)(2,1)S(1)}, bf16[64,3584]{1,0:T(8,128)(2,1)S(1)}, u32[]{:S(2)}, u32[]{:S(2)}) %collective-permute-start.7) | collective-permute-done | bytes 458784 | tf_op jit(solution)/shard_map/ppermute | solution.py:437
  52.9 6.8 %round_logits.7 = (bf16[384,2048]{1,0:T(8,128)(2,1)}, f32[32,128]{1,0:T(8,128)S(1)}) custom-call(bf16[64,3584]{1,0:T(8,128)(2,1)S(1)} %collective-permute-done.3.refs_0_, bf16[64,3584]{1,0:T(8,128)(2,1)S(1)} %collective-permute-done.7.refs_1_, bf16[64,3584]{1,0:T(8,128)(2,1)S(1)} %collective-permute-done.6.refs_2_, ...), custom_call_target="tpu_custom_call" | custom-call | flops 1024 | bytes 1024 | tf_op jit(solution)/shard_map/round_logits/pallas_call | solution.py:192
  59.8 0.6 collective-permute-start.12
  60.4 0.9 turned_features.2
  61.5 1.5 %collective-permute-start.15 = (bf16[64,3584]{1,0:T(8,128)(2,1)S(1)}, bf16[64,3584]{1,0:T(8,128)(2,1)S(1)}, u32[]{:S(2)}, u32[]{:S(2)}) collective-permute-start(bf16[64,3584]{1,0:T(8,128)(2,1)S(1)} %collective-permute-done.8.refs_0_.refs_4_), channel_id=1, source_target_pairs={{0,16},{8,24},{16,0},{24,8},{1,17},{9,25},{17,1},{25,9},{2,18},{10... | collective-permute-start | bytes 1376264 | tf_op jit(solution)/shard_map/ppermute | solution.py:437
  63.0 1.5 %collective-permute-start.14 = (bf16[64,3584]{1,0:T(8,128)(2,1)S(1)}, bf16[64,3584]{1,0:T(8,128)(2,1)S(1)}, u32[]{:S(2)}, u32[]{:S(2)}) collective-permute-start(bf16[64,3584]{1,0:T(8,128)(2,1)S(1)} %collective-permute-done.6.refs_2_), channel_id=1, source_target_pairs={{0,1},{1,0},{2,3},{3,2},{4,5},{5,4},{6,7},{7,6},{8,9},{9,8},{10,11... | collective-permute-start | bytes 1376264 | tf_op jit(solution)/shard_map/ppermute | solution.py:443
  64.6 4.7 %round_logits.8 = (bf16[384,2048]{1,0:T(8,128)(2,1)}, f32[32,128]{1,0:T(8,128)S(1)}) custom-call(bf16[64,3584]{1,0:T(8,128)(2,1)S(1)} %collective-permute-done.8.refs_0_.refs_4_, bf16[64,3584]{1,0:T(8,128)(2,1)S(1)} %collective-permute-done.10.refs_1_.refs_5_, ...), custom_call_target="tpu_custom_call", output_to_operand_aliasing={{0}: (4, {})} | custom-call | flops 1024 | bytes 1024 | tf_op jit(solution)/shard_map/round_logits/pallas_call | solution.py:192
  69.3 3.9 %collective-permute-done.12.refs_0_.refs_6_ = bf16[64,3584]{1,0:T(8,128)(2,1)S(1)} collective-permute-done((bf16[64,3584]{1,0:T(8,128)(2,1)S(1)}, bf16[64,3584]{1,0:T(8,128)(2,1)S(1)}, u32[]{:S(2)}, u32[]{:S(2)}) %collective-permute-start.12) | collective-permute-done | bytes 458784 | tf_op jit(solution)/shard_map/ppermute | solution.py:437
  73.2 1.5 %collective-permute-start.16 = (bf16[64,3584]{1,0:T(8,128)(2,1)S(1)}, bf16[64,3584]{1,0:T(8,128)(2,1)S(1)}, u32[]{:S(2)}, u32[]{:S(2)}) collective-permute-start(bf16[64,3584]{1,0:T(8,128)(2,1)S(1)} %collective-permute-done.12.refs_0_.refs_6_), channel_id=1, source_target_pairs={{0,1},{1,0},{2,3},{3,2},{4,5},{5,4},{6,7},{7,6},{8,9},{9,8},{10,11... | collective-permute-start | bytes 1376264 | tf_op jit(solution)/shard_map/ppermute | solution.py:443
  74.8 8.7 %one_hot_sums.1 = (bf16[896,2048]{1,0:T(8,128)(2,1)}, bf16[896,2048]{1,0:T(8,128)(2,1)}) custom-call(bf16[896,384]{1,0:T(8,128)(2,1)S(1)} %get-tuple-element.79.refs_0_, bf16[896,384]{1,0:T(8,128)(2,1)S(1)} %collective-permute-done.11.refs_1_, s32[1,768]{1,0:T(1,128)S(1)} %squeeze.12.refs_0_.refs_2_, s32[1,768]{1,0:T(1,128)S(1)} %squeeze.13.refs_1_.refs_3_), custom_call_target="tpu_custom_call" | custom-call | flops 1024 | bytes 1024 | tf_op jit(solution)/shard_map/one_hot_sums/pallas_call | solution.py:271
  83.4 1.9 %collective-permute-done.16.refs_3_.refs_9_ = bf16[64,3584]{1,0:T(8,128)(2,1)S(1)} collective-permute-done((bf16[64,3584]{1,0:T(8,128)(2,1)S(1)}, bf16[64,3584]{1,0:T(8,128)(2,1)S(1)}, u32[]{:S(2)}, u32[]{:S(2)}) %collective-permute-start.16) | collective-permute-done | bytes 458784 | tf_op jit(solution)/shard_map/ppermute | solution.py:443
  85.4 6.8 %round_logits.9 = (bf16[256,2048]{1,0:T(8,128)(2,1)}, f32[32,128]{1,0:T(8,128)S(1)}) custom-call(bf16[64,3584]{1,0:T(8,128)(2,1)S(1)} %collective-permute-done.12.refs_0_.refs_6_, bf16[64,3584]{1,0:T(8,128)(2,1)S(1)} %collective-permute-done.14.refs_1_.refs_7_, bf16[64,3584]{1,0:T(8,128)(2,1)S(1)} %collective-permute-done.15.refs_2_.refs_8_, ...), custom_call_target="tpu_custom_call" | custom-call | flops 1024 | bytes 1024 | tf_op jit(solution)/shard_map/round_logits/pallas_call | solution.py:192
  92.3 1.4 %turned_features.3 = (bf16[896,640]{1,0:T(8,128)(2,1)S(1)}, bf16[896,640]{1,0:T(8,128)(2,1)S(1)}) custom-call(s32[1]{0:T(128)} %bitcast.5.rep_ref, bf16[64,3584]{1,0:T(8,128)(2,1)S(1)} %collective-permute-done.3.refs_0_, bf16[64,3584]{1,0:T(8,128)(2,1)S(1)} %collective-permute-done.7.refs_1_, bf16[64,3584]{1,0:T(8,128)(2,1)S(1)} %collective-permute-done.6.refs_2_, ...), custom_call_target="tpu_custom_call" | custom-call | flops 1024 | bytes 1024 | tf_op jit(solution)/shard_map/turned_features/pallas_call | solution.py:234
  93.7 0.5 collective-permute-start.17
  94.2 1.2 collective-permute-start.21
  96.3 1.0 collective-permute-done.21.both_ref
  97.4 2.2 %collective-permute-done.19.across_ref = f32[32,128]{1,0:T(8,128)S(1)} collective-permute-done((f32[32,128]{1,0:T(8,128)S(1)}, f32[32,128]{1,0:T(8,128)S(1)}, u32[]{:S(2)}, u32[]{:S(2)}) %collective-permute-start.19) | collective-permute-done | bytes 16416 | tf_op jit(solution)/shard_map/ppermute | solution.py:443
  99.7 1.6 %collective-permute-start.25 = (f32[64,128]{1,0:T(8,128)S(1)}, f32[64,128]{1,0:T(8,128)S(1)}, u32[]{:S(2)}, u32[]{:S(2)}) collective-permute-start(f32[64,128]{1,0:T(8,128)S(1)} %get-tuple-element.106.refs_10_), channel_id=1, source_target_pairs={{0,2},{1,3},{2,4},{3,5},{4,6},{5,7},{6,0},{7,1},{8,10},{9,11},{10,... | collective-permute-start | bytes 98312 | tf_op jit(solution)/shard_map/ppermute | solution.py:453
  101.3 1.3 %collective-permute-start.24 = (f32[64,128]{1,0:T(8,128)S(1)}, f32[64,128]{1,0:T(8,128)S(1)}, u32[]{:S(2)}, u32[]{:S(2)}) collective-permute-start(f32[64,128]{1,0:T(8,128)S(1)} %get-tuple-element.106.refs_10_), channel_id=1, source_target_pairs={{0,4},{1,5},{2,6},{3,7},{4,0},{5,1},{6,2},{7,3},{8,12},{9,13},{10,... | collective-permute-start | bytes 98312 | tf_op jit(solution)/shard_map/ppermute | solution.py:453
  102.6 2.6 %collective-permute-start.23 = (f32[64,128]{1,0:T(8,128)S(1)}, f32[64,128]{1,0:T(8,128)S(1)}, u32[]{:S(2)}, u32[]{:S(2)}) collective-permute-start(f32[64,128]{1,0:T(8,128)S(1)} %get-tuple-element.106.refs_10_), channel_id=1, source_target_pairs={{0,6},{1,7},{2,0},{3,1},{4,2},{5,3},{6,4},{7,5},{8,14},{9,15},{10,... | collective-permute-start | bytes 98312 | tf_op jit(solution)/shard_map/ppermute | solution.py:453
  105.6 1.0 collective-permute-done.24.refs_12_
  106.8 20.0 %refresh_states.1 = (bf16[896,2048]{1,0:T(8,128)(2,1)}, bf16[896,2048]{1,0:T(8,128)(2,1)}, bf16[896,2048]{1,0:T(8,128)(2,1)}) custom-call(bf16[896,384]{1,0:T(8,128)(2,1)S(1)} %get-tuple-element.79.refs_0_, bf16[896,384]{1,0:T(8,128)(2,1)S(1)} %collective-permute-done.11.refs_1_, bf16[896,640]{1,0:T(8,128)(2,1)S(1)} %get-tuple-element.101.refs_2_, ...), custom_call_target="tpu_custom_call" | custom-call | flops 1024 | bytes 1024 | tf_op jit(solution)/shard_map/refresh_states/pallas_call | solution.py:400
  (47 shorter events, 2.7 us)
Async XLA Ops:
  3.1 18.4 %collective-permute-start.2 = (bf16[64,3584]{1,0:T(8,128)(2,1)S(1)}, bf16[64,3584]{1,0:T(8,128)(2,1)S(1)}, u32[]{:S(2)}, u32[]{:S(2)}) collective-permute-start(bf16[64,3584]{1,0:T(8,128)(2,1)S(1)} %fusion.2.refs_0_), channel_id=1, source_target_pairs={{0,1},{1,0},{2,3},{3,2},{4,5},{5,4},{6,7},{7,6},{8,9},{9,8},{10,11... | collective-permute-start | bytes 1376264 | tf_op jit(solution)/shard_map/ppermute | solution.py:443
  6.1 15.4 %collective-permute-start.1 = (bf16[64,3584]{1,0:T(8,128)(2,1)S(1)}, bf16[64,3584]{1,0:T(8,128)(2,1)S(1)}, u32[]{:S(2)}, u32[]{:S(2)}) collective-permute-start(bf16[64,3584]{1,0:T(8,128)(2,1)S(1)} %fusion.2.refs_0_), channel_id=1, source_target_pairs={{0,16},{8,24},{16,0},{24,8},{1,17},{9,25},{17,1},{25,9},{2,18},{10... | collective-permute-start | bytes 1376264 | tf_op jit(solution)/shard_map/ppermute | solution.py:437
  7.6 13.9 %collective-permute-start = (bf16[64,3584]{1,0:T(8,128)(2,1)S(1)}, bf16[64,3584]{1,0:T(8,128)(2,1)S(1)}, u32[]{:S(2)}, u32[]{:S(2)}) collective-permute-start(bf16[64,3584]{1,0:T(8,128)(2,1)S(1)} %fusion.2.refs_0_), channel_id=1, source_target_pairs={{0,2},{1,3},{2,4},{3,5},{4,6},{5,7},{6,0},{7,1},{8,10},{9,11},{10,... | collective-permute-start | bytes 1376264 | tf_op jit(solution)/shard_map/ppermute | solution.py:453
  21.5 11.5 %collective-permute-start.5 = (bf16[64,3584]{1,0:T(8,128)(2,1)S(1)}, bf16[64,3584]{1,0:T(8,128)(2,1)S(1)}, u32[]{:S(2)}, u32[]{:S(2)}) collective-permute-start(bf16[64,3584]{1,0:T(8,128)(2,1)S(1)} %collective-permute-done.refs_0_.refs_3_), channel_id=1, source_target_pairs={{0,1},{1,0},{2,3},{3,2},{4,5},{5,4},{6,7},{7,6},{8,9},{9,8},{10,11... | collective-permute-start | bytes 1376264 | tf_op jit(solution)/shard_map/ppermute | solution.py:443
  22.1 13.5 %collective-permute-start.4 = (bf16[64,3584]{1,0:T(8,128)(2,1)S(1)}, bf16[64,3584]{1,0:T(8,128)(2,1)S(1)}, u32[]{:S(2)}, u32[]{:S(2)}) collective-permute-start(bf16[64,3584]{1,0:T(8,128)(2,1)S(1)} %collective-permute-done.refs_0_.refs_3_), channel_id=1, source_target_pairs={{0,16},{8,24},{16,0},{24,8},{1,17},{9,25},{17,1},{25,9},{2,18},{10... | collective-permute-start | bytes 1376264 | tf_op jit(solution)/shard_map/ppermute | solution.py:437
  22.6 12.9 %collective-permute-start.3 = (bf16[64,3584]{1,0:T(8,128)(2,1)S(1)}, bf16[64,3584]{1,0:T(8,128)(2,1)S(1)}, u32[]{:S(2)}, u32[]{:S(2)}) collective-permute-start(bf16[64,3584]{1,0:T(8,128)(2,1)S(1)} %collective-permute-done.refs_0_.refs_3_), channel_id=1, source_target_pairs={{0,2},{1,3},{2,4},{3,5},{4,6},{5,7},{6,0},{7,1},{8,10},{9,11},{10,... | collective-permute-start | bytes 1376264 | tf_op jit(solution)/shard_map/ppermute | solution.py:453
  24.2 21.3 %collective-permute-start.9 = (bf16[64,3584]{1,0:T(8,128)(2,1)S(1)}, bf16[64,3584]{1,0:T(8,128)(2,1)S(1)}, u32[]{:S(2)}, u32[]{:S(2)}) collective-permute-start(bf16[64,3584]{1,0:T(8,128)(2,1)S(1)} %collective-permute-done.2.refs_2_), channel_id=1, source_target_pairs={{0,16},{8,24},{16,0},{24,8},{1,17},{9,25},{17,1},{25,9},{2,18},{10... | collective-permute-start | bytes 1376264 | tf_op jit(solution)/shard_map/ppermute | solution.py:437
  35.5 17.3 %collective-permute-start.7 = (bf16[64,3584]{1,0:T(8,128)(2,1)S(1)}, bf16[64,3584]{1,0:T(8,128)(2,1)S(1)}, u32[]{:S(2)}, u32[]{:S(2)}) collective-permute-start(bf16[64,3584]{1,0:T(8,128)(2,1)S(1)} %collective-permute-done.3.refs_0_), channel_id=1, source_target_pairs={{0,16},{8,24},{16,0},{24,8},{1,17},{9,25},{17,1},{25,9},{2,18},{10... | collective-permute-start | bytes 1376264 | tf_op jit(solution)/shard_map/ppermute | solution.py:437
  36.8 16.1 %collective-permute-start.6 = (bf16[64,3584]{1,0:T(8,128)(2,1)S(1)}, bf16[64,3584]{1,0:T(8,128)(2,1)S(1)}, u32[]{:S(2)}, u32[]{:S(2)}) collective-permute-start(bf16[64,3584]{1,0:T(8,128)(2,1)S(1)} %collective-permute-done.3.refs_0_), channel_id=1, source_target_pairs={{0,2},{1,3},{2,4},{3,5},{4,6},{5,7},{6,0},{7,1},{8,10},{9,11},{10,... | collective-permute-start | bytes 1376264 | tf_op jit(solution)/shard_map/ppermute | solution.py:453
  37.7 22.1 %collective-permute-start.10 = (bf16[64,3584]{1,0:T(8,128)(2,1)S(1)}, bf16[64,3584]{1,0:T(8,128)(2,1)S(1)}, u32[]{:S(2)}, u32[]{:S(2)}) collective-permute-start(bf16[64,3584]{1,0:T(8,128)(2,1)S(1)} %collective-permute-done.4.refs_1_.refs_4_), channel_id=1, source_target_pairs={{0,1},{1,0},{2,3},{3,2},{4,5},{5,4},{6,7},{7,6},{8,9},{9,8},{10,11... | collective-permute-start | bytes 1376264 | tf_op jit(solution)/shard_map/ppermute | solution.py:443
  39.2 20.6 %collective-permute-start.8 = (bf16[64,3584]{1,0:T(8,128)(2,1)S(1)}, bf16[64,3584]{1,0:T(8,128)(2,1)S(1)}, u32[]{:S(2)}, u32[]{:S(2)}) collective-permute-start(bf16[64,3584]{1,0:T(8,128)(2,1)S(1)} %collective-permute-done.3.refs_0_), channel_id=1, source_target_pairs={{0,1},{1,0},{2,3},{3,2},{4,5},{5,4},{6,7},{7,6},{8,9},{9,8},{10,11... | collective-permute-start | bytes 1376264 | tf_op jit(solution)/shard_map/ppermute | solution.py:443
  52.9 6.9 %copy-start.1 = (bf16[384,2048]{1,0:T(8,128)(2,1)S(1)}, bf16[384,2048]{1,0:T(8,128)(2,1)}, u32[]{:S(2)}) copy-start(bf16[384,2048]{1,0:T(8,128)(2,1)} %get-tuple-element.89.refs_4_) | copy-start | bytes 4718596
  59.8 15.0 %collective-permute-start.13 = (bf16[384,2048]{1,0:T(8,128)(2,1)S(1)}, bf16[384,2048]{1,0:T(8,128)(2,1)S(1)}, u32[]{:S(2)}, u32[]{:S(2)}) collective-permute-start(bf16[384,2048]{1,0:T(8,128)(2,1)S(1)} %copy-done.1), channel_id=1, source_target_pairs={{0,8},{8,0},{16,24},{24,16},{1,9},{9,1},{17,25},{25,17},{2,10},{10... | collective-permute-start | bytes 4718600 | tf_op jit(solution)/shard_map/ppermute | solution.py:440
  59.8 13.4 %collective-permute-start.12 = (bf16[64,3584]{1,0:T(8,128)(2,1)S(1)}, bf16[64,3584]{1,0:T(8,128)(2,1)S(1)}, u32[]{:S(2)}, u32[]{:S(2)}) collective-permute-start(bf16[64,3584]{1,0:T(8,128)(2,1)S(1)} %collective-permute-done.6.refs_2_), channel_id=1, source_target_pairs={{0,16},{8,24},{16,0},{24,8},{1,17},{9,25},{17,1},{25,9},{2,18},{10... | collective-permute-start | bytes 1376264 | tf_op jit(solution)/shard_map/ppermute | solution.py:437
  61.3 13.5 %collective-permute-start.11 = (bf16[896,384]{1,0:T(8,128)(2,1)S(1)}, bf16[896,384]{1,0:T(8,128)(2,1)S(1)}, u32[]{:S(2)}, u32[]{:S(2)}) collective-permute-start(bf16[896,384]{1,0:T(8,128)(2,1)S(1)} %get-tuple-element.80), channel_id=1, source_target_pairs={{0,8},{8,0},{16,24},{24,16},{1,9},{9,1},{17,25},{25,17},{2,10},{10... | collective-permute-start | bytes 2064392 | tf_op jit(solution)/shard_map/ppermute | solution.py:440
  61.5 21.9 %collective-permute-start.15 = (bf16[64,3584]{1,0:T(8,128)(2,1)S(1)}, bf16[64,3584]{1,0:T(8,128)(2,1)S(1)}, u32[]{:S(2)}, u32[]{:S(2)}) collective-permute-start(bf16[64,3584]{1,0:T(8,128)(2,1)S(1)} %collective-permute-done.8.refs_0_.refs_4_), channel_id=1, source_target_pairs={{0,16},{8,24},{16,0},{24,8},{1,17},{9,25},{17,1},{25,9},{2,18},{10... | collective-permute-start | bytes 1376264 | tf_op jit(solution)/shard_map/ppermute | solution.py:437
  63.0 20.4 %collective-permute-start.14 = (bf16[64,3584]{1,0:T(8,128)(2,1)S(1)}, bf16[64,3584]{1,0:T(8,128)(2,1)S(1)}, u32[]{:S(2)}, u32[]{:S(2)}) collective-permute-start(bf16[64,3584]{1,0:T(8,128)(2,1)S(1)} %collective-permute-done.6.refs_2_), channel_id=1, source_target_pairs={{0,1},{1,0},{2,3},{3,2},{4,5},{5,4},{6,7},{7,6},{8,9},{9,8},{10,11... | collective-permute-start | bytes 1376264 | tf_op jit(solution)/shard_map/ppermute | solution.py:443
  73.2 12.1 %collective-permute-start.16 = (bf16[64,3584]{1,0:T(8,128)(2,1)S(1)}, bf16[64,3584]{1,0:T(8,128)(2,1)S(1)}, u32[]{:S(2)}, u32[]{:S(2)}) collective-permute-start(bf16[64,3584]{1,0:T(8,128)(2,1)S(1)} %collective-permute-done.12.refs_0_.refs_6_), channel_id=1, source_target_pairs={{0,1},{1,0},{2,3},{3,2},{4,5},{5,4},{6,7},{7,6},{8,9},{9,8},{10,11... | collective-permute-start | bytes 1376264 | tf_op jit(solution)/shard_map/ppermute | solution.py:443
  85.4 6.9 %copy-start = (bf16[384,2048]{1,0:T(8,128)(2,1)S(1)}, bf16[384,2048]{1,0:T(8,128)(2,1)}, u32[]{:S(2)}) copy-start(bf16[384,2048]{1,0:T(8,128)(2,1)} %get-tuple-element.104.refs_5_) | copy-start | bytes 4718596
  92.2 7.4 %copy-start.2 = (bf16[256,2048]{1,0:T(8,128)(2,1)S(1)}, bf16[256,2048]{1,0:T(8,128)(2,1)}, u32[]{:S(2)}) copy-start(bf16[256,2048]{1,0:T(8,128)(2,1)} %get-tuple-element.107.refs_6_) | copy-start | bytes 3145732
  92.2 4.1 %collective-permute-start.18 = (bf16[384,2048]{1,0:T(8,128)(2,1)S(1)}, bf16[384,2048]{1,0:T(8,128)(2,1)S(1)}, u32[]{:S(2)}, u32[]{:S(2)}) collective-permute-start(bf16[384,2048]{1,0:T(8,128)(2,1)S(1)} %copy-done), channel_id=1, source_target_pairs={{0,8},{8,0},{16,24},{24,16},{1,9},{9,1},{17,25},{25,17},{2,10},{10... | collective-permute-start | bytes 4718600 | tf_op jit(solution)/shard_map/ppermute | solution.py:440
  93.7 11.6 %collective-permute-start.17 = (bf16[896,640]{1,0:T(8,128)(2,1)S(1)}, bf16[896,640]{1,0:T(8,128)(2,1)S(1)}, u32[]{:S(2)}, u32[]{:S(2)}) collective-permute-start(bf16[896,640]{1,0:T(8,128)(2,1)S(1)} %get-tuple-element.102), channel_id=1, source_target_pairs={{0,8},{8,0},{16,24},{24,16},{1,9},{9,1},{17,25},{25,17},{2,10},{10... | collective-permute-start | bytes 3440648 | tf_op jit(solution)/shard_map/ppermute | solution.py:440
  94.2 3.2 %collective-permute-start.21 = (f32[32,128]{1,0:T(8,128)S(1)}, f32[32,128]{1,0:T(8,128)S(1)}, u32[]{:S(2)}, u32[]{:S(2)}) collective-permute-start(f32[32,128]{1,0:T(8,128)S(1)} %get-tuple-element.105.own_ref), channel_id=1, source_target_pairs={{0,9},{1,8},{2,11},{3,10},{4,13},{5,12},{6,15},{7,14},{8,1},{9,0},... | collective-permute-start | bytes 49160 | tf_op jit(solution)/shard_map/ppermute | solution.py:450
  95.4 2.0 %collective-permute-start.20 = (f32[32,128]{1,0:T(8,128)S(1)}, f32[32,128]{1,0:T(8,128)S(1)}, u32[]{:S(2)}, u32[]{:S(2)}) collective-permute-start(f32[32,128]{1,0:T(8,128)S(1)} %get-tuple-element.105.own_ref), channel_id=1, source_target_pairs={{0,8},{8,0},{16,24},{24,16},{1,9},{9,1},{17,25},{25,17},{2,10},{10... | collective-permute-start | bytes 49160 | tf_op jit(solution)/shard_map/ppermute | solution.py:440
  95.8 3.7 %collective-permute-start.19 = (f32[32,128]{1,0:T(8,128)S(1)}, f32[32,128]{1,0:T(8,128)S(1)}, u32[]{:S(2)}, u32[]{:S(2)}) collective-permute-start(f32[32,128]{1,0:T(8,128)S(1)} %get-tuple-element.105.own_ref), channel_id=1, source_target_pairs={{0,1},{1,0},{2,3},{3,2},{4,5},{5,4},{6,7},{7,6},{8,9},{9,8},{10,11... | collective-permute-start | bytes 49160 | tf_op jit(solution)/shard_map/ppermute | solution.py:443
  99.6 7.2 %collective-permute-start.22 = (bf16[256,2048]{1,0:T(8,128)(2,1)S(1)}, bf16[256,2048]{1,0:T(8,128)(2,1)S(1)}, u32[]{:S(2)}, u32[]{:S(2)}) collective-permute-start(bf16[256,2048]{1,0:T(8,128)(2,1)S(1)} %copy-done.2), channel_id=1, source_target_pairs={{0,8},{8,0},{16,24},{24,16},{1,9},{9,1},{17,25},{25,17},{2,10},{10... | collective-permute-start | bytes 3145736 | tf_op jit(solution)/shard_map/ppermute | solution.py:440
  99.7 5.9 %collective-permute-start.25 = (f32[64,128]{1,0:T(8,128)S(1)}, f32[64,128]{1,0:T(8,128)S(1)}, u32[]{:S(2)}, u32[]{:S(2)}) collective-permute-start(f32[64,128]{1,0:T(8,128)S(1)} %get-tuple-element.106.refs_10_), channel_id=1, source_target_pairs={{0,2},{1,3},{2,4},{3,5},{4,6},{5,7},{6,0},{7,1},{8,10},{9,11},{10,... | collective-permute-start | bytes 98312 | tf_op jit(solution)/shard_map/ppermute | solution.py:453
  101.3 5.3 %collective-permute-start.24 = (f32[64,128]{1,0:T(8,128)S(1)}, f32[64,128]{1,0:T(8,128)S(1)}, u32[]{:S(2)}, u32[]{:S(2)}) collective-permute-start(f32[64,128]{1,0:T(8,128)S(1)} %get-tuple-element.106.refs_10_), channel_id=1, source_target_pairs={{0,4},{1,5},{2,6},{3,7},{4,0},{5,1},{6,2},{7,3},{8,12},{9,13},{10,... | collective-permute-start | bytes 98312 | tf_op jit(solution)/shard_map/ppermute | solution.py:453
  102.6 4.2 %collective-permute-start.23 = (f32[64,128]{1,0:T(8,128)S(1)}, f32[64,128]{1,0:T(8,128)S(1)}, u32[]{:S(2)}, u32[]{:S(2)}) collective-permute-start(f32[64,128]{1,0:T(8,128)S(1)} %get-tuple-element.106.refs_10_), channel_id=1, source_target_pairs={{0,6},{1,7},{2,0},{3,1},{4,2},{5,3},{6,4},{7,5},{8,14},{9,15},{10,... | collective-permute-start | bytes 98312 | tf_op jit(solution)/shard_map/ppermute | solution.py:453

commit v8 on v7

--- a/solution.py
+++ b/solution.py
@@ -456,8 +456,8 @@
     plain = [(0, 0), (0, 1), (1, 0)]
     groups = [[(*kind, turn) for kind in plain] for turn in range(split)]
     groups += [
-        [(0, 0, split), (0, 1, split), (0, 0, split + 1), (1, 1, 0)],
-        [(1, 0, split), (1, 1, 1)],
+        [(0, 0, split), (1, 1, 0)],
+        [(0, 1, split), (1, 0, split), (0, 0, split + 1), (1, 1, 1)],
         [(0, 1, split + 1), (1, 0, split + 1), (1, 1, split), (1, 1, split + 1)],
     ]
     early_blocks, late_blocks = sum(groups[:split], []), sum(groups[split:], [])
@@ -508,7 +508,6 @@
             elif turn < split:
                 arrived += [early_exp]
             else:
-                held[0, 0, turn + 1], held[0, 1, turn] = arrived[0], arrived[1]
                 middle_exp, stats = logits(
                     groups[split], stats, exp_rows=6 * length
                 )
@@ -537,27 +536,26 @@
     early = [early[0], to_core(early[1])]
     other_exps = [to_core(early_exp)]
     middle_exp, stats = logits(
-        groups[split + 1], stats, held[0, 0, lines - 1],
-        first_row=4 * length, exp_rows=6 * length, into=middle_exp,
+        groups[split + 1], stats, held[0, 0, lines - 1], early[0],
+        first_row=2 * length, exp_rows=6 * length, into=middle_exp,
     )
     held[0, 1, lines - 1] = after(held[0, 1, lines - 1], middle_exp)
     held[1, 1, lines - 1] = diagonal(lines - 1)
     early_ids[0] = after(early_ids[0], middle_exp, held[0, 1, lines - 1], *other_exps)
     sums = one_hot_sums(early, early_ids, columns)
-    last_exp, stats = logits(groups[-1], stats, *sums)
+    late = [held[block] for block in late_blocks]
+    late[0] = after(late[0], *sums)
+    late = turned_features(rep_scalar, late, rows)
+    late = [late[0], to_core(late[1])]
+    other_exps.append(to_core(after(middle_exp, late[0])))
+    last_exp, stats = logits(groups[-1], stats, late[0], *sums)
     exps = [early_exp, middle_exp, last_exp]
-    stats = after(stats, *other_exps)
-    other_exps.append(to_core(after(middle_exp, stats)))
     across_stats, core_stats, both_stats = to_y(stats), to_core(stats), to_y_core(stats)
-    late = [held[block] for block in late_blocks]
-    late[0] = after(late[0], stats)
-    late = turned_features(rep_scalar, late, rows)
     merged, first = merged_stats(
-        after(stats, *other_exps), across_stats, core_stats, both_stats
+        after(stats, late[1], *other_exps), across_stats, core_stats, both_stats
     )
     all_stats = [merged] + [to_z(merged, -along) for along in range(1, lines)]
     other_exps.append(to_core(after(last_exp, merged)))
-    late = [late[0], to_core(late[1])]
     return tuple(refresh_states(
         lines, length, [stat_row(block) for block in early_blocks + late_blocks], early, late,
         exps + other_exps, all_stats, first, late_ids, sums, moment, curvature,

time: 127 us -> 122 us (0.961)
  waiting for transfers between devices: 22.2 us -> 18 us
  starting transfers between devices: 28.2 us -> 26.6 us
    ppermute x6, waiting for transfers between devices: 13.9 us -> 4.36 us  [to_x(): return lax.ppermute(values, 'rep', swap_pairs(reps, 2))]
    ppermute x7, waiting for transfers between devices: 5.67 us -> 10.2 us  [to_y(): return lax.ppermute(values, 'shard', swap_pairs(shards, 1))]
    ppermute x6, starting transfers between devices: 9.6 us -> 7.92 us  [to_z(): return lax.ppermute(values, 'shard', shift_pairs(lines, along, 0))]
  transfers between devices with their start and end apart: 26 -> 26, of which waited for: 10 -> 9; matrix products, arithmetic and copies ran while one was open for 5% -> 6% of each run, Pallas kernels for 31% -> 37%
where the time goes in v8:
time: 122 us; the launch traced here: 121 us
  Pallas kernels  66.4 us (54%)
  starting transfers between devices  26.6 us (22%)
  waiting for transfers between devices  18 us (15%)
  other arithmetic  6.04 us (5%)
  local copies, waits for them, and re-layouts  3.16 us (3%)
    pallas_call x5, Pallas kernels, round_logits(): pl.pallas_call(functools.partial(logits_kernel, stat_rows, first_row, len...  30 us
    pallas_call x1, Pallas kernels, refresh_states(): pl.pallas_call(functools.partial(refresh_kernel, lines, length, block_row...  20 us
    ppermute x7, waiting for transfers between devices, to_y(): return lax.ppermute(values, 'shard', swap_pairs(shards, 1))  10.2 us
    ppermute x7, starting transfers between devices, to_y(): return lax.ppermute(values, 'shard', swap_pairs(shards, 1))  9.18 us
    pallas_call x1, Pallas kernels, one_hot_sums(): pl.pallas_call(functools.partial(one_hot_kernel, len(features)), grid=(co...  8.69 us
    ppermute x6, starting transfers between devices, to_z(): return lax.ppermute(values, 'shard', shift_pairs(lines, along, 0))  7.92 us
    ppermute x6, starting transfers between devices, to_x(): return lax.ppermute(values, 'rep', swap_pairs(reps, 2))  6.83 us
    pallas_call x1, Pallas kernels, prepared(): pl.pallas_call(prepare_kernel, in_specs=[pl.BlockSpec(memory_space=pltpu....  5.52 us
  transfers between devices with their start and end apart: 26, of which 9 were waited for; matrix products, arithmetic and copies ran while one was open for 6% of the time, Pallas kernels for 37%

profile of v8, /device:TPU:0, one launch (start us, length us, event | category | flops | bytes accessed | tf_op | source)
XLA Modules:
  0.0 121.1 jit_solution(8983756003038034451)
XLA Ops:
  0.6 1.2 fusion
  1.9 1.2 fusion.2.refs_0_
  3.1 3.0 %collective-permute-start.2 = (bf16[64,3584]{1,0:T(8,128)(2,1)S(1)}, bf16[64,3584]{1,0:T(8,128)(2,1)S(1)}, u32[]{:S(2)}, u32[]{:S(2)}) collective-permute-start(bf16[64,3584]{1,0:T(8,128)(2,1)S(1)} %fusion.2.refs_0_), channel_id=1, source_target_pairs={{0,1},{1,0},{2,3},{3,2},{4,5},{5,4},{6,7},{7,6},{8,9},{9,8},{10,11... | collective-permute-start | bytes 1376264 | tf_op jit(solution)/shard_map/ppermute | solution.py:443
  6.1 1.5 %collective-permute-start.1 = (bf16[64,3584]{1,0:T(8,128)(2,1)S(1)}, bf16[64,3584]{1,0:T(8,128)(2,1)S(1)}, u32[]{:S(2)}, u32[]{:S(2)}) collective-permute-start(bf16[64,3584]{1,0:T(8,128)(2,1)S(1)} %fusion.2.refs_0_), channel_id=1, source_target_pairs={{0,16},{8,24},{16,0},{24,8},{1,17},{9,25},{17,1},{25,9},{2,18},{10... | collective-permute-start | bytes 1376264 | tf_op jit(solution)/shard_map/ppermute | solution.py:437
  7.6 1.6 %collective-permute-start = (bf16[64,3584]{1,0:T(8,128)(2,1)S(1)}, bf16[64,3584]{1,0:T(8,128)(2,1)S(1)}, u32[]{:S(2)}, u32[]{:S(2)}) collective-permute-start(bf16[64,3584]{1,0:T(8,128)(2,1)S(1)} %fusion.2.refs_0_), channel_id=1, source_target_pairs={{0,2},{1,3},{2,4},{3,5},{4,6},{5,7},{6,0},{7,1},{8,10},{9,11},{10,... | collective-permute-start | bytes 1376264 | tf_op jit(solution)/shard_map/ppermute | solution.py:453
  9.2 0.7 fusion.7
  9.8 0.7 compare_and_fusion
  10.5 0.7 multiply_add_fusion
  11.2 1.2 slice.31
  12.4 0.8 slice.30
  13.3 0.7 broadcast_subtract_fusion
  14.1 0.7 fusion.4
  14.9 0.6 gather_fusion
  16.0 5.5 %prepared.1 = (bf16[3584,2048]{1,0:T(8,128)(2,1)S(1)}, s32[1280,128]{1,0:T(8,128)S(1)}, s32[1280,128]{1,0:T(8,128)S(1)}) custom-call(bf16[3584,2048]{1,0:T(8,128)(2,1)} %weight_ref.1, s32[1,1280]{1,0:T(1,128)S(1)} %squeeze.14.true_ids, s32[1,1280]{1,0:T(1,128)S(1)} %squeeze.15.sample_ids, s32[1,768]{1,0:T(1,128)S(1)} %squeeze.12.refs_0_.refs_2_, ...), custom_call_target="tpu_custom_call" | custom-call | flops 1024 | bytes 1024 | tf_op jit(solution)/shard_map/prepared/pallas_call | solution.py:113
  21.5 0.6 collective-permute-start.5
  22.1 0.5 collective-permute-start.4
  22.6 1.6 %collective-permute-start.3 = (bf16[64,3584]{1,0:T(8,128)(2,1)S(1)}, bf16[64,3584]{1,0:T(8,128)(2,1)S(1)}, u32[]{:S(2)}, u32[]{:S(2)}) collective-permute-start(bf16[64,3584]{1,0:T(8,128)(2,1)S(1)} %collective-permute-done.refs_0_.refs_3_), channel_id=1, source_target_pairs={{0,2},{1,3},{2,4},{3,5},{4,6},{5,7},{6,0},{7,1},{8,10},{9,11},{10,... | collective-permute-start | bytes 1376264 | tf_op jit(solution)/shard_map/ppermute | solution.py:453
  24.2 1.5 %collective-permute-start.9 = (bf16[64,3584]{1,0:T(8,128)(2,1)S(1)}, bf16[64,3584]{1,0:T(8,128)(2,1)S(1)}, u32[]{:S(2)}, u32[]{:S(2)}) collective-permute-start(bf16[64,3584]{1,0:T(8,128)(2,1)S(1)} %collective-permute-done.2.refs_2_), channel_id=1, source_target_pairs={{0,16},{8,24},{16,0},{24,8},{1,17},{9,25},{17,1},{25,9},{2,18},{10... | collective-permute-start | bytes 1376264 | tf_op jit(solution)/shard_map/ppermute | solution.py:437
  25.7 5.8 %round_logits.5 = (bf16[384,2048]{1,0:T(8,128)(2,1)}, f32[32,128]{1,0:T(8,128)S(1)}) custom-call(bf16[64,3584]{1,0:T(8,128)(2,1)S(1)} %fusion.2.refs_0_, bf16[64,3584]{1,0:T(8,128)(2,1)S(1)} %collective-permute-done.1.refs_1_, bf16[64,3584]{1,0:T(8,128)(2,1)S(1)} %collective-permute-done.2.refs_2_, ...), custom_call_target="tpu_custom_call" | custom-call | flops 1024 | bytes 1024 | tf_op jit(solution)/shard_map/round_logits/pallas_call | solution.py:192
  31.5 1.5 %collective-permute-done.5.refs_2_.refs_5_ = bf16[64,3584]{1,0:T(8,128)(2,1)S(1)} collective-permute-done((bf16[64,3584]{1,0:T(8,128)(2,1)S(1)}, bf16[64,3584]{1,0:T(8,128)(2,1)S(1)}, u32[]{:S(2)}, u32[]{:S(2)}) %collective-permute-start.5) | collective-permute-done | bytes 458784 | tf_op jit(solution)/shard_map/ppermute | solution.py:443
  33.0 2.5 %collective-permute-done.4.refs_1_.refs_4_ = bf16[64,3584]{1,0:T(8,128)(2,1)S(1)} collective-permute-done((bf16[64,3584]{1,0:T(8,128)(2,1)S(1)}, bf16[64,3584]{1,0:T(8,128)(2,1)S(1)}, u32[]{:S(2)}, u32[]{:S(2)}) %collective-permute-start.4) | collective-permute-done | bytes 458784 | tf_op jit(solution)/shard_map/ppermute | solution.py:437
  35.5 1.5 %collective-permute-start.10 = (bf16[64,3584]{1,0:T(8,128)(2,1)S(1)}, bf16[64,3584]{1,0:T(8,128)(2,1)S(1)}, u32[]{:S(2)}, u32[]{:S(2)}) collective-permute-start(bf16[64,3584]{1,0:T(8,128)(2,1)S(1)} %collective-permute-done.4.refs_1_.refs_4_), channel_id=1, source_target_pairs={{0,1},{1,0},{2,3},{3,2},{4,5},{5,4},{6,7},{7,6},{8,9},{9,8},{10,11... | collective-permute-start | bytes 1376264 | tf_op jit(solution)/shard_map/ppermute | solution.py:443
  37.1 0.5 collective-permute-start.8
  37.6 1.2 %collective-permute-start.7 = (bf16[64,3584]{1,0:T(8,128)(2,1)S(1)}, bf16[64,3584]{1,0:T(8,128)(2,1)S(1)}, u32[]{:S(2)}, u32[]{:S(2)}) collective-permute-start(bf16[64,3584]{1,0:T(8,128)(2,1)S(1)} %collective-permute-done.3.refs_0_), channel_id=1, source_target_pairs={{0,16},{8,24},{16,0},{24,8},{1,17},{9,25},{17,1},{25,9},{2,18},{10... | collective-permute-start | bytes 1376264 | tf_op jit(solution)/shard_map/ppermute | solution.py:437
  38.8 0.9 collective-permute-start.6
  39.7 5.8 %round_logits.6 = (bf16[384,2048]{1,0:T(8,128)(2,1)}, f32[32,128]{1,0:T(8,128)S(1)}) custom-call(bf16[64,3584]{1,0:T(8,128)(2,1)S(1)} %collective-permute-done.refs_0_.refs_3_, bf16[64,3584]{1,0:T(8,128)(2,1)S(1)} %collective-permute-done.4.refs_1_.refs_4_, ...), custom_call_target="tpu_custom_call", output_to_operand_aliasing={{0}: (5, {})} | custom-call | flops 1024 | bytes 1024 | tf_op jit(solution)/shard_map/round_logits/pallas_call | solution.py:192
  45.5 4.7 %round_logits.7 = (bf16[384,2048]{1,0:T(8,128)(2,1)}, f32[32,128]{1,0:T(8,128)S(1)}) custom-call(bf16[64,3584]{1,0:T(8,128)(2,1)S(1)} %collective-permute-done.3.refs_0_, bf16[64,3584]{1,0:T(8,128)(2,1)S(1)} %collective-permute-done.9.refs_1_, bf16[3584,2048]{1,0:T(8,128)(2,1)S(1)} %get-tuple-element.64.refs_3_.refs_2_.refs_4_, ...), custom_call_target="tpu_custom_call" | custom-call | flops 1024 | bytes 1024 | tf_op jit(solution)/shard_map/round_logits/pallas_call | solution.py:192
  50.3 4.8 %collective-permute-done.8.refs_1_.refs_3_ = bf16[64,3584]{1,0:T(8,128)(2,1)S(1)} collective-permute-done((bf16[64,3584]{1,0:T(8,128)(2,1)S(1)}, bf16[64,3584]{1,0:T(8,128)(2,1)S(1)}, u32[]{:S(2)}, u32[]{:S(2)}) %collective-permute-start.8) | collective-permute-done | bytes 458784 | tf_op jit(solution)/shard_map/ppermute | solution.py:443
  55.1 1.6 %collective-permute-start.12 = (bf16[64,3584]{1,0:T(8,128)(2,1)S(1)}, bf16[64,3584]{1,0:T(8,128)(2,1)S(1)}, u32[]{:S(2)}, u32[]{:S(2)}) collective-permute-start(bf16[64,3584]{1,0:T(8,128)(2,1)S(1)} %collective-permute-done.6.refs_2_.refs_4_), channel_id=1, source_target_pairs={{0,16},{8,24},{16,0},{24,8},{1,17},{9,25},{17,1},{25,9},{2,18},{10... | collective-permute-start | bytes 1376264 | tf_op jit(solution)/shard_map/ppermute | solution.py:437
  56.7 0.9 turned_features.2
  57.8 1.5 %collective-permute-start.14 = (bf16[64,3584]{1,0:T(8,128)(2,1)S(1)}, bf16[64,3584]{1,0:T(8,128)(2,1)S(1)}, u32[]{:S(2)}, u32[]{:S(2)}) collective-permute-start(bf16[64,3584]{1,0:T(8,128)(2,1)S(1)} %collective-permute-done.6.refs_2_.refs_4_), channel_id=1, source_target_pairs={{0,1},{1,0},{2,3},{3,2},{4,5},{5,4},{6,7},{7,6},{8,9},{9,8},{10,11... | collective-permute-start | bytes 1376264 | tf_op jit(solution)/shard_map/ppermute | solution.py:443
  59.3 0.5 collective-permute-start.15
  59.8 6.9 %round_logits.8 = (bf16[384,2048]{1,0:T(8,128)(2,1)}, f32[32,128]{1,0:T(8,128)S(1)}) custom-call(bf16[64,3584]{1,0:T(8,128)(2,1)S(1)} %collective-permute-done.7.refs_0_.refs_2_, bf16[64,3584]{1,0:T(8,128)(2,1)S(1)} %collective-permute-done.8.refs_1_.refs_3_, ...), custom_call_target="tpu_custom_call", output_to_operand_aliasing={{0}: (6, {})} | custom-call | flops 1024 | bytes 1024 | tf_op jit(solution)/shard_map/round_logits/pallas_call | solution.py:192
  66.7 1.8 %collective-permute-done.12.refs_6_.refs_0_ = bf16[64,3584]{1,0:T(8,128)(2,1)S(1)} collective-permute-done((bf16[64,3584]{1,0:T(8,128)(2,1)S(1)}, bf16[64,3584]{1,0:T(8,128)(2,1)S(1)}, u32[]{:S(2)}, u32[]{:S(2)}) %collective-permute-start.12) | collective-permute-done | bytes 458784 | tf_op jit(solution)/shard_map/ppermute | solution.py:437
  68.5 1.5 %collective-permute-start.16 = (bf16[64,3584]{1,0:T(8,128)(2,1)S(1)}, bf16[64,3584]{1,0:T(8,128)(2,1)S(1)}, u32[]{:S(2)}, u32[]{:S(2)}) collective-permute-start(bf16[64,3584]{1,0:T(8,128)(2,1)S(1)} %collective-permute-done.12.refs_6_.refs_0_), channel_id=1, source_target_pairs={{0,1},{1,0},{2,3},{3,2},{4,5},{5,4},{6,7},{7,6},{8,9},{9,8},{10,11... | collective-permute-start | bytes 1376264 | tf_op jit(solution)/shard_map/ppermute | solution.py:443
  70.0 8.7 %one_hot_sums.1 = (bf16[896,2048]{1,0:T(8,128)(2,1)}, bf16[896,2048]{1,0:T(8,128)(2,1)}) custom-call(bf16[896,384]{1,0:T(8,128)(2,1)S(1)} %get-tuple-element.78.refs_0_, bf16[896,384]{1,0:T(8,128)(2,1)S(1)} %collective-permute-done.11.refs_1_, s32[1,768]{1,0:T(1,128)S(1)} %squeeze.12.refs_0_.refs_2_, s32[1,768]{1,0:T(1,128)S(1)} %squeeze.13.refs_1_.refs_3_), custom_call_target="tpu_custom_call" | custom-call | flops 1024 | bytes 1024 | tf_op jit(solution)/shard_map/one_hot_sums/pallas_call | solution.py:271
  78.7 1.6 %collective-permute-done.16.refs_9_.refs_3_ = bf16[64,3584]{1,0:T(8,128)(2,1)S(1)} collective-permute-done((bf16[64,3584]{1,0:T(8,128)(2,1)S(1)}, bf16[64,3584]{1,0:T(8,128)(2,1)S(1)}, u32[]{:S(2)}, u32[]{:S(2)}) %collective-permute-start.16) | collective-permute-done | bytes 458784 | tf_op jit(solution)/shard_map/ppermute | solution.py:443
  80.4 1.3 %turned_features.3 = (bf16[896,640]{1,0:T(8,128)(2,1)S(1)}, bf16[896,640]{1,0:T(8,128)(2,1)S(1)}) custom-call(s32[1]{0:T(128)} %bitcast.5.rep_ref, bf16[64,3584]{1,0:T(8,128)(2,1)S(1)} %collective-permute-done.3.refs_0_, bf16[64,3584]{1,0:T(8,128)(2,1)S(1)} %collective-permute-done.9.refs_1_, bf16[64,3584]{1,0:T(8,128)(2,1)S(1)} %collective-permute-done.7.refs_0_.refs_2_, ...), custom_call_target="tpu_custom_call" | custom-call | flops 1024 | bytes 1024 | tf_op jit(solution)/shard_map/turned_features/pallas_call | solution.py:234
  81.8 0.5 collective-permute-start.17
  82.3 6.8 %round_logits.9 = (bf16[256,2048]{1,0:T(8,128)(2,1)}, f32[32,128]{1,0:T(8,128)S(1)}) custom-call(bf16[64,3584]{1,0:T(8,128)(2,1)S(1)} %collective-permute-done.12.refs_6_.refs_0_, bf16[64,3584]{1,0:T(8,128)(2,1)S(1)} %collective-permute-done.14.refs_7_.refs_1_, bf16[64,3584]{1,0:T(8,128)(2,1)S(1)} %collective-permute-done.15.refs_8_.refs_2_, ...), custom_call_target="tpu_custom_call" | custom-call | flops 1024 | bytes 1024 | tf_op jit(solution)/shard_map/round_logits/pallas_call | solution.py:192
  89.2 1.3 %collective-permute-start.21 = (f32[32,128]{1,0:T(8,128)S(1)}, f32[32,128]{1,0:T(8,128)S(1)}, u32[]{:S(2)}, u32[]{:S(2)}) collective-permute-start(f32[32,128]{1,0:T(8,128)S(1)} %get-tuple-element.103.own_ref), channel_id=1, source_target_pairs={{0,9},{1,8},{2,11},{3,10},{4,13},{5,12},{6,15},{7,14},{8,1},{9,0},... | collective-permute-start | bytes 49160 | tf_op jit(solution)/shard_map/ppermute | solution.py:450
  90.9 0.5 collective-permute-start.19
  91.4 1.0 collective-permute-done.21.both_ref
  92.4 2.2 %collective-permute-done.19.across_ref = f32[32,128]{1,0:T(8,128)S(1)} collective-permute-done((f32[32,128]{1,0:T(8,128)S(1)}, f32[32,128]{1,0:T(8,128)S(1)}, u32[]{:S(2)}, u32[]{:S(2)}) %collective-permute-start.19) | collective-permute-done | bytes 16416 | tf_op jit(solution)/shard_map/ppermute | solution.py:443
  94.8 1.1 collective-permute-start.24
  95.9 2.7 %collective-permute-start.23 = (f32[64,128]{1,0:T(8,128)S(1)}, f32[64,128]{1,0:T(8,128)S(1)}, u32[]{:S(2)}, u32[]{:S(2)}) collective-permute-start(f32[64,128]{1,0:T(8,128)S(1)} %get-tuple-element.104.refs_10_), channel_id=1, source_target_pairs={{0,6},{1,7},{2,0},{3,1},{4,2},{5,3},{6,4},{7,5},{8,14},{9,15},{10,... | collective-permute-start | bytes 98312 | tf_op jit(solution)/shard_map/ppermute | solution.py:453
  98.6 2.2 %collective-permute-done.25.refs_13_ = f32[64,128]{1,0:T(8,128)S(1)} collective-permute-done((f32[64,128]{1,0:T(8,128)S(1)}, f32[64,128]{1,0:T(8,128)S(1)}, u32[]{:S(2)}, u32[]{:S(2)}) %collective-permute-start.25) | collective-permute-done | bytes 32800 | tf_op jit(solution)/shard_map/ppermute | solution.py:453
  101.1 20.0 %refresh_states.1 = (bf16[896,2048]{1,0:T(8,128)(2,1)}, bf16[896,2048]{1,0:T(8,128)(2,1)}, bf16[896,2048]{1,0:T(8,128)(2,1)}) custom-call(bf16[896,384]{1,0:T(8,128)(2,1)S(1)} %get-tuple-element.78.refs_0_, bf16[896,384]{1,0:T(8,128)(2,1)S(1)} %collective-permute-done.11.refs_1_, bf16[896,640]{1,0:T(8,128)(2,1)S(1)} %get-tuple-element.96.refs_2_, ...), custom_call_target="tpu_custom_call" | custom-call | flops 1024 | bytes 1024 | tf_op jit(solution)/shard_map/refresh_states/pallas_call | solution.py:400
  (45 shorter events, 2.0 us)
Async XLA Ops:
  3.1 18.4 %collective-permute-start.2 = (bf16[64,3584]{1,0:T(8,128)(2,1)S(1)}, bf16[64,3584]{1,0:T(8,128)(2,1)S(1)}, u32[]{:S(2)}, u32[]{:S(2)}) collective-permute-start(bf16[64,3584]{1,0:T(8,128)(2,1)S(1)} %fusion.2.refs_0_), channel_id=1, source_target_pairs={{0,1},{1,0},{2,3},{3,2},{4,5},{5,4},{6,7},{7,6},{8,9},{9,8},{10,11... | collective-permute-start | bytes 1376264 | tf_op jit(solution)/shard_map/ppermute | solution.py:443
  6.1 15.4 %collective-permute-start.1 = (bf16[64,3584]{1,0:T(8,128)(2,1)S(1)}, bf16[64,3584]{1,0:T(8,128)(2,1)S(1)}, u32[]{:S(2)}, u32[]{:S(2)}) collective-permute-start(bf16[64,3584]{1,0:T(8,128)(2,1)S(1)} %fusion.2.refs_0_), channel_id=1, source_target_pairs={{0,16},{8,24},{16,0},{24,8},{1,17},{9,25},{17,1},{25,9},{2,18},{10... | collective-permute-start | bytes 1376264 | tf_op jit(solution)/shard_map/ppermute | solution.py:437
  7.6 13.9 %collective-permute-start = (bf16[64,3584]{1,0:T(8,128)(2,1)S(1)}, bf16[64,3584]{1,0:T(8,128)(2,1)S(1)}, u32[]{:S(2)}, u32[]{:S(2)}) collective-permute-start(bf16[64,3584]{1,0:T(8,128)(2,1)S(1)} %fusion.2.refs_0_), channel_id=1, source_target_pairs={{0,2},{1,3},{2,4},{3,5},{4,6},{5,7},{6,0},{7,1},{8,10},{9,11},{10,... | collective-permute-start | bytes 1376264 | tf_op jit(solution)/shard_map/ppermute | solution.py:453
  21.5 11.5 %collective-permute-start.5 = (bf16[64,3584]{1,0:T(8,128)(2,1)S(1)}, bf16[64,3584]{1,0:T(8,128)(2,1)S(1)}, u32[]{:S(2)}, u32[]{:S(2)}) collective-permute-start(bf16[64,3584]{1,0:T(8,128)(2,1)S(1)} %collective-permute-done.refs_0_.refs_3_), channel_id=1, source_target_pairs={{0,1},{1,0},{2,3},{3,2},{4,5},{5,4},{6,7},{7,6},{8,9},{9,8},{10,11... | collective-permute-start | bytes 1376264 | tf_op jit(solution)/shard_map/ppermute | solution.py:443
  22.1 13.5 %collective-permute-start.4 = (bf16[64,3584]{1,0:T(8,128)(2,1)S(1)}, bf16[64,3584]{1,0:T(8,128)(2,1)S(1)}, u32[]{:S(2)}, u32[]{:S(2)}) collective-permute-start(bf16[64,3584]{1,0:T(8,128)(2,1)S(1)} %collective-permute-done.refs_0_.refs_3_), channel_id=1, source_target_pairs={{0,16},{8,24},{16,0},{24,8},{1,17},{9,25},{17,1},{25,9},{2,18},{10... | collective-permute-start | bytes 1376264 | tf_op jit(solution)/shard_map/ppermute | solution.py:437
  22.6 12.9 %collective-permute-start.3 = (bf16[64,3584]{1,0:T(8,128)(2,1)S(1)}, bf16[64,3584]{1,0:T(8,128)(2,1)S(1)}, u32[]{:S(2)}, u32[]{:S(2)}) collective-permute-start(bf16[64,3584]{1,0:T(8,128)(2,1)S(1)} %collective-permute-done.refs_0_.refs_3_), channel_id=1, source_target_pairs={{0,2},{1,3},{2,4},{3,5},{4,6},{5,7},{6,0},{7,1},{8,10},{9,11},{10,... | collective-permute-start | bytes 1376264 | tf_op jit(solution)/shard_map/ppermute | solution.py:453
  24.2 21.3 %collective-permute-start.9 = (bf16[64,3584]{1,0:T(8,128)(2,1)S(1)}, bf16[64,3584]{1,0:T(8,128)(2,1)S(1)}, u32[]{:S(2)}, u32[]{:S(2)}) collective-permute-start(bf16[64,3584]{1,0:T(8,128)(2,1)S(1)} %collective-permute-done.2.refs_2_), channel_id=1, source_target_pairs={{0,16},{8,24},{16,0},{24,8},{1,17},{9,25},{17,1},{25,9},{2,18},{10... | collective-permute-start | bytes 1376264 | tf_op jit(solution)/shard_map/ppermute | solution.py:437
  35.5 14.7 %collective-permute-start.10 = (bf16[64,3584]{1,0:T(8,128)(2,1)S(1)}, bf16[64,3584]{1,0:T(8,128)(2,1)S(1)}, u32[]{:S(2)}, u32[]{:S(2)}) collective-permute-start(bf16[64,3584]{1,0:T(8,128)(2,1)S(1)} %collective-permute-done.4.refs_1_.refs_4_), channel_id=1, source_target_pairs={{0,1},{1,0},{2,3},{3,2},{4,5},{5,4},{6,7},{7,6},{8,9},{9,8},{10,11... | collective-permute-start | bytes 1376264 | tf_op jit(solution)/shard_map/ppermute | solution.py:443
  37.1 18.0 %collective-permute-start.8 = (bf16[64,3584]{1,0:T(8,128)(2,1)S(1)}, bf16[64,3584]{1,0:T(8,128)(2,1)S(1)}, u32[]{:S(2)}, u32[]{:S(2)}) collective-permute-start(bf16[64,3584]{1,0:T(8,128)(2,1)S(1)} %collective-permute-done.3.refs_0_), channel_id=1, source_target_pairs={{0,1},{1,0},{2,3},{3,2},{4,5},{5,4},{6,7},{7,6},{8,9},{9,8},{10,11... | collective-permute-start | bytes 1376264 | tf_op jit(solution)/shard_map/ppermute | solution.py:443
  37.6 17.5 %collective-permute-start.7 = (bf16[64,3584]{1,0:T(8,128)(2,1)S(1)}, bf16[64,3584]{1,0:T(8,128)(2,1)S(1)}, u32[]{:S(2)}, u32[]{:S(2)}) collective-permute-start(bf16[64,3584]{1,0:T(8,128)(2,1)S(1)} %collective-permute-done.3.refs_0_), channel_id=1, source_target_pairs={{0,16},{8,24},{16,0},{24,8},{1,17},{9,25},{17,1},{25,9},{2,18},{10... | collective-permute-start | bytes 1376264 | tf_op jit(solution)/shard_map/ppermute | solution.py:437
  38.8 16.3 %collective-permute-start.6 = (bf16[64,3584]{1,0:T(8,128)(2,1)S(1)}, bf16[64,3584]{1,0:T(8,128)(2,1)S(1)}, u32[]{:S(2)}, u32[]{:S(2)}) collective-permute-start(bf16[64,3584]{1,0:T(8,128)(2,1)S(1)} %collective-permute-done.3.refs_0_), channel_id=1, source_target_pairs={{0,2},{1,3},{2,4},{3,5},{4,6},{5,7},{6,0},{7,1},{8,10},{9,11},{10,... | collective-permute-start | bytes 1376264 | tf_op jit(solution)/shard_map/ppermute | solution.py:453
  45.5 9.5 %copy-start.1 = (bf16[384,2048]{1,0:T(8,128)(2,1)S(1)}, bf16[384,2048]{1,0:T(8,128)(2,1)}, u32[]{:S(2)}) copy-start(bf16[384,2048]{1,0:T(8,128)(2,1)} %get-tuple-element.89.refs_4_) | copy-start | bytes 4718596
  55.1 15.0 %collective-permute-start.13 = (bf16[384,2048]{1,0:T(8,128)(2,1)S(1)}, bf16[384,2048]{1,0:T(8,128)(2,1)S(1)}, u32[]{:S(2)}, u32[]{:S(2)}) collective-permute-start(bf16[384,2048]{1,0:T(8,128)(2,1)S(1)} %copy-done.1), channel_id=1, source_target_pairs={{0,8},{8,0},{16,24},{24,16},{1,9},{9,1},{17,25},{25,17},{2,10},{10... | collective-permute-start | bytes 4718600 | tf_op jit(solution)/shard_map/ppermute | solution.py:440
  55.1 13.4 %collective-permute-start.12 = (bf16[64,3584]{1,0:T(8,128)(2,1)S(1)}, bf16[64,3584]{1,0:T(8,128)(2,1)S(1)}, u32[]{:S(2)}, u32[]{:S(2)}) collective-permute-start(bf16[64,3584]{1,0:T(8,128)(2,1)S(1)} %collective-permute-done.6.refs_2_.refs_4_), channel_id=1, source_target_pairs={{0,16},{8,24},{16,0},{24,8},{1,17},{9,25},{17,1},{25,9},{2,18},{10... | collective-permute-start | bytes 1376264 | tf_op jit(solution)/shard_map/ppermute | solution.py:437
  57.6 12.5 %collective-permute-start.11 = (bf16[896,384]{1,0:T(8,128)(2,1)S(1)}, bf16[896,384]{1,0:T(8,128)(2,1)S(1)}, u32[]{:S(2)}, u32[]{:S(2)}) collective-permute-start(bf16[896,384]{1,0:T(8,128)(2,1)S(1)} %get-tuple-element.79), channel_id=1, source_target_pairs={{0,8},{8,0},{16,24},{24,16},{1,9},{9,1},{17,25},{25,17},{2,10},{10... | collective-permute-start | bytes 2064392 | tf_op jit(solution)/shard_map/ppermute | solution.py:440
  57.8 21.0 %collective-permute-start.14 = (bf16[64,3584]{1,0:T(8,128)(2,1)S(1)}, bf16[64,3584]{1,0:T(8,128)(2,1)S(1)}, u32[]{:S(2)}, u32[]{:S(2)}) collective-permute-start(bf16[64,3584]{1,0:T(8,128)(2,1)S(1)} %collective-permute-done.6.refs_2_.refs_4_), channel_id=1, source_target_pairs={{0,1},{1,0},{2,3},{3,2},{4,5},{5,4},{6,7},{7,6},{8,9},{9,8},{10,11... | collective-permute-start | bytes 1376264 | tf_op jit(solution)/shard_map/ppermute | solution.py:443
  59.3 19.4 %collective-permute-start.15 = (bf16[64,3584]{1,0:T(8,128)(2,1)S(1)}, bf16[64,3584]{1,0:T(8,128)(2,1)S(1)}, u32[]{:S(2)}, u32[]{:S(2)}) collective-permute-start(bf16[64,3584]{1,0:T(8,128)(2,1)S(1)} %collective-permute-done.8.refs_1_.refs_3_), channel_id=1, source_target_pairs={{0,16},{8,24},{16,0},{24,8},{1,17},{9,25},{17,1},{25,9},{2,18},{10... | collective-permute-start | bytes 1376264 | tf_op jit(solution)/shard_map/ppermute | solution.py:437
  66.7 15.0 %copy-start = (bf16[384,2048]{1,0:T(8,128)(2,1)S(1)}, bf16[384,2048]{1,0:T(8,128)(2,1)}, u32[]{:S(2)}) copy-start(bf16[384,2048]{1,0:T(8,128)(2,1)} %get-tuple-element.101.refs_5_) | copy-start | bytes 4718596
  68.5 11.9 %collective-permute-start.16 = (bf16[64,3584]{1,0:T(8,128)(2,1)S(1)}, bf16[64,3584]{1,0:T(8,128)(2,1)S(1)}, u32[]{:S(2)}, u32[]{:S(2)}) collective-permute-start(bf16[64,3584]{1,0:T(8,128)(2,1)S(1)} %collective-permute-done.12.refs_6_.refs_0_), channel_id=1, source_target_pairs={{0,1},{1,0},{2,3},{3,2},{4,5},{5,4},{6,7},{7,6},{8,9},{9,8},{10,11... | collective-permute-start | bytes 1376264 | tf_op jit(solution)/shard_map/ppermute | solution.py:443
  81.7 9.6 %collective-permute-start.18 = (bf16[384,2048]{1,0:T(8,128)(2,1)S(1)}, bf16[384,2048]{1,0:T(8,128)(2,1)S(1)}, u32[]{:S(2)}, u32[]{:S(2)}) collective-permute-start(bf16[384,2048]{1,0:T(8,128)(2,1)S(1)} %copy-done), channel_id=1, source_target_pairs={{0,8},{8,0},{16,24},{24,16},{1,9},{9,1},{17,25},{25,17},{2,10},{10... | collective-permute-start | bytes 4718600 | tf_op jit(solution)/shard_map/ppermute | solution.py:440
  81.8 9.6 %collective-permute-start.17 = (bf16[896,640]{1,0:T(8,128)(2,1)S(1)}, bf16[896,640]{1,0:T(8,128)(2,1)S(1)}, u32[]{:S(2)}, u32[]{:S(2)}) collective-permute-start(bf16[896,640]{1,0:T(8,128)(2,1)S(1)} %get-tuple-element.97), channel_id=1, source_target_pairs={{0,8},{8,0},{16,24},{24,16},{1,9},{9,1},{17,25},{25,17},{2,10},{10... | collective-permute-start | bytes 3440648 | tf_op jit(solution)/shard_map/ppermute | solution.py:440
  89.2 3.2 %collective-permute-start.21 = (f32[32,128]{1,0:T(8,128)S(1)}, f32[32,128]{1,0:T(8,128)S(1)}, u32[]{:S(2)}, u32[]{:S(2)}) collective-permute-start(f32[32,128]{1,0:T(8,128)S(1)} %get-tuple-element.103.own_ref), channel_id=1, source_target_pairs={{0,9},{1,8},{2,11},{3,10},{4,13},{5,12},{6,15},{7,14},{8,1},{9,0},... | collective-permute-start | bytes 49160 | tf_op jit(solution)/shard_map/ppermute | solution.py:450
  90.4 2.0 %collective-permute-start.20 = (f32[32,128]{1,0:T(8,128)S(1)}, f32[32,128]{1,0:T(8,128)S(1)}, u32[]{:S(2)}, u32[]{:S(2)}) collective-permute-start(f32[32,128]{1,0:T(8,128)S(1)} %get-tuple-element.103.own_ref), channel_id=1, source_target_pairs={{0,8},{8,0},{16,24},{24,16},{1,9},{9,1},{17,25},{25,17},{2,10},{10... | collective-permute-start | bytes 49160 | tf_op jit(solution)/shard_map/ppermute | solution.py:440
  90.9 3.7 %collective-permute-start.19 = (f32[32,128]{1,0:T(8,128)S(1)}, f32[32,128]{1,0:T(8,128)S(1)}, u32[]{:S(2)}, u32[]{:S(2)}) collective-permute-start(f32[32,128]{1,0:T(8,128)S(1)} %get-tuple-element.103.own_ref), channel_id=1, source_target_pairs={{0,1},{1,0},{2,3},{3,2},{4,5},{5,4},{6,7},{7,6},{8,9},{9,8},{10,11... | collective-permute-start | bytes 49160 | tf_op jit(solution)/shard_map/ppermute | solution.py:443
  94.6 6.4 %collective-permute-start.22 = (bf16[256,2048]{1,0:T(8,128)(2,1)}, bf16[256,2048]{1,0:T(8,128)(2,1)S(1)}, u32[]{:S(2)}, u32[]{:S(2)}) collective-permute-start(bf16[256,2048]{1,0:T(8,128)(2,1)} %get-tuple-element.105.refs_6_), channel_id=1, source_target_pairs={{0,8},{8,0},{16,24},{24,16},{1,9},{9,1},{17,25},{25,17},{2,10},{10... | collective-permute-start | bytes 3145736 | tf_op jit(solution)/shard_map/ppermute | solution.py:440
  94.7 6.0 %collective-permute-start.25 = (f32[64,128]{1,0:T(8,128)S(1)}, f32[64,128]{1,0:T(8,128)S(1)}, u32[]{:S(2)}, u32[]{:S(2)}) collective-permute-start(f32[64,128]{1,0:T(8,128)S(1)} %get-tuple-element.104.refs_10_), channel_id=1, source_target_pairs={{0,2},{1,3},{2,4},{3,5},{4,6},{5,7},{6,0},{7,1},{8,10},{9,11},{10,... | collective-permute-start | bytes 98312 | tf_op jit(solution)/shard_map/ppermute | solution.py:453
  94.8 6.0 %collective-permute-start.24 = (f32[64,128]{1,0:T(8,128)S(1)}, f32[64,128]{1,0:T(8,128)S(1)}, u32[]{:S(2)}, u32[]{:S(2)}) collective-permute-start(f32[64,128]{1,0:T(8,128)S(1)} %get-tuple-element.104.refs_10_), channel_id=1, source_target_pairs={{0,4},{1,5},{2,6},{3,7},{4,0},{5,1},{6,2},{7,3},{8,12},{9,13},{10,... | collective-permute-start | bytes 98312 | tf_op jit(solution)/shard_map/ppermute | solution.py:453
  95.9 5.2 %collective-permute-start.23 = (f32[64,128]{1,0:T(8,128)S(1)}, f32[64,128]{1,0:T(8,128)S(1)}, u32[]{:S(2)}, u32[]{:S(2)}) collective-permute-start(f32[64,128]{1,0:T(8,128)S(1)} %get-tuple-element.104.refs_10_), channel_id=1, source_target_pairs={{0,6},{1,7},{2,0},{3,1},{4,2},{5,3},{6,4},{7,5},{8,14},{9,15},{10,... | collective-permute-start | bytes 98312 | tf_op jit(solution)/shard_map/ppermute | solution.py:453

commit v9 on v8

--- a/solution.py
+++ b/solution.py
@@ -83,6 +83,20 @@
             source = 2 * place + side
             pairs.append((source, 2 * ((place + along) % lines) + (side ^ across)))
     return pairs
+
+
+def normalize_kernel(hidden_ref, gain_ref, normed_ref):
+    normed_ref[...] = normalize(hidden_ref[...], gain_ref[...])
+
+
+def normalized(hidden, norm_gain):
+    return pl.pallas_call(
+        normalize_kernel,
+        out_shape=jax.ShapeDtypeStruct(hidden.shape, jnp.bfloat16),
+        compiler_params=pltpu.CompilerParams(vmem_limit_bytes=8 * 1024 * 1024),
+        cost_estimate=BRIEF,
+        name="normalized",
+    )(*in_hbm([hidden]), norm_gain.reshape(1, -1))
 
 
 def prepare_kernel(weight_ref, true_ids, sample_ids, *refs):
@@ -465,7 +479,7 @@
     def stat_row(block):
         return (2 * block[0] + block[1]) * lines + block[2]
 
-    normed = normalize(hidden, norm_gain)
+    normed = normalized(hidden, norm_gain)
 
     last = jnp.arange(input_ids.shape[0]) % group_len == group_len - 1
     targets = jnp.where(last, -1, jnp.roll(input_ids, -1) - first_col)
@@ -498,10 +512,11 @@
 
     for turn in range(lines):
         block = held[0, 0, turn]
+        following = to_z(block, 1) if turn + 1 < lines else None
         held[0, 1, turn] = to_x(block)
         held[1, 0, turn] = to_y(block)
         if turn + 1 < lines:
-            arrived = [to_z(block, 1), held[0, 1, turn], held[1, 0, turn]]
+            arrived = [following, held[0, 1, turn], held[1, 0, turn]]
             if turn == 0:
                 head_weight, *late_ids = prepared(head_weight, *late_ids, *early_ids, stats)
                 arrived += [*early_ids, *late_ids, rep_scalar, stats, head_weight]
@@ -511,8 +526,7 @@
                 middle_exp, stats = logits(
                     groups[split], stats, exp_rows=6 * length
                 )
-                arrived += [early_exp] + [held[1, 1, past] for past in range(split)]
-                arrived += [middle_exp]
+                arrived += [early_exp, middle_exp]
             arrived = lax.optimization_barrier(tuple(arrived))
             held[0, 0, turn + 1], held[0, 1, turn], held[1, 0, turn] = arrived[:3]
             if turn == 0:
@@ -521,7 +535,7 @@
             else:
                 early_exp = arrived[3]
                 if turn == split:
-                    held[1, 1, 0], held[1, 1, 1], middle_exp = arrived[4:]
+                    middle_exp = arrived[4]
             held[1, 1, turn] = diagonal(turn)
         if turn < split:
             size = len(groups[turn]) * length
@@ -534,20 +548,20 @@
     early[0] = after(early[0], held[0, 0, lines - 1])
     early = turned_features(rep_scalar, early, rows)
     early = [early[0], to_core(early[1])]
-    other_exps = [to_core(early_exp)]
     middle_exp, stats = logits(
         groups[split + 1], stats, held[0, 0, lines - 1], early[0],
         first_row=2 * length, exp_rows=6 * length, into=middle_exp,
     )
     held[0, 1, lines - 1] = after(held[0, 1, lines - 1], middle_exp)
     held[1, 1, lines - 1] = diagonal(lines - 1)
-    early_ids[0] = after(early_ids[0], middle_exp, held[0, 1, lines - 1], *other_exps)
+    early_ids[0] = after(early_ids[0], middle_exp, held[0, 1, lines - 1])
     sums = one_hot_sums(early, early_ids, columns)
     late = [held[block] for block in late_blocks]
     late[0] = after(late[0], *sums)
     late = turned_features(rep_scalar, late, rows)
     late = [late[0], to_core(late[1])]
-    other_exps.append(to_core(after(middle_exp, late[0])))
+    ready = lax.optimization_barrier((early_exp, middle_exp, late[0]))
+    other_exps = [to_core(exp) for exp in ready[:2]]
     last_exp, stats = logits(groups[-1], stats, late[0], *sums)
     exps = [early_exp, middle_exp, last_exp]
     across_stats, core_stats, both_stats = to_y(stats), to_core(stats), to_y_core(stats)

time: 122 us -> 119 us (0.975)
  waiting for transfers between devices: 18 us -> 14.2 us
  other arithmetic: 6.04 us -> 3.62 us
  starting transfers between devices: 26.6 us -> 28.1 us
    ppermute x7, waiting for transfers between devices: 10.2 us -> 4.35 us  [to_y(): return lax.ppermute(values, 'shard', swap_pairs(shards, 1))]
    ppermute x6, waiting for transfers between devices: 4.36 us -> 7.24 us  [to_x(): return lax.ppermute(values, 'rep', swap_pairs(reps, 2))]
    ppermute x6, starting transfers between devices: 7.92 us -> 9.61 us  [to_z(): return lax.ppermute(values, 'shard', shift_pairs(lines, along, 0))]
    pallas_call x0 -> x1, Pallas kernels: none -> 1.23 us  [normalized(): pl.pallas_call(normalize_kernel, out_shape=jax.ShapeDtypeStruct(hidden.sh...]
  transfers between devices with their start and end apart: 26 -> 26, of which waited for: 9 -> 10; matrix products, arithmetic and copies ran while one was open for 6% -> 6% of each run, Pallas kernels for 37% -> 38%
where the time goes in v9:
time: 119 us; the launch traced here: 118 us
  Pallas kernels  67.5 us (57%)
  starting transfers between devices  28.1 us (24%)
  waiting for transfers between devices  14.2 us (12%)
  local copies, waits for them, and re-layouts  3.89 us (3%)
  other arithmetic  3.62 us (3%)
    pallas_call x5, Pallas kernels, round_logits(): pl.pallas_call(functools.partial(logits_kernel, stat_rows, first_row, len...  30 us
    pallas_call x1, Pallas kernels, refresh_states(): pl.pallas_call(functools.partial(refresh_kernel, lines, length, block_row...  20 us
    ppermute x6, starting transfers between devices, to_z(): return lax.ppermute(values, 'shard', shift_pairs(lines, along, 0))  9.61 us
    ppermute x7, starting transfers between devices, to_y(): return lax.ppermute(values, 'shard', swap_pairs(shards, 1))  9.24 us
    pallas_call x1, Pallas kernels, one_hot_sums(): pl.pallas_call(functools.partial(one_hot_kernel, len(features)), grid=(co...  8.63 us
    ppermute x6, waiting for transfers between devices, to_x(): return lax.ppermute(values, 'rep', swap_pairs(reps, 2))  7.24 us
    ppermute x6, starting transfers between devices, to_x(): return lax.ppermute(values, 'rep', swap_pairs(reps, 2))  6.76 us
    pallas_call x1, Pallas kernels, prepared(): pl.pallas_call(prepare_kernel, in_specs=[pl.BlockSpec(memory_space=pltpu....  5.52 us
  transfers between devices with their start and end apart: 26, of which 10 were waited for; matrix products, arithmetic and copies ran while one was open for 6% of the time, Pallas kernels for 38%

profile of v9, /device:TPU:0, one launch (start us, length us, event | category | flops | bytes accessed | tf_op | source)
XLA Modules:
  0.0 118.2 jit_solution(10186684567247860653)
XLA Ops:
  0.6 0.7 reshape.138.gain_ref
  1.4 1.2 %normalized.1.refs_0_ = bf16[64,3584]{1,0:T(8,128)(2,1)S(1)} custom-call(bf16[64,3584]{1,0:T(8,128)(2,1)} %hidden_ref.1, f32[1,3584]{1,0:T(1,128)S(1)} %reshape.138.gain_ref), custom_call_target="tpu_custom_call" | custom-call | flops 1024 | bytes 1024 | tf_op jit(solution)/shard_map/normalized/pallas_call | solution.py:93
  2.6 3.0 %collective-permute-start.2 = (bf16[64,3584]{1,0:T(8,128)(2,1)S(1)}, bf16[64,3584]{1,0:T(8,128)(2,1)S(1)}, u32[]{:S(2)}, u32[]{:S(2)}) collective-permute-start(bf16[64,3584]{1,0:T(8,128)(2,1)S(1)} %normalized.1.refs_0_), channel_id=1, source_target_pairs={{0,1},{1,0},{2,3},{3,2},{4,5},{5,4},{6,7},{7,6},{8,9},{9,8},{10,11... | collective-permute-start | bytes 1376264 | tf_op jit(solution)/shard_map/ppermute | solution.py:457
  5.6 1.5 %collective-permute-start.1 = (bf16[64,3584]{1,0:T(8,128)(2,1)S(1)}, bf16[64,3584]{1,0:T(8,128)(2,1)S(1)}, u32[]{:S(2)}, u32[]{:S(2)}) collective-permute-start(bf16[64,3584]{1,0:T(8,128)(2,1)S(1)} %normalized.1.refs_0_), channel_id=1, source_target_pairs={{0,16},{8,24},{16,0},{24,8},{1,17},{9,25},{17,1},{25,9},{2,18},{10... | collective-permute-start | bytes 1376264 | tf_op jit(solution)/shard_map/ppermute | solution.py:451
  7.1 1.6 %collective-permute-start = (bf16[64,3584]{1,0:T(8,128)(2,1)S(1)}, bf16[64,3584]{1,0:T(8,128)(2,1)S(1)}, u32[]{:S(2)}, u32[]{:S(2)}) collective-permute-start(bf16[64,3584]{1,0:T(8,128)(2,1)S(1)} %normalized.1.refs_0_), channel_id=1, source_target_pairs={{0,2},{1,3},{2,4},{3,5},{4,6},{5,7},{6,0},{7,1},{8,10},{9,11},{10,... | collective-permute-start | bytes 1376264 | tf_op jit(solution)/shard_map/ppermute | solution.py:467
  8.7 0.7 fusion.4
  9.4 0.7 compare_and_fusion
  10.1 0.7 multiply_add_fusion
  10.7 1.2 %slice.31 = s32[1]{0:T(128)} slice(s32[2048]{0:T(1024)} %param.12), slice={[0:1]} | slice | bytes 8 | tf_op jit(solution)/shard_map/jit(_roll_static)/slice | solution.py:485
  11.9 0.8 slice.30
  12.8 0.7 broadcast_subtract_fusion
  13.6 0.7 fusion.1
  14.5 0.6 gather_fusion
  15.5 5.5 %prepared.1 = (bf16[3584,2048]{1,0:T(8,128)(2,1)S(1)}, s32[1280,128]{1,0:T(8,128)S(1)}, s32[1280,128]{1,0:T(8,128)S(1)}) custom-call(bf16[3584,2048]{1,0:T(8,128)(2,1)} %weight_ref.1, s32[1,1280]{1,0:T(1,128)S(1)} %squeeze.14.true_ids, s32[1,1280]{1,0:T(1,128)S(1)} %squeeze.15.sample_ids, s32[1,768]{1,0:T(1,128)S(1)} %squeeze.12.refs_0_.refs_2_, ...), custom_call_target="tpu_custom_call" | custom-call | flops 1024 | bytes 1024 | tf_op jit(solution)/shard_map/prepared/pallas_call | solution.py:127
  21.0 0.6 collective-permute-start.5
  21.6 0.5 collective-permute-start.4
  22.2 1.6 %collective-permute-start.3 = (bf16[64,3584]{1,0:T(8,128)(2,1)S(1)}, bf16[64,3584]{1,0:T(8,128)(2,1)S(1)}, u32[]{:S(2)}, u32[]{:S(2)}) collective-permute-start(bf16[64,3584]{1,0:T(8,128)(2,1)S(1)} %collective-permute-done.refs_0_.refs_3_), channel_id=1, source_target_pairs={{0,2},{1,3},{2,4},{3,5},{4,6},{5,7},{6,0},{7,1},{8,10},{9,11},{10,... | collective-permute-start | bytes 1376264 | tf_op jit(solution)/shard_map/ppermute | solution.py:467
  23.7 1.5 %collective-permute-start.9 = (bf16[64,3584]{1,0:T(8,128)(2,1)S(1)}, bf16[64,3584]{1,0:T(8,128)(2,1)S(1)}, u32[]{:S(2)}, u32[]{:S(2)}) collective-permute-start(bf16[64,3584]{1,0:T(8,128)(2,1)S(1)} %collective-permute-done.2.refs_2_), channel_id=1, source_target_pairs={{0,16},{8,24},{16,0},{24,8},{1,17},{9,25},{17,1},{25,9},{2,18},{10... | collective-permute-start | bytes 1376264 | tf_op jit(solution)/shard_map/ppermute | solution.py:451
  25.2 5.8 %round_logits.5 = (bf16[384,2048]{1,0:T(8,128)(2,1)}, f32[32,128]{1,0:T(8,128)S(1)}) custom-call(bf16[64,3584]{1,0:T(8,128)(2,1)S(1)} %normalized.1.refs_0_, bf16[64,3584]{1,0:T(8,128)(2,1)S(1)} %collective-permute-done.1.refs_1_, bf16[64,3584]{1,0:T(8,128)(2,1)S(1)} %collective-permute-done.2.refs_2_, ...), custom_call_target="tpu_custom_call" | custom-call | flops 1024 | bytes 1024 | tf_op jit(solution)/shard_map/round_logits/pallas_call | solution.py:206
  31.0 1.5 %collective-permute-done.5.refs_2_.refs_5_ = bf16[64,3584]{1,0:T(8,128)(2,1)S(1)} collective-permute-done((bf16[64,3584]{1,0:T(8,128)(2,1)S(1)}, bf16[64,3584]{1,0:T(8,128)(2,1)S(1)}, u32[]{:S(2)}, u32[]{:S(2)}) %collective-permute-start.5) | collective-permute-done | bytes 458784 | tf_op jit(solution)/shard_map/ppermute | solution.py:457
  32.5 2.5 %collective-permute-done.4.refs_1_.refs_4_ = bf16[64,3584]{1,0:T(8,128)(2,1)S(1)} collective-permute-done((bf16[64,3584]{1,0:T(8,128)(2,1)S(1)}, bf16[64,3584]{1,0:T(8,128)(2,1)S(1)}, u32[]{:S(2)}, u32[]{:S(2)}) %collective-permute-start.4) | collective-permute-done | bytes 458784 | tf_op jit(solution)/shard_map/ppermute | solution.py:451
  35.1 1.5 %collective-permute-start.8 = (bf16[64,3584]{1,0:T(8,128)(2,1)S(1)}, bf16[64,3584]{1,0:T(8,128)(2,1)S(1)}, u32[]{:S(2)}, u32[]{:S(2)}) collective-permute-start(bf16[64,3584]{1,0:T(8,128)(2,1)S(1)} %collective-permute-done.3.refs_0_), channel_id=1, source_target_pairs={{0,1},{1,0},{2,3},{3,2},{4,5},{5,4},{6,7},{7,6},{8,9},{9,8},{10,11... | collective-permute-start | bytes 1376264 | tf_op jit(solution)/shard_map/ppermute | solution.py:457
  36.6 1.2 %collective-permute-start.7 = (bf16[64,3584]{1,0:T(8,128)(2,1)S(1)}, bf16[64,3584]{1,0:T(8,128)(2,1)S(1)}, u32[]{:S(2)}, u32[]{:S(2)}) collective-permute-start(bf16[64,3584]{1,0:T(8,128)(2,1)S(1)} %collective-permute-done.3.refs_0_), channel_id=1, source_target_pairs={{0,16},{8,24},{16,0},{24,8},{1,17},{9,25},{17,1},{25,9},{2,18},{10... | collective-permute-start | bytes 1376264 | tf_op jit(solution)/shard_map/ppermute | solution.py:451
  37.8 0.9 collective-permute-start.6
  38.7 0.5 collective-permute-start.11
  39.2 5.8 %round_logits.6 = (bf16[384,2048]{1,0:T(8,128)(2,1)}, f32[32,128]{1,0:T(8,128)S(1)}) custom-call(bf16[64,3584]{1,0:T(8,128)(2,1)S(1)} %collective-permute-done.refs_0_.refs_3_, bf16[64,3584]{1,0:T(8,128)(2,1)S(1)} %collective-permute-done.4.refs_1_.refs_4_, ...), custom_call_target="tpu_custom_call", output_to_operand_aliasing={{0}: (5, {})} | custom-call | flops 1024 | bytes 1024 | tf_op jit(solution)/shard_map/round_logits/pallas_call | solution.py:206
  45.0 4.7 %round_logits.7 = (bf16[384,2048]{1,0:T(8,128)(2,1)}, f32[32,128]{1,0:T(8,128)S(1)}) custom-call(bf16[64,3584]{1,0:T(8,128)(2,1)S(1)} %collective-permute-done.3.refs_0_, bf16[64,3584]{1,0:T(8,128)(2,1)S(1)} %collective-permute-done.9.refs_1_, bf16[3584,2048]{1,0:T(8,128)(2,1)S(1)} %get-tuple-element.63.refs_3_.refs_2_.refs_4_, ...), custom_call_target="tpu_custom_call" | custom-call | flops 1024 | bytes 1024 | tf_op jit(solution)/shard_map/round_logits/pallas_call | solution.py:206
  49.8 2.7 %collective-permute-done.7.refs_0_.refs_2_ = bf16[64,3584]{1,0:T(8,128)(2,1)S(1)} collective-permute-done((bf16[64,3584]{1,0:T(8,128)(2,1)S(1)}, bf16[64,3584]{1,0:T(8,128)(2,1)S(1)}, u32[]{:S(2)}, u32[]{:S(2)}) %collective-permute-start.7) | collective-permute-done | bytes 458784 | tf_op jit(solution)/shard_map/ppermute | solution.py:451
  52.4 0.5 collective-permute-start.12
  53.0 0.9 turned_features.2
  53.9 1.6 %collective-permute-start.13 = (bf16[64,3584]{1,0:T(8,128)(2,1)S(1)}, bf16[64,3584]{1,0:T(8,128)(2,1)S(1)}, u32[]{:S(2)}, u32[]{:S(2)}) collective-permute-start(bf16[64,3584]{1,0:T(8,128)(2,1)S(1)} %collective-permute-done.6.refs_2_.refs_4_), channel_id=1, source_target_pairs={{0,1},{1,0},{2,3},{3,2},{4,5},{5,4},{6,7},{7,6},{8,9},{9,8},{10,11... | collective-permute-start | bytes 1376264 | tf_op jit(solution)/shard_map/ppermute | solution.py:457
  55.5 1.5 %collective-permute-start.14 = (bf16[64,3584]{1,0:T(8,128)(2,1)S(1)}, bf16[64,3584]{1,0:T(8,128)(2,1)S(1)}, u32[]{:S(2)}, u32[]{:S(2)}) collective-permute-start(bf16[64,3584]{1,0:T(8,128)(2,1)S(1)} %collective-permute-done.8.refs_1_.refs_3_), channel_id=1, source_target_pairs={{0,16},{8,24},{16,0},{24,8},{1,17},{9,25},{17,1},{25,9},{2,18},{10... | collective-permute-start | bytes 1376264 | tf_op jit(solution)/shard_map/ppermute | solution.py:451
  57.0 6.8 %round_logits.8 = (bf16[384,2048]{1,0:T(8,128)(2,1)}, f32[32,128]{1,0:T(8,128)S(1)}) custom-call(bf16[64,3584]{1,0:T(8,128)(2,1)S(1)} %collective-permute-done.7.refs_0_.refs_2_, bf16[64,3584]{1,0:T(8,128)(2,1)S(1)} %collective-permute-done.8.refs_1_.refs_3_, ...), custom_call_target="tpu_custom_call", output_to_operand_aliasing={{0}: (6, {})} | custom-call | flops 1024 | bytes 1024 | tf_op jit(solution)/shard_map/round_logits/pallas_call | solution.py:206
  63.9 2.0 %collective-permute-done.12.refs_6_.refs_0_ = bf16[64,3584]{1,0:T(8,128)(2,1)S(1)} collective-permute-done((bf16[64,3584]{1,0:T(8,128)(2,1)S(1)}, bf16[64,3584]{1,0:T(8,128)(2,1)S(1)}, u32[]{:S(2)}, u32[]{:S(2)}) %collective-permute-start.12) | collective-permute-done | bytes 458784 | tf_op jit(solution)/shard_map/ppermute | solution.py:451
  65.9 1.5 %collective-permute-start.15 = (bf16[64,3584]{1,0:T(8,128)(2,1)S(1)}, bf16[64,3584]{1,0:T(8,128)(2,1)S(1)}, u32[]{:S(2)}, u32[]{:S(2)}) collective-permute-start(bf16[64,3584]{1,0:T(8,128)(2,1)S(1)} %collective-permute-done.12.refs_6_.refs_0_), channel_id=1, source_target_pairs={{0,1},{1,0},{2,3},{3,2},{4,5},{5,4},{6,7},{7,6},{8,9},{9,8},{10,11... | collective-permute-start | bytes 1376264 | tf_op jit(solution)/shard_map/ppermute | solution.py:457
  67.4 8.6 %one_hot_sums.1 = (bf16[896,2048]{1,0:T(8,128)(2,1)}, bf16[896,2048]{1,0:T(8,128)(2,1)}) custom-call(bf16[896,384]{1,0:T(8,128)(2,1)S(1)} %get-tuple-element.77.refs_0_, bf16[896,384]{1,0:T(8,128)(2,1)S(1)} %collective-permute-done.10.refs_1_, s32[1,768]{1,0:T(1,128)S(1)} %squeeze.12.refs_0_.refs_2_, s32[1,768]{1,0:T(1,128)S(1)} %squeeze.13.refs_1_.refs_3_), custom_call_target="tpu_custom_call" | custom-call | flops 1024 | bytes 1024 | tf_op jit(solution)/shard_map/one_hot_sums/pallas_call | solution.py:285
  76.0 0.6 collective-permute-done.15.refs_9_.refs_3_
  76.7 1.3 %turned_features.3 = (bf16[896,640]{1,0:T(8,128)(2,1)S(1)}, bf16[896,640]{1,0:T(8,128)(2,1)S(1)}) custom-call(s32[1]{0:T(128)} %bitcast.5.rep_ref, bf16[64,3584]{1,0:T(8,128)(2,1)S(1)} %collective-permute-done.3.refs_0_, bf16[64,3584]{1,0:T(8,128)(2,1)S(1)} %collective-permute-done.9.refs_1_, bf16[64,3584]{1,0:T(8,128)(2,1)S(1)} %collective-permute-done.7.refs_0_.refs_2_, ...), custom_call_target="tpu_custom_call" | custom-call | flops 1024 | bytes 1024 | tf_op jit(solution)/shard_map/turned_features/pallas_call | solution.py:248
  78.7 6.8 %round_logits.9 = (bf16[256,2048]{1,0:T(8,128)(2,1)}, f32[32,128]{1,0:T(8,128)S(1)}) custom-call(bf16[64,3584]{1,0:T(8,128)(2,1)S(1)} %collective-permute-done.12.refs_6_.refs_0_, bf16[64,3584]{1,0:T(8,128)(2,1)S(1)} %collective-permute-done.13.refs_7_.refs_1_, bf16[64,3584]{1,0:T(8,128)(2,1)S(1)} %collective-permute-done.14.refs_8_.refs_2_, ...), custom_call_target="tpu_custom_call" | custom-call | flops 1024 | bytes 1024 | tf_op jit(solution)/shard_map/round_logits/pallas_call | solution.py:206
  85.5 1.6 %collective-permute-start.21 = (f32[32,128]{1,0:T(8,128)S(1)}, f32[32,128]{1,0:T(8,128)S(1)}, u32[]{:S(2)}, u32[]{:S(2)}) collective-permute-start(f32[32,128]{1,0:T(8,128)S(1)} %get-tuple-element.101.own_ref), channel_id=1, source_target_pairs={{0,9},{1,8},{2,11},{3,10},{4,13},{5,12},{6,15},{7,14},{8,1},{9,0},... | collective-permute-start | bytes 49160 | tf_op jit(solution)/shard_map/ppermute | solution.py:464
  87.2 0.5 collective-permute-start.19
  87.7 1.0 collective-permute-done.21.both_ref
  88.7 2.2 %collective-permute-done.19.across_ref = f32[32,128]{1,0:T(8,128)S(1)} collective-permute-done((f32[32,128]{1,0:T(8,128)S(1)}, f32[32,128]{1,0:T(8,128)S(1)}, u32[]{:S(2)}, u32[]{:S(2)}) %collective-permute-start.19) | collective-permute-done | bytes 16416 | tf_op jit(solution)/shard_map/ppermute | solution.py:457
  91.1 1.6 %collective-permute-start.25 = (f32[64,128]{1,0:T(8,128)S(1)}, f32[64,128]{1,0:T(8,128)S(1)}, u32[]{:S(2)}, u32[]{:S(2)}) collective-permute-start(f32[64,128]{1,0:T(8,128)S(1)} %get-tuple-element.102.refs_10_), channel_id=1, source_target_pairs={{0,2},{1,3},{2,4},{3,5},{4,6},{5,7},{6,0},{7,1},{8,10},{9,11},{10,... | collective-permute-start | bytes 98312 | tf_op jit(solution)/shard_map/ppermute | solution.py:467
  92.7 1.3 %collective-permute-start.24 = (f32[64,128]{1,0:T(8,128)S(1)}, f32[64,128]{1,0:T(8,128)S(1)}, u32[]{:S(2)}, u32[]{:S(2)}) collective-permute-start(f32[64,128]{1,0:T(8,128)S(1)} %get-tuple-element.102.refs_10_), channel_id=1, source_target_pairs={{0,4},{1,5},{2,6},{3,7},{4,0},{5,1},{6,2},{7,3},{8,12},{9,13},{10,... | collective-permute-start | bytes 98312 | tf_op jit(solution)/shard_map/ppermute | solution.py:467
  94.0 2.6 %collective-permute-start.23 = (f32[64,128]{1,0:T(8,128)S(1)}, f32[64,128]{1,0:T(8,128)S(1)}, u32[]{:S(2)}, u32[]{:S(2)}) collective-permute-start(f32[64,128]{1,0:T(8,128)S(1)} %get-tuple-element.102.refs_10_), channel_id=1, source_target_pairs={{0,6},{1,7},{2,0},{3,1},{4,2},{5,3},{6,4},{7,5},{8,14},{9,15},{10,... | collective-permute-start | bytes 98312 | tf_op jit(solution)/shard_map/ppermute | solution.py:467
  97.0 1.0 collective-permute-done.24.refs_12_
  98.2 20.0 %refresh_states.1 = (bf16[896,2048]{1,0:T(8,128)(2,1)}, bf16[896,2048]{1,0:T(8,128)(2,1)}, bf16[896,2048]{1,0:T(8,128)(2,1)}) custom-call(bf16[896,384]{1,0:T(8,128)(2,1)S(1)} %get-tuple-element.77.refs_0_, bf16[896,384]{1,0:T(8,128)(2,1)S(1)} %collective-permute-done.10.refs_1_, bf16[896,640]{1,0:T(8,128)(2,1)S(1)} %get-tuple-element.92.refs_2_, ...), custom_call_target="tpu_custom_call" | custom-call | flops 1024 | bytes 1024 | tf_op jit(solution)/shard_map/refresh_states/pallas_call | solution.py:414
  (44 shorter events, 2.2 us)
Async XLA Ops:
  2.6 18.4 %collective-permute-start.2 = (bf16[64,3584]{1,0:T(8,128)(2,1)S(1)}, bf16[64,3584]{1,0:T(8,128)(2,1)S(1)}, u32[]{:S(2)}, u32[]{:S(2)}) collective-permute-start(bf16[64,3584]{1,0:T(8,128)(2,1)S(1)} %normalized.1.refs_0_), channel_id=1, source_target_pairs={{0,1},{1,0},{2,3},{3,2},{4,5},{5,4},{6,7},{7,6},{8,9},{9,8},{10,11... | collective-permute-start | bytes 1376264 | tf_op jit(solution)/shard_map/ppermute | solution.py:457
  5.6 15.4 %collective-permute-start.1 = (bf16[64,3584]{1,0:T(8,128)(2,1)S(1)}, bf16[64,3584]{1,0:T(8,128)(2,1)S(1)}, u32[]{:S(2)}, u32[]{:S(2)}) collective-permute-start(bf16[64,3584]{1,0:T(8,128)(2,1)S(1)} %normalized.1.refs_0_), channel_id=1, source_target_pairs={{0,16},{8,24},{16,0},{24,8},{1,17},{9,25},{17,1},{25,9},{2,18},{10... | collective-permute-start | bytes 1376264 | tf_op jit(solution)/shard_map/ppermute | solution.py:451
  7.1 13.9 %collective-permute-start = (bf16[64,3584]{1,0:T(8,128)(2,1)S(1)}, bf16[64,3584]{1,0:T(8,128)(2,1)S(1)}, u32[]{:S(2)}, u32[]{:S(2)}) collective-permute-start(bf16[64,3584]{1,0:T(8,128)(2,1)S(1)} %normalized.1.refs_0_), channel_id=1, source_target_pairs={{0,2},{1,3},{2,4},{3,5},{4,6},{5,7},{6,0},{7,1},{8,10},{9,11},{10,... | collective-permute-start | bytes 1376264 | tf_op jit(solution)/shard_map/ppermute | solution.py:467
  21.0 11.5 %collective-permute-start.5 = (bf16[64,3584]{1,0:T(8,128)(2,1)S(1)}, bf16[64,3584]{1,0:T(8,128)(2,1)S(1)}, u32[]{:S(2)}, u32[]{:S(2)}) collective-permute-start(bf16[64,3584]{1,0:T(8,128)(2,1)S(1)} %collective-permute-done.refs_0_.refs_3_), channel_id=1, source_target_pairs={{0,1},{1,0},{2,3},{3,2},{4,5},{5,4},{6,7},{7,6},{8,9},{9,8},{10,11... | collective-permute-start | bytes 1376264 | tf_op jit(solution)/shard_map/ppermute | solution.py:457
  21.6 13.5 %collective-permute-start.4 = (bf16[64,3584]{1,0:T(8,128)(2,1)S(1)}, bf16[64,3584]{1,0:T(8,128)(2,1)S(1)}, u32[]{:S(2)}, u32[]{:S(2)}) collective-permute-start(bf16[64,3584]{1,0:T(8,128)(2,1)S(1)} %collective-permute-done.refs_0_.refs_3_), channel_id=1, source_target_pairs={{0,16},{8,24},{16,0},{24,8},{1,17},{9,25},{17,1},{25,9},{2,18},{10... | collective-permute-start | bytes 1376264 | tf_op jit(solution)/shard_map/ppermute | solution.py:451
  22.2 12.9 %collective-permute-start.3 = (bf16[64,3584]{1,0:T(8,128)(2,1)S(1)}, bf16[64,3584]{1,0:T(8,128)(2,1)S(1)}, u32[]{:S(2)}, u32[]{:S(2)}) collective-permute-start(bf16[64,3584]{1,0:T(8,128)(2,1)S(1)} %collective-permute-done.refs_0_.refs_3_), channel_id=1, source_target_pairs={{0,2},{1,3},{2,4},{3,5},{4,6},{5,7},{6,0},{7,1},{8,10},{9,11},{10,... | collective-permute-start | bytes 1376264 | tf_op jit(solution)/shard_map/ppermute | solution.py:467
  23.7 21.3 %collective-permute-start.9 = (bf16[64,3584]{1,0:T(8,128)(2,1)S(1)}, bf16[64,3584]{1,0:T(8,128)(2,1)S(1)}, u32[]{:S(2)}, u32[]{:S(2)}) collective-permute-start(bf16[64,3584]{1,0:T(8,128)(2,1)S(1)} %collective-permute-done.2.refs_2_), channel_id=1, source_target_pairs={{0,16},{8,24},{16,0},{24,8},{1,17},{9,25},{17,1},{25,9},{2,18},{10... | collective-permute-start | bytes 1376264 | tf_op jit(solution)/shard_map/ppermute | solution.py:451
  35.1 14.7 %collective-permute-start.8 = (bf16[64,3584]{1,0:T(8,128)(2,1)S(1)}, bf16[64,3584]{1,0:T(8,128)(2,1)S(1)}, u32[]{:S(2)}, u32[]{:S(2)}) collective-permute-start(bf16[64,3584]{1,0:T(8,128)(2,1)S(1)} %collective-permute-done.3.refs_0_), channel_id=1, source_target_pairs={{0,1},{1,0},{2,3},{3,2},{4,5},{5,4},{6,7},{7,6},{8,9},{9,8},{10,11... | collective-permute-start | bytes 1376264 | tf_op jit(solution)/shard_map/ppermute | solution.py:457
  36.6 15.8 %collective-permute-start.7 = (bf16[64,3584]{1,0:T(8,128)(2,1)S(1)}, bf16[64,3584]{1,0:T(8,128)(2,1)S(1)}, u32[]{:S(2)}, u32[]{:S(2)}) collective-permute-start(bf16[64,3584]{1,0:T(8,128)(2,1)S(1)} %collective-permute-done.3.refs_0_), channel_id=1, source_target_pairs={{0,16},{8,24},{16,0},{24,8},{1,17},{9,25},{17,1},{25,9},{2,18},{10... | collective-permute-start | bytes 1376264 | tf_op jit(solution)/shard_map/ppermute | solution.py:451
  37.8 14.6 %collective-permute-start.6 = (bf16[64,3584]{1,0:T(8,128)(2,1)S(1)}, bf16[64,3584]{1,0:T(8,128)(2,1)S(1)}, u32[]{:S(2)}, u32[]{:S(2)}) collective-permute-start(bf16[64,3584]{1,0:T(8,128)(2,1)S(1)} %collective-permute-done.3.refs_0_), channel_id=1, source_target_pairs={{0,2},{1,3},{2,4},{3,5},{4,6},{5,7},{6,0},{7,1},{8,10},{9,11},{10,... | collective-permute-start | bytes 1376264 | tf_op jit(solution)/shard_map/ppermute | solution.py:467
  38.7 18.3 %collective-permute-start.11 = (bf16[64,3584]{1,0:T(8,128)(2,1)S(1)}, bf16[64,3584]{1,0:T(8,128)(2,1)S(1)}, u32[]{:S(2)}, u32[]{:S(2)}) collective-permute-start(bf16[64,3584]{1,0:T(8,128)(2,1)S(1)} %collective-permute-done.4.refs_1_.refs_4_), channel_id=1, source_target_pairs={{0,1},{1,0},{2,3},{3,2},{4,5},{5,4},{6,7},{7,6},{8,9},{9,8},{10,11... | collective-permute-start | bytes 1376264 | tf_op jit(solution)/shard_map/ppermute | solution.py:457
  52.4 13.5 %collective-permute-start.12 = (bf16[64,3584]{1,0:T(8,128)(2,1)S(1)}, bf16[64,3584]{1,0:T(8,128)(2,1)S(1)}, u32[]{:S(2)}, u32[]{:S(2)}) collective-permute-start(bf16[64,3584]{1,0:T(8,128)(2,1)S(1)} %collective-permute-done.6.refs_2_.refs_4_), channel_id=1, source_target_pairs={{0,16},{8,24},{16,0},{24,8},{1,17},{9,25},{17,1},{25,9},{2,18},{10... | collective-permute-start | bytes 1376264 | tf_op jit(solution)/shard_map/ppermute | solution.py:451
  53.8 13.6 %collective-permute-start.10 = (bf16[896,384]{1,0:T(8,128)(2,1)S(1)}, bf16[896,384]{1,0:T(8,128)(2,1)S(1)}, u32[]{:S(2)}, u32[]{:S(2)}) collective-permute-start(bf16[896,384]{1,0:T(8,128)(2,1)S(1)} %get-tuple-element.78), channel_id=1, source_target_pairs={{0,8},{8,0},{16,24},{24,16},{1,9},{9,1},{17,25},{25,17},{2,10},{10... | collective-permute-start | bytes 2064392 | tf_op jit(solution)/shard_map/ppermute | solution.py:454
  53.9 22.1 %collective-permute-start.13 = (bf16[64,3584]{1,0:T(8,128)(2,1)S(1)}, bf16[64,3584]{1,0:T(8,128)(2,1)S(1)}, u32[]{:S(2)}, u32[]{:S(2)}) collective-permute-start(bf16[64,3584]{1,0:T(8,128)(2,1)S(1)} %collective-permute-done.6.refs_2_.refs_4_), channel_id=1, source_target_pairs={{0,1},{1,0},{2,3},{3,2},{4,5},{5,4},{6,7},{7,6},{8,9},{9,8},{10,11... | collective-permute-start | bytes 1376264 | tf_op jit(solution)/shard_map/ppermute | solution.py:457
  55.5 20.5 %collective-permute-start.14 = (bf16[64,3584]{1,0:T(8,128)(2,1)S(1)}, bf16[64,3584]{1,0:T(8,128)(2,1)S(1)}, u32[]{:S(2)}, u32[]{:S(2)}) collective-permute-start(bf16[64,3584]{1,0:T(8,128)(2,1)S(1)} %collective-permute-done.8.refs_1_.refs_3_), channel_id=1, source_target_pairs={{0,16},{8,24},{16,0},{24,8},{1,17},{9,25},{17,1},{25,9},{2,18},{10... | collective-permute-start | bytes 1376264 | tf_op jit(solution)/shard_map/ppermute | solution.py:451
  63.8 14.2 %copy-start.1 = (bf16[384,2048]{1,0:T(8,128)(2,1)S(1)}, bf16[384,2048]{1,0:T(8,128)(2,1)}, u32[]{:S(2)}) copy-start(bf16[384,2048]{1,0:T(8,128)(2,1)} %get-tuple-element.98.refs_4_) | copy-start | bytes 4718596
  63.8 14.2 %copy-start = (bf16[384,2048]{1,0:T(8,128)(2,1)S(1)}, bf16[384,2048]{1,0:T(8,128)(2,1)}, u32[]{:S(2)}) copy-start(bf16[384,2048]{1,0:T(8,128)(2,1)} %get-tuple-element.99.refs_5_) | copy-start | bytes 4718596
  65.9 10.8 %collective-permute-start.15 = (bf16[64,3584]{1,0:T(8,128)(2,1)S(1)}, bf16[64,3584]{1,0:T(8,128)(2,1)S(1)}, u32[]{:S(2)}, u32[]{:S(2)}) collective-permute-start(bf16[64,3584]{1,0:T(8,128)(2,1)S(1)} %collective-permute-done.12.refs_6_.refs_0_), channel_id=1, source_target_pairs={{0,1},{1,0},{2,3},{3,2},{4,5},{5,4},{6,7},{7,6},{8,9},{9,8},{10,11... | collective-permute-start | bytes 1376264 | tf_op jit(solution)/shard_map/ppermute | solution.py:457
  78.0 9.7 %collective-permute-start.17 = (bf16[384,2048]{1,0:T(8,128)(2,1)S(1)}, bf16[384,2048]{1,0:T(8,128)(2,1)S(1)}, u32[]{:S(2)}, u32[]{:S(2)}) collective-permute-start(bf16[384,2048]{1,0:T(8,128)(2,1)S(1)} %copy-done.1), channel_id=1, source_target_pairs={{0,8},{8,0},{16,24},{24,16},{1,9},{9,1},{17,25},{25,17},{2,10},{10... | collective-permute-start | bytes 4718600 | tf_op jit(solution)/shard_map/ppermute | solution.py:454
  78.1 9.6 %collective-permute-start.18 = (bf16[384,2048]{1,0:T(8,128)(2,1)S(1)}, bf16[384,2048]{1,0:T(8,128)(2,1)S(1)}, u32[]{:S(2)}, u32[]{:S(2)}) collective-permute-start(bf16[384,2048]{1,0:T(8,128)(2,1)S(1)} %copy-done), channel_id=1, source_target_pairs={{0,8},{8,0},{16,24},{24,16},{1,9},{9,1},{17,25},{25,17},{2,10},{10... | collective-permute-start | bytes 4718600 | tf_op jit(solution)/shard_map/ppermute | solution.py:454
  78.6 8.6 %collective-permute-start.16 = (bf16[896,640]{1,0:T(8,128)(2,1)S(1)}, bf16[896,640]{1,0:T(8,128)(2,1)S(1)}, u32[]{:S(2)}, u32[]{:S(2)}) collective-permute-start(bf16[896,640]{1,0:T(8,128)(2,1)S(1)} %get-tuple-element.93), channel_id=1, source_target_pairs={{0,8},{8,0},{16,24},{24,16},{1,9},{9,1},{17,25},{25,17},{2,10},{10... | collective-permute-start | bytes 3440648 | tf_op jit(solution)/shard_map/ppermute | solution.py:454
  85.5 3.2 %collective-permute-start.21 = (f32[32,128]{1,0:T(8,128)S(1)}, f32[32,128]{1,0:T(8,128)S(1)}, u32[]{:S(2)}, u32[]{:S(2)}) collective-permute-start(f32[32,128]{1,0:T(8,128)S(1)} %get-tuple-element.101.own_ref), channel_id=1, source_target_pairs={{0,9},{1,8},{2,11},{3,10},{4,13},{5,12},{6,15},{7,14},{8,1},{9,0},... | collective-permute-start | bytes 49160 | tf_op jit(solution)/shard_map/ppermute | solution.py:464
  87.1 1.6 %collective-permute-start.20 = (f32[32,128]{1,0:T(8,128)S(1)}, f32[32,128]{1,0:T(8,128)S(1)}, u32[]{:S(2)}, u32[]{:S(2)}) collective-permute-start(f32[32,128]{1,0:T(8,128)S(1)} %get-tuple-element.101.own_ref), channel_id=1, source_target_pairs={{0,8},{8,0},{16,24},{24,16},{1,9},{9,1},{17,25},{25,17},{2,10},{10... | collective-permute-start | bytes 49160 | tf_op jit(solution)/shard_map/ppermute | solution.py:454
  87.2 3.7 %collective-permute-start.19 = (f32[32,128]{1,0:T(8,128)S(1)}, f32[32,128]{1,0:T(8,128)S(1)}, u32[]{:S(2)}, u32[]{:S(2)}) collective-permute-start(f32[32,128]{1,0:T(8,128)S(1)} %get-tuple-element.101.own_ref), channel_id=1, source_target_pairs={{0,1},{1,0},{2,3},{3,2},{4,5},{5,4},{6,7},{7,6},{8,9},{9,8},{10,11... | collective-permute-start | bytes 49160 | tf_op jit(solution)/shard_map/ppermute | solution.py:457
  91.0 7.2 %collective-permute-start.22 = (bf16[256,2048]{1,0:T(8,128)(2,1)}, bf16[256,2048]{1,0:T(8,128)(2,1)S(1)}, u32[]{:S(2)}, u32[]{:S(2)}) collective-permute-start(bf16[256,2048]{1,0:T(8,128)(2,1)} %get-tuple-element.103.refs_6_), channel_id=1, source_target_pairs={{0,8},{8,0},{16,24},{24,16},{1,9},{9,1},{17,25},{25,17},{2,10},{10... | collective-permute-start | bytes 3145736 | tf_op jit(solution)/shard_map/ppermute | solution.py:454
  91.1 5.9 %collective-permute-start.25 = (f32[64,128]{1,0:T(8,128)S(1)}, f32[64,128]{1,0:T(8,128)S(1)}, u32[]{:S(2)}, u32[]{:S(2)}) collective-permute-start(f32[64,128]{1,0:T(8,128)S(1)} %get-tuple-element.102.refs_10_), channel_id=1, source_target_pairs={{0,2},{1,3},{2,4},{3,5},{4,6},{5,7},{6,0},{7,1},{8,10},{9,11},{10,... | collective-permute-start | bytes 98312 | tf_op jit(solution)/shard_map/ppermute | solution.py:467
  92.7 5.3 %collective-permute-start.24 = (f32[64,128]{1,0:T(8,128)S(1)}, f32[64,128]{1,0:T(8,128)S(1)}, u32[]{:S(2)}, u32[]{:S(2)}) collective-permute-start(f32[64,128]{1,0:T(8,128)S(1)} %get-tuple-element.102.refs_10_), channel_id=1, source_target_pairs={{0,4},{1,5},{2,6},{3,7},{4,0},{5,1},{6,2},{7,3},{8,12},{9,13},{10,... | collective-permute-start | bytes 98312 | tf_op jit(solution)/shard_map/ppermute | solution.py:467
  94.0 4.2 %collective-permute-start.23 = (f32[64,128]{1,0:T(8,128)S(1)}, f32[64,128]{1,0:T(8,128)S(1)}, u32[]{:S(2)}, u32[]{:S(2)}) collective-permute-start(f32[64,128]{1,0:T(8,128)S(1)} %get-tuple-element.102.refs_10_), channel_id=1, source_target_pairs={{0,6},{1,7},{2,0},{3,1},{4,2},{5,3},{6,4},{7,5},{8,14},{9,15},{10,... | collective-permute-start | bytes 98312 | tf_op jit(solution)/shard_map/ppermute | solution.py:467

commit v10 on v9

--- a/solution.py
+++ b/solution.py
@@ -96,7 +96,7 @@
         compiler_params=pltpu.CompilerParams(vmem_limit_bytes=8 * 1024 * 1024),
         cost_estimate=BRIEF,
         name="normalized",
-    )(*in_hbm([hidden]), norm_gain.reshape(1, -1))
+    )(*in_hbm([hidden]), norm_gain)
 
 
 def prepare_kernel(weight_ref, true_ids, sample_ids, *refs):
@@ -500,7 +500,8 @@
 
     def logits(group, stats, *gates, first_row=0, exp_rows=None, into=None):
         blocks = [held[block] for block in group]
-        blocks[0] = after(blocks[0], *gates)
+        at = -1 if group is groups[0] else 0
+        blocks[at] = after(blocks[at], *gates)
         rows = [stat_row(block) for block in group]
         exp_rows = exp_rows or len(group) * length
         return round_logits(blocks, rows, head_weight, stats, first_row, exp_rows, into)
@@ -518,8 +519,7 @@
         if turn + 1 < lines:
             arrived = [following, held[0, 1, turn], held[1, 0, turn]]
             if turn == 0:
-                head_weight, *late_ids = prepared(head_weight, *late_ids, *early_ids, stats)
-                arrived += [*early_ids, *late_ids, rep_scalar, stats, head_weight]
+                arrived = [following, *early_ids, *late_ids, stats]
             elif turn < split:
                 arrived += [early_exp]
             else:
@@ -528,11 +528,13 @@
                 )
                 arrived += [early_exp, middle_exp]
             arrived = lax.optimization_barrier(tuple(arrived))
-            held[0, 0, turn + 1], held[0, 1, turn], held[1, 0, turn] = arrived[:3]
+            held[0, 0, turn + 1] = arrived[0]
             if turn == 0:
-                early_ids, late_ids = list(arrived[3:5]), list(arrived[5:7])
-                rep_scalar, stats, head_weight = arrived[7:]
+                early_ids, late_ids = list(arrived[1:3]), list(arrived[3:5])
+                stats, = arrived[5:]
+                head_weight, *late_ids = prepared(head_weight, *late_ids, stats)
             else:
+                held[0, 1, turn], held[1, 0, turn] = arrived[1:3]
                 early_exp = arrived[3]
                 if turn == split:
                     middle_exp = arrived[4]
@@ -545,7 +547,7 @@
             )
 
     early = [held[block] for block in early_blocks]
-    early[0] = after(early[0], held[0, 0, lines - 1])
+    early[-1] = after(early[-1], held[0, 0, lines - 1])
     early = turned_features(rep_scalar, early, rows)
     early = [early[0], to_core(early[1])]
     middle_exp, stats = logits(

time: 119 us -> 116 us (0.975)
  starting transfers between devices: 28.1 us -> 24.3 us
    ppermute x6, waiting for transfers between devices: 1.6 us -> 5.96 us  [to_z(): return lax.ppermute(values, 'shard', shift_pairs(lines, along, 0))]
    ppermute x6, waiting for transfers between devices: 7.24 us -> 4.77 us  [to_x(): return lax.ppermute(values, 'rep', swap_pairs(reps, 2))]
    ppermute x6, starting transfers between devices: 9.61 us -> 8.24 us  [to_z(): return lax.ppermute(values, 'shard', shift_pairs(lines, along, 0))]
    ppermute x7, starting transfers between devices: 9.24 us -> 7.91 us  [to_y(): return lax.ppermute(values, 'shard', swap_pairs(shards, 1))]
  transfers between devices with their start and end apart: 26 -> 26, of which waited for: 10 -> 9; matrix products, arithmetic and copies ran while one was open for 6% -> 6% of each run, Pallas kernels for 38% -> 39%
where the time goes in v10:
time: 116 us; the launch traced here: 115 us
  Pallas kernels  67.6 us (58%)
  starting transfers between devices  24.3 us (21%)
  waiting for transfers between devices  15.3 us (13%)
  local copies, waits for them, and re-layouts  3.87 us (3%)
  other arithmetic  3.62 us (3%)
    pallas_call x5, Pallas kernels, round_logits(): pl.pallas_call(functools.partial(logits_kernel, stat_rows, first_row, len...  30 us
    pallas_call x1, Pallas kernels, refresh_states(): pl.pallas_call(functools.partial(refresh_kernel, lines, length, block_row...  20 us
    pallas_call x1, Pallas kernels, one_hot_sums(): pl.pallas_call(functools.partial(one_hot_kernel, len(features)), grid=(co...  8.66 us
    ppermute x6, starting transfers between devices, to_z(): return lax.ppermute(values, 'shard', shift_pairs(lines, along, 0))  8.24 us
    ppermute x7, starting transfers between devices, to_y(): return lax.ppermute(values, 'shard', swap_pairs(shards, 1))  7.91 us
    ppermute x6, starting transfers between devices, to_x(): return lax.ppermute(values, 'rep', swap_pairs(reps, 2))  6.67 us
    ppermute x6, waiting for transfers between devices, to_z(): return lax.ppermute(values, 'shard', shift_pairs(lines, along, 0))  5.96 us
    pallas_call x1, Pallas kernels, prepared(): pl.pallas_call(prepare_kernel, in_specs=[pl.BlockSpec(memory_space=pltpu....  5.52 us
  transfers between devices with their start and end apart: 26, of which 9 were waited for; matrix products, arithmetic and copies ran while one was open for 6% of the time, Pallas kernels for 39%

profile of v10, /device:TPU:0, one launch (start us, length us, event | category | flops | bytes accessed | tf_op | source)
XLA Modules:
  0.0 115.5 jit_solution(11641763579536395973)
XLA Ops:
  0.6 0.7 copy-done
  1.3 1.2 %normalized.1.refs_0_ = bf16[64,3584]{1,0:T(8,128)(2,1)S(1)} custom-call(bf16[64,3584]{1,0:T(8,128)(2,1)} %hidden_ref.1, f32[3584]{0:T(1024)S(1)} %copy-done), custom_call_target="tpu_custom_call" | custom-call | flops 1024 | bytes 1024 | tf_op jit(solution)/shard_map/normalized/pallas_call | solution.py:93
  2.6 3.1 %collective-permute-start.2 = (bf16[64,3584]{1,0:T(8,128)(2,1)S(1)}, bf16[64,3584]{1,0:T(8,128)(2,1)S(1)}, u32[]{:S(2)}, u32[]{:S(2)}) collective-permute-start(bf16[64,3584]{1,0:T(8,128)(2,1)S(1)} %normalized.1.refs_0_), channel_id=1, source_target_pairs={{0,2},{1,3},{2,4},{3,5},{4,6},{5,7},{6,0},{7,1},{8,10},{9,11},{10,... | collective-permute-start | bytes 1376264 | tf_op jit(solution)/shard_map/ppermute | solution.py:467
  5.7 1.5 %collective-permute-start.1 = (bf16[64,3584]{1,0:T(8,128)(2,1)S(1)}, bf16[64,3584]{1,0:T(8,128)(2,1)S(1)}, u32[]{:S(2)}, u32[]{:S(2)}) collective-permute-start(bf16[64,3584]{1,0:T(8,128)(2,1)S(1)} %normalized.1.refs_0_), channel_id=1, source_target_pairs={{0,1},{1,0},{2,3},{3,2},{4,5},{5,4},{6,7},{7,6},{8,9},{9,8},{10,11... | collective-permute-start | bytes 1376264 | tf_op jit(solution)/shard_map/ppermute | solution.py:457
  7.2 1.5 %collective-permute-start = (bf16[64,3584]{1,0:T(8,128)(2,1)S(1)}, bf16[64,3584]{1,0:T(8,128)(2,1)S(1)}, u32[]{:S(2)}, u32[]{:S(2)}) collective-permute-start(bf16[64,3584]{1,0:T(8,128)(2,1)S(1)} %normalized.1.refs_0_), channel_id=1, source_target_pairs={{0,16},{8,24},{16,0},{24,8},{1,17},{9,25},{17,1},{25,9},{2,18},{10... | collective-permute-start | bytes 1376264 | tf_op jit(solution)/shard_map/ppermute | solution.py:451
  8.7 0.7 fusion.4
  9.3 0.7 compare_and_fusion
  10.0 0.7 multiply_add_fusion
  10.7 1.2 %slice.31 = s32[1]{0:T(128)} slice(s32[2048]{0:T(1024)} %param.12), slice={[0:1]} | slice | bytes 8 | tf_op jit(solution)/shard_map/jit(_roll_static)/slice | solution.py:485
  11.9 0.8 slice.30
  12.8 0.7 broadcast_subtract_fusion
  13.6 0.7 fusion.1
  14.4 0.6 gather_fusion
  15.5 2.7 %collective-permute-done.2.refs_0_.refs_3_ = bf16[64,3584]{1,0:T(8,128)(2,1)S(1)} collective-permute-done((bf16[64,3584]{1,0:T(8,128)(2,1)S(1)}, bf16[64,3584]{1,0:T(8,128)(2,1)S(1)}, u32[]{:S(2)}, u32[]{:S(2)}) %collective-permute-start.2) | collective-permute-done | bytes 458784 | tf_op jit(solution)/shard_map/ppermute | solution.py:467
  18.2 1.5 %collective-permute-start.5 = (bf16[64,3584]{1,0:T(8,128)(2,1)S(1)}, bf16[64,3584]{1,0:T(8,128)(2,1)S(1)}, u32[]{:S(2)}, u32[]{:S(2)}) collective-permute-start(bf16[64,3584]{1,0:T(8,128)(2,1)S(1)} %collective-permute-done.2.refs_0_.refs_3_), channel_id=1, source_target_pairs={{0,1},{1,0},{2,3},{3,2},{4,5},{5,4},{6,7},{7,6},{8,9},{9,8},{10,11... | collective-permute-start | bytes 1376264 | tf_op jit(solution)/shard_map/ppermute | solution.py:457
  19.7 1.5 %collective-permute-start.4 = (bf16[64,3584]{1,0:T(8,128)(2,1)S(1)}, bf16[64,3584]{1,0:T(8,128)(2,1)S(1)}, u32[]{:S(2)}, u32[]{:S(2)}) collective-permute-start(bf16[64,3584]{1,0:T(8,128)(2,1)S(1)} %collective-permute-done.2.refs_0_.refs_3_), channel_id=1, source_target_pairs={{0,16},{8,24},{16,0},{24,8},{1,17},{9,25},{17,1},{25,9},{2,18},{10... | collective-permute-start | bytes 1376264 | tf_op jit(solution)/shard_map/ppermute | solution.py:451
  21.2 5.5 %prepared.1 = (bf16[3584,2048]{1,0:T(8,128)(2,1)S(1)}, s32[1280,128]{1,0:T(8,128)S(1)}, s32[1280,128]{1,0:T(8,128)S(1)}) custom-call(bf16[3584,2048]{1,0:T(8,128)(2,1)} %weight_ref.1, s32[1,1280]{1,0:T(1,128)S(1)} %squeeze.14.true_ids, s32[1,1280]{1,0:T(1,128)S(1)} %squeeze.15.sample_ids, f32[32,128]{1,0:T(8,128)S(1)} %broadcast_in_dim.20.refs_0_.refs_4_), custom_call_target="tpu_custom_call" | custom-call | flops 1024 | bytes 1024 | tf_op jit(solution)/shard_map/prepared/pallas_call | solution.py:127
  26.7 0.6 collective-permute-start.9
  27.4 5.8 %round_logits.5 = (bf16[384,2048]{1,0:T(8,128)(2,1)}, f32[32,128]{1,0:T(8,128)S(1)}) custom-call(bf16[64,3584]{1,0:T(8,128)(2,1)S(1)} %normalized.1.refs_0_, bf16[64,3584]{1,0:T(8,128)(2,1)S(1)} %collective-permute-done.refs_1_, bf16[64,3584]{1,0:T(8,128)(2,1)S(1)} %collective-permute-done.1.refs_2_, ...), custom_call_target="tpu_custom_call" | custom-call | flops 1024 | bytes 1024 | tf_op jit(solution)/shard_map/round_logits/pallas_call | solution.py:206
  33.2 0.7 collective-permute-done.3.refs_0_
  33.9 0.5 collective-permute-start.8
  34.4 0.8 collective-permute-start.7
  35.2 1.3 %collective-permute-start.6 = (bf16[64,3584]{1,0:T(8,128)(2,1)S(1)}, bf16[64,3584]{1,0:T(8,128)(2,1)S(1)}, u32[]{:S(2)}, u32[]{:S(2)}) collective-permute-start(bf16[64,3584]{1,0:T(8,128)(2,1)S(1)} %collective-permute-done.3.refs_0_), channel_id=1, source_target_pairs={{0,2},{1,3},{2,4},{3,5},{4,6},{5,7},{6,0},{7,1},{8,10},{9,11},{10,... | collective-permute-start | bytes 1376264 | tf_op jit(solution)/shard_map/ppermute | solution.py:467
  36.5 1.5 %collective-permute-start.11 = (bf16[64,3584]{1,0:T(8,128)(2,1)S(1)}, bf16[64,3584]{1,0:T(8,128)(2,1)S(1)}, u32[]{:S(2)}, u32[]{:S(2)}) collective-permute-start(bf16[64,3584]{1,0:T(8,128)(2,1)S(1)} %collective-permute-done.4.refs_1_.refs_4_), channel_id=1, source_target_pairs={{0,1},{1,0},{2,3},{3,2},{4,5},{5,4},{6,7},{7,6},{8,9},{9,8},{10,11... | collective-permute-start | bytes 1376264 | tf_op jit(solution)/shard_map/ppermute | solution.py:457
  38.0 5.8 %round_logits.6 = (bf16[384,2048]{1,0:T(8,128)(2,1)}, f32[32,128]{1,0:T(8,128)S(1)}) custom-call(bf16[64,3584]{1,0:T(8,128)(2,1)S(1)} %collective-permute-done.2.refs_0_.refs_3_, bf16[64,3584]{1,0:T(8,128)(2,1)S(1)} %collective-permute-done.4.refs_1_.refs_4_, ...), custom_call_target="tpu_custom_call", output_to_operand_aliasing={{0}: (5, {})} | custom-call | flops 1024 | bytes 1024 | tf_op jit(solution)/shard_map/round_logits/pallas_call | solution.py:206
  43.8 4.7 %round_logits.7 = (bf16[384,2048]{1,0:T(8,128)(2,1)}, f32[32,128]{1,0:T(8,128)S(1)}) custom-call(bf16[64,3584]{1,0:T(8,128)(2,1)S(1)} %collective-permute-done.3.refs_0_, bf16[64,3584]{1,0:T(8,128)(2,1)S(1)} %collective-permute-done.9.refs_1_, bf16[3584,2048]{1,0:T(8,128)(2,1)S(1)} %get-tuple-element.56.refs_3_.refs_2_.refs_4_, ...), custom_call_target="tpu_custom_call" | custom-call | flops 1024 | bytes 1024 | tf_op jit(solution)/shard_map/round_logits/pallas_call | solution.py:206
  48.6 2.0 %collective-permute-done.7.refs_0_.refs_2_ = bf16[64,3584]{1,0:T(8,128)(2,1)S(1)} collective-permute-done((bf16[64,3584]{1,0:T(8,128)(2,1)S(1)}, bf16[64,3584]{1,0:T(8,128)(2,1)S(1)}, u32[]{:S(2)}, u32[]{:S(2)}) %collective-permute-start.7) | collective-permute-done | bytes 458784 | tf_op jit(solution)/shard_map/ppermute | solution.py:451
  50.6 1.5 %collective-permute-start.12 = (bf16[64,3584]{1,0:T(8,128)(2,1)S(1)}, bf16[64,3584]{1,0:T(8,128)(2,1)S(1)}, u32[]{:S(2)}, u32[]{:S(2)}) collective-permute-start(bf16[64,3584]{1,0:T(8,128)(2,1)S(1)} %collective-permute-done.6.refs_2_.refs_4_), channel_id=1, source_target_pairs={{0,16},{8,24},{16,0},{24,8},{1,17},{9,25},{17,1},{25,9},{2,18},{10... | collective-permute-start | bytes 1376264 | tf_op jit(solution)/shard_map/ppermute | solution.py:451
  52.1 0.9 turned_features.2
  53.0 0.6 collective-permute-start.13
  53.6 0.8 collective-permute-start.14
  54.4 6.9 %round_logits.8 = (bf16[384,2048]{1,0:T(8,128)(2,1)}, f32[32,128]{1,0:T(8,128)S(1)}) custom-call(bf16[64,3584]{1,0:T(8,128)(2,1)S(1)} %collective-permute-done.7.refs_0_.refs_2_, bf16[64,3584]{1,0:T(8,128)(2,1)S(1)} %collective-permute-done.8.refs_1_.refs_3_, ...), custom_call_target="tpu_custom_call", output_to_operand_aliasing={{0}: (6, {})} | custom-call | flops 1024 | bytes 1024 | tf_op jit(solution)/shard_map/round_logits/pallas_call | solution.py:206
  61.3 2.8 %collective-permute-done.12.refs_6_.refs_0_ = bf16[64,3584]{1,0:T(8,128)(2,1)S(1)} collective-permute-done((bf16[64,3584]{1,0:T(8,128)(2,1)S(1)}, bf16[64,3584]{1,0:T(8,128)(2,1)S(1)}, u32[]{:S(2)}, u32[]{:S(2)}) %collective-permute-start.12) | collective-permute-done | bytes 458784 | tf_op jit(solution)/shard_map/ppermute | solution.py:451
  64.0 0.8 collective-permute-start.15
  64.8 8.7 %one_hot_sums.1 = (bf16[896,2048]{1,0:T(8,128)(2,1)}, bf16[896,2048]{1,0:T(8,128)(2,1)}) custom-call(bf16[896,384]{1,0:T(8,128)(2,1)S(1)} %get-tuple-element.69.refs_0_, bf16[896,384]{1,0:T(8,128)(2,1)S(1)} %collective-permute-done.10.refs_1_, s32[1,768]{1,0:T(1,128)S(1)} %squeeze.12.refs_2_, s32[1,768]{1,0:T(1,128)S(1)} %squeeze.13.refs_3_), custom_call_target="tpu_custom_call" | custom-call | flops 1024 | bytes 1024 | tf_op jit(solution)/shard_map/one_hot_sums/pallas_call | solution.py:285
  73.4 2.3 %collective-permute-done.15.refs_9_.refs_3_ = bf16[64,3584]{1,0:T(8,128)(2,1)S(1)} collective-permute-done((bf16[64,3584]{1,0:T(8,128)(2,1)S(1)}, bf16[64,3584]{1,0:T(8,128)(2,1)S(1)}, u32[]{:S(2)}, u32[]{:S(2)}) %collective-permute-start.15) | collective-permute-done | bytes 458784 | tf_op jit(solution)/shard_map/ppermute | solution.py:457
  75.8 1.3 %turned_features.3 = (bf16[896,640]{1,0:T(8,128)(2,1)S(1)}, bf16[896,640]{1,0:T(8,128)(2,1)S(1)}) custom-call(s32[1]{0:T(128)} %bitcast.rep_ref, bf16[64,3584]{1,0:T(8,128)(2,1)S(1)} %collective-permute-done.3.refs_0_, bf16[64,3584]{1,0:T(8,128)(2,1)S(1)} %collective-permute-done.9.refs_1_, bf16[64,3584]{1,0:T(8,128)(2,1)S(1)} %collective-permute-done.7.refs_0_.refs_2_, ...), custom_call_target="tpu_custom_call" | custom-call | flops 1024 | bytes 1024 | tf_op jit(solution)/shard_map/turned_features/pallas_call | solution.py:248
  77.2 0.5 collective-permute-start.18
  77.8 6.8 %round_logits.9 = (bf16[256,2048]{1,0:T(8,128)(2,1)}, f32[32,128]{1,0:T(8,128)S(1)}) custom-call(bf16[64,3584]{1,0:T(8,128)(2,1)S(1)} %collective-permute-done.12.refs_6_.refs_0_, bf16[64,3584]{1,0:T(8,128)(2,1)S(1)} %collective-permute-done.13.refs_7_.refs_1_, bf16[64,3584]{1,0:T(8,128)(2,1)S(1)} %collective-permute-done.14.refs_8_.refs_2_, ...), custom_call_target="tpu_custom_call" | custom-call | flops 1024 | bytes 1024 | tf_op jit(solution)/shard_map/round_logits/pallas_call | solution.py:206
  84.6 0.6 collective-permute-start.21
  85.3 1.5 %collective-permute-start.19 = (f32[32,128]{1,0:T(8,128)S(1)}, f32[32,128]{1,0:T(8,128)S(1)}, u32[]{:S(2)}, u32[]{:S(2)}) collective-permute-start(f32[32,128]{1,0:T(8,128)S(1)} %get-tuple-element.93.own_ref), channel_id=1, source_target_pairs={{0,1},{1,0},{2,3},{3,2},{4,5},{5,4},{6,7},{7,6},{8,9},{9,8},{10,11... | collective-permute-start | bytes 49160 | tf_op jit(solution)/shard_map/ppermute | solution.py:457
  86.8 1.0 collective-permute-done.21.both_ref
  87.8 1.2 %collective-permute-done.19.across_ref = f32[32,128]{1,0:T(8,128)S(1)} collective-permute-done((f32[32,128]{1,0:T(8,128)S(1)}, f32[32,128]{1,0:T(8,128)S(1)}, u32[]{:S(2)}, u32[]{:S(2)}) %collective-permute-start.19) | collective-permute-done | bytes 16416 | tf_op jit(solution)/shard_map/ppermute | solution.py:457
  89.2 2.2 %collective-permute-start.24 = (f32[64,128]{1,0:T(8,128)S(1)}, f32[64,128]{1,0:T(8,128)S(1)}, u32[]{:S(2)}, u32[]{:S(2)}) collective-permute-start(f32[64,128]{1,0:T(8,128)S(1)} %get-tuple-element.94.refs_10_), channel_id=1, source_target_pairs={{0,4},{1,5},{2,6},{3,7},{4,0},{5,1},{6,2},{7,3},{8,12},{9,13},{10,... | collective-permute-start | bytes 98312 | tf_op jit(solution)/shard_map/ppermute | solution.py:467
  91.4 1.6 %collective-permute-start.23 = (f32[64,128]{1,0:T(8,128)S(1)}, f32[64,128]{1,0:T(8,128)S(1)}, u32[]{:S(2)}, u32[]{:S(2)}) collective-permute-start(f32[64,128]{1,0:T(8,128)S(1)} %get-tuple-element.94.refs_10_), channel_id=1, source_target_pairs={{0,6},{1,7},{2,0},{3,1},{4,2},{5,3},{6,4},{7,5},{8,14},{9,15},{10,... | collective-permute-start | bytes 98312 | tf_op jit(solution)/shard_map/ppermute | solution.py:467
  93.0 2.2 %collective-permute-done.25.refs_13_ = f32[64,128]{1,0:T(8,128)S(1)} collective-permute-done((f32[64,128]{1,0:T(8,128)S(1)}, f32[64,128]{1,0:T(8,128)S(1)}, u32[]{:S(2)}, u32[]{:S(2)}) %collective-permute-start.25) | collective-permute-done | bytes 32800 | tf_op jit(solution)/shard_map/ppermute | solution.py:467
  95.2 0.3 collective-permute-done.23.refs_11_
  95.5 20.0 %refresh_states.1 = (bf16[896,2048]{1,0:T(8,128)(2,1)}, bf16[896,2048]{1,0:T(8,128)(2,1)}, bf16[896,2048]{1,0:T(8,128)(2,1)}) custom-call(bf16[896,384]{1,0:T(8,128)(2,1)S(1)} %get-tuple-element.69.refs_0_, bf16[896,384]{1,0:T(8,128)(2,1)S(1)} %collective-permute-done.10.refs_1_, bf16[896,640]{1,0:T(8,128)(2,1)S(1)} %get-tuple-element.84.refs_2_, ...), custom_call_target="tpu_custom_call" | custom-call | flops 1024 | bytes 1024 | tf_op jit(solution)/shard_map/refresh_states/pallas_call | solution.py:414
  (45 shorter events, 1.2 us)
Async XLA Ops:
  0.6 0.7 copy-start
  2.6 15.6 %collective-permute-start.2 = (bf16[64,3584]{1,0:T(8,128)(2,1)S(1)}, bf16[64,3584]{1,0:T(8,128)(2,1)S(1)}, u32[]{:S(2)}, u32[]{:S(2)}) collective-permute-start(bf16[64,3584]{1,0:T(8,128)(2,1)S(1)} %normalized.1.refs_0_), channel_id=1, source_target_pairs={{0,2},{1,3},{2,4},{3,5},{4,6},{5,7},{6,0},{7,1},{8,10},{9,11},{10,... | collective-permute-start | bytes 1376264 | tf_op jit(solution)/shard_map/ppermute | solution.py:467
  5.7 21.1 %collective-permute-start.1 = (bf16[64,3584]{1,0:T(8,128)(2,1)S(1)}, bf16[64,3584]{1,0:T(8,128)(2,1)S(1)}, u32[]{:S(2)}, u32[]{:S(2)}) collective-permute-start(bf16[64,3584]{1,0:T(8,128)(2,1)S(1)} %normalized.1.refs_0_), channel_id=1, source_target_pairs={{0,1},{1,0},{2,3},{3,2},{4,5},{5,4},{6,7},{7,6},{8,9},{9,8},{10,11... | collective-permute-start | bytes 1376264 | tf_op jit(solution)/shard_map/ppermute | solution.py:457
  7.2 20.2 %collective-permute-start = (bf16[64,3584]{1,0:T(8,128)(2,1)S(1)}, bf16[64,3584]{1,0:T(8,128)(2,1)S(1)}, u32[]{:S(2)}, u32[]{:S(2)}) collective-permute-start(bf16[64,3584]{1,0:T(8,128)(2,1)S(1)} %normalized.1.refs_0_), channel_id=1, source_target_pairs={{0,16},{8,24},{16,0},{24,8},{1,17},{9,25},{17,1},{25,9},{2,18},{10... | collective-permute-start | bytes 1376264 | tf_op jit(solution)/shard_map/ppermute | solution.py:451
  18.2 14.9 %collective-permute-start.5 = (bf16[64,3584]{1,0:T(8,128)(2,1)S(1)}, bf16[64,3584]{1,0:T(8,128)(2,1)S(1)}, u32[]{:S(2)}, u32[]{:S(2)}) collective-permute-start(bf16[64,3584]{1,0:T(8,128)(2,1)S(1)} %collective-permute-done.2.refs_0_.refs_3_), channel_id=1, source_target_pairs={{0,1},{1,0},{2,3},{3,2},{4,5},{5,4},{6,7},{7,6},{8,9},{9,8},{10,11... | collective-permute-start | bytes 1376264 | tf_op jit(solution)/shard_map/ppermute | solution.py:457
  19.7 13.5 %collective-permute-start.4 = (bf16[64,3584]{1,0:T(8,128)(2,1)S(1)}, bf16[64,3584]{1,0:T(8,128)(2,1)S(1)}, u32[]{:S(2)}, u32[]{:S(2)}) collective-permute-start(bf16[64,3584]{1,0:T(8,128)(2,1)S(1)} %collective-permute-done.2.refs_0_.refs_3_), channel_id=1, source_target_pairs={{0,16},{8,24},{16,0},{24,8},{1,17},{9,25},{17,1},{25,9},{2,18},{10... | collective-permute-start | bytes 1376264 | tf_op jit(solution)/shard_map/ppermute | solution.py:451
  21.2 12.7 %collective-permute-start.3 = (bf16[64,3584]{1,0:T(8,128)(2,1)S(1)}, bf16[64,3584]{1,0:T(8,128)(2,1)S(1)}, u32[]{:S(2)}, u32[]{:S(2)}) collective-permute-start(bf16[64,3584]{1,0:T(8,128)(2,1)S(1)} %collective-permute-done.2.refs_0_.refs_3_), channel_id=1, source_target_pairs={{0,2},{1,3},{2,4},{3,5},{4,6},{5,7},{6,0},{7,1},{8,10},{9,11},{10,... | collective-permute-start | bytes 1376264 | tf_op jit(solution)/shard_map/ppermute | solution.py:467
  26.7 17.1 %collective-permute-start.9 = (bf16[64,3584]{1,0:T(8,128)(2,1)S(1)}, bf16[64,3584]{1,0:T(8,128)(2,1)S(1)}, u32[]{:S(2)}, u32[]{:S(2)}) collective-permute-start(bf16[64,3584]{1,0:T(8,128)(2,1)S(1)} %collective-permute-done.1.refs_2_), channel_id=1, source_target_pairs={{0,16},{8,24},{16,0},{24,8},{1,17},{9,25},{17,1},{25,9},{2,18},{10... | collective-permute-start | bytes 1376264 | tf_op jit(solution)/shard_map/ppermute | solution.py:451
  33.9 14.7 %collective-permute-start.8 = (bf16[64,3584]{1,0:T(8,128)(2,1)S(1)}, bf16[64,3584]{1,0:T(8,128)(2,1)S(1)}, u32[]{:S(2)}, u32[]{:S(2)}) collective-permute-start(bf16[64,3584]{1,0:T(8,128)(2,1)S(1)} %collective-permute-done.3.refs_0_), channel_id=1, source_target_pairs={{0,1},{1,0},{2,3},{3,2},{4,5},{5,4},{6,7},{7,6},{8,9},{9,8},{10,11... | collective-permute-start | bytes 1376264 | tf_op jit(solution)/shard_map/ppermute | solution.py:457
  34.4 16.1 %collective-permute-start.7 = (bf16[64,3584]{1,0:T(8,128)(2,1)S(1)}, bf16[64,3584]{1,0:T(8,128)(2,1)S(1)}, u32[]{:S(2)}, u32[]{:S(2)}) collective-permute-start(bf16[64,3584]{1,0:T(8,128)(2,1)S(1)} %collective-permute-done.3.refs_0_), channel_id=1, source_target_pairs={{0,16},{8,24},{16,0},{24,8},{1,17},{9,25},{17,1},{25,9},{2,18},{10... | collective-permute-start | bytes 1376264 | tf_op jit(solution)/shard_map/ppermute | solution.py:451
  35.2 15.3 %collective-permute-start.6 = (bf16[64,3584]{1,0:T(8,128)(2,1)S(1)}, bf16[64,3584]{1,0:T(8,128)(2,1)S(1)}, u32[]{:S(2)}, u32[]{:S(2)}) collective-permute-start(bf16[64,3584]{1,0:T(8,128)(2,1)S(1)} %collective-permute-done.3.refs_0_), channel_id=1, source_target_pairs={{0,2},{1,3},{2,4},{3,5},{4,6},{5,7},{6,0},{7,1},{8,10},{9,11},{10,... | collective-permute-start | bytes 1376264 | tf_op jit(solution)/shard_map/ppermute | solution.py:467
  36.5 17.8 %collective-permute-start.11 = (bf16[64,3584]{1,0:T(8,128)(2,1)S(1)}, bf16[64,3584]{1,0:T(8,128)(2,1)S(1)}, u32[]{:S(2)}, u32[]{:S(2)}) collective-permute-start(bf16[64,3584]{1,0:T(8,128)(2,1)S(1)} %collective-permute-done.4.refs_1_.refs_4_), channel_id=1, source_target_pairs={{0,1},{1,0},{2,3},{3,2},{4,5},{5,4},{6,7},{7,6},{8,9},{9,8},{10,11... | collective-permute-start | bytes 1376264 | tf_op jit(solution)/shard_map/ppermute | solution.py:457
  50.6 13.5 %collective-permute-start.12 = (bf16[64,3584]{1,0:T(8,128)(2,1)S(1)}, bf16[64,3584]{1,0:T(8,128)(2,1)S(1)}, u32[]{:S(2)}, u32[]{:S(2)}) collective-permute-start(bf16[64,3584]{1,0:T(8,128)(2,1)S(1)} %collective-permute-done.6.refs_2_.refs_4_), channel_id=1, source_target_pairs={{0,16},{8,24},{16,0},{24,8},{1,17},{9,25},{17,1},{25,9},{2,18},{10... | collective-permute-start | bytes 1376264 | tf_op jit(solution)/shard_map/ppermute | solution.py:451
  52.9 11.9 %collective-permute-start.10 = (bf16[896,384]{1,0:T(8,128)(2,1)S(1)}, bf16[896,384]{1,0:T(8,128)(2,1)S(1)}, u32[]{:S(2)}, u32[]{:S(2)}) collective-permute-start(bf16[896,384]{1,0:T(8,128)(2,1)S(1)} %get-tuple-element.70), channel_id=1, source_target_pairs={{0,8},{8,0},{16,24},{24,16},{1,9},{9,1},{17,25},{25,17},{2,10},{10... | collective-permute-start | bytes 2064392 | tf_op jit(solution)/shard_map/ppermute | solution.py:454
  53.0 20.4 %collective-permute-start.13 = (bf16[64,3584]{1,0:T(8,128)(2,1)S(1)}, bf16[64,3584]{1,0:T(8,128)(2,1)S(1)}, u32[]{:S(2)}, u32[]{:S(2)}) collective-permute-start(bf16[64,3584]{1,0:T(8,128)(2,1)S(1)} %collective-permute-done.6.refs_2_.refs_4_), channel_id=1, source_target_pairs={{0,1},{1,0},{2,3},{3,2},{4,5},{5,4},{6,7},{7,6},{8,9},{9,8},{10,11... | collective-permute-start | bytes 1376264 | tf_op jit(solution)/shard_map/ppermute | solution.py:457
  53.6 19.9 %collective-permute-start.14 = (bf16[64,3584]{1,0:T(8,128)(2,1)S(1)}, bf16[64,3584]{1,0:T(8,128)(2,1)S(1)}, u32[]{:S(2)}, u32[]{:S(2)}) collective-permute-start(bf16[64,3584]{1,0:T(8,128)(2,1)S(1)} %collective-permute-done.8.refs_1_.refs_3_), channel_id=1, source_target_pairs={{0,16},{8,24},{16,0},{24,8},{1,17},{9,25},{17,1},{25,9},{2,18},{10... | collective-permute-start | bytes 1376264 | tf_op jit(solution)/shard_map/ppermute | solution.py:451
  61.2 15.9 %copy-start.2 = (bf16[384,2048]{1,0:T(8,128)(2,1)S(1)}, bf16[384,2048]{1,0:T(8,128)(2,1)}, u32[]{:S(2)}) copy-start(bf16[384,2048]{1,0:T(8,128)(2,1)} %get-tuple-element.90.refs_4_) | copy-start | bytes 4718596
  61.2 15.9 %copy-start.1 = (bf16[384,2048]{1,0:T(8,128)(2,1)S(1)}, bf16[384,2048]{1,0:T(8,128)(2,1)}, u32[]{:S(2)}) copy-start(bf16[384,2048]{1,0:T(8,128)(2,1)} %get-tuple-element.91.refs_5_) | copy-start | bytes 4718596
  64.0 11.7 %collective-permute-start.15 = (bf16[64,3584]{1,0:T(8,128)(2,1)S(1)}, bf16[64,3584]{1,0:T(8,128)(2,1)S(1)}, u32[]{:S(2)}, u32[]{:S(2)}) collective-permute-start(bf16[64,3584]{1,0:T(8,128)(2,1)S(1)} %collective-permute-done.12.refs_6_.refs_0_), channel_id=1, source_target_pairs={{0,1},{1,0},{2,3},{3,2},{4,5},{5,4},{6,7},{7,6},{8,9},{9,8},{10,11... | collective-permute-start | bytes 1376264 | tf_op jit(solution)/shard_map/ppermute | solution.py:457
  77.1 9.7 %collective-permute-start.17 = (bf16[384,2048]{1,0:T(8,128)(2,1)S(1)}, bf16[384,2048]{1,0:T(8,128)(2,1)S(1)}, u32[]{:S(2)}, u32[]{:S(2)}) collective-permute-start(bf16[384,2048]{1,0:T(8,128)(2,1)S(1)} %copy-done.2), channel_id=1, source_target_pairs={{0,8},{8,0},{16,24},{24,16},{1,9},{9,1},{17,25},{25,17},{2,10},{10... | collective-permute-start | bytes 4718600 | tf_op jit(solution)/shard_map/ppermute | solution.py:454
  77.2 9.6 %collective-permute-start.18 = (bf16[384,2048]{1,0:T(8,128)(2,1)S(1)}, bf16[384,2048]{1,0:T(8,128)(2,1)S(1)}, u32[]{:S(2)}, u32[]{:S(2)}) collective-permute-start(bf16[384,2048]{1,0:T(8,128)(2,1)S(1)} %copy-done.1), channel_id=1, source_target_pairs={{0,8},{8,0},{16,24},{24,16},{1,9},{9,1},{17,25},{25,17},{2,10},{10... | collective-permute-start | bytes 4718600 | tf_op jit(solution)/shard_map/ppermute | solution.py:454
  77.7 7.6 %collective-permute-start.16 = (bf16[896,640]{1,0:T(8,128)(2,1)S(1)}, bf16[896,640]{1,0:T(8,128)(2,1)S(1)}, u32[]{:S(2)}, u32[]{:S(2)}) collective-permute-start(bf16[896,640]{1,0:T(8,128)(2,1)S(1)} %get-tuple-element.85), channel_id=1, source_target_pairs={{0,8},{8,0},{16,24},{24,16},{1,9},{9,1},{17,25},{25,17},{2,10},{10... | collective-permute-start | bytes 3440648 | tf_op jit(solution)/shard_map/ppermute | solution.py:454
  84.6 3.2 %collective-permute-start.21 = (f32[32,128]{1,0:T(8,128)S(1)}, f32[32,128]{1,0:T(8,128)S(1)}, u32[]{:S(2)}, u32[]{:S(2)}) collective-permute-start(f32[32,128]{1,0:T(8,128)S(1)} %get-tuple-element.93.own_ref), channel_id=1, source_target_pairs={{0,9},{1,8},{2,11},{3,10},{4,13},{5,12},{6,15},{7,14},{8,1},{9,0},... | collective-permute-start | bytes 49160 | tf_op jit(solution)/shard_map/ppermute | solution.py:464
  85.2 2.6 %collective-permute-start.20 = (f32[32,128]{1,0:T(8,128)S(1)}, f32[32,128]{1,0:T(8,128)S(1)}, u32[]{:S(2)}, u32[]{:S(2)}) collective-permute-start(f32[32,128]{1,0:T(8,128)S(1)} %get-tuple-element.93.own_ref), channel_id=1, source_target_pairs={{0,8},{8,0},{16,24},{24,16},{1,9},{9,1},{17,25},{25,17},{2,10},{10... | collective-permute-start | bytes 49160 | tf_op jit(solution)/shard_map/ppermute | solution.py:454
  85.3 3.7 %collective-permute-start.19 = (f32[32,128]{1,0:T(8,128)S(1)}, f32[32,128]{1,0:T(8,128)S(1)}, u32[]{:S(2)}, u32[]{:S(2)}) collective-permute-start(f32[32,128]{1,0:T(8,128)S(1)} %get-tuple-element.93.own_ref), channel_id=1, source_target_pairs={{0,1},{1,0},{2,3},{3,2},{4,5},{5,4},{6,7},{7,6},{8,9},{9,8},{10,11... | collective-permute-start | bytes 49160 | tf_op jit(solution)/shard_map/ppermute | solution.py:457
  89.1 6.4 %collective-permute-start.22 = (bf16[256,2048]{1,0:T(8,128)(2,1)}, bf16[256,2048]{1,0:T(8,128)(2,1)S(1)}, u32[]{:S(2)}, u32[]{:S(2)}) collective-permute-start(bf16[256,2048]{1,0:T(8,128)(2,1)} %get-tuple-element.95.refs_6_), channel_id=1, source_target_pairs={{0,8},{8,0},{16,24},{24,16},{1,9},{9,1},{17,25},{25,17},{2,10},{10... | collective-permute-start | bytes 3145736 | tf_op jit(solution)/shard_map/ppermute | solution.py:454
  89.1 6.0 %collective-permute-start.25 = (f32[64,128]{1,0:T(8,128)S(1)}, f32[64,128]{1,0:T(8,128)S(1)}, u32[]{:S(2)}, u32[]{:S(2)}) collective-permute-start(f32[64,128]{1,0:T(8,128)S(1)} %get-tuple-element.94.refs_10_), channel_id=1, source_target_pairs={{0,2},{1,3},{2,4},{3,5},{4,6},{5,7},{6,0},{7,1},{8,10},{9,11},{10,... | collective-permute-start | bytes 98312 | tf_op jit(solution)/shard_map/ppermute | solution.py:467
  89.2 6.0 %collective-permute-start.24 = (f32[64,128]{1,0:T(8,128)S(1)}, f32[64,128]{1,0:T(8,128)S(1)}, u32[]{:S(2)}, u32[]{:S(2)}) collective-permute-start(f32[64,128]{1,0:T(8,128)S(1)} %get-tuple-element.94.refs_10_), channel_id=1, source_target_pairs={{0,4},{1,5},{2,6},{3,7},{4,0},{5,1},{6,2},{7,3},{8,12},{9,13},{10,... | collective-permute-start | bytes 98312 | tf_op jit(solution)/shard_map/ppermute | solution.py:467
  91.4 4.1 %collective-permute-start.23 = (f32[64,128]{1,0:T(8,128)S(1)}, f32[64,128]{1,0:T(8,128)S(1)}, u32[]{:S(2)}, u32[]{:S(2)}) collective-permute-start(f32[64,128]{1,0:T(8,128)S(1)} %get-tuple-element.94.refs_10_), channel_id=1, source_target_pairs={{0,6},{1,7},{2,0},{3,1},{4,2},{5,3},{6,4},{7,5},{8,14},{9,15},{10,... | collective-permute-start | bytes 98312 | tf_op jit(solution)/shard_map/ppermute | solution.py:467

commit v11 on v10

--- a/solution.py
+++ b/solution.py
@@ -471,8 +471,8 @@
     groups = [[(*kind, turn) for kind in plain] for turn in range(split)]
     groups += [
         [(0, 0, split), (1, 1, 0)],
-        [(0, 1, split), (1, 0, split), (0, 0, split + 1), (1, 1, 1)],
-        [(0, 1, split + 1), (1, 0, split + 1), (1, 1, split), (1, 1, split + 1)],
+        [(0, 1, split), (1, 0, split), (0, 0, split + 1)],
+        [(0, 1, split + 1), (1, 0, split + 1)] + [(1, 1, turn) for turn in range(1, lines)],
     ]
     early_blocks, late_blocks = sum(groups[:split], []), sum(groups[split:], [])
 
@@ -507,7 +507,9 @@
         return round_logits(blocks, rows, head_weight, stats, first_row, exp_rows, into)
 
     def diagonal(turn):
-        if turn % 2 == 0:
+        if turn == 1:
+            return to_z(held[1, 1, 0], 1)
+        if turn == 2:
             return to_x(held[1, 0, turn])
         return to_y(held[0, 1, turn])
 
@@ -524,20 +526,19 @@
                 arrived += [early_exp]
             else:
                 middle_exp, stats = logits(
-                    groups[split], stats, exp_rows=6 * length
+                    groups[split], stats, exp_rows=5 * length
                 )
-                arrived += [early_exp, middle_exp]
+                arrived = [following, held[0, 1, turn], early_exp, middle_exp]
             arrived = lax.optimization_barrier(tuple(arrived))
             held[0, 0, turn + 1] = arrived[0]
             if turn == 0:
                 early_ids, late_ids = list(arrived[1:3]), list(arrived[3:5])
                 stats, = arrived[5:]
                 head_weight, *late_ids = prepared(head_weight, *late_ids, stats)
+            elif turn < split:
+                held[0, 1, turn], held[1, 0, turn], early_exp = arrived[1:]
             else:
-                held[0, 1, turn], held[1, 0, turn] = arrived[1:3]
-                early_exp = arrived[3]
-                if turn == split:
-                    middle_exp = arrived[4]
+                held[0, 1, turn], early_exp, middle_exp = arrived[1:]
             held[1, 1, turn] = diagonal(turn)
         if turn < split:
             size = len(groups[turn]) * length
@@ -552,7 +553,7 @@
     early = [early[0], to_core(early[1])]
     middle_exp, stats = logits(
         groups[split + 1], stats, held[0, 0, lines - 1], early[0],
-        first_row=2 * length, exp_rows=6 * length, into=middle_exp,
+        first_row=2 * length, exp_rows=5 * length, into=middle_exp,
     )
     held[0, 1, lines - 1] = after(held[0, 1, lines - 1], middle_exp)
     held[1, 1, lines - 1] = diagonal(lines - 1)

time: 116 us -> 116 us (level)
    ppermute x6 -> x5, waiting for transfers between devices: 4.77 us -> 0.89 us  [to_x(): return lax.ppermute(values, 'rep', swap_pairs(reps, 2))]
    ppermute x7, waiting for transfers between devices: 3.53 us -> 6.59 us  [to_y(): return lax.ppermute(values, 'shard', swap_pairs(shards, 1))]
    ppermute x6 -> x7, starting transfers between devices: 8.24 us -> 10.4 us  [to_z(): return lax.ppermute(values, 'shard', shift_pairs(lines, along, 0))]
    ppermute x6 -> x5, starting transfers between devices: 6.67 us -> 5.62 us  [to_x(): return lax.ppermute(values, 'rep', swap_pairs(reps, 2))]
    ppermute x6 -> x7, waiting for transfers between devices: 5.96 us -> 5.87 us  [to_z(): return lax.ppermute(values, 'shard', shift_pairs(lines, along, 0))]
  transfers between devices with their start and end apart: 26 -> 26, of which waited for: 9 -> 8; matrix products, arithmetic and copies ran while one was open for 6% -> 6% of each run, Pallas kernels for 39% -> 39%
where the time goes in v11:
time: 116 us
  Pallas kernels  67.6 us (58%)
  starting transfers between devices  25.4 us (22%)
  waiting for transfers between devices  14.4 us (12%)
  local copies, waits for them, and re-layouts  3.87 us (3%)
  other arithmetic  3.62 us (3%)
    pallas_call x5, Pallas kernels, round_logits(): pl.pallas_call(functools.partial(logits_kernel, stat_rows, first_row, len...  30 us
    pallas_call x1, Pallas kernels, refresh_states(): pl.pallas_call(functools.partial(refresh_kernel, lines, length, block_row...  20 us
    ppermute x7, starting transfers between devices, to_z(): return lax.ppermute(values, 'shard', shift_pairs(lines, along, 0))  10.4 us
    pallas_call x1, Pallas kernels, one_hot_sums(): pl.pallas_call(functools.partial(one_hot_kernel, len(features)), grid=(co...  8.66 us
    ppermute x7, starting transfers between devices, to_y(): return lax.ppermute(values, 'shard', swap_pairs(shards, 1))  7.86 us
    ppermute x7, waiting for transfers between devices, to_y(): return lax.ppermute(values, 'shard', swap_pairs(shards, 1))  6.59 us
    ppermute x7, waiting for transfers between devices, to_z(): return lax.ppermute(values, 'shard', shift_pairs(lines, along, 0))  5.87 us
    ppermute x5, starting transfers between devices, to_x(): return lax.ppermute(values, 'rep', swap_pairs(reps, 2))  5.62 us
  transfers between devices with their start and end apart: 26, of which 8 were waited for; matrix products, arithmetic and copies ran while one was open for 6% of the time, Pallas kernels for 39%

profile of v11, /device:TPU:0, one launch (start us, length us, event | category | flops | bytes accessed | tf_op | source)
XLA Modules:
  0.0 115.7 jit_solution(10730698988680091226)
XLA Ops:
  0.6 0.7 copy-done
  1.3 1.2 %normalized.1.refs_0_ = bf16[64,3584]{1,0:T(8,128)(2,1)S(1)} custom-call(bf16[64,3584]{1,0:T(8,128)(2,1)} %hidden_ref.1, f32[3584]{0:T(1024)S(1)} %copy-done), custom_call_target="tpu_custom_call" | custom-call | flops 1024 | bytes 1024 | tf_op jit(solution)/shard_map/normalized/pallas_call | solution.py:93
  2.6 3.1 %collective-permute-start.2 = (bf16[64,3584]{1,0:T(8,128)(2,1)S(1)}, bf16[64,3584]{1,0:T(8,128)(2,1)S(1)}, u32[]{:S(2)}, u32[]{:S(2)}) collective-permute-start(bf16[64,3584]{1,0:T(8,128)(2,1)S(1)} %normalized.1.refs_0_), channel_id=1, source_target_pairs={{0,2},{1,3},{2,4},{3,5},{4,6},{5,7},{6,0},{7,1},{8,10},{9,11},{10,... | collective-permute-start | bytes 1376264 | tf_op jit(solution)/shard_map/ppermute | solution.py:467
  5.7 1.5 %collective-permute-start.1 = (bf16[64,3584]{1,0:T(8,128)(2,1)S(1)}, bf16[64,3584]{1,0:T(8,128)(2,1)S(1)}, u32[]{:S(2)}, u32[]{:S(2)}) collective-permute-start(bf16[64,3584]{1,0:T(8,128)(2,1)S(1)} %normalized.1.refs_0_), channel_id=1, source_target_pairs={{0,1},{1,0},{2,3},{3,2},{4,5},{5,4},{6,7},{7,6},{8,9},{9,8},{10,11... | collective-permute-start | bytes 1376264 | tf_op jit(solution)/shard_map/ppermute | solution.py:457
  7.2 1.5 %collective-permute-start = (bf16[64,3584]{1,0:T(8,128)(2,1)S(1)}, bf16[64,3584]{1,0:T(8,128)(2,1)S(1)}, u32[]{:S(2)}, u32[]{:S(2)}) collective-permute-start(bf16[64,3584]{1,0:T(8,128)(2,1)S(1)} %normalized.1.refs_0_), channel_id=1, source_target_pairs={{0,16},{8,24},{16,0},{24,8},{1,17},{9,25},{17,1},{25,9},{2,18},{10... | collective-permute-start | bytes 1376264 | tf_op jit(solution)/shard_map/ppermute | solution.py:451
  8.7 0.7 fusion.4
  9.3 0.7 compare_and_fusion
  10.0 0.7 multiply_add_fusion
  10.7 1.2 %slice.31 = s32[1]{0:T(128)} slice(s32[2048]{0:T(1024)} %param.12), slice={[0:1]} | slice | bytes 8 | tf_op jit(solution)/shard_map/jit(_roll_static)/slice | solution.py:485
  11.9 0.8 slice.30
  12.8 0.7 broadcast_subtract_fusion
  13.6 0.7 fusion.1
  14.4 0.6 gather_fusion
  15.5 2.7 %collective-permute-done.2.refs_0_.refs_3_ = bf16[64,3584]{1,0:T(8,128)(2,1)S(1)} collective-permute-done((bf16[64,3584]{1,0:T(8,128)(2,1)S(1)}, bf16[64,3584]{1,0:T(8,128)(2,1)S(1)}, u32[]{:S(2)}, u32[]{:S(2)}) %collective-permute-start.2) | collective-permute-done | bytes 458784 | tf_op jit(solution)/shard_map/ppermute | solution.py:467
  18.2 1.5 %collective-permute-start.5 = (bf16[64,3584]{1,0:T(8,128)(2,1)S(1)}, bf16[64,3584]{1,0:T(8,128)(2,1)S(1)}, u32[]{:S(2)}, u32[]{:S(2)}) collective-permute-start(bf16[64,3584]{1,0:T(8,128)(2,1)S(1)} %collective-permute-done.2.refs_0_.refs_3_), channel_id=1, source_target_pairs={{0,1},{1,0},{2,3},{3,2},{4,5},{5,4},{6,7},{7,6},{8,9},{9,8},{10,11... | collective-permute-start | bytes 1376264 | tf_op jit(solution)/shard_map/ppermute | solution.py:457
  19.7 1.5 %collective-permute-start.4 = (bf16[64,3584]{1,0:T(8,128)(2,1)S(1)}, bf16[64,3584]{1,0:T(8,128)(2,1)S(1)}, u32[]{:S(2)}, u32[]{:S(2)}) collective-permute-start(bf16[64,3584]{1,0:T(8,128)(2,1)S(1)} %collective-permute-done.2.refs_0_.refs_3_), channel_id=1, source_target_pairs={{0,16},{8,24},{16,0},{24,8},{1,17},{9,25},{17,1},{25,9},{2,18},{10... | collective-permute-start | bytes 1376264 | tf_op jit(solution)/shard_map/ppermute | solution.py:451
  21.2 5.5 %prepared.1 = (bf16[3584,2048]{1,0:T(8,128)(2,1)S(1)}, s32[1280,128]{1,0:T(8,128)S(1)}, s32[1280,128]{1,0:T(8,128)S(1)}) custom-call(bf16[3584,2048]{1,0:T(8,128)(2,1)} %weight_ref.1, s32[1,1280]{1,0:T(1,128)S(1)} %squeeze.14.true_ids, s32[1,1280]{1,0:T(1,128)S(1)} %squeeze.15.sample_ids, f32[32,128]{1,0:T(8,128)S(1)} %broadcast_in_dim.20.refs_0_.refs_4_), custom_call_target="tpu_custom_call" | custom-call | flops 1024 | bytes 1024 | tf_op jit(solution)/shard_map/prepared/pallas_call | solution.py:127
  26.8 0.6 collective-permute-start.8
  27.3 5.8 %round_logits.5 = (bf16[384,2048]{1,0:T(8,128)(2,1)}, f32[32,128]{1,0:T(8,128)S(1)}) custom-call(bf16[64,3584]{1,0:T(8,128)(2,1)S(1)} %normalized.1.refs_0_, bf16[64,3584]{1,0:T(8,128)(2,1)S(1)} %collective-permute-done.refs_1_, bf16[64,3584]{1,0:T(8,128)(2,1)S(1)} %collective-permute-done.1.refs_2_, ...), custom_call_target="tpu_custom_call" | custom-call | flops 1024 | bytes 1024 | tf_op jit(solution)/shard_map/round_logits/pallas_call | solution.py:206
  33.1 0.8 collective-permute-done.3.refs_0_
  33.9 0.5 collective-permute-start.7
  34.4 0.6 collective-permute-start.6
  35.0 1.5 %collective-permute-start.10 = (bf16[64,3584]{1,0:T(8,128)(2,1)S(1)}, bf16[64,3584]{1,0:T(8,128)(2,1)S(1)}, u32[]{:S(2)}, u32[]{:S(2)}) collective-permute-start(bf16[64,3584]{1,0:T(8,128)(2,1)S(1)} %collective-permute-done.3.refs_0_), channel_id=1, source_target_pairs={{0,1},{1,0},{2,3},{3,2},{4,5},{5,4},{6,7},{7,6},{8,9},{9,8},{10,11... | collective-permute-start | bytes 1376264 | tf_op jit(solution)/shard_map/ppermute | solution.py:457
  36.5 5.8 %round_logits.6 = (bf16[384,2048]{1,0:T(8,128)(2,1)}, f32[32,128]{1,0:T(8,128)S(1)}) custom-call(bf16[64,3584]{1,0:T(8,128)(2,1)S(1)} %collective-permute-done.2.refs_0_.refs_3_, bf16[64,3584]{1,0:T(8,128)(2,1)S(1)} %collective-permute-done.4.refs_1_.refs_4_, ...), custom_call_target="tpu_custom_call", output_to_operand_aliasing={{0}: (5, {})} | custom-call | flops 1024 | bytes 1024 | tf_op jit(solution)/shard_map/round_logits/pallas_call | solution.py:206
  42.3 4.7 %round_logits.7 = (bf16[320,2048]{1,0:T(8,128)(2,1)}, f32[32,128]{1,0:T(8,128)S(1)}) custom-call(bf16[64,3584]{1,0:T(8,128)(2,1)S(1)} %collective-permute-done.3.refs_0_, bf16[64,3584]{1,0:T(8,128)(2,1)S(1)} %collective-permute-done.8.refs_1_, bf16[3584,2048]{1,0:T(8,128)(2,1)S(1)} %get-tuple-element.55.refs_3_.refs_2_.refs_5_, ...), custom_call_target="tpu_custom_call" | custom-call | flops 1024 | bytes 1024 | tf_op jit(solution)/shard_map/round_logits/pallas_call | solution.py:206
  47.1 1.6 %collective-permute-start.11 = (bf16[64,3584]{1,0:T(8,128)(2,1)S(1)}, bf16[64,3584]{1,0:T(8,128)(2,1)S(1)}, u32[]{:S(2)}, u32[]{:S(2)}) collective-permute-start(bf16[64,3584]{1,0:T(8,128)(2,1)S(1)} %collective-permute-done.6.refs_2_.refs_4_), channel_id=1, source_target_pairs={{0,16},{8,24},{16,0},{24,8},{1,17},{9,25},{17,1},{25,9},{2,18},{10... | collective-permute-start | bytes 1376264 | tf_op jit(solution)/shard_map/ppermute | solution.py:451
  48.7 0.9 turned_features.2
  49.6 1.6 %collective-permute-start.13 = (bf16[64,3584]{1,0:T(8,128)(2,1)S(1)}, bf16[64,3584]{1,0:T(8,128)(2,1)S(1)}, u32[]{:S(2)}, u32[]{:S(2)}) collective-permute-start(bf16[64,3584]{1,0:T(8,128)(2,1)S(1)} %collective-permute-done.8.refs_1_), channel_id=1, source_target_pairs={{0,2},{1,3},{2,4},{3,5},{4,6},{5,7},{6,0},{7,1},{8,10},{9,11},{10,... | collective-permute-start | bytes 1376264 | tf_op jit(solution)/shard_map/ppermute | solution.py:467
  51.3 0.5 collective-permute-start.12
  51.8 0.5 collective-permute-start.14
  52.3 5.8 %round_logits.8 = (bf16[320,2048]{1,0:T(8,128)(2,1)}, f32[32,128]{1,0:T(8,128)S(1)}) custom-call(bf16[64,3584]{1,0:T(8,128)(2,1)S(1)} %collective-permute-done.7.refs_0_.refs_2_, bf16[64,3584]{1,0:T(8,128)(2,1)S(1)} %collective-permute-done.10.refs_1_.refs_3_, ...), custom_call_target="tpu_custom_call", output_to_operand_aliasing={{0}: (5, {})} | custom-call | flops 1024 | bytes 1024 | tf_op jit(solution)/shard_map/round_logits/pallas_call | solution.py:206
  58.1 0.9 collective-permute-done.11.refs_5_.refs_0_
  58.9 0.7 collective-permute-start.15
  59.6 8.7 %one_hot_sums.1 = (bf16[896,2048]{1,0:T(8,128)(2,1)}, bf16[896,2048]{1,0:T(8,128)(2,1)}) custom-call(bf16[896,384]{1,0:T(8,128)(2,1)S(1)} %get-tuple-element.68.refs_0_, bf16[896,384]{1,0:T(8,128)(2,1)S(1)} %collective-permute-done.9.refs_1_, s32[1,768]{1,0:T(1,128)S(1)} %squeeze.12.refs_2_, s32[1,768]{1,0:T(1,128)S(1)} %squeeze.13.refs_3_), custom_call_target="tpu_custom_call" | custom-call | flops 1024 | bytes 1024 | tf_op jit(solution)/shard_map/one_hot_sums/pallas_call | solution.py:285
  68.3 5.4 %collective-permute-done.15.refs_9_.refs_4_ = bf16[64,3584]{1,0:T(8,128)(2,1)S(1)} collective-permute-done((bf16[64,3584]{1,0:T(8,128)(2,1)S(1)}, bf16[64,3584]{1,0:T(8,128)(2,1)S(1)}, u32[]{:S(2)}, u32[]{:S(2)}) %collective-permute-start.15) | collective-permute-done | bytes 458784 | tf_op jit(solution)/shard_map/ppermute | solution.py:457
  73.7 1.3 %turned_features.3 = (bf16[896,640]{1,0:T(8,128)(2,1)S(1)}, bf16[896,640]{1,0:T(8,128)(2,1)S(1)}) custom-call(s32[1]{0:T(128)} %bitcast.rep_ref, bf16[64,3584]{1,0:T(8,128)(2,1)S(1)} %collective-permute-done.3.refs_0_, bf16[64,3584]{1,0:T(8,128)(2,1)S(1)} %collective-permute-done.8.refs_1_, bf16[64,3584]{1,0:T(8,128)(2,1)S(1)} %collective-permute-done.7.refs_0_.refs_2_, ...), custom_call_target="tpu_custom_call" | custom-call | flops 1024 | bytes 1024 | tf_op jit(solution)/shard_map/turned_features/pallas_call | solution.py:248
  75.1 0.5 collective-permute-start.18
  75.7 8.0 %round_logits.9 = (bf16[320,2048]{1,0:T(8,128)(2,1)}, f32[32,128]{1,0:T(8,128)S(1)}) custom-call(bf16[64,3584]{1,0:T(8,128)(2,1)S(1)} %collective-permute-done.11.refs_5_.refs_0_, bf16[64,3584]{1,0:T(8,128)(2,1)S(1)} %collective-permute-done.12.refs_6_.refs_1_, bf16[64,3584]{1,0:T(8,128)(2,1)S(1)} %collective-permute-done.13.refs_7_.refs_2_, ...), custom_call_target="tpu_custom_call" | custom-call | flops 1024 | bytes 1024 | tf_op jit(solution)/shard_map/round_logits/pallas_call | solution.py:206
  83.7 0.6 collective-permute-start.21
  84.4 1.5 %collective-permute-start.19 = (f32[32,128]{1,0:T(8,128)S(1)}, f32[32,128]{1,0:T(8,128)S(1)}, u32[]{:S(2)}, u32[]{:S(2)}) collective-permute-start(f32[32,128]{1,0:T(8,128)S(1)} %get-tuple-element.91.own_ref), channel_id=1, source_target_pairs={{0,1},{1,0},{2,3},{3,2},{4,5},{5,4},{6,7},{7,6},{8,9},{9,8},{10,11... | collective-permute-start | bytes 49160 | tf_op jit(solution)/shard_map/ppermute | solution.py:457
  85.9 1.0 collective-permute-done.21.both_ref
  86.9 1.2 %collective-permute-done.19.across_ref = f32[32,128]{1,0:T(8,128)S(1)} collective-permute-done((f32[32,128]{1,0:T(8,128)S(1)}, f32[32,128]{1,0:T(8,128)S(1)}, u32[]{:S(2)}, u32[]{:S(2)}) %collective-permute-start.19) | collective-permute-done | bytes 16416 | tf_op jit(solution)/shard_map/ppermute | solution.py:457
  88.2 2.1 %collective-permute-start.25 = (f32[64,128]{1,0:T(8,128)S(1)}, f32[64,128]{1,0:T(8,128)S(1)}, u32[]{:S(2)}, u32[]{:S(2)}) collective-permute-start(f32[64,128]{1,0:T(8,128)S(1)} %get-tuple-element.92.refs_10_), channel_id=1, source_target_pairs={{0,2},{1,3},{2,4},{3,5},{4,6},{5,7},{6,0},{7,1},{8,10},{9,11},{10,... | collective-permute-start | bytes 98312 | tf_op jit(solution)/shard_map/ppermute | solution.py:467
  90.3 0.9 collective-permute-start.24
  91.2 2.2 %collective-permute-start.23 = (f32[64,128]{1,0:T(8,128)S(1)}, f32[64,128]{1,0:T(8,128)S(1)}, u32[]{:S(2)}, u32[]{:S(2)}) collective-permute-start(f32[64,128]{1,0:T(8,128)S(1)} %get-tuple-element.92.refs_10_), channel_id=1, source_target_pairs={{0,6},{1,7},{2,0},{3,1},{4,2},{5,3},{6,4},{7,5},{8,14},{9,15},{10,... | collective-permute-start | bytes 98312 | tf_op jit(solution)/shard_map/ppermute | solution.py:467
  93.4 0.6 collective-permute-done.25.refs_13_
  94.0 1.7 %collective-permute-done.24.refs_12_ = f32[64,128]{1,0:T(8,128)S(1)} collective-permute-done((f32[64,128]{1,0:T(8,128)S(1)}, f32[64,128]{1,0:T(8,128)S(1)}, u32[]{:S(2)}, u32[]{:S(2)}) %collective-permute-start.24) | collective-permute-done | bytes 32800 | tf_op jit(solution)/shard_map/ppermute | solution.py:467
  95.7 20.0 %refresh_states.1 = (bf16[896,2048]{1,0:T(8,128)(2,1)}, bf16[896,2048]{1,0:T(8,128)(2,1)}, bf16[896,2048]{1,0:T(8,128)(2,1)}) custom-call(bf16[896,384]{1,0:T(8,128)(2,1)S(1)} %get-tuple-element.68.refs_0_, bf16[896,384]{1,0:T(8,128)(2,1)S(1)} %collective-permute-done.9.refs_1_, bf16[896,640]{1,0:T(8,128)(2,1)S(1)} %get-tuple-element.82.refs_2_, ...), custom_call_target="tpu_custom_call" | custom-call | flops 1024 | bytes 1024 | tf_op jit(solution)/shard_map/refresh_states/pallas_call | solution.py:414
  (45 shorter events, 1.2 us)
Async XLA Ops:
  0.6 0.7 copy-start
  2.6 15.6 %collective-permute-start.2 = (bf16[64,3584]{1,0:T(8,128)(2,1)S(1)}, bf16[64,3584]{1,0:T(8,128)(2,1)S(1)}, u32[]{:S(2)}, u32[]{:S(2)}) collective-permute-start(bf16[64,3584]{1,0:T(8,128)(2,1)S(1)} %normalized.1.refs_0_), channel_id=1, source_target_pairs={{0,2},{1,3},{2,4},{3,5},{4,6},{5,7},{6,0},{7,1},{8,10},{9,11},{10,... | collective-permute-start | bytes 1376264 | tf_op jit(solution)/shard_map/ppermute | solution.py:467
  5.7 21.1 %collective-permute-start.1 = (bf16[64,3584]{1,0:T(8,128)(2,1)S(1)}, bf16[64,3584]{1,0:T(8,128)(2,1)S(1)}, u32[]{:S(2)}, u32[]{:S(2)}) collective-permute-start(bf16[64,3584]{1,0:T(8,128)(2,1)S(1)} %normalized.1.refs_0_), channel_id=1, source_target_pairs={{0,1},{1,0},{2,3},{3,2},{4,5},{5,4},{6,7},{7,6},{8,9},{9,8},{10,11... | collective-permute-start | bytes 1376264 | tf_op jit(solution)/shard_map/ppermute | solution.py:457
  7.2 19.6 %collective-permute-start = (bf16[64,3584]{1,0:T(8,128)(2,1)S(1)}, bf16[64,3584]{1,0:T(8,128)(2,1)S(1)}, u32[]{:S(2)}, u32[]{:S(2)}) collective-permute-start(bf16[64,3584]{1,0:T(8,128)(2,1)S(1)} %normalized.1.refs_0_), channel_id=1, source_target_pairs={{0,16},{8,24},{16,0},{24,8},{1,17},{9,25},{17,1},{25,9},{2,18},{10... | collective-permute-start | bytes 1376264 | tf_op jit(solution)/shard_map/ppermute | solution.py:451
  18.2 14.9 %collective-permute-start.5 = (bf16[64,3584]{1,0:T(8,128)(2,1)S(1)}, bf16[64,3584]{1,0:T(8,128)(2,1)S(1)}, u32[]{:S(2)}, u32[]{:S(2)}) collective-permute-start(bf16[64,3584]{1,0:T(8,128)(2,1)S(1)} %collective-permute-done.2.refs_0_.refs_3_), channel_id=1, source_target_pairs={{0,1},{1,0},{2,3},{3,2},{4,5},{5,4},{6,7},{7,6},{8,9},{9,8},{10,11... | collective-permute-start | bytes 1376264 | tf_op jit(solution)/shard_map/ppermute | solution.py:457
  19.7 13.4 %collective-permute-start.4 = (bf16[64,3584]{1,0:T(8,128)(2,1)S(1)}, bf16[64,3584]{1,0:T(8,128)(2,1)S(1)}, u32[]{:S(2)}, u32[]{:S(2)}) collective-permute-start(bf16[64,3584]{1,0:T(8,128)(2,1)S(1)} %collective-permute-done.2.refs_0_.refs_3_), channel_id=1, source_target_pairs={{0,16},{8,24},{16,0},{24,8},{1,17},{9,25},{17,1},{25,9},{2,18},{10... | collective-permute-start | bytes 1376264 | tf_op jit(solution)/shard_map/ppermute | solution.py:451
  21.2 12.7 %collective-permute-start.3 = (bf16[64,3584]{1,0:T(8,128)(2,1)S(1)}, bf16[64,3584]{1,0:T(8,128)(2,1)S(1)}, u32[]{:S(2)}, u32[]{:S(2)}) collective-permute-start(bf16[64,3584]{1,0:T(8,128)(2,1)S(1)} %collective-permute-done.2.refs_0_.refs_3_), channel_id=1, source_target_pairs={{0,2},{1,3},{2,4},{3,5},{4,6},{5,7},{6,0},{7,1},{8,10},{9,11},{10,... | collective-permute-start | bytes 1376264 | tf_op jit(solution)/shard_map/ppermute | solution.py:467
  26.8 15.6 %collective-permute-start.8 = (bf16[64,3584]{1,0:T(8,128)(2,1)S(1)}, bf16[64,3584]{1,0:T(8,128)(2,1)S(1)}, u32[]{:S(2)}, u32[]{:S(2)}) collective-permute-start(bf16[64,3584]{1,0:T(8,128)(2,1)S(1)} %collective-permute-done.refs_1_), channel_id=1, source_target_pairs={{0,1},{1,0},{2,3},{3,2},{4,5},{5,4},{6,7},{7,6},{8,9},{9,8},{10,11... | collective-permute-start | bytes 1376264 | tf_op jit(solution)/shard_map/ppermute | solution.py:457
  33.9 13.2 %collective-permute-start.7 = (bf16[64,3584]{1,0:T(8,128)(2,1)S(1)}, bf16[64,3584]{1,0:T(8,128)(2,1)S(1)}, u32[]{:S(2)}, u32[]{:S(2)}) collective-permute-start(bf16[64,3584]{1,0:T(8,128)(2,1)S(1)} %collective-permute-done.3.refs_0_), channel_id=1, source_target_pairs={{0,16},{8,24},{16,0},{24,8},{1,17},{9,25},{17,1},{25,9},{2,18},{10... | collective-permute-start | bytes 1376264 | tf_op jit(solution)/shard_map/ppermute | solution.py:451
  34.4 12.7 %collective-permute-start.6 = (bf16[64,3584]{1,0:T(8,128)(2,1)S(1)}, bf16[64,3584]{1,0:T(8,128)(2,1)S(1)}, u32[]{:S(2)}, u32[]{:S(2)}) collective-permute-start(bf16[64,3584]{1,0:T(8,128)(2,1)S(1)} %collective-permute-done.3.refs_0_), channel_id=1, source_target_pairs={{0,2},{1,3},{2,4},{3,5},{4,6},{5,7},{6,0},{7,1},{8,10},{9,11},{10,... | collective-permute-start | bytes 1376264 | tf_op jit(solution)/shard_map/ppermute | solution.py:467
  35.0 16.8 %collective-permute-start.10 = (bf16[64,3584]{1,0:T(8,128)(2,1)S(1)}, bf16[64,3584]{1,0:T(8,128)(2,1)S(1)}, u32[]{:S(2)}, u32[]{:S(2)}) collective-permute-start(bf16[64,3584]{1,0:T(8,128)(2,1)S(1)} %collective-permute-done.3.refs_0_), channel_id=1, source_target_pairs={{0,1},{1,0},{2,3},{3,2},{4,5},{5,4},{6,7},{7,6},{8,9},{9,8},{10,11... | collective-permute-start | bytes 1376264 | tf_op jit(solution)/shard_map/ppermute | solution.py:457
  47.1 11.8 %collective-permute-start.11 = (bf16[64,3584]{1,0:T(8,128)(2,1)S(1)}, bf16[64,3584]{1,0:T(8,128)(2,1)S(1)}, u32[]{:S(2)}, u32[]{:S(2)}) collective-permute-start(bf16[64,3584]{1,0:T(8,128)(2,1)S(1)} %collective-permute-done.6.refs_2_.refs_4_), channel_id=1, source_target_pairs={{0,16},{8,24},{16,0},{24,8},{1,17},{9,25},{17,1},{25,9},{2,18},{10... | collective-permute-start | bytes 1376264 | tf_op jit(solution)/shard_map/ppermute | solution.py:451
  49.6 10.1 %collective-permute-start.9 = (bf16[896,384]{1,0:T(8,128)(2,1)S(1)}, bf16[896,384]{1,0:T(8,128)(2,1)S(1)}, u32[]{:S(2)}, u32[]{:S(2)}) collective-permute-start(bf16[896,384]{1,0:T(8,128)(2,1)S(1)} %get-tuple-element.69), channel_id=1, source_target_pairs={{0,8},{8,0},{16,24},{24,16},{1,9},{9,1},{17,25},{25,17},{2,10},{10... | collective-permute-start | bytes 2064392 | tf_op jit(solution)/shard_map/ppermute | solution.py:454
  49.6 18.7 %collective-permute-start.13 = (bf16[64,3584]{1,0:T(8,128)(2,1)S(1)}, bf16[64,3584]{1,0:T(8,128)(2,1)S(1)}, u32[]{:S(2)}, u32[]{:S(2)}) collective-permute-start(bf16[64,3584]{1,0:T(8,128)(2,1)S(1)} %collective-permute-done.8.refs_1_), channel_id=1, source_target_pairs={{0,2},{1,3},{2,4},{3,5},{4,6},{5,7},{6,0},{7,1},{8,10},{9,11},{10,... | collective-permute-start | bytes 1376264 | tf_op jit(solution)/shard_map/ppermute | solution.py:467
  51.3 17.0 %collective-permute-start.12 = (bf16[64,3584]{1,0:T(8,128)(2,1)S(1)}, bf16[64,3584]{1,0:T(8,128)(2,1)S(1)}, u32[]{:S(2)}, u32[]{:S(2)}) collective-permute-start(bf16[64,3584]{1,0:T(8,128)(2,1)S(1)} %collective-permute-done.6.refs_2_.refs_4_), channel_id=1, source_target_pairs={{0,1},{1,0},{2,3},{3,2},{4,5},{5,4},{6,7},{7,6},{8,9},{9,8},{10,11... | collective-permute-start | bytes 1376264 | tf_op jit(solution)/shard_map/ppermute | solution.py:457
  51.8 16.5 %collective-permute-start.14 = (bf16[64,3584]{1,0:T(8,128)(2,1)S(1)}, bf16[64,3584]{1,0:T(8,128)(2,1)S(1)}, u32[]{:S(2)}, u32[]{:S(2)}) collective-permute-start(bf16[64,3584]{1,0:T(8,128)(2,1)S(1)} %collective-permute-done.10.refs_1_.refs_3_), channel_id=1, source_target_pairs={{0,16},{8,24},{16,0},{24,8},{1,17},{9,25},{17,1},{25,9},{2,18},{10... | collective-permute-start | bytes 1376264 | tf_op jit(solution)/shard_map/ppermute | solution.py:451
  58.9 14.8 %collective-permute-start.15 = (bf16[64,3584]{1,0:T(8,128)(2,1)S(1)}, bf16[64,3584]{1,0:T(8,128)(2,1)S(1)}, u32[]{:S(2)}, u32[]{:S(2)}) collective-permute-start(bf16[64,3584]{1,0:T(8,128)(2,1)S(1)} %collective-permute-done.11.refs_5_.refs_0_), channel_id=1, source_target_pairs={{0,1},{1,0},{2,3},{3,2},{4,5},{5,4},{6,7},{7,6},{8,9},{9,8},{10,11... | collective-permute-start | bytes 1376264 | tf_op jit(solution)/shard_map/ppermute | solution.py:457
  68.3 6.7 %copy-start.1 = (bf16[384,2048]{1,0:T(8,128)(2,1)S(1)}, bf16[384,2048]{1,0:T(8,128)(2,1)}, u32[]{:S(2)}) copy-start(bf16[384,2048]{1,0:T(8,128)(2,1)} %get-tuple-element.88.refs_4_) | copy-start | bytes 4718596
  68.3 6.8 %copy-start.2 = (bf16[320,2048]{1,0:T(8,128)(2,1)S(1)}, bf16[320,2048]{1,0:T(8,128)(2,1)}, u32[]{:S(2)}) copy-start(bf16[320,2048]{1,0:T(8,128)(2,1)} %get-tuple-element.89.refs_5_) | copy-start | bytes 3932164
  75.0 10.8 %collective-permute-start.17 = (bf16[384,2048]{1,0:T(8,128)(2,1)S(1)}, bf16[384,2048]{1,0:T(8,128)(2,1)S(1)}, u32[]{:S(2)}, u32[]{:S(2)}) collective-permute-start(bf16[384,2048]{1,0:T(8,128)(2,1)S(1)} %copy-done.1), channel_id=1, source_target_pairs={{0,8},{8,0},{16,24},{24,16},{1,9},{9,1},{17,25},{25,17},{2,10},{10... | collective-permute-start | bytes 4718600 | tf_op jit(solution)/shard_map/ppermute | solution.py:454
  75.1 10.7 %collective-permute-start.18 = (bf16[320,2048]{1,0:T(8,128)(2,1)S(1)}, bf16[320,2048]{1,0:T(8,128)(2,1)S(1)}, u32[]{:S(2)}, u32[]{:S(2)}) collective-permute-start(bf16[320,2048]{1,0:T(8,128)(2,1)S(1)} %copy-done.2), channel_id=1, source_target_pairs={{0,8},{8,0},{16,24},{24,16},{1,9},{9,1},{17,25},{25,17},{2,10},{10... | collective-permute-start | bytes 3932168 | tf_op jit(solution)/shard_map/ppermute | solution.py:454
  75.6 8.7 %collective-permute-start.16 = (bf16[896,640]{1,0:T(8,128)(2,1)S(1)}, bf16[896,640]{1,0:T(8,128)(2,1)S(1)}, u32[]{:S(2)}, u32[]{:S(2)}) collective-permute-start(bf16[896,640]{1,0:T(8,128)(2,1)S(1)} %get-tuple-element.83), channel_id=1, source_target_pairs={{0,8},{8,0},{16,24},{24,16},{1,9},{9,1},{17,25},{25,17},{2,10},{10... | collective-permute-start | bytes 3440648 | tf_op jit(solution)/shard_map/ppermute | solution.py:454
  83.7 3.2 %collective-permute-start.21 = (f32[32,128]{1,0:T(8,128)S(1)}, f32[32,128]{1,0:T(8,128)S(1)}, u32[]{:S(2)}, u32[]{:S(2)}) collective-permute-start(f32[32,128]{1,0:T(8,128)S(1)} %get-tuple-element.91.own_ref), channel_id=1, source_target_pairs={{0,9},{1,8},{2,11},{3,10},{4,13},{5,12},{6,15},{7,14},{8,1},{9,0},... | collective-permute-start | bytes 49160 | tf_op jit(solution)/shard_map/ppermute | solution.py:464
  84.3 2.6 %collective-permute-start.20 = (f32[32,128]{1,0:T(8,128)S(1)}, f32[32,128]{1,0:T(8,128)S(1)}, u32[]{:S(2)}, u32[]{:S(2)}) collective-permute-start(f32[32,128]{1,0:T(8,128)S(1)} %get-tuple-element.91.own_ref), channel_id=1, source_target_pairs={{0,8},{8,0},{16,24},{24,16},{1,9},{9,1},{17,25},{25,17},{2,10},{10... | collective-permute-start | bytes 49160 | tf_op jit(solution)/shard_map/ppermute | solution.py:454
  84.4 3.7 %collective-permute-start.19 = (f32[32,128]{1,0:T(8,128)S(1)}, f32[32,128]{1,0:T(8,128)S(1)}, u32[]{:S(2)}, u32[]{:S(2)}) collective-permute-start(f32[32,128]{1,0:T(8,128)S(1)} %get-tuple-element.91.own_ref), channel_id=1, source_target_pairs={{0,1},{1,0},{2,3},{3,2},{4,5},{5,4},{6,7},{7,6},{8,9},{9,8},{10,11... | collective-permute-start | bytes 49160 | tf_op jit(solution)/shard_map/ppermute | solution.py:457
  88.1 7.6 %collective-permute-start.22 = (bf16[320,2048]{1,0:T(8,128)(2,1)}, bf16[320,2048]{1,0:T(8,128)(2,1)S(1)}, u32[]{:S(2)}, u32[]{:S(2)}) collective-permute-start(bf16[320,2048]{1,0:T(8,128)(2,1)} %get-tuple-element.93.refs_6_), channel_id=1, source_target_pairs={{0,8},{8,0},{16,24},{24,16},{1,9},{9,1},{17,25},{25,17},{2,10},{10... | collective-permute-start | bytes 3932168 | tf_op jit(solution)/shard_map/ppermute | solution.py:454
  88.2 5.8 %collective-permute-start.25 = (f32[64,128]{1,0:T(8,128)S(1)}, f32[64,128]{1,0:T(8,128)S(1)}, u32[]{:S(2)}, u32[]{:S(2)}) collective-permute-start(f32[64,128]{1,0:T(8,128)S(1)} %get-tuple-element.92.refs_10_), channel_id=1, source_target_pairs={{0,2},{1,3},{2,4},{3,5},{4,6},{5,7},{6,0},{7,1},{8,10},{9,11},{10,... | collective-permute-start | bytes 98312 | tf_op jit(solution)/shard_map/ppermute | solution.py:467
  90.3 5.4 %collective-permute-start.24 = (f32[64,128]{1,0:T(8,128)S(1)}, f32[64,128]{1,0:T(8,128)S(1)}, u32[]{:S(2)}, u32[]{:S(2)}) collective-permute-start(f32[64,128]{1,0:T(8,128)S(1)} %get-tuple-element.92.refs_10_), channel_id=1, source_target_pairs={{0,4},{1,5},{2,6},{3,7},{4,0},{5,1},{6,2},{7,3},{8,12},{9,13},{10,... | collective-permute-start | bytes 98312 | tf_op jit(solution)/shard_map/ppermute | solution.py:467
  91.2 4.5 %collective-permute-start.23 = (f32[64,128]{1,0:T(8,128)S(1)}, f32[64,128]{1,0:T(8,128)S(1)}, u32[]{:S(2)}, u32[]{:S(2)}) collective-permute-start(f32[64,128]{1,0:T(8,128)S(1)} %get-tuple-element.92.refs_10_), channel_id=1, source_target_pairs={{0,6},{1,7},{2,0},{3,1},{4,2},{5,3},{6,4},{7,5},{8,14},{9,15},{10,... | collective-permute-start | bytes 98312 | tf_op jit(solution)/shard_map/ppermute | solution.py:467

commit v12 on v11

--- a/solution.py
+++ b/solution.py
@@ -472,7 +472,8 @@
     groups += [
         [(0, 0, split), (1, 1, 0)],
         [(0, 1, split), (1, 0, split), (0, 0, split + 1)],
-        [(0, 1, split + 1), (1, 0, split + 1)] + [(1, 1, turn) for turn in range(1, lines)],
+        [(0, 1, split + 1), (1, 0, split + 1), (1, 1, 1)],
+        [(1, 1, turn) for turn in range(split, lines)],
     ]
     early_blocks, late_blocks = sum(groups[:split], []), sum(groups[split:], [])
 
@@ -509,7 +510,7 @@
     def diagonal(turn):
         if turn == 1:
             return to_z(held[1, 1, 0], 1)
-        if turn == 2:
+        if turn % 2 == 0:
             return to_x(held[1, 0, turn])
         return to_y(held[0, 1, turn])
 
@@ -559,13 +560,16 @@
     held[1, 1, lines - 1] = diagonal(lines - 1)
     early_ids[0] = after(early_ids[0], middle_exp, held[0, 1, lines - 1])
     sums = one_hot_sums(early, early_ids, columns)
+    last_exp, stats = logits(groups[split + 2], stats, *sums, exp_rows=5 * length)
     late = [held[block] for block in late_blocks]
-    late[0] = after(late[0], *sums)
+    late[0] = after(late[0], last_exp)
     late = turned_features(rep_scalar, late, rows)
     late = [late[0], to_core(late[1])]
     ready = lax.optimization_barrier((early_exp, middle_exp, late[0]))
     other_exps = [to_core(exp) for exp in ready[:2]]
-    last_exp, stats = logits(groups[-1], stats, late[0], *sums)
+    last_exp, stats = logits(
+        groups[-1], stats, late[0], first_row=3 * length, exp_rows=5 * length, into=last_exp
+    )
     exps = [early_exp, middle_exp, last_exp]
     across_stats, core_stats, both_stats = to_y(stats), to_core(stats), to_y_core(stats)
     merged, first = merged_stats(

time: 116 us -> 118 us (1.017)
  Pallas kernels: 67.6 us -> 70.1 us
  starting transfers between devices: 25.4 us -> 23.2 us
  waiting for transfers between devices: 14.4 us -> 15.8 us
    ppermute x5 -> x6, waiting for transfers between devices: 0.89 us -> 7.3 us  [to_x(): return lax.ppermute(values, 'rep', swap_pairs(reps, 2))]
    ppermute x7 -> x6, waiting for transfers between devices: 6.59 us -> 1.97 us  [to_y(): return lax.ppermute(values, 'shard', swap_pairs(shards, 1))]
    pallas_call x5 -> x6, Pallas kernels: 30 us -> 32.5 us  [round_logits(): pl.pallas_call(functools.partial(logits_kernel, stat_rows, first_row, len...]
    ppermute x7, starting transfers between devices: 10.4 us -> 8.3 us  [to_z(): return lax.ppermute(values, 'shard', shift_pairs(lines, along, 0))]
    ppermute x7 -> x6, starting transfers between devices: 7.86 us -> 6.09 us  [to_y(): return lax.ppermute(values, 'shard', swap_pairs(shards, 1))]
    ppermute x5 -> x6, starting transfers between devices: 5.62 us -> 6.67 us  [to_x(): return lax.ppermute(values, 'rep', swap_pairs(reps, 2))]
  transfers between devices with their start and end apart: 26 -> 26, of which waited for: 8 -> 9; matrix products, arithmetic and copies ran while one was open for 6% -> 6% of each run, Pallas kernels for 39% -> 40%
where the time goes in v12:
time: 118 us
  Pallas kernels  70.1 us (59%)
  starting transfers between devices  23.2 us (20%)
  waiting for transfers between devices  15.8 us (13%)
  local copies, waits for them, and re-layouts  4.15 us (4%)
  other arithmetic  3.62 us (3%)
    pallas_call x6, Pallas kernels, round_logits(): pl.pallas_call(functools.partial(logits_kernel, stat_rows, first_row, len...  32.5 us
    pallas_call x1, Pallas kernels, refresh_states(): pl.pallas_call(functools.partial(refresh_kernel, lines, length, block_row...  20 us
    pallas_call x1, Pallas kernels, one_hot_sums(): pl.pallas_call(functools.partial(one_hot_kernel, len(features)), grid=(co...  8.63 us
    ppermute x7, starting transfers between devices, to_z(): return lax.ppermute(values, 'shard', shift_pairs(lines, along, 0))  8.3 us
    ppermute x6, waiting for transfers between devices, to_x(): return lax.ppermute(values, 'rep', swap_pairs(reps, 2))  7.3 us
    ppermute x6, starting transfers between devices, to_x(): return lax.ppermute(values, 'rep', swap_pairs(reps, 2))  6.67 us
    ppermute x6, starting transfers between devices, to_y(): return lax.ppermute(values, 'shard', swap_pairs(shards, 1))  6.09 us
    ppermute x7, waiting for transfers between devices, to_z(): return lax.ppermute(values, 'shard', shift_pairs(lines, along, 0))  5.96 us
  transfers between devices with their start and end apart: 26, of which 9 were waited for; matrix products, arithmetic and copies ran while one was open for 6% of the time, Pallas kernels for 40%

profile of v12, /device:TPU:0, one launch (start us, length us, event | category | flops | bytes accessed | tf_op | source)
XLA Modules:
  0.0 117.8 jit_solution(15438469567629351505)
XLA Ops:
  0.6 0.7 copy-done
  1.3 1.2 %normalized.1.refs_0_ = bf16[64,3584]{1,0:T(8,128)(2,1)S(1)} custom-call(bf16[64,3584]{1,0:T(8,128)(2,1)} %hidden_ref.1, f32[3584]{0:T(1024)S(1)} %copy-done), custom_call_target="tpu_custom_call" | custom-call | flops 1024 | bytes 1024 | tf_op jit(solution)/shard_map/normalized/pallas_call | solution.py:93
  2.6 3.1 %collective-permute-start.2 = (bf16[64,3584]{1,0:T(8,128)(2,1)S(1)}, bf16[64,3584]{1,0:T(8,128)(2,1)S(1)}, u32[]{:S(2)}, u32[]{:S(2)}) collective-permute-start(bf16[64,3584]{1,0:T(8,128)(2,1)S(1)} %normalized.1.refs_0_), channel_id=1, source_target_pairs={{0,2},{1,3},{2,4},{3,5},{4,6},{5,7},{6,0},{7,1},{8,10},{9,11},{10,... | collective-permute-start | bytes 1376264 | tf_op jit(solution)/shard_map/ppermute | solution.py:467
  5.7 1.5 %collective-permute-start.1 = (bf16[64,3584]{1,0:T(8,128)(2,1)S(1)}, bf16[64,3584]{1,0:T(8,128)(2,1)S(1)}, u32[]{:S(2)}, u32[]{:S(2)}) collective-permute-start(bf16[64,3584]{1,0:T(8,128)(2,1)S(1)} %normalized.1.refs_0_), channel_id=1, source_target_pairs={{0,1},{1,0},{2,3},{3,2},{4,5},{5,4},{6,7},{7,6},{8,9},{9,8},{10,11... | collective-permute-start | bytes 1376264 | tf_op jit(solution)/shard_map/ppermute | solution.py:457
  7.2 1.5 %collective-permute-start = (bf16[64,3584]{1,0:T(8,128)(2,1)S(1)}, bf16[64,3584]{1,0:T(8,128)(2,1)S(1)}, u32[]{:S(2)}, u32[]{:S(2)}) collective-permute-start(bf16[64,3584]{1,0:T(8,128)(2,1)S(1)} %normalized.1.refs_0_), channel_id=1, source_target_pairs={{0,16},{8,24},{16,0},{24,8},{1,17},{9,25},{17,1},{25,9},{2,18},{10... | collective-permute-start | bytes 1376264 | tf_op jit(solution)/shard_map/ppermute | solution.py:451
  8.7 0.7 fusion.4
  9.3 0.7 compare_and_fusion
  10.0 0.7 multiply_add_fusion
  10.7 1.2 %slice.31 = s32[1]{0:T(128)} slice(s32[2048]{0:T(1024)} %param.12), slice={[0:1]} | slice | bytes 8 | tf_op jit(solution)/shard_map/jit(_roll_static)/slice | solution.py:486
  11.9 0.8 slice.30
  12.8 0.7 broadcast_subtract_fusion
  13.6 0.7 fusion.1
  14.4 0.6 gather_fusion
  15.5 2.7 %collective-permute-done.2.refs_0_.refs_3_ = bf16[64,3584]{1,0:T(8,128)(2,1)S(1)} collective-permute-done((bf16[64,3584]{1,0:T(8,128)(2,1)S(1)}, bf16[64,3584]{1,0:T(8,128)(2,1)S(1)}, u32[]{:S(2)}, u32[]{:S(2)}) %collective-permute-start.2) | collective-permute-done | bytes 458784 | tf_op jit(solution)/shard_map/ppermute | solution.py:467
  18.2 1.5 %collective-permute-start.5 = (bf16[64,3584]{1,0:T(8,128)(2,1)S(1)}, bf16[64,3584]{1,0:T(8,128)(2,1)S(1)}, u32[]{:S(2)}, u32[]{:S(2)}) collective-permute-start(bf16[64,3584]{1,0:T(8,128)(2,1)S(1)} %collective-permute-done.2.refs_0_.refs_3_), channel_id=1, source_target_pairs={{0,1},{1,0},{2,3},{3,2},{4,5},{5,4},{6,7},{7,6},{8,9},{9,8},{10,11... | collective-permute-start | bytes 1376264 | tf_op jit(solution)/shard_map/ppermute | solution.py:457
  19.7 1.5 %collective-permute-start.4 = (bf16[64,3584]{1,0:T(8,128)(2,1)S(1)}, bf16[64,3584]{1,0:T(8,128)(2,1)S(1)}, u32[]{:S(2)}, u32[]{:S(2)}) collective-permute-start(bf16[64,3584]{1,0:T(8,128)(2,1)S(1)} %collective-permute-done.2.refs_0_.refs_3_), channel_id=1, source_target_pairs={{0,16},{8,24},{16,0},{24,8},{1,17},{9,25},{17,1},{25,9},{2,18},{10... | collective-permute-start | bytes 1376264 | tf_op jit(solution)/shard_map/ppermute | solution.py:451
  21.2 5.5 %prepared.1 = (bf16[3584,2048]{1,0:T(8,128)(2,1)S(1)}, s32[1280,128]{1,0:T(8,128)S(1)}, s32[1280,128]{1,0:T(8,128)S(1)}) custom-call(bf16[3584,2048]{1,0:T(8,128)(2,1)} %weight_ref.1, s32[1,1280]{1,0:T(1,128)S(1)} %squeeze.14.true_ids, s32[1,1280]{1,0:T(1,128)S(1)} %squeeze.15.sample_ids, f32[32,128]{1,0:T(8,128)S(1)} %broadcast_in_dim.20.refs_0_.refs_4_), custom_call_target="tpu_custom_call" | custom-call | flops 1024 | bytes 1024 | tf_op jit(solution)/shard_map/prepared/pallas_call | solution.py:127
  26.7 0.6 collective-permute-start.8
  27.4 5.8 %round_logits.6 = (bf16[384,2048]{1,0:T(8,128)(2,1)}, f32[32,128]{1,0:T(8,128)S(1)}) custom-call(bf16[64,3584]{1,0:T(8,128)(2,1)S(1)} %normalized.1.refs_0_, bf16[64,3584]{1,0:T(8,128)(2,1)S(1)} %collective-permute-done.refs_1_, bf16[64,3584]{1,0:T(8,128)(2,1)S(1)} %collective-permute-done.1.refs_2_, ...), custom_call_target="tpu_custom_call" | custom-call | flops 1024 | bytes 1024 | tf_op jit(solution)/shard_map/round_logits/pallas_call | solution.py:206
  33.2 0.7 collective-permute-done.3.refs_0_
  33.9 0.8 collective-permute-start.7
  34.7 1.3 %collective-permute-start.6 = (bf16[64,3584]{1,0:T(8,128)(2,1)S(1)}, bf16[64,3584]{1,0:T(8,128)(2,1)S(1)}, u32[]{:S(2)}, u32[]{:S(2)}) collective-permute-start(bf16[64,3584]{1,0:T(8,128)(2,1)S(1)} %collective-permute-done.3.refs_0_), channel_id=1, source_target_pairs={{0,2},{1,3},{2,4},{3,5},{4,6},{5,7},{6,0},{7,1},{8,10},{9,11},{10,... | collective-permute-start | bytes 1376264 | tf_op jit(solution)/shard_map/ppermute | solution.py:467
  36.0 0.5 collective-permute-start.11
  36.5 5.8 %round_logits.7 = (bf16[384,2048]{1,0:T(8,128)(2,1)}, f32[32,128]{1,0:T(8,128)S(1)}) custom-call(bf16[64,3584]{1,0:T(8,128)(2,1)S(1)} %collective-permute-done.2.refs_0_.refs_3_, bf16[64,3584]{1,0:T(8,128)(2,1)S(1)} %collective-permute-done.4.refs_1_.refs_4_, ...), custom_call_target="tpu_custom_call", output_to_operand_aliasing={{0}: (5, {})} | custom-call | flops 1024 | bytes 1024 | tf_op jit(solution)/shard_map/round_logits/pallas_call | solution.py:206
  42.3 0.7 collective-permute-done.8.refs_1_
  43.0 4.7 %round_logits.8 = (bf16[320,2048]{1,0:T(8,128)(2,1)}, f32[32,128]{1,0:T(8,128)S(1)}) custom-call(bf16[64,3584]{1,0:T(8,128)(2,1)S(1)} %collective-permute-done.3.refs_0_, bf16[64,3584]{1,0:T(8,128)(2,1)S(1)} %collective-permute-done.8.refs_1_, bf16[3584,2048]{1,0:T(8,128)(2,1)S(1)} %get-tuple-element.58.refs_3_.refs_2_, f32[32,128]{1,0:T(8,128)S(1)} %get-tuple-element.67.refs_3_), custom_call_target="tpu_custom_call" | custom-call | flops 1024 | bytes 1024 | tf_op jit(solution)/shard_map/round_logits/pallas_call | solution.py:206
  47.8 2.8 %collective-permute-done.7.refs_0_.refs_2_ = bf16[64,3584]{1,0:T(8,128)(2,1)S(1)} collective-permute-done((bf16[64,3584]{1,0:T(8,128)(2,1)S(1)}, bf16[64,3584]{1,0:T(8,128)(2,1)S(1)}, u32[]{:S(2)}, u32[]{:S(2)}) %collective-permute-start.7) | collective-permute-done | bytes 458784 | tf_op jit(solution)/shard_map/ppermute | solution.py:451
  50.6 1.5 %collective-permute-start.10 = (bf16[64,3584]{1,0:T(8,128)(2,1)S(1)}, bf16[64,3584]{1,0:T(8,128)(2,1)S(1)}, u32[]{:S(2)}, u32[]{:S(2)}) collective-permute-start(bf16[64,3584]{1,0:T(8,128)(2,1)S(1)} %collective-permute-done.6.refs_2_.refs_4_), channel_id=1, source_target_pairs={{0,16},{8,24},{16,0},{24,8},{1,17},{9,25},{17,1},{25,9},{2,18},{10... | collective-permute-start | bytes 1376264 | tf_op jit(solution)/shard_map/ppermute | solution.py:451
  52.1 0.9 turned_features.2
  53.1 0.6 collective-permute-start.12
  53.7 0.8 collective-permute-start.14
  54.4 5.8 %round_logits.9 = (bf16[320,2048]{1,0:T(8,128)(2,1)}, f32[32,128]{1,0:T(8,128)S(1)}) custom-call(bf16[64,3584]{1,0:T(8,128)(2,1)S(1)} %collective-permute-done.7.refs_0_.refs_2_, bf16[64,3584]{1,0:T(8,128)(2,1)S(1)} %collective-permute-done.11.refs_1_.refs_3_, ...), custom_call_target="tpu_custom_call", output_to_operand_aliasing={{0}: (5, {})} | custom-call | flops 1024 | bytes 1024 | tf_op jit(solution)/shard_map/round_logits/pallas_call | solution.py:206
  60.2 3.8 %collective-permute-done.10.refs_0_.refs_5_ = bf16[64,3584]{1,0:T(8,128)(2,1)S(1)} collective-permute-done((bf16[64,3584]{1,0:T(8,128)(2,1)S(1)}, bf16[64,3584]{1,0:T(8,128)(2,1)S(1)}, u32[]{:S(2)}, u32[]{:S(2)}) %collective-permute-start.10) | collective-permute-done | bytes 458784 | tf_op jit(solution)/shard_map/ppermute | solution.py:451
  64.0 0.8 collective-permute-start.15
  64.8 8.6 %one_hot_sums.1 = (bf16[896,2048]{1,0:T(8,128)(2,1)}, bf16[896,2048]{1,0:T(8,128)(2,1)}) custom-call(bf16[896,384]{1,0:T(8,128)(2,1)S(1)} %get-tuple-element.71.refs_0_, bf16[896,384]{1,0:T(8,128)(2,1)S(1)} %collective-permute-done.9.refs_1_, s32[1,768]{1,0:T(1,128)S(1)} %squeeze.12.refs_2_, s32[1,768]{1,0:T(1,128)S(1)} %squeeze.13.refs_3_), custom_call_target="tpu_custom_call" | custom-call | flops 1024 | bytes 1024 | tf_op jit(solution)/shard_map/one_hot_sums/pallas_call | solution.py:285
  73.4 5.7 %round_logits.10 = (bf16[320,2048]{1,0:T(8,128)(2,1)}, f32[32,128]{1,0:T(8,128)S(1)}) custom-call(bf16[64,3584]{1,0:T(8,128)(2,1)S(1)} %collective-permute-done.10.refs_0_.refs_5_, bf16[64,3584]{1,0:T(8,128)(2,1)S(1)} %collective-permute-done.12.refs_1_.refs_6_, bf16[64,3584]{1,0:T(8,128)(2,1)S(1)} %collective-permute-done.13.refs_2_.refs_7_, ...), custom_call_target="tpu_custom_call" | custom-call | flops 1024 | bytes 1024 | tf_op jit(solution)/shard_map/round_logits/pallas_call | solution.py:206
  79.2 1.4 %turned_features.3 = (bf16[896,640]{1,0:T(8,128)(2,1)S(1)}, bf16[896,640]{1,0:T(8,128)(2,1)S(1)}) custom-call(s32[1]{0:T(128)} %bitcast.rep_ref, bf16[64,3584]{1,0:T(8,128)(2,1)S(1)} %collective-permute-done.3.refs_0_, bf16[64,3584]{1,0:T(8,128)(2,1)S(1)} %collective-permute-done.8.refs_1_, bf16[64,3584]{1,0:T(8,128)(2,1)S(1)} %collective-permute-done.7.refs_0_.refs_2_, ...), custom_call_target="tpu_custom_call" | custom-call | flops 1024 | bytes 1024 | tf_op jit(solution)/shard_map/turned_features/pallas_call | solution.py:248
  81.1 0.3 collective-permute-start.16
  81.4 4.7 %round_logits.11 = (bf16[320,2048]{1,0:T(8,128)(2,1)}, f32[32,128]{1,0:T(8,128)S(1)}) custom-call(bf16[64,3584]{1,0:T(8,128)(2,1)S(1)} %collective-permute-done.14.refs_8_.refs_0_, bf16[64,3584]{1,0:T(8,128)(2,1)S(1)} %collective-permute-done.15.refs_9_.refs_1_, ...), custom_call_target="tpu_custom_call", output_to_operand_aliasing={{0}: (4, {})} | custom-call | flops 1024 | bytes 1024 | tf_op jit(solution)/shard_map/round_logits/pallas_call | solution.py:206
  86.2 1.2 collective-permute-start.21
  87.6 1.2 %collective-permute-start.19 = (f32[32,128]{1,0:T(8,128)S(1)}, f32[32,128]{1,0:T(8,128)S(1)}, u32[]{:S(2)}, u32[]{:S(2)}) collective-permute-start(f32[32,128]{1,0:T(8,128)S(1)} %get-tuple-element.97.own_ref), channel_id=1, source_target_pairs={{0,1},{1,0},{2,3},{3,2},{4,5},{5,4},{6,7},{7,6},{8,9},{9,8},{10,11... | collective-permute-start | bytes 49160 | tf_op jit(solution)/shard_map/ppermute | solution.py:457
  88.8 0.6 collective-permute-done.21.both_ref
  89.4 2.0 %collective-permute-done.19.across_ref = f32[32,128]{1,0:T(8,128)S(1)} collective-permute-done((f32[32,128]{1,0:T(8,128)S(1)}, f32[32,128]{1,0:T(8,128)S(1)}, u32[]{:S(2)}, u32[]{:S(2)}) %collective-permute-start.19) | collective-permute-done | bytes 16416 | tf_op jit(solution)/shard_map/ppermute | solution.py:457
  91.5 2.2 %collective-permute-start.24 = (f32[64,128]{1,0:T(8,128)S(1)}, f32[64,128]{1,0:T(8,128)S(1)}, u32[]{:S(2)}, u32[]{:S(2)}) collective-permute-start(f32[64,128]{1,0:T(8,128)S(1)} %get-tuple-element.98.refs_10_), channel_id=1, source_target_pairs={{0,4},{1,5},{2,6},{3,7},{4,0},{5,1},{6,2},{7,3},{8,12},{9,13},{10,... | collective-permute-start | bytes 98312 | tf_op jit(solution)/shard_map/ppermute | solution.py:467
  93.8 1.6 %collective-permute-start.23 = (f32[64,128]{1,0:T(8,128)S(1)}, f32[64,128]{1,0:T(8,128)S(1)}, u32[]{:S(2)}, u32[]{:S(2)}) collective-permute-start(f32[64,128]{1,0:T(8,128)S(1)} %get-tuple-element.98.refs_10_), channel_id=1, source_target_pairs={{0,6},{1,7},{2,0},{3,1},{4,2},{5,3},{6,4},{7,5},{8,14},{9,15},{10,... | collective-permute-start | bytes 98312 | tf_op jit(solution)/shard_map/ppermute | solution.py:467
  95.3 2.2 %collective-permute-done.25.refs_13_ = f32[64,128]{1,0:T(8,128)S(1)} collective-permute-done((f32[64,128]{1,0:T(8,128)S(1)}, f32[64,128]{1,0:T(8,128)S(1)}, u32[]{:S(2)}, u32[]{:S(2)}) %collective-permute-start.25) | collective-permute-done | bytes 32800 | tf_op jit(solution)/shard_map/ppermute | solution.py:467
  97.5 0.3 collective-permute-done.23.refs_11_
  97.8 20.0 %refresh_states.1 = (bf16[896,2048]{1,0:T(8,128)(2,1)}, bf16[896,2048]{1,0:T(8,128)(2,1)}, bf16[896,2048]{1,0:T(8,128)(2,1)}) custom-call(bf16[896,384]{1,0:T(8,128)(2,1)S(1)} %get-tuple-element.71.refs_0_, bf16[896,384]{1,0:T(8,128)(2,1)S(1)} %collective-permute-done.9.refs_1_, bf16[896,640]{1,0:T(8,128)(2,1)S(1)} %get-tuple-element.88.refs_2_, ...), custom_call_target="tpu_custom_call" | custom-call | flops 1024 | bytes 1024 | tf_op jit(solution)/shard_map/refresh_states/pallas_call | solution.py:414
  (46 shorter events, 1.9 us)
Async XLA Ops:
  0.6 0.7 copy-start
  2.6 15.6 %collective-permute-start.2 = (bf16[64,3584]{1,0:T(8,128)(2,1)S(1)}, bf16[64,3584]{1,0:T(8,128)(2,1)S(1)}, u32[]{:S(2)}, u32[]{:S(2)}) collective-permute-start(bf16[64,3584]{1,0:T(8,128)(2,1)S(1)} %normalized.1.refs_0_), channel_id=1, source_target_pairs={{0,2},{1,3},{2,4},{3,5},{4,6},{5,7},{6,0},{7,1},{8,10},{9,11},{10,... | collective-permute-start | bytes 1376264 | tf_op jit(solution)/shard_map/ppermute | solution.py:467
  5.7 21.1 %collective-permute-start.1 = (bf16[64,3584]{1,0:T(8,128)(2,1)S(1)}, bf16[64,3584]{1,0:T(8,128)(2,1)S(1)}, u32[]{:S(2)}, u32[]{:S(2)}) collective-permute-start(bf16[64,3584]{1,0:T(8,128)(2,1)S(1)} %normalized.1.refs_0_), channel_id=1, source_target_pairs={{0,1},{1,0},{2,3},{3,2},{4,5},{5,4},{6,7},{7,6},{8,9},{9,8},{10,11... | collective-permute-start | bytes 1376264 | tf_op jit(solution)/shard_map/ppermute | solution.py:457
  7.2 20.2 %collective-permute-start = (bf16[64,3584]{1,0:T(8,128)(2,1)S(1)}, bf16[64,3584]{1,0:T(8,128)(2,1)S(1)}, u32[]{:S(2)}, u32[]{:S(2)}) collective-permute-start(bf16[64,3584]{1,0:T(8,128)(2,1)S(1)} %normalized.1.refs_0_), channel_id=1, source_target_pairs={{0,16},{8,24},{16,0},{24,8},{1,17},{9,25},{17,1},{25,9},{2,18},{10... | collective-permute-start | bytes 1376264 | tf_op jit(solution)/shard_map/ppermute | solution.py:451
  18.2 15.0 %collective-permute-start.5 = (bf16[64,3584]{1,0:T(8,128)(2,1)S(1)}, bf16[64,3584]{1,0:T(8,128)(2,1)S(1)}, u32[]{:S(2)}, u32[]{:S(2)}) collective-permute-start(bf16[64,3584]{1,0:T(8,128)(2,1)S(1)} %collective-permute-done.2.refs_0_.refs_3_), channel_id=1, source_target_pairs={{0,1},{1,0},{2,3},{3,2},{4,5},{5,4},{6,7},{7,6},{8,9},{9,8},{10,11... | collective-permute-start | bytes 1376264 | tf_op jit(solution)/shard_map/ppermute | solution.py:457
  19.7 13.5 %collective-permute-start.4 = (bf16[64,3584]{1,0:T(8,128)(2,1)S(1)}, bf16[64,3584]{1,0:T(8,128)(2,1)S(1)}, u32[]{:S(2)}, u32[]{:S(2)}) collective-permute-start(bf16[64,3584]{1,0:T(8,128)(2,1)S(1)} %collective-permute-done.2.refs_0_.refs_3_), channel_id=1, source_target_pairs={{0,16},{8,24},{16,0},{24,8},{1,17},{9,25},{17,1},{25,9},{2,18},{10... | collective-permute-start | bytes 1376264 | tf_op jit(solution)/shard_map/ppermute | solution.py:451
  21.2 12.7 %collective-permute-start.3 = (bf16[64,3584]{1,0:T(8,128)(2,1)S(1)}, bf16[64,3584]{1,0:T(8,128)(2,1)S(1)}, u32[]{:S(2)}, u32[]{:S(2)}) collective-permute-start(bf16[64,3584]{1,0:T(8,128)(2,1)S(1)} %collective-permute-done.2.refs_0_.refs_3_), channel_id=1, source_target_pairs={{0,2},{1,3},{2,4},{3,5},{4,6},{5,7},{6,0},{7,1},{8,10},{9,11},{10,... | collective-permute-start | bytes 1376264 | tf_op jit(solution)/shard_map/ppermute | solution.py:467
  26.7 16.3 %collective-permute-start.8 = (bf16[64,3584]{1,0:T(8,128)(2,1)S(1)}, bf16[64,3584]{1,0:T(8,128)(2,1)S(1)}, u32[]{:S(2)}, u32[]{:S(2)}) collective-permute-start(bf16[64,3584]{1,0:T(8,128)(2,1)S(1)} %collective-permute-done.1.refs_2_), channel_id=1, source_target_pairs={{0,16},{8,24},{16,0},{24,8},{1,17},{9,25},{17,1},{25,9},{2,18},{10... | collective-permute-start | bytes 1376264 | tf_op jit(solution)/shard_map/ppermute | solution.py:451
  33.9 16.7 %collective-permute-start.7 = (bf16[64,3584]{1,0:T(8,128)(2,1)S(1)}, bf16[64,3584]{1,0:T(8,128)(2,1)S(1)}, u32[]{:S(2)}, u32[]{:S(2)}) collective-permute-start(bf16[64,3584]{1,0:T(8,128)(2,1)S(1)} %collective-permute-done.3.refs_0_), channel_id=1, source_target_pairs={{0,16},{8,24},{16,0},{24,8},{1,17},{9,25},{17,1},{25,9},{2,18},{10... | collective-permute-start | bytes 1376264 | tf_op jit(solution)/shard_map/ppermute | solution.py:451
  34.7 15.8 %collective-permute-start.6 = (bf16[64,3584]{1,0:T(8,128)(2,1)S(1)}, bf16[64,3584]{1,0:T(8,128)(2,1)S(1)}, u32[]{:S(2)}, u32[]{:S(2)}) collective-permute-start(bf16[64,3584]{1,0:T(8,128)(2,1)S(1)} %collective-permute-done.3.refs_0_), channel_id=1, source_target_pairs={{0,2},{1,3},{2,4},{3,5},{4,6},{5,7},{6,0},{7,1},{8,10},{9,11},{10,... | collective-permute-start | bytes 1376264 | tf_op jit(solution)/shard_map/ppermute | solution.py:467
  36.0 17.6 %collective-permute-start.11 = (bf16[64,3584]{1,0:T(8,128)(2,1)S(1)}, bf16[64,3584]{1,0:T(8,128)(2,1)S(1)}, u32[]{:S(2)}, u32[]{:S(2)}) collective-permute-start(bf16[64,3584]{1,0:T(8,128)(2,1)S(1)} %collective-permute-done.3.refs_0_), channel_id=1, source_target_pairs={{0,1},{1,0},{2,3},{3,2},{4,5},{5,4},{6,7},{7,6},{8,9},{9,8},{10,11... | collective-permute-start | bytes 1376264 | tf_op jit(solution)/shard_map/ppermute | solution.py:457
  50.6 13.5 %collective-permute-start.10 = (bf16[64,3584]{1,0:T(8,128)(2,1)S(1)}, bf16[64,3584]{1,0:T(8,128)(2,1)S(1)}, u32[]{:S(2)}, u32[]{:S(2)}) collective-permute-start(bf16[64,3584]{1,0:T(8,128)(2,1)S(1)} %collective-permute-done.6.refs_2_.refs_4_), channel_id=1, source_target_pairs={{0,16},{8,24},{16,0},{24,8},{1,17},{9,25},{17,1},{25,9},{2,18},{10... | collective-permute-start | bytes 1376264 | tf_op jit(solution)/shard_map/ppermute | solution.py:451
  52.9 11.9 %collective-permute-start.9 = (bf16[896,384]{1,0:T(8,128)(2,1)S(1)}, bf16[896,384]{1,0:T(8,128)(2,1)S(1)}, u32[]{:S(2)}, u32[]{:S(2)}) collective-permute-start(bf16[896,384]{1,0:T(8,128)(2,1)S(1)} %get-tuple-element.72), channel_id=1, source_target_pairs={{0,8},{8,0},{16,24},{24,16},{1,9},{9,1},{17,25},{25,17},{2,10},{10... | collective-permute-start | bytes 2064392 | tf_op jit(solution)/shard_map/ppermute | solution.py:454
  53.0 20.4 %collective-permute-start.13 = (bf16[64,3584]{1,0:T(8,128)(2,1)S(1)}, bf16[64,3584]{1,0:T(8,128)(2,1)S(1)}, u32[]{:S(2)}, u32[]{:S(2)}) collective-permute-start(bf16[64,3584]{1,0:T(8,128)(2,1)S(1)} %collective-permute-done.8.refs_1_), channel_id=1, source_target_pairs={{0,2},{1,3},{2,4},{3,5},{4,6},{5,7},{6,0},{7,1},{8,10},{9,11},{10,... | collective-permute-start | bytes 1376264 | tf_op jit(solution)/shard_map/ppermute | solution.py:467
  53.1 20.3 %collective-permute-start.12 = (bf16[64,3584]{1,0:T(8,128)(2,1)S(1)}, bf16[64,3584]{1,0:T(8,128)(2,1)S(1)}, u32[]{:S(2)}, u32[]{:S(2)}) collective-permute-start(bf16[64,3584]{1,0:T(8,128)(2,1)S(1)} %collective-permute-done.6.refs_2_.refs_4_), channel_id=1, source_target_pairs={{0,1},{1,0},{2,3},{3,2},{4,5},{5,4},{6,7},{7,6},{8,9},{9,8},{10,11... | collective-permute-start | bytes 1376264 | tf_op jit(solution)/shard_map/ppermute | solution.py:457
  53.7 25.5 %collective-permute-start.14 = (bf16[64,3584]{1,0:T(8,128)(2,1)S(1)}, bf16[64,3584]{1,0:T(8,128)(2,1)S(1)}, u32[]{:S(2)}, u32[]{:S(2)}) collective-permute-start(bf16[64,3584]{1,0:T(8,128)(2,1)S(1)} %collective-permute-done.11.refs_1_.refs_3_), channel_id=1, source_target_pairs={{0,16},{8,24},{16,0},{24,8},{1,17},{9,25},{17,1},{25,9},{2,18},{10... | collective-permute-start | bytes 1376264 | tf_op jit(solution)/shard_map/ppermute | solution.py:451
  64.0 15.2 %collective-permute-start.15 = (bf16[64,3584]{1,0:T(8,128)(2,1)S(1)}, bf16[64,3584]{1,0:T(8,128)(2,1)S(1)}, u32[]{:S(2)}, u32[]{:S(2)}) collective-permute-start(bf16[64,3584]{1,0:T(8,128)(2,1)S(1)} %collective-permute-done.10.refs_0_.refs_5_), channel_id=1, source_target_pairs={{0,1},{1,0},{2,3},{3,2},{4,5},{5,4},{6,7},{7,6},{8,9},{9,8},{10,11... | collective-permute-start | bytes 1376264 | tf_op jit(solution)/shard_map/ppermute | solution.py:457
  79.1 1.4 %copy-start.1 = (bf16[384,2048]{1,0:T(8,128)(2,1)S(1)}, bf16[384,2048]{1,0:T(8,128)(2,1)}, u32[]{:S(2)}) copy-start(bf16[384,2048]{1,0:T(8,128)(2,1)} %get-tuple-element.94.refs_4_) | copy-start | bytes 4718596
  79.2 1.8 %copy-start.2 = (bf16[320,2048]{1,0:T(8,128)(2,1)S(1)}, bf16[320,2048]{1,0:T(8,128)(2,1)}, u32[]{:S(2)}) copy-start(bf16[320,2048]{1,0:T(8,128)(2,1)} %get-tuple-element.95.refs_5_) | copy-start | bytes 3932164
  80.6 8.3 %collective-permute-start.17 = (bf16[384,2048]{1,0:T(8,128)(2,1)S(1)}, bf16[384,2048]{1,0:T(8,128)(2,1)S(1)}, u32[]{:S(2)}, u32[]{:S(2)}) collective-permute-start(bf16[384,2048]{1,0:T(8,128)(2,1)S(1)} %copy-done.1), channel_id=1, source_target_pairs={{0,8},{8,0},{16,24},{24,16},{1,9},{9,1},{17,25},{25,17},{2,10},{10... | collective-permute-start | bytes 4718600 | tf_op jit(solution)/shard_map/ppermute | solution.py:454
  80.9 7.9 %collective-permute-start.18 = (bf16[320,2048]{1,0:T(8,128)(2,1)S(1)}, bf16[320,2048]{1,0:T(8,128)(2,1)S(1)}, u32[]{:S(2)}, u32[]{:S(2)}) collective-permute-start(bf16[320,2048]{1,0:T(8,128)(2,1)S(1)} %copy-done.2), channel_id=1, source_target_pairs={{0,8},{8,0},{16,24},{24,16},{1,9},{9,1},{17,25},{25,17},{2,10},{10... | collective-permute-start | bytes 3932168 | tf_op jit(solution)/shard_map/ppermute | solution.py:454
  81.1 6.5 %collective-permute-start.16 = (bf16[896,640]{1,0:T(8,128)(2,1)S(1)}, bf16[896,640]{1,0:T(8,128)(2,1)S(1)}, u32[]{:S(2)}, u32[]{:S(2)}) collective-permute-start(bf16[896,640]{1,0:T(8,128)(2,1)S(1)} %get-tuple-element.89), channel_id=1, source_target_pairs={{0,8},{8,0},{16,24},{24,16},{1,9},{9,1},{17,25},{25,17},{2,10},{10... | collective-permute-start | bytes 3440648 | tf_op jit(solution)/shard_map/ppermute | solution.py:454
  86.2 3.2 %collective-permute-start.21 = (f32[32,128]{1,0:T(8,128)S(1)}, f32[32,128]{1,0:T(8,128)S(1)}, u32[]{:S(2)}, u32[]{:S(2)}) collective-permute-start(f32[32,128]{1,0:T(8,128)S(1)} %get-tuple-element.97.own_ref), channel_id=1, source_target_pairs={{0,9},{1,8},{2,11},{3,10},{4,13},{5,12},{6,15},{7,14},{8,1},{9,0},... | collective-permute-start | bytes 49160 | tf_op jit(solution)/shard_map/ppermute | solution.py:464
  87.3 2.1 %collective-permute-start.20 = (f32[32,128]{1,0:T(8,128)S(1)}, f32[32,128]{1,0:T(8,128)S(1)}, u32[]{:S(2)}, u32[]{:S(2)}) collective-permute-start(f32[32,128]{1,0:T(8,128)S(1)} %get-tuple-element.97.own_ref), channel_id=1, source_target_pairs={{0,8},{8,0},{16,24},{24,16},{1,9},{9,1},{17,25},{25,17},{2,10},{10... | collective-permute-start | bytes 49160 | tf_op jit(solution)/shard_map/ppermute | solution.py:454
  87.6 3.7 %collective-permute-start.19 = (f32[32,128]{1,0:T(8,128)S(1)}, f32[32,128]{1,0:T(8,128)S(1)}, u32[]{:S(2)}, u32[]{:S(2)}) collective-permute-start(f32[32,128]{1,0:T(8,128)S(1)} %get-tuple-element.97.own_ref), channel_id=1, source_target_pairs={{0,1},{1,0},{2,3},{3,2},{4,5},{5,4},{6,7},{7,6},{8,9},{9,8},{10,11... | collective-permute-start | bytes 49160 | tf_op jit(solution)/shard_map/ppermute | solution.py:457
  91.4 6.4 %collective-permute-start.22 = (bf16[320,2048]{1,0:T(8,128)(2,1)}, bf16[320,2048]{1,0:T(8,128)(2,1)S(1)}, u32[]{:S(2)}, u32[]{:S(2)}) collective-permute-start(bf16[320,2048]{1,0:T(8,128)(2,1)} %get-tuple-element.99.refs_6_), channel_id=1, source_target_pairs={{0,8},{8,0},{16,24},{24,16},{1,9},{9,1},{17,25},{25,17},{2,10},{10... | collective-permute-start | bytes 3932168 | tf_op jit(solution)/shard_map/ppermute | solution.py:454
  91.5 6.0 %collective-permute-start.25 = (f32[64,128]{1,0:T(8,128)S(1)}, f32[64,128]{1,0:T(8,128)S(1)}, u32[]{:S(2)}, u32[]{:S(2)}) collective-permute-start(f32[64,128]{1,0:T(8,128)S(1)} %get-tuple-element.98.refs_10_), channel_id=1, source_target_pairs={{0,2},{1,3},{2,4},{3,5},{4,6},{5,7},{6,0},{7,1},{8,10},{9,11},{10,... | collective-permute-start | bytes 98312 | tf_op jit(solution)/shard_map/ppermute | solution.py:467
  91.5 6.0 %collective-permute-start.24 = (f32[64,128]{1,0:T(8,128)S(1)}, f32[64,128]{1,0:T(8,128)S(1)}, u32[]{:S(2)}, u32[]{:S(2)}) collective-permute-start(f32[64,128]{1,0:T(8,128)S(1)} %get-tuple-element.98.refs_10_), channel_id=1, source_target_pairs={{0,4},{1,5},{2,6},{3,7},{4,0},{5,1},{6,2},{7,3},{8,12},{9,13},{10,... | collective-permute-start | bytes 98312 | tf_op jit(solution)/shard_map/ppermute | solution.py:467
  93.8 4.1 %collective-permute-start.23 = (f32[64,128]{1,0:T(8,128)S(1)}, f32[64,128]{1,0:T(8,128)S(1)}, u32[]{:S(2)}, u32[]{:S(2)}) collective-permute-start(f32[64,128]{1,0:T(8,128)S(1)} %get-tuple-element.98.refs_10_), channel_id=1, source_target_pairs={{0,6},{1,7},{2,0},{3,1},{4,2},{5,3},{6,4},{7,5},{8,14},{9,15},{10,... | collective-permute-start | bytes 98312 | tf_op jit(solution)/shard_map/ppermute | solution.py:467

commit v13 on v12

--- a/solution.py
+++ b/solution.py
@@ -96,7 +96,7 @@
         compiler_params=pltpu.CompilerParams(vmem_limit_bytes=8 * 1024 * 1024),
         cost_estimate=BRIEF,
         name="normalized",
-    )(*in_hbm([hidden]), norm_gain)
+    )(*in_hbm([hidden, norm_gain]))
 
 
 def prepare_kernel(weight_ref, true_ids, sample_ids, *refs):
@@ -510,7 +510,7 @@
     def diagonal(turn):
         if turn == 1:
             return to_z(held[1, 1, 0], 1)
-        if turn % 2 == 0:
+        if turn == 2:
             return to_x(held[1, 0, turn])
         return to_y(held[0, 1, turn])
 

time: 118 us -> 115 us (0.975)
  waiting for transfers between devices: 15.8 us -> 8.61 us
  starting transfers between devices: 23.2 us -> 27.7 us
    ppermute x6 -> x5, waiting for transfers between devices: 7.3 us -> 0.91 us  [to_x(): return lax.ppermute(values, 'rep', swap_pairs(reps, 2))]
    ppermute x7, starting transfers between devices: 8.3 us -> 12.3 us  [to_z(): return lax.ppermute(values, 'shard', shift_pairs(lines, along, 0))]
    ppermute x6 -> x7, starting transfers between devices: 6.09 us -> 7.55 us  [to_y(): return lax.ppermute(values, 'shard', swap_pairs(shards, 1))]
    ppermute x6 -> x5, starting transfers between devices: 6.67 us -> 5.58 us  [to_x(): return lax.ppermute(values, 'rep', swap_pairs(reps, 2))]
  transfers between devices with their start and end apart: 26 -> 26, of which waited for: 9 -> 6; matrix products, arithmetic and copies ran while one was open for 6% -> 6% of each run, Pallas kernels for 40% -> 42%
where the time goes in v13:
time: 115 us; the launch traced here: 114 us
  Pallas kernels  70.1 us (61%)
  starting transfers between devices  27.7 us (24%)
  waiting for transfers between devices  8.61 us (7%)
  other arithmetic  3.62 us (3%)
  local copies, waits for them, and re-layouts  3.44 us (3%)
    pallas_call x6, Pallas kernels, round_logits(): pl.pallas_call(functools.partial(logits_kernel, stat_rows, first_row, len...  32.5 us
    pallas_call x1, Pallas kernels, refresh_states(): pl.pallas_call(functools.partial(refresh_kernel, lines, length, block_row...  20 us
    ppermute x7, starting transfers between devices, to_z(): return lax.ppermute(values, 'shard', shift_pairs(lines, along, 0))  12.3 us
    pallas_call x1, Pallas kernels, one_hot_sums(): pl.pallas_call(functools.partial(one_hot_kernel, len(features)), grid=(co...  8.66 us
    ppermute x7, starting transfers between devices, to_y(): return lax.ppermute(values, 'shard', swap_pairs(shards, 1))  7.55 us
    ppermute x5, starting transfers between devices, to_x(): return lax.ppermute(values, 'rep', swap_pairs(reps, 2))  5.58 us
    pallas_call x1, Pallas kernels, prepared(): pl.pallas_call(prepare_kernel, in_specs=[pl.BlockSpec(memory_space=pltpu....  5.52 us
    ppermute x7, waiting for transfers between devices, to_z(): return lax.ppermute(values, 'shard', shift_pairs(lines, along, 0))  5.12 us
  transfers between devices with their start and end apart: 26, of which 6 were waited for; matrix products, arithmetic and copies ran while one was open for 6% of the time, Pallas kernels for 42%

profile of v13, /device:TPU:0, one launch (start us, length us, event | category | flops | bytes accessed | tf_op | source)
XLA Modules:
  0.0 114.4 jit_solution(15148789811004504426)
XLA Ops:
  0.6 1.2 %normalized.1.refs_0_ = bf16[64,3584]{1,0:T(8,128)(2,1)S(1)} custom-call(bf16[64,3584]{1,0:T(8,128)(2,1)} %hidden_ref.1, f32[3584]{0:T(1024)} %gain_ref.1), custom_call_target="tpu_custom_call" | custom-call | flops 1024 | bytes 1024 | tf_op jit(solution)/shard_map/normalized/pallas_call | solution.py:93
  1.9 3.1 %collective-permute-start.2 = (bf16[64,3584]{1,0:T(8,128)(2,1)S(1)}, bf16[64,3584]{1,0:T(8,128)(2,1)S(1)}, u32[]{:S(2)}, u32[]{:S(2)}) collective-permute-start(bf16[64,3584]{1,0:T(8,128)(2,1)S(1)} %normalized.1.refs_0_), channel_id=1, source_target_pairs={{0,2},{1,3},{2,4},{3,5},{4,6},{5,7},{6,0},{7,1},{8,10},{9,11},{10,... | collective-permute-start | bytes 1376264 | tf_op jit(solution)/shard_map/ppermute | solution.py:467
  4.9 1.5 %collective-permute-start.1 = (bf16[64,3584]{1,0:T(8,128)(2,1)S(1)}, bf16[64,3584]{1,0:T(8,128)(2,1)S(1)}, u32[]{:S(2)}, u32[]{:S(2)}) collective-permute-start(bf16[64,3584]{1,0:T(8,128)(2,1)S(1)} %normalized.1.refs_0_), channel_id=1, source_target_pairs={{0,1},{1,0},{2,3},{3,2},{4,5},{5,4},{6,7},{7,6},{8,9},{9,8},{10,11... | collective-permute-start | bytes 1376264 | tf_op jit(solution)/shard_map/ppermute | solution.py:457
  6.5 1.5 %collective-permute-start = (bf16[64,3584]{1,0:T(8,128)(2,1)S(1)}, bf16[64,3584]{1,0:T(8,128)(2,1)S(1)}, u32[]{:S(2)}, u32[]{:S(2)}) collective-permute-start(bf16[64,3584]{1,0:T(8,128)(2,1)S(1)} %normalized.1.refs_0_), channel_id=1, source_target_pairs={{0,16},{8,24},{16,0},{24,8},{1,17},{9,25},{17,1},{25,9},{2,18},{10... | collective-permute-start | bytes 1376264 | tf_op jit(solution)/shard_map/ppermute | solution.py:451
  7.9 0.7 fusion.4
  8.6 0.7 compare_and_fusion
  9.3 0.7 multiply_add_fusion
  10.0 1.2 %slice.31 = s32[1]{0:T(128)} slice(s32[2048]{0:T(1024)} %param.12), slice={[0:1]} | slice | bytes 8 | tf_op jit(solution)/shard_map/jit(_roll_static)/slice | solution.py:486
  11.2 0.8 slice.30
  12.1 0.7 broadcast_subtract_fusion
  12.9 0.7 fusion.1
  13.7 0.6 gather_fusion
  14.7 2.7 %collective-permute-done.2.refs_0_.refs_3_ = bf16[64,3584]{1,0:T(8,128)(2,1)S(1)} collective-permute-done((bf16[64,3584]{1,0:T(8,128)(2,1)S(1)}, bf16[64,3584]{1,0:T(8,128)(2,1)S(1)}, u32[]{:S(2)}, u32[]{:S(2)}) %collective-permute-start.2) | collective-permute-done | bytes 458784 | tf_op jit(solution)/shard_map/ppermute | solution.py:467
  17.5 1.5 %collective-permute-start.5 = (bf16[64,3584]{1,0:T(8,128)(2,1)S(1)}, bf16[64,3584]{1,0:T(8,128)(2,1)S(1)}, u32[]{:S(2)}, u32[]{:S(2)}) collective-permute-start(bf16[64,3584]{1,0:T(8,128)(2,1)S(1)} %collective-permute-done.2.refs_0_.refs_3_), channel_id=1, source_target_pairs={{0,1},{1,0},{2,3},{3,2},{4,5},{5,4},{6,7},{7,6},{8,9},{9,8},{10,11... | collective-permute-start | bytes 1376264 | tf_op jit(solution)/shard_map/ppermute | solution.py:457
  19.0 1.5 %collective-permute-start.4 = (bf16[64,3584]{1,0:T(8,128)(2,1)S(1)}, bf16[64,3584]{1,0:T(8,128)(2,1)S(1)}, u32[]{:S(2)}, u32[]{:S(2)}) collective-permute-start(bf16[64,3584]{1,0:T(8,128)(2,1)S(1)} %collective-permute-done.2.refs_0_.refs_3_), channel_id=1, source_target_pairs={{0,16},{8,24},{16,0},{24,8},{1,17},{9,25},{17,1},{25,9},{2,18},{10... | collective-permute-start | bytes 1376264 | tf_op jit(solution)/shard_map/ppermute | solution.py:451
  20.5 5.5 %prepared.1 = (bf16[3584,2048]{1,0:T(8,128)(2,1)S(1)}, s32[1280,128]{1,0:T(8,128)S(1)}, s32[1280,128]{1,0:T(8,128)S(1)}) custom-call(bf16[3584,2048]{1,0:T(8,128)(2,1)} %weight_ref.1, s32[1,1280]{1,0:T(1,128)S(1)} %squeeze.14.true_ids, s32[1,1280]{1,0:T(1,128)S(1)} %squeeze.15.sample_ids, f32[32,128]{1,0:T(8,128)S(1)} %broadcast_in_dim.20.refs_0_.refs_4_), custom_call_target="tpu_custom_call" | custom-call | flops 1024 | bytes 1024 | tf_op jit(solution)/shard_map/prepared/pallas_call | solution.py:127
  26.0 0.6 collective-permute-start.8
  26.6 5.8 %round_logits.6 = (bf16[384,2048]{1,0:T(8,128)(2,1)}, f32[32,128]{1,0:T(8,128)S(1)}) custom-call(bf16[64,3584]{1,0:T(8,128)(2,1)S(1)} %normalized.1.refs_0_, bf16[64,3584]{1,0:T(8,128)(2,1)S(1)} %collective-permute-done.refs_1_, bf16[64,3584]{1,0:T(8,128)(2,1)S(1)} %collective-permute-done.1.refs_2_, ...), custom_call_target="tpu_custom_call" | custom-call | flops 1024 | bytes 1024 | tf_op jit(solution)/shard_map/round_logits/pallas_call | solution.py:206
  32.4 0.8 collective-permute-done.3.refs_0_
  33.2 0.5 collective-permute-start.7
  33.7 0.6 collective-permute-start.6
  34.3 1.5 %collective-permute-start.11 = (bf16[64,3584]{1,0:T(8,128)(2,1)S(1)}, bf16[64,3584]{1,0:T(8,128)(2,1)S(1)}, u32[]{:S(2)}, u32[]{:S(2)}) collective-permute-start(bf16[64,3584]{1,0:T(8,128)(2,1)S(1)} %collective-permute-done.3.refs_0_), channel_id=1, source_target_pairs={{0,1},{1,0},{2,3},{3,2},{4,5},{5,4},{6,7},{7,6},{8,9},{9,8},{10,11... | collective-permute-start | bytes 1376264 | tf_op jit(solution)/shard_map/ppermute | solution.py:457
  35.8 5.8 %round_logits.7 = (bf16[384,2048]{1,0:T(8,128)(2,1)}, f32[32,128]{1,0:T(8,128)S(1)}) custom-call(bf16[64,3584]{1,0:T(8,128)(2,1)S(1)} %collective-permute-done.2.refs_0_.refs_3_, bf16[64,3584]{1,0:T(8,128)(2,1)S(1)} %collective-permute-done.4.refs_1_.refs_4_, ...), custom_call_target="tpu_custom_call", output_to_operand_aliasing={{0}: (5, {})} | custom-call | flops 1024 | bytes 1024 | tf_op jit(solution)/shard_map/round_logits/pallas_call | solution.py:206
  41.6 4.7 %round_logits.8 = (bf16[320,2048]{1,0:T(8,128)(2,1)}, f32[32,128]{1,0:T(8,128)S(1)}) custom-call(bf16[64,3584]{1,0:T(8,128)(2,1)S(1)} %collective-permute-done.3.refs_0_, bf16[64,3584]{1,0:T(8,128)(2,1)S(1)} %collective-permute-done.8.refs_1_, bf16[3584,2048]{1,0:T(8,128)(2,1)S(1)} %get-tuple-element.58.refs_3_.refs_2_, f32[32,128]{1,0:T(8,128)S(1)} %get-tuple-element.67.refs_3_), custom_call_target="tpu_custom_call" | custom-call | flops 1024 | bytes 1024 | tf_op jit(solution)/shard_map/round_logits/pallas_call | solution.py:206
  46.4 1.6 %collective-permute-start.10 = (bf16[64,3584]{1,0:T(8,128)(2,1)S(1)}, bf16[64,3584]{1,0:T(8,128)(2,1)S(1)}, u32[]{:S(2)}, u32[]{:S(2)}) collective-permute-start(bf16[64,3584]{1,0:T(8,128)(2,1)S(1)} %collective-permute-done.6.refs_2_.refs_4_), channel_id=1, source_target_pairs={{0,16},{8,24},{16,0},{24,8},{1,17},{9,25},{17,1},{25,9},{2,18},{10... | collective-permute-start | bytes 1376264 | tf_op jit(solution)/shard_map/ppermute | solution.py:451
  48.0 0.9 turned_features.2
  48.9 1.6 %collective-permute-start.13 = (bf16[64,3584]{1,0:T(8,128)(2,1)S(1)}, bf16[64,3584]{1,0:T(8,128)(2,1)S(1)}, u32[]{:S(2)}, u32[]{:S(2)}) collective-permute-start(bf16[64,3584]{1,0:T(8,128)(2,1)S(1)} %collective-permute-done.8.refs_1_), channel_id=1, source_target_pairs={{0,2},{1,3},{2,4},{3,5},{4,6},{5,7},{6,0},{7,1},{8,10},{9,11},{10,... | collective-permute-start | bytes 1376264 | tf_op jit(solution)/shard_map/ppermute | solution.py:467
  50.5 0.5 collective-permute-start.12
  51.1 0.5 collective-permute-start.14
  51.6 5.8 %round_logits.9 = (bf16[320,2048]{1,0:T(8,128)(2,1)}, f32[32,128]{1,0:T(8,128)S(1)}) custom-call(bf16[64,3584]{1,0:T(8,128)(2,1)S(1)} %collective-permute-done.7.refs_0_.refs_2_, bf16[64,3584]{1,0:T(8,128)(2,1)S(1)} %collective-permute-done.11.refs_1_.refs_3_, ...), custom_call_target="tpu_custom_call", output_to_operand_aliasing={{0}: (5, {})} | custom-call | flops 1024 | bytes 1024 | tf_op jit(solution)/shard_map/round_logits/pallas_call | solution.py:206
  57.3 0.9 collective-permute-done.10.refs_0_.refs_5_
  58.2 0.7 collective-permute-start.15
  58.9 8.7 %one_hot_sums.1 = (bf16[896,2048]{1,0:T(8,128)(2,1)}, bf16[896,2048]{1,0:T(8,128)(2,1)}) custom-call(bf16[896,384]{1,0:T(8,128)(2,1)S(1)} %get-tuple-element.71.refs_0_, bf16[896,384]{1,0:T(8,128)(2,1)S(1)} %collective-permute-done.9.refs_1_, s32[1,768]{1,0:T(1,128)S(1)} %squeeze.12.refs_2_, s32[1,768]{1,0:T(1,128)S(1)} %squeeze.13.refs_3_), custom_call_target="tpu_custom_call" | custom-call | flops 1024 | bytes 1024 | tf_op jit(solution)/shard_map/one_hot_sums/pallas_call | solution.py:285
  67.6 5.7 %round_logits.10 = (bf16[320,2048]{1,0:T(8,128)(2,1)}, f32[32,128]{1,0:T(8,128)S(1)}) custom-call(bf16[64,3584]{1,0:T(8,128)(2,1)S(1)} %collective-permute-done.10.refs_0_.refs_5_, bf16[64,3584]{1,0:T(8,128)(2,1)S(1)} %collective-permute-done.12.refs_1_.refs_6_, bf16[64,3584]{1,0:T(8,128)(2,1)S(1)} %collective-permute-done.13.refs_2_.refs_7_, ...), custom_call_target="tpu_custom_call" | custom-call | flops 1024 | bytes 1024 | tf_op jit(solution)/shard_map/round_logits/pallas_call | solution.py:206
  73.4 1.4 %turned_features.3 = (bf16[896,640]{1,0:T(8,128)(2,1)S(1)}, bf16[896,640]{1,0:T(8,128)(2,1)S(1)}) custom-call(s32[1]{0:T(128)} %bitcast.rep_ref, bf16[64,3584]{1,0:T(8,128)(2,1)S(1)} %collective-permute-done.3.refs_0_, bf16[64,3584]{1,0:T(8,128)(2,1)S(1)} %collective-permute-done.8.refs_1_, bf16[64,3584]{1,0:T(8,128)(2,1)S(1)} %collective-permute-done.7.refs_0_.refs_2_, ...), custom_call_target="tpu_custom_call" | custom-call | flops 1024 | bytes 1024 | tf_op jit(solution)/shard_map/turned_features/pallas_call | solution.py:248
  74.8 0.3 copy-done.1
  75.3 0.3 collective-permute-start.16
  75.6 4.7 %round_logits.11 = (bf16[320,2048]{1,0:T(8,128)(2,1)}, f32[32,128]{1,0:T(8,128)S(1)}) custom-call(bf16[64,3584]{1,0:T(8,128)(2,1)S(1)} %collective-permute-done.14.refs_8_.refs_0_, bf16[64,3584]{1,0:T(8,128)(2,1)S(1)} %collective-permute-done.15.refs_9_.refs_1_, ...), custom_call_target="tpu_custom_call", output_to_operand_aliasing={{0}: (4, {})} | custom-call | flops 1024 | bytes 1024 | tf_op jit(solution)/shard_map/round_logits/pallas_call | solution.py:206
  80.4 1.2 %collective-permute-start.21 = (f32[32,128]{1,0:T(8,128)S(1)}, f32[32,128]{1,0:T(8,128)S(1)}, u32[]{:S(2)}, u32[]{:S(2)}) collective-permute-start(f32[32,128]{1,0:T(8,128)S(1)} %get-tuple-element.97.own_ref), channel_id=1, source_target_pairs={{0,9},{1,8},{2,11},{3,10},{4,13},{5,12},{6,15},{7,14},{8,1},{9,0},... | collective-permute-start | bytes 49160 | tf_op jit(solution)/shard_map/ppermute | solution.py:464
  81.6 0.3 collective-permute-start.20
  81.9 1.2 %collective-permute-start.19 = (f32[32,128]{1,0:T(8,128)S(1)}, f32[32,128]{1,0:T(8,128)S(1)}, u32[]{:S(2)}, u32[]{:S(2)}) collective-permute-start(f32[32,128]{1,0:T(8,128)S(1)} %get-tuple-element.97.own_ref), channel_id=1, source_target_pairs={{0,1},{1,0},{2,3},{3,2},{4,5},{5,4},{6,7},{7,6},{8,9},{9,8},{10,11... | collective-permute-start | bytes 49160 | tf_op jit(solution)/shard_map/ppermute | solution.py:457
  83.1 0.5 collective-permute-done.21.both_ref
  83.6 2.0 %collective-permute-done.19.across_ref = f32[32,128]{1,0:T(8,128)S(1)} collective-permute-done((f32[32,128]{1,0:T(8,128)S(1)}, f32[32,128]{1,0:T(8,128)S(1)}, u32[]{:S(2)}, u32[]{:S(2)}) %collective-permute-start.19) | collective-permute-done | bytes 16416 | tf_op jit(solution)/shard_map/ppermute | solution.py:457
  85.7 2.0 %collective-permute-start.25 = (f32[64,128]{1,0:T(8,128)S(1)}, f32[64,128]{1,0:T(8,128)S(1)}, u32[]{:S(2)}, u32[]{:S(2)}) collective-permute-start(f32[64,128]{1,0:T(8,128)S(1)} %get-tuple-element.98.refs_10_), channel_id=1, source_target_pairs={{0,2},{1,3},{2,4},{3,5},{4,6},{5,7},{6,0},{7,1},{8,10},{9,11},{10,... | collective-permute-start | bytes 98312 | tf_op jit(solution)/shard_map/ppermute | solution.py:467
  87.7 2.2 %collective-permute-start.24 = (f32[64,128]{1,0:T(8,128)S(1)}, f32[64,128]{1,0:T(8,128)S(1)}, u32[]{:S(2)}, u32[]{:S(2)}) collective-permute-start(f32[64,128]{1,0:T(8,128)S(1)} %get-tuple-element.98.refs_10_), channel_id=1, source_target_pairs={{0,4},{1,5},{2,6},{3,7},{4,0},{5,1},{6,2},{7,3},{8,12},{9,13},{10,... | collective-permute-start | bytes 98312 | tf_op jit(solution)/shard_map/ppermute | solution.py:467
  89.9 2.8 %collective-permute-start.23 = (f32[64,128]{1,0:T(8,128)S(1)}, f32[64,128]{1,0:T(8,128)S(1)}, u32[]{:S(2)}, u32[]{:S(2)}) collective-permute-start(f32[64,128]{1,0:T(8,128)S(1)} %get-tuple-element.98.refs_10_), channel_id=1, source_target_pairs={{0,6},{1,7},{2,0},{3,1},{4,2},{5,3},{6,4},{7,5},{8,14},{9,15},{10,... | collective-permute-start | bytes 98312 | tf_op jit(solution)/shard_map/ppermute | solution.py:467
  92.8 1.6 %collective-permute-done.23.refs_11_ = f32[64,128]{1,0:T(8,128)S(1)} collective-permute-done((f32[64,128]{1,0:T(8,128)S(1)}, f32[64,128]{1,0:T(8,128)S(1)}, u32[]{:S(2)}, u32[]{:S(2)}) %collective-permute-start.23) | collective-permute-done | bytes 32800 | tf_op jit(solution)/shard_map/ppermute | solution.py:467
  94.4 20.0 %refresh_states.1 = (bf16[896,2048]{1,0:T(8,128)(2,1)}, bf16[896,2048]{1,0:T(8,128)(2,1)}, bf16[896,2048]{1,0:T(8,128)(2,1)}) custom-call(bf16[896,384]{1,0:T(8,128)(2,1)S(1)} %get-tuple-element.71.refs_0_, bf16[896,384]{1,0:T(8,128)(2,1)S(1)} %collective-permute-done.9.refs_1_, bf16[896,640]{1,0:T(8,128)(2,1)S(1)} %get-tuple-element.88.refs_2_, ...), custom_call_target="tpu_custom_call" | custom-call | flops 1024 | bytes 1024 | tf_op jit(solution)/shard_map/refresh_states/pallas_call | solution.py:414
  (44 shorter events, 1.2 us)
Async XLA Ops:
  1.9 15.6 %collective-permute-start.2 = (bf16[64,3584]{1,0:T(8,128)(2,1)S(1)}, bf16[64,3584]{1,0:T(8,128)(2,1)S(1)}, u32[]{:S(2)}, u32[]{:S(2)}) collective-permute-start(bf16[64,3584]{1,0:T(8,128)(2,1)S(1)} %normalized.1.refs_0_), channel_id=1, source_target_pairs={{0,2},{1,3},{2,4},{3,5},{4,6},{5,7},{6,0},{7,1},{8,10},{9,11},{10,... | collective-permute-start | bytes 1376264 | tf_op jit(solution)/shard_map/ppermute | solution.py:467
  4.9 21.1 %collective-permute-start.1 = (bf16[64,3584]{1,0:T(8,128)(2,1)S(1)}, bf16[64,3584]{1,0:T(8,128)(2,1)S(1)}, u32[]{:S(2)}, u32[]{:S(2)}) collective-permute-start(bf16[64,3584]{1,0:T(8,128)(2,1)S(1)} %normalized.1.refs_0_), channel_id=1, source_target_pairs={{0,1},{1,0},{2,3},{3,2},{4,5},{5,4},{6,7},{7,6},{8,9},{9,8},{10,11... | collective-permute-start | bytes 1376264 | tf_op jit(solution)/shard_map/ppermute | solution.py:457
  6.5 19.6 %collective-permute-start = (bf16[64,3584]{1,0:T(8,128)(2,1)S(1)}, bf16[64,3584]{1,0:T(8,128)(2,1)S(1)}, u32[]{:S(2)}, u32[]{:S(2)}) collective-permute-start(bf16[64,3584]{1,0:T(8,128)(2,1)S(1)} %normalized.1.refs_0_), channel_id=1, source_target_pairs={{0,16},{8,24},{16,0},{24,8},{1,17},{9,25},{17,1},{25,9},{2,18},{10... | collective-permute-start | bytes 1376264 | tf_op jit(solution)/shard_map/ppermute | solution.py:451
  17.5 14.9 %collective-permute-start.5 = (bf16[64,3584]{1,0:T(8,128)(2,1)S(1)}, bf16[64,3584]{1,0:T(8,128)(2,1)S(1)}, u32[]{:S(2)}, u32[]{:S(2)}) collective-permute-start(bf16[64,3584]{1,0:T(8,128)(2,1)S(1)} %collective-permute-done.2.refs_0_.refs_3_), channel_id=1, source_target_pairs={{0,1},{1,0},{2,3},{3,2},{4,5},{5,4},{6,7},{7,6},{8,9},{9,8},{10,11... | collective-permute-start | bytes 1376264 | tf_op jit(solution)/shard_map/ppermute | solution.py:457
  19.0 13.4 %collective-permute-start.4 = (bf16[64,3584]{1,0:T(8,128)(2,1)S(1)}, bf16[64,3584]{1,0:T(8,128)(2,1)S(1)}, u32[]{:S(2)}, u32[]{:S(2)}) collective-permute-start(bf16[64,3584]{1,0:T(8,128)(2,1)S(1)} %collective-permute-done.2.refs_0_.refs_3_), channel_id=1, source_target_pairs={{0,16},{8,24},{16,0},{24,8},{1,17},{9,25},{17,1},{25,9},{2,18},{10... | collective-permute-start | bytes 1376264 | tf_op jit(solution)/shard_map/ppermute | solution.py:451
  20.5 12.7 %collective-permute-start.3 = (bf16[64,3584]{1,0:T(8,128)(2,1)S(1)}, bf16[64,3584]{1,0:T(8,128)(2,1)S(1)}, u32[]{:S(2)}, u32[]{:S(2)}) collective-permute-start(bf16[64,3584]{1,0:T(8,128)(2,1)S(1)} %collective-permute-done.2.refs_0_.refs_3_), channel_id=1, source_target_pairs={{0,2},{1,3},{2,4},{3,5},{4,6},{5,7},{6,0},{7,1},{8,10},{9,11},{10,... | collective-permute-start | bytes 1376264 | tf_op jit(solution)/shard_map/ppermute | solution.py:467
  26.0 15.6 %collective-permute-start.8 = (bf16[64,3584]{1,0:T(8,128)(2,1)S(1)}, bf16[64,3584]{1,0:T(8,128)(2,1)S(1)}, u32[]{:S(2)}, u32[]{:S(2)}) collective-permute-start(bf16[64,3584]{1,0:T(8,128)(2,1)S(1)} %collective-permute-done.refs_1_), channel_id=1, source_target_pairs={{0,1},{1,0},{2,3},{3,2},{4,5},{5,4},{6,7},{7,6},{8,9},{9,8},{10,11... | collective-permute-start | bytes 1376264 | tf_op jit(solution)/shard_map/ppermute | solution.py:457
  33.2 13.2 %collective-permute-start.7 = (bf16[64,3584]{1,0:T(8,128)(2,1)S(1)}, bf16[64,3584]{1,0:T(8,128)(2,1)S(1)}, u32[]{:S(2)}, u32[]{:S(2)}) collective-permute-start(bf16[64,3584]{1,0:T(8,128)(2,1)S(1)} %collective-permute-done.3.refs_0_), channel_id=1, source_target_pairs={{0,16},{8,24},{16,0},{24,8},{1,17},{9,25},{17,1},{25,9},{2,18},{10... | collective-permute-start | bytes 1376264 | tf_op jit(solution)/shard_map/ppermute | solution.py:451
  33.7 12.7 %collective-permute-start.6 = (bf16[64,3584]{1,0:T(8,128)(2,1)S(1)}, bf16[64,3584]{1,0:T(8,128)(2,1)S(1)}, u32[]{:S(2)}, u32[]{:S(2)}) collective-permute-start(bf16[64,3584]{1,0:T(8,128)(2,1)S(1)} %collective-permute-done.3.refs_0_), channel_id=1, source_target_pairs={{0,2},{1,3},{2,4},{3,5},{4,6},{5,7},{6,0},{7,1},{8,10},{9,11},{10,... | collective-permute-start | bytes 1376264 | tf_op jit(solution)/shard_map/ppermute | solution.py:467
  34.3 16.7 %collective-permute-start.11 = (bf16[64,3584]{1,0:T(8,128)(2,1)S(1)}, bf16[64,3584]{1,0:T(8,128)(2,1)S(1)}, u32[]{:S(2)}, u32[]{:S(2)}) collective-permute-start(bf16[64,3584]{1,0:T(8,128)(2,1)S(1)} %collective-permute-done.3.refs_0_), channel_id=1, source_target_pairs={{0,1},{1,0},{2,3},{3,2},{4,5},{5,4},{6,7},{7,6},{8,9},{9,8},{10,11... | collective-permute-start | bytes 1376264 | tf_op jit(solution)/shard_map/ppermute | solution.py:457
  46.4 11.8 %collective-permute-start.10 = (bf16[64,3584]{1,0:T(8,128)(2,1)S(1)}, bf16[64,3584]{1,0:T(8,128)(2,1)S(1)}, u32[]{:S(2)}, u32[]{:S(2)}) collective-permute-start(bf16[64,3584]{1,0:T(8,128)(2,1)S(1)} %collective-permute-done.6.refs_2_.refs_4_), channel_id=1, source_target_pairs={{0,16},{8,24},{16,0},{24,8},{1,17},{9,25},{17,1},{25,9},{2,18},{10... | collective-permute-start | bytes 1376264 | tf_op jit(solution)/shard_map/ppermute | solution.py:451
  48.8 10.1 %collective-permute-start.9 = (bf16[896,384]{1,0:T(8,128)(2,1)S(1)}, bf16[896,384]{1,0:T(8,128)(2,1)S(1)}, u32[]{:S(2)}, u32[]{:S(2)}) collective-permute-start(bf16[896,384]{1,0:T(8,128)(2,1)S(1)} %get-tuple-element.72), channel_id=1, source_target_pairs={{0,8},{8,0},{16,24},{24,16},{1,9},{9,1},{17,25},{25,17},{2,10},{10... | collective-permute-start | bytes 2064392 | tf_op jit(solution)/shard_map/ppermute | solution.py:454
  48.9 18.7 %collective-permute-start.13 = (bf16[64,3584]{1,0:T(8,128)(2,1)S(1)}, bf16[64,3584]{1,0:T(8,128)(2,1)S(1)}, u32[]{:S(2)}, u32[]{:S(2)}) collective-permute-start(bf16[64,3584]{1,0:T(8,128)(2,1)S(1)} %collective-permute-done.8.refs_1_), channel_id=1, source_target_pairs={{0,2},{1,3},{2,4},{3,5},{4,6},{5,7},{6,0},{7,1},{8,10},{9,11},{10,... | collective-permute-start | bytes 1376264 | tf_op jit(solution)/shard_map/ppermute | solution.py:467
  50.5 17.1 %collective-permute-start.12 = (bf16[64,3584]{1,0:T(8,128)(2,1)S(1)}, bf16[64,3584]{1,0:T(8,128)(2,1)S(1)}, u32[]{:S(2)}, u32[]{:S(2)}) collective-permute-start(bf16[64,3584]{1,0:T(8,128)(2,1)S(1)} %collective-permute-done.6.refs_2_.refs_4_), channel_id=1, source_target_pairs={{0,1},{1,0},{2,3},{3,2},{4,5},{5,4},{6,7},{7,6},{8,9},{9,8},{10,11... | collective-permute-start | bytes 1376264 | tf_op jit(solution)/shard_map/ppermute | solution.py:457
  51.1 22.3 %collective-permute-start.14 = (bf16[64,3584]{1,0:T(8,128)(2,1)S(1)}, bf16[64,3584]{1,0:T(8,128)(2,1)S(1)}, u32[]{:S(2)}, u32[]{:S(2)}) collective-permute-start(bf16[64,3584]{1,0:T(8,128)(2,1)S(1)} %collective-permute-done.11.refs_1_.refs_3_), channel_id=1, source_target_pairs={{0,16},{8,24},{16,0},{24,8},{1,17},{9,25},{17,1},{25,9},{2,18},{10... | collective-permute-start | bytes 1376264 | tf_op jit(solution)/shard_map/ppermute | solution.py:451
  58.2 15.1 %collective-permute-start.15 = (bf16[64,3584]{1,0:T(8,128)(2,1)S(1)}, bf16[64,3584]{1,0:T(8,128)(2,1)S(1)}, u32[]{:S(2)}, u32[]{:S(2)}) collective-permute-start(bf16[64,3584]{1,0:T(8,128)(2,1)S(1)} %collective-permute-done.10.refs_0_.refs_5_), channel_id=1, source_target_pairs={{0,1},{1,0},{2,3},{3,2},{4,5},{5,4},{6,7},{7,6},{8,9},{9,8},{10,11... | collective-permute-start | bytes 1376264 | tf_op jit(solution)/shard_map/ppermute | solution.py:457
  73.3 1.4 %copy-start = (bf16[384,2048]{1,0:T(8,128)(2,1)S(1)}, bf16[384,2048]{1,0:T(8,128)(2,1)}, u32[]{:S(2)}) copy-start(bf16[384,2048]{1,0:T(8,128)(2,1)} %get-tuple-element.94.refs_4_) | copy-start | bytes 4718596
  73.3 1.8 %copy-start.1 = (bf16[320,2048]{1,0:T(8,128)(2,1)S(1)}, bf16[320,2048]{1,0:T(8,128)(2,1)}, u32[]{:S(2)}) copy-start(bf16[320,2048]{1,0:T(8,128)(2,1)} %get-tuple-element.95.refs_5_) | copy-start | bytes 3932164
  74.8 8.3 %collective-permute-start.17 = (bf16[384,2048]{1,0:T(8,128)(2,1)S(1)}, bf16[384,2048]{1,0:T(8,128)(2,1)S(1)}, u32[]{:S(2)}, u32[]{:S(2)}) collective-permute-start(bf16[384,2048]{1,0:T(8,128)(2,1)S(1)} %copy-done), channel_id=1, source_target_pairs={{0,8},{8,0},{16,24},{24,16},{1,9},{9,1},{17,25},{25,17},{2,10},{10... | collective-permute-start | bytes 4718600 | tf_op jit(solution)/shard_map/ppermute | solution.py:454
  75.1 7.9 %collective-permute-start.18 = (bf16[320,2048]{1,0:T(8,128)(2,1)S(1)}, bf16[320,2048]{1,0:T(8,128)(2,1)S(1)}, u32[]{:S(2)}, u32[]{:S(2)}) collective-permute-start(bf16[320,2048]{1,0:T(8,128)(2,1)S(1)} %copy-done.1), channel_id=1, source_target_pairs={{0,8},{8,0},{16,24},{24,16},{1,9},{9,1},{17,25},{25,17},{2,10},{10... | collective-permute-start | bytes 3932168 | tf_op jit(solution)/shard_map/ppermute | solution.py:454
  75.3 6.5 %collective-permute-start.16 = (bf16[896,640]{1,0:T(8,128)(2,1)S(1)}, bf16[896,640]{1,0:T(8,128)(2,1)S(1)}, u32[]{:S(2)}, u32[]{:S(2)}) collective-permute-start(bf16[896,640]{1,0:T(8,128)(2,1)S(1)} %get-tuple-element.89), channel_id=1, source_target_pairs={{0,8},{8,0},{16,24},{24,16},{1,9},{9,1},{17,25},{25,17},{2,10},{10... | collective-permute-start | bytes 3440648 | tf_op jit(solution)/shard_map/ppermute | solution.py:454
  80.4 3.2 %collective-permute-start.21 = (f32[32,128]{1,0:T(8,128)S(1)}, f32[32,128]{1,0:T(8,128)S(1)}, u32[]{:S(2)}, u32[]{:S(2)}) collective-permute-start(f32[32,128]{1,0:T(8,128)S(1)} %get-tuple-element.97.own_ref), channel_id=1, source_target_pairs={{0,9},{1,8},{2,11},{3,10},{4,13},{5,12},{6,15},{7,14},{8,1},{9,0},... | collective-permute-start | bytes 49160 | tf_op jit(solution)/shard_map/ppermute | solution.py:464
  81.6 2.0 %collective-permute-start.20 = (f32[32,128]{1,0:T(8,128)S(1)}, f32[32,128]{1,0:T(8,128)S(1)}, u32[]{:S(2)}, u32[]{:S(2)}) collective-permute-start(f32[32,128]{1,0:T(8,128)S(1)} %get-tuple-element.97.own_ref), channel_id=1, source_target_pairs={{0,8},{8,0},{16,24},{24,16},{1,9},{9,1},{17,25},{25,17},{2,10},{10... | collective-permute-start | bytes 49160 | tf_op jit(solution)/shard_map/ppermute | solution.py:454
  81.9 3.7 %collective-permute-start.19 = (f32[32,128]{1,0:T(8,128)S(1)}, f32[32,128]{1,0:T(8,128)S(1)}, u32[]{:S(2)}, u32[]{:S(2)}) collective-permute-start(f32[32,128]{1,0:T(8,128)S(1)} %get-tuple-element.97.own_ref), channel_id=1, source_target_pairs={{0,1},{1,0},{2,3},{3,2},{4,5},{5,4},{6,7},{7,6},{8,9},{9,8},{10,11... | collective-permute-start | bytes 49160 | tf_op jit(solution)/shard_map/ppermute | solution.py:457
  85.6 8.7 %collective-permute-start.22 = (bf16[320,2048]{1,0:T(8,128)(2,1)}, bf16[320,2048]{1,0:T(8,128)(2,1)S(1)}, u32[]{:S(2)}, u32[]{:S(2)}) collective-permute-start(bf16[320,2048]{1,0:T(8,128)(2,1)} %get-tuple-element.99.refs_6_), channel_id=1, source_target_pairs={{0,8},{8,0},{16,24},{24,16},{1,9},{9,1},{17,25},{25,17},{2,10},{10... | collective-permute-start | bytes 3932168 | tf_op jit(solution)/shard_map/ppermute | solution.py:454
  85.7 7.1 %collective-permute-start.25 = (f32[64,128]{1,0:T(8,128)S(1)}, f32[64,128]{1,0:T(8,128)S(1)}, u32[]{:S(2)}, u32[]{:S(2)}) collective-permute-start(f32[64,128]{1,0:T(8,128)S(1)} %get-tuple-element.98.refs_10_), channel_id=1, source_target_pairs={{0,2},{1,3},{2,4},{3,5},{4,6},{5,7},{6,0},{7,1},{8,10},{9,11},{10,... | collective-permute-start | bytes 98312 | tf_op jit(solution)/shard_map/ppermute | solution.py:467
  87.7 5.1 %collective-permute-start.24 = (f32[64,128]{1,0:T(8,128)S(1)}, f32[64,128]{1,0:T(8,128)S(1)}, u32[]{:S(2)}, u32[]{:S(2)}) collective-permute-start(f32[64,128]{1,0:T(8,128)S(1)} %get-tuple-element.98.refs_10_), channel_id=1, source_target_pairs={{0,4},{1,5},{2,6},{3,7},{4,0},{5,1},{6,2},{7,3},{8,12},{9,13},{10,... | collective-permute-start | bytes 98312 | tf_op jit(solution)/shard_map/ppermute | solution.py:467
  89.9 4.4 %collective-permute-start.23 = (f32[64,128]{1,0:T(8,128)S(1)}, f32[64,128]{1,0:T(8,128)S(1)}, u32[]{:S(2)}, u32[]{:S(2)}) collective-permute-start(f32[64,128]{1,0:T(8,128)S(1)} %get-tuple-element.98.refs_10_), channel_id=1, source_target_pairs={{0,6},{1,7},{2,0},{3,1},{4,2},{5,3},{6,4},{7,5},{8,14},{9,15},{10,... | collective-permute-start | bytes 98312 | tf_op jit(solution)/shard_map/ppermute | solution.py:467

commit v14 on v13

--- a/solution.py
+++ b/solution.py
@@ -473,7 +473,7 @@
         [(0, 0, split), (1, 1, 0)],
         [(0, 1, split), (1, 0, split), (0, 0, split + 1)],
         [(0, 1, split + 1), (1, 0, split + 1), (1, 1, 1)],
-        [(1, 1, turn) for turn in range(split, lines)],
+        [(1, 1, turn) for turn in range(lines - 1, split - 1, -1)],
     ]
     early_blocks, late_blocks = sum(groups[:split], []), sum(groups[split:], [])
 
@@ -561,19 +561,19 @@
     early_ids[0] = after(early_ids[0], middle_exp, held[0, 1, lines - 1])
     sums = one_hot_sums(early, early_ids, columns)
     last_exp, stats = logits(groups[split + 2], stats, *sums, exp_rows=5 * length)
+    last_exp, stats = logits(
+        groups[-1], stats, first_row=3 * length, exp_rows=5 * length, into=last_exp
+    )
+    exps = [early_exp, middle_exp, last_exp]
+    across_stats, core_stats, both_stats = to_y(stats), to_core(stats), to_y_core(stats)
+    ready = lax.optimization_barrier((early_exp, middle_exp, stats))
+    other_exps = [to_core(exp) for exp in ready[:2]]
     late = [held[block] for block in late_blocks]
-    late[0] = after(late[0], last_exp)
+    late[0] = after(late[0], across_stats)
     late = turned_features(rep_scalar, late, rows)
     late = [late[0], to_core(late[1])]
-    ready = lax.optimization_barrier((early_exp, middle_exp, late[0]))
-    other_exps = [to_core(exp) for exp in ready[:2]]
-    last_exp, stats = logits(
-        groups[-1], stats, late[0], first_row=3 * length, exp_rows=5 * length, into=last_exp
-    )
-    exps = [early_exp, middle_exp, last_exp]
-    across_stats, core_stats, both_stats = to_y(stats), to_core(stats), to_y_core(stats)
     merged, first = merged_stats(
-        after(stats, late[1], *other_exps), across_stats, core_stats, both_stats
+        after(stats, *other_exps), across_stats, core_stats, both_stats
     )
     all_stats = [merged] + [to_z(merged, -along) for along in range(1, lines)]
     other_exps.append(to_core(after(last_exp, merged)))

time: 115 us -> 113 us (0.983)
    ppermute x6, waiting for transfers between devices: 0.02 us -> 2.66 us  [to_core(): return lax.ppermute(values, 'rep', swap_pairs(reps, 1))]
    ppermute x7, waiting for transfers between devices: 2.02 us -> 0.02 us  [to_y(): return lax.ppermute(values, 'shard', swap_pairs(shards, 1))]
    ppermute x7, starting transfers between devices: 12.3 us -> 11 us  [to_z(): return lax.ppermute(values, 'shard', shift_pairs(lines, along, 0))]
  transfers between devices with their start and end apart: 26 -> 26, of which waited for: 6 -> 6; matrix products, arithmetic and copies ran while one was open for 6% -> 6% of each run, Pallas kernels for 42% -> 39%
where the time goes in v14:
time: 113 us
  Pallas kernels  70.1 us (62%)
  starting transfers between devices  27.2 us (24%)
  waiting for transfers between devices  7.83 us (7%)
  other arithmetic  3.62 us (3%)
  local copies, waits for them, and re-layouts  3.16 us (3%)
    pallas_call x6, Pallas kernels, round_logits(): pl.pallas_call(functools.partial(logits_kernel, stat_rows, first_row, len...  32.5 us
    pallas_call x1, Pallas kernels, refresh_states(): pl.pallas_call(functools.partial(refresh_kernel, lines, length, block_row...  20 us
    ppermute x7, starting transfers between devices, to_z(): return lax.ppermute(values, 'shard', shift_pairs(lines, along, 0))  11 us
    ppermute x7, starting transfers between devices, to_y(): return lax.ppermute(values, 'shard', swap_pairs(shards, 1))  8.68 us
    pallas_call x1, Pallas kernels, one_hot_sums(): pl.pallas_call(functools.partial(one_hot_kernel, len(features)), grid=(co...  8.66 us
    ppermute x5, starting transfers between devices, to_x(): return lax.ppermute(values, 'rep', swap_pairs(reps, 2))  5.58 us
    pallas_call x1, Pallas kernels, prepared(): pl.pallas_call(prepare_kernel, in_specs=[pl.BlockSpec(memory_space=pltpu....  5.52 us
    ppermute x7, waiting for transfers between devices, to_z(): return lax.ppermute(values, 'shard', shift_pairs(lines, along, 0))  5.14 us
  transfers between devices with their start and end apart: 26, of which 6 were waited for; matrix products, arithmetic and copies ran while one was open for 6% of the time, Pallas kernels for 39%

profile of v14, /device:TPU:0, one launch (start us, length us, event | category | flops | bytes accessed | tf_op | source)
XLA Modules:
  0.0 112.7 jit_solution(7570075822833584792)
XLA Ops:
  0.6 1.2 %normalized.1.refs_0_ = bf16[64,3584]{1,0:T(8,128)(2,1)S(1)} custom-call(bf16[64,3584]{1,0:T(8,128)(2,1)} %hidden_ref.1, f32[3584]{0:T(1024)} %gain_ref.1), custom_call_target="tpu_custom_call" | custom-call | flops 1024 | bytes 1024 | tf_op jit(solution)/shard_map/normalized/pallas_call | solution.py:93
  1.9 3.1 %collective-permute-start.2 = (bf16[64,3584]{1,0:T(8,128)(2,1)S(1)}, bf16[64,3584]{1,0:T(8,128)(2,1)S(1)}, u32[]{:S(2)}, u32[]{:S(2)}) collective-permute-start(bf16[64,3584]{1,0:T(8,128)(2,1)S(1)} %normalized.1.refs_0_), channel_id=1, source_target_pairs={{0,2},{1,3},{2,4},{3,5},{4,6},{5,7},{6,0},{7,1},{8,10},{9,11},{10,... | collective-permute-start | bytes 1376264 | tf_op jit(solution)/shard_map/ppermute | solution.py:467
  4.9 1.5 %collective-permute-start.1 = (bf16[64,3584]{1,0:T(8,128)(2,1)S(1)}, bf16[64,3584]{1,0:T(8,128)(2,1)S(1)}, u32[]{:S(2)}, u32[]{:S(2)}) collective-permute-start(bf16[64,3584]{1,0:T(8,128)(2,1)S(1)} %normalized.1.refs_0_), channel_id=1, source_target_pairs={{0,1},{1,0},{2,3},{3,2},{4,5},{5,4},{6,7},{7,6},{8,9},{9,8},{10,11... | collective-permute-start | bytes 1376264 | tf_op jit(solution)/shard_map/ppermute | solution.py:457
  6.5 1.5 %collective-permute-start = (bf16[64,3584]{1,0:T(8,128)(2,1)S(1)}, bf16[64,3584]{1,0:T(8,128)(2,1)S(1)}, u32[]{:S(2)}, u32[]{:S(2)}) collective-permute-start(bf16[64,3584]{1,0:T(8,128)(2,1)S(1)} %normalized.1.refs_0_), channel_id=1, source_target_pairs={{0,16},{8,24},{16,0},{24,8},{1,17},{9,25},{17,1},{25,9},{2,18},{10... | collective-permute-start | bytes 1376264 | tf_op jit(solution)/shard_map/ppermute | solution.py:451
  7.9 0.7 fusion.4
  8.6 0.7 compare_and_fusion
  9.3 0.7 multiply_add_fusion
  10.0 1.2 %slice.31 = s32[1]{0:T(128)} slice(s32[2048]{0:T(1024)} %param.12), slice={[0:1]} | slice | bytes 8 | tf_op jit(solution)/shard_map/jit(_roll_static)/slice | solution.py:486
  11.2 0.8 slice.30
  12.1 0.7 broadcast_subtract_fusion
  12.9 0.7 fusion.1
  13.7 0.6 gather_fusion
  14.7 2.7 %collective-permute-done.2.refs_0_.refs_3_ = bf16[64,3584]{1,0:T(8,128)(2,1)S(1)} collective-permute-done((bf16[64,3584]{1,0:T(8,128)(2,1)S(1)}, bf16[64,3584]{1,0:T(8,128)(2,1)S(1)}, u32[]{:S(2)}, u32[]{:S(2)}) %collective-permute-start.2) | collective-permute-done | bytes 458784 | tf_op jit(solution)/shard_map/ppermute | solution.py:467
  17.5 1.5 %collective-permute-start.5 = (bf16[64,3584]{1,0:T(8,128)(2,1)S(1)}, bf16[64,3584]{1,0:T(8,128)(2,1)S(1)}, u32[]{:S(2)}, u32[]{:S(2)}) collective-permute-start(bf16[64,3584]{1,0:T(8,128)(2,1)S(1)} %collective-permute-done.2.refs_0_.refs_3_), channel_id=1, source_target_pairs={{0,1},{1,0},{2,3},{3,2},{4,5},{5,4},{6,7},{7,6},{8,9},{9,8},{10,11... | collective-permute-start | bytes 1376264 | tf_op jit(solution)/shard_map/ppermute | solution.py:457
  19.0 1.5 %collective-permute-start.4 = (bf16[64,3584]{1,0:T(8,128)(2,1)S(1)}, bf16[64,3584]{1,0:T(8,128)(2,1)S(1)}, u32[]{:S(2)}, u32[]{:S(2)}) collective-permute-start(bf16[64,3584]{1,0:T(8,128)(2,1)S(1)} %collective-permute-done.2.refs_0_.refs_3_), channel_id=1, source_target_pairs={{0,16},{8,24},{16,0},{24,8},{1,17},{9,25},{17,1},{25,9},{2,18},{10... | collective-permute-start | bytes 1376264 | tf_op jit(solution)/shard_map/ppermute | solution.py:451
  20.5 5.5 %prepared.1 = (bf16[3584,2048]{1,0:T(8,128)(2,1)S(1)}, s32[1280,128]{1,0:T(8,128)S(1)}, s32[1280,128]{1,0:T(8,128)S(1)}) custom-call(bf16[3584,2048]{1,0:T(8,128)(2,1)} %weight_ref.1, s32[1,1280]{1,0:T(1,128)S(1)} %squeeze.14.true_ids, s32[1,1280]{1,0:T(1,128)S(1)} %squeeze.15.sample_ids, f32[32,128]{1,0:T(8,128)S(1)} %broadcast_in_dim.20.refs_0_.refs_4_), custom_call_target="tpu_custom_call" | custom-call | flops 1024 | bytes 1024 | tf_op jit(solution)/shard_map/prepared/pallas_call | solution.py:127
  26.0 0.6 collective-permute-start.8
  26.6 5.8 %round_logits.6 = (bf16[384,2048]{1,0:T(8,128)(2,1)}, f32[32,128]{1,0:T(8,128)S(1)}) custom-call(bf16[64,3584]{1,0:T(8,128)(2,1)S(1)} %normalized.1.refs_0_, bf16[64,3584]{1,0:T(8,128)(2,1)S(1)} %collective-permute-done.refs_1_, bf16[64,3584]{1,0:T(8,128)(2,1)S(1)} %collective-permute-done.1.refs_2_, ...), custom_call_target="tpu_custom_call" | custom-call | flops 1024 | bytes 1024 | tf_op jit(solution)/shard_map/round_logits/pallas_call | solution.py:206
  32.4 0.8 collective-permute-done.3.refs_0_
  33.2 0.5 collective-permute-start.7
  33.7 0.6 collective-permute-start.6
  34.3 1.5 %collective-permute-start.11 = (bf16[64,3584]{1,0:T(8,128)(2,1)S(1)}, bf16[64,3584]{1,0:T(8,128)(2,1)S(1)}, u32[]{:S(2)}, u32[]{:S(2)}) collective-permute-start(bf16[64,3584]{1,0:T(8,128)(2,1)S(1)} %collective-permute-done.3.refs_0_), channel_id=1, source_target_pairs={{0,1},{1,0},{2,3},{3,2},{4,5},{5,4},{6,7},{7,6},{8,9},{9,8},{10,11... | collective-permute-start | bytes 1376264 | tf_op jit(solution)/shard_map/ppermute | solution.py:457
  35.8 5.8 %round_logits.7 = (bf16[384,2048]{1,0:T(8,128)(2,1)}, f32[32,128]{1,0:T(8,128)S(1)}) custom-call(bf16[64,3584]{1,0:T(8,128)(2,1)S(1)} %collective-permute-done.2.refs_0_.refs_3_, bf16[64,3584]{1,0:T(8,128)(2,1)S(1)} %collective-permute-done.4.refs_1_.refs_4_, ...), custom_call_target="tpu_custom_call", output_to_operand_aliasing={{0}: (5, {})} | custom-call | flops 1024 | bytes 1024 | tf_op jit(solution)/shard_map/round_logits/pallas_call | solution.py:206
  41.6 4.7 %round_logits.8 = (bf16[320,2048]{1,0:T(8,128)(2,1)}, f32[32,128]{1,0:T(8,128)S(1)}) custom-call(bf16[64,3584]{1,0:T(8,128)(2,1)S(1)} %collective-permute-done.3.refs_0_, bf16[64,3584]{1,0:T(8,128)(2,1)S(1)} %collective-permute-done.8.refs_1_, bf16[3584,2048]{1,0:T(8,128)(2,1)S(1)} %get-tuple-element.57.refs_3_.refs_2_, f32[32,128]{1,0:T(8,128)S(1)} %get-tuple-element.66.refs_3_), custom_call_target="tpu_custom_call" | custom-call | flops 1024 | bytes 1024 | tf_op jit(solution)/shard_map/round_logits/pallas_call | solution.py:206
  46.4 1.6 %collective-permute-start.10 = (bf16[64,3584]{1,0:T(8,128)(2,1)S(1)}, bf16[64,3584]{1,0:T(8,128)(2,1)S(1)}, u32[]{:S(2)}, u32[]{:S(2)}) collective-permute-start(bf16[64,3584]{1,0:T(8,128)(2,1)S(1)} %collective-permute-done.6.refs_2_.refs_4_), channel_id=1, source_target_pairs={{0,16},{8,24},{16,0},{24,8},{1,17},{9,25},{17,1},{25,9},{2,18},{10... | collective-permute-start | bytes 1376264 | tf_op jit(solution)/shard_map/ppermute | solution.py:451
  48.0 0.9 turned_features.2
  48.9 1.6 %collective-permute-start.15 = (bf16[64,3584]{1,0:T(8,128)(2,1)S(1)}, bf16[64,3584]{1,0:T(8,128)(2,1)S(1)}, u32[]{:S(2)}, u32[]{:S(2)}) collective-permute-start(bf16[64,3584]{1,0:T(8,128)(2,1)S(1)} %collective-permute-done.8.refs_1_), channel_id=1, source_target_pairs={{0,2},{1,3},{2,4},{3,5},{4,6},{5,7},{6,0},{7,1},{8,10},{9,11},{10,... | collective-permute-start | bytes 1376264 | tf_op jit(solution)/shard_map/ppermute | solution.py:467
  50.5 0.5 collective-permute-start.14
  51.1 5.8 %round_logits.9 = (bf16[320,2048]{1,0:T(8,128)(2,1)}, f32[32,128]{1,0:T(8,128)S(1)}) custom-call(bf16[64,3584]{1,0:T(8,128)(2,1)S(1)} %collective-permute-done.7.refs_0_.refs_2_, bf16[64,3584]{1,0:T(8,128)(2,1)S(1)} %collective-permute-done.11.refs_1_.refs_3_, ...), custom_call_target="tpu_custom_call", output_to_operand_aliasing={{0}: (5, {})} | custom-call | flops 1024 | bytes 1024 | tf_op jit(solution)/shard_map/round_logits/pallas_call | solution.py:206
  56.8 1.6 %collective-permute-start.12 = (bf16[64,3584]{1,0:T(8,128)(2,1)S(1)}, bf16[64,3584]{1,0:T(8,128)(2,1)S(1)}, u32[]{:S(2)}, u32[]{:S(2)}) collective-permute-start(bf16[64,3584]{1,0:T(8,128)(2,1)S(1)} %collective-permute-done.10.refs_0_.refs_5_), channel_id=1, source_target_pairs={{0,1},{1,0},{2,3},{3,2},{4,5},{5,4},{6,7},{7,6},{8,9},{9,8},{10,11... | collective-permute-start | bytes 1376264 | tf_op jit(solution)/shard_map/ppermute | solution.py:457
  58.4 0.5 collective-permute-start.13
  58.9 8.7 %one_hot_sums.1 = (bf16[896,2048]{1,0:T(8,128)(2,1)}, bf16[896,2048]{1,0:T(8,128)(2,1)}) custom-call(bf16[896,384]{1,0:T(8,128)(2,1)S(1)} %get-tuple-element.70.refs_0_, bf16[896,384]{1,0:T(8,128)(2,1)S(1)} %collective-permute-done.9.refs_1_, s32[1,768]{1,0:T(1,128)S(1)} %squeeze.12.refs_2_, s32[1,768]{1,0:T(1,128)S(1)} %squeeze.13.refs_3_), custom_call_target="tpu_custom_call" | custom-call | flops 1024 | bytes 1024 | tf_op jit(solution)/shard_map/one_hot_sums/pallas_call | solution.py:285
  67.6 5.7 %round_logits.10 = (bf16[320,2048]{1,0:T(8,128)(2,1)}, f32[32,128]{1,0:T(8,128)S(1)}) custom-call(bf16[64,3584]{1,0:T(8,128)(2,1)S(1)} %collective-permute-done.10.refs_0_.refs_5_, bf16[64,3584]{1,0:T(8,128)(2,1)S(1)} %collective-permute-done.14.refs_1_.refs_6_, bf16[64,3584]{1,0:T(8,128)(2,1)S(1)} %collective-permute-done.15.refs_2_.refs_7_, ...), custom_call_target="tpu_custom_call" | custom-call | flops 1024 | bytes 1024 | tf_op jit(solution)/shard_map/round_logits/pallas_call | solution.py:206
  73.3 4.7 %round_logits.11 = (bf16[320,2048]{1,0:T(8,128)(2,1)}, f32[32,128]{1,0:T(8,128)S(1)}) custom-call(bf16[64,3584]{1,0:T(8,128)(2,1)S(1)} %collective-permute-done.12.refs_0_.refs_8_, bf16[64,3584]{1,0:T(8,128)(2,1)S(1)} %collective-permute-done.13.refs_1_.refs_9_, ...), custom_call_target="tpu_custom_call", output_to_operand_aliasing={{0}: (4, {})} | custom-call | flops 1024 | bytes 1024 | tf_op jit(solution)/shard_map/round_logits/pallas_call | solution.py:206
  78.2 0.5 collective-permute-start.19
  78.7 0.2 collective-permute-start.21
  78.9 0.4 collective-permute-start.20
  79.3 1.5 %collective-permute-start.16 = (f32[32,128]{1,0:T(8,128)S(1)}, f32[32,128]{1,0:T(8,128)S(1)}, u32[]{:S(2)}, u32[]{:S(2)}) collective-permute-start(f32[32,128]{1,0:T(8,128)S(1)} %get-tuple-element.95.own_ref), channel_id=1, source_target_pairs={{0,1},{1,0},{2,3},{3,2},{4,5},{5,4},{6,7},{7,6},{8,9},{9,8},{10,11... | collective-permute-start | bytes 49160 | tf_op jit(solution)/shard_map/ppermute | solution.py:457
  80.8 2.6 %collective-permute-done.19.refs_8_ = bf16[320,2048]{1,0:T(8,128)(2,1)S(1)} collective-permute-done((bf16[320,2048]{1,0:T(8,128)(2,1)S(1)}, bf16[320,2048]{1,0:T(8,128)(2,1)S(1)}, u32[]{:S(2)}, u32[]{:S(2)}) %collective-permute-start.19) | collective-permute-done | bytes 1310752 | tf_op jit(solution)/shard_map/ppermute | solution.py:454
  83.5 0.2 collective-permute-start.22
  83.7 1.3 %turned_features.3 = (bf16[896,640]{1,0:T(8,128)(2,1)S(1)}, bf16[896,640]{1,0:T(8,128)(2,1)S(1)}) custom-call(s32[1]{0:T(128)} %bitcast.rep_ref, bf16[64,3584]{1,0:T(8,128)(2,1)S(1)} %collective-permute-done.3.refs_0_, bf16[64,3584]{1,0:T(8,128)(2,1)S(1)} %collective-permute-done.8.refs_1_, bf16[64,3584]{1,0:T(8,128)(2,1)S(1)} %collective-permute-done.7.refs_0_.refs_2_, ...), custom_call_target="tpu_custom_call" | custom-call | flops 1024 | bytes 1024 | tf_op jit(solution)/shard_map/turned_features/pallas_call | solution.py:248
  85.0 0.4 collective-permute-start.17
  85.4 2.1 %collective-permute-start.25 = (f32[64,128]{1,0:T(8,128)S(1)}, f32[64,128]{1,0:T(8,128)S(1)}, u32[]{:S(2)}, u32[]{:S(2)}) collective-permute-start(f32[64,128]{1,0:T(8,128)S(1)} %get-tuple-element.96.refs_10_), channel_id=1, source_target_pairs={{0,2},{1,3},{2,4},{3,5},{4,6},{5,7},{6,0},{7,1},{8,10},{9,11},{10,... | collective-permute-start | bytes 98312 | tf_op jit(solution)/shard_map/ppermute | solution.py:467
  87.6 0.9 collective-permute-start.24
  88.5 2.6 %collective-permute-start.23 = (f32[64,128]{1,0:T(8,128)S(1)}, f32[64,128]{1,0:T(8,128)S(1)}, u32[]{:S(2)}, u32[]{:S(2)}) collective-permute-start(f32[64,128]{1,0:T(8,128)S(1)} %get-tuple-element.96.refs_10_), channel_id=1, source_target_pairs={{0,6},{1,7},{2,0},{3,1},{4,2},{5,3},{6,4},{7,5},{8,14},{9,15},{10,... | collective-permute-start | bytes 98312 | tf_op jit(solution)/shard_map/ppermute | solution.py:467
  91.3 1.3 %collective-permute-done.24.refs_12_ = f32[64,128]{1,0:T(8,128)S(1)} collective-permute-done((f32[64,128]{1,0:T(8,128)S(1)}, f32[64,128]{1,0:T(8,128)S(1)}, u32[]{:S(2)}, u32[]{:S(2)}) %collective-permute-start.24) | collective-permute-done | bytes 32800 | tf_op jit(solution)/shard_map/ppermute | solution.py:467
  92.6 0.2 collective-permute-done.23.refs_11_
  92.7 20.0 %refresh_states.1 = (bf16[896,2048]{1,0:T(8,128)(2,1)}, bf16[896,2048]{1,0:T(8,128)(2,1)}, bf16[896,2048]{1,0:T(8,128)(2,1)}) custom-call(bf16[896,384]{1,0:T(8,128)(2,1)S(1)} %get-tuple-element.70.refs_0_, bf16[896,384]{1,0:T(8,128)(2,1)S(1)} %collective-permute-done.9.refs_1_, bf16[896,640]{1,0:T(8,128)(2,1)S(1)} %get-tuple-element.89.refs_2_, ...), custom_call_target="tpu_custom_call" | custom-call | flops 1024 | bytes 1024 | tf_op jit(solution)/shard_map/refresh_states/pallas_call | solution.py:414
  (44 shorter events, 1.1 us)
Async XLA Ops:
  1.9 15.6 %collective-permute-start.2 = (bf16[64,3584]{1,0:T(8,128)(2,1)S(1)}, bf16[64,3584]{1,0:T(8,128)(2,1)S(1)}, u32[]{:S(2)}, u32[]{:S(2)}) collective-permute-start(bf16[64,3584]{1,0:T(8,128)(2,1)S(1)} %normalized.1.refs_0_), channel_id=1, source_target_pairs={{0,2},{1,3},{2,4},{3,5},{4,6},{5,7},{6,0},{7,1},{8,10},{9,11},{10,... | collective-permute-start | bytes 1376264 | tf_op jit(solution)/shard_map/ppermute | solution.py:467
  4.9 21.1 %collective-permute-start.1 = (bf16[64,3584]{1,0:T(8,128)(2,1)S(1)}, bf16[64,3584]{1,0:T(8,128)(2,1)S(1)}, u32[]{:S(2)}, u32[]{:S(2)}) collective-permute-start(bf16[64,3584]{1,0:T(8,128)(2,1)S(1)} %normalized.1.refs_0_), channel_id=1, source_target_pairs={{0,1},{1,0},{2,3},{3,2},{4,5},{5,4},{6,7},{7,6},{8,9},{9,8},{10,11... | collective-permute-start | bytes 1376264 | tf_op jit(solution)/shard_map/ppermute | solution.py:457
  6.5 19.6 %collective-permute-start = (bf16[64,3584]{1,0:T(8,128)(2,1)S(1)}, bf16[64,3584]{1,0:T(8,128)(2,1)S(1)}, u32[]{:S(2)}, u32[]{:S(2)}) collective-permute-start(bf16[64,3584]{1,0:T(8,128)(2,1)S(1)} %normalized.1.refs_0_), channel_id=1, source_target_pairs={{0,16},{8,24},{16,0},{24,8},{1,17},{9,25},{17,1},{25,9},{2,18},{10... | collective-permute-start | bytes 1376264 | tf_op jit(solution)/shard_map/ppermute | solution.py:451
  17.5 14.9 %collective-permute-start.5 = (bf16[64,3584]{1,0:T(8,128)(2,1)S(1)}, bf16[64,3584]{1,0:T(8,128)(2,1)S(1)}, u32[]{:S(2)}, u32[]{:S(2)}) collective-permute-start(bf16[64,3584]{1,0:T(8,128)(2,1)S(1)} %collective-permute-done.2.refs_0_.refs_3_), channel_id=1, source_target_pairs={{0,1},{1,0},{2,3},{3,2},{4,5},{5,4},{6,7},{7,6},{8,9},{9,8},{10,11... | collective-permute-start | bytes 1376264 | tf_op jit(solution)/shard_map/ppermute | solution.py:457
  19.0 13.4 %collective-permute-start.4 = (bf16[64,3584]{1,0:T(8,128)(2,1)S(1)}, bf16[64,3584]{1,0:T(8,128)(2,1)S(1)}, u32[]{:S(2)}, u32[]{:S(2)}) collective-permute-start(bf16[64,3584]{1,0:T(8,128)(2,1)S(1)} %collective-permute-done.2.refs_0_.refs_3_), channel_id=1, source_target_pairs={{0,16},{8,24},{16,0},{24,8},{1,17},{9,25},{17,1},{25,9},{2,18},{10... | collective-permute-start | bytes 1376264 | tf_op jit(solution)/shard_map/ppermute | solution.py:451
  20.5 12.7 %collective-permute-start.3 = (bf16[64,3584]{1,0:T(8,128)(2,1)S(1)}, bf16[64,3584]{1,0:T(8,128)(2,1)S(1)}, u32[]{:S(2)}, u32[]{:S(2)}) collective-permute-start(bf16[64,3584]{1,0:T(8,128)(2,1)S(1)} %collective-permute-done.2.refs_0_.refs_3_), channel_id=1, source_target_pairs={{0,2},{1,3},{2,4},{3,5},{4,6},{5,7},{6,0},{7,1},{8,10},{9,11},{10,... | collective-permute-start | bytes 1376264 | tf_op jit(solution)/shard_map/ppermute | solution.py:467
  26.0 15.6 %collective-permute-start.8 = (bf16[64,3584]{1,0:T(8,128)(2,1)S(1)}, bf16[64,3584]{1,0:T(8,128)(2,1)S(1)}, u32[]{:S(2)}, u32[]{:S(2)}) collective-permute-start(bf16[64,3584]{1,0:T(8,128)(2,1)S(1)} %collective-permute-done.refs_1_), channel_id=1, source_target_pairs={{0,1},{1,0},{2,3},{3,2},{4,5},{5,4},{6,7},{7,6},{8,9},{9,8},{10,11... | collective-permute-start | bytes 1376264 | tf_op jit(solution)/shard_map/ppermute | solution.py:457
  33.2 13.2 %collective-permute-start.7 = (bf16[64,3584]{1,0:T(8,128)(2,1)S(1)}, bf16[64,3584]{1,0:T(8,128)(2,1)S(1)}, u32[]{:S(2)}, u32[]{:S(2)}) collective-permute-start(bf16[64,3584]{1,0:T(8,128)(2,1)S(1)} %collective-permute-done.3.refs_0_), channel_id=1, source_target_pairs={{0,16},{8,24},{16,0},{24,8},{1,17},{9,25},{17,1},{25,9},{2,18},{10... | collective-permute-start | bytes 1376264 | tf_op jit(solution)/shard_map/ppermute | solution.py:451
  33.7 12.7 %collective-permute-start.6 = (bf16[64,3584]{1,0:T(8,128)(2,1)S(1)}, bf16[64,3584]{1,0:T(8,128)(2,1)S(1)}, u32[]{:S(2)}, u32[]{:S(2)}) collective-permute-start(bf16[64,3584]{1,0:T(8,128)(2,1)S(1)} %collective-permute-done.3.refs_0_), channel_id=1, source_target_pairs={{0,2},{1,3},{2,4},{3,5},{4,6},{5,7},{6,0},{7,1},{8,10},{9,11},{10,... | collective-permute-start | bytes 1376264 | tf_op jit(solution)/shard_map/ppermute | solution.py:467
  34.3 16.7 %collective-permute-start.11 = (bf16[64,3584]{1,0:T(8,128)(2,1)S(1)}, bf16[64,3584]{1,0:T(8,128)(2,1)S(1)}, u32[]{:S(2)}, u32[]{:S(2)}) collective-permute-start(bf16[64,3584]{1,0:T(8,128)(2,1)S(1)} %collective-permute-done.3.refs_0_), channel_id=1, source_target_pairs={{0,1},{1,0},{2,3},{3,2},{4,5},{5,4},{6,7},{7,6},{8,9},{9,8},{10,11... | collective-permute-start | bytes 1376264 | tf_op jit(solution)/shard_map/ppermute | solution.py:457
  46.4 10.4 %collective-permute-start.10 = (bf16[64,3584]{1,0:T(8,128)(2,1)S(1)}, bf16[64,3584]{1,0:T(8,128)(2,1)S(1)}, u32[]{:S(2)}, u32[]{:S(2)}) collective-permute-start(bf16[64,3584]{1,0:T(8,128)(2,1)S(1)} %collective-permute-done.6.refs_2_.refs_4_), channel_id=1, source_target_pairs={{0,16},{8,24},{16,0},{24,8},{1,17},{9,25},{17,1},{25,9},{2,18},{10... | collective-permute-start | bytes 1376264 | tf_op jit(solution)/shard_map/ppermute | solution.py:451
  48.8 10.1 %collective-permute-start.9 = (bf16[896,384]{1,0:T(8,128)(2,1)S(1)}, bf16[896,384]{1,0:T(8,128)(2,1)S(1)}, u32[]{:S(2)}, u32[]{:S(2)}) collective-permute-start(bf16[896,384]{1,0:T(8,128)(2,1)S(1)} %get-tuple-element.71), channel_id=1, source_target_pairs={{0,8},{8,0},{16,24},{24,16},{1,9},{9,1},{17,25},{25,17},{2,10},{10... | collective-permute-start | bytes 2064392 | tf_op jit(solution)/shard_map/ppermute | solution.py:454
  48.9 18.7 %collective-permute-start.15 = (bf16[64,3584]{1,0:T(8,128)(2,1)S(1)}, bf16[64,3584]{1,0:T(8,128)(2,1)S(1)}, u32[]{:S(2)}, u32[]{:S(2)}) collective-permute-start(bf16[64,3584]{1,0:T(8,128)(2,1)S(1)} %collective-permute-done.8.refs_1_), channel_id=1, source_target_pairs={{0,2},{1,3},{2,4},{3,5},{4,6},{5,7},{6,0},{7,1},{8,10},{9,11},{10,... | collective-permute-start | bytes 1376264 | tf_op jit(solution)/shard_map/ppermute | solution.py:467
  50.5 17.0 %collective-permute-start.14 = (bf16[64,3584]{1,0:T(8,128)(2,1)S(1)}, bf16[64,3584]{1,0:T(8,128)(2,1)S(1)}, u32[]{:S(2)}, u32[]{:S(2)}) collective-permute-start(bf16[64,3584]{1,0:T(8,128)(2,1)S(1)} %collective-permute-done.6.refs_2_.refs_4_), channel_id=1, source_target_pairs={{0,1},{1,0},{2,3},{3,2},{4,5},{5,4},{6,7},{7,6},{8,9},{9,8},{10,11... | collective-permute-start | bytes 1376264 | tf_op jit(solution)/shard_map/ppermute | solution.py:457
  56.8 16.5 %collective-permute-start.12 = (bf16[64,3584]{1,0:T(8,128)(2,1)S(1)}, bf16[64,3584]{1,0:T(8,128)(2,1)S(1)}, u32[]{:S(2)}, u32[]{:S(2)}) collective-permute-start(bf16[64,3584]{1,0:T(8,128)(2,1)S(1)} %collective-permute-done.10.refs_0_.refs_5_), channel_id=1, source_target_pairs={{0,1},{1,0},{2,3},{3,2},{4,5},{5,4},{6,7},{7,6},{8,9},{9,8},{10,11... | collective-permute-start | bytes 1376264 | tf_op jit(solution)/shard_map/ppermute | solution.py:457
  58.4 14.9 %collective-permute-start.13 = (bf16[64,3584]{1,0:T(8,128)(2,1)S(1)}, bf16[64,3584]{1,0:T(8,128)(2,1)S(1)}, u32[]{:S(2)}, u32[]{:S(2)}) collective-permute-start(bf16[64,3584]{1,0:T(8,128)(2,1)S(1)} %collective-permute-done.11.refs_1_.refs_3_), channel_id=1, source_target_pairs={{0,16},{8,24},{16,0},{24,8},{1,17},{9,25},{17,1},{25,9},{2,18},{10... | collective-permute-start | bytes 1376264 | tf_op jit(solution)/shard_map/ppermute | solution.py:451
  73.3 4.8 %copy-start = (bf16[384,2048]{1,0:T(8,128)(2,1)S(1)}, bf16[384,2048]{1,0:T(8,128)(2,1)}, u32[]{:S(2)}) copy-start(bf16[384,2048]{1,0:T(8,128)(2,1)} %get-tuple-element.93.refs_4_) | copy-start | bytes 4718596
  73.3 4.8 %copy-start.1 = (bf16[320,2048]{1,0:T(8,128)(2,1)S(1)}, bf16[320,2048]{1,0:T(8,128)(2,1)}, u32[]{:S(2)}) copy-start(bf16[320,2048]{1,0:T(8,128)(2,1)} %get-tuple-element.94.refs_5_) | copy-start | bytes 3932164
  78.1 5.4 %collective-permute-start.18 = (bf16[384,2048]{1,0:T(8,128)(2,1)S(1)}, bf16[384,2048]{1,0:T(8,128)(2,1)S(1)}, u32[]{:S(2)}, u32[]{:S(2)}) collective-permute-start(bf16[384,2048]{1,0:T(8,128)(2,1)S(1)} %copy-done), channel_id=1, source_target_pairs={{0,8},{8,0},{16,24},{24,16},{1,9},{9,1},{17,25},{25,17},{2,10},{10... | collective-permute-start | bytes 4718600 | tf_op jit(solution)/shard_map/ppermute | solution.py:454
  78.2 5.3 %collective-permute-start.19 = (bf16[320,2048]{1,0:T(8,128)(2,1)S(1)}, bf16[320,2048]{1,0:T(8,128)(2,1)S(1)}, u32[]{:S(2)}, u32[]{:S(2)}) collective-permute-start(bf16[320,2048]{1,0:T(8,128)(2,1)S(1)} %copy-done.1), channel_id=1, source_target_pairs={{0,8},{8,0},{16,24},{24,16},{1,9},{9,1},{17,25},{25,17},{2,10},{10... | collective-permute-start | bytes 3932168 | tf_op jit(solution)/shard_map/ppermute | solution.py:454
  78.7 4.8 %collective-permute-start.21 = (f32[32,128]{1,0:T(8,128)S(1)}, f32[32,128]{1,0:T(8,128)S(1)}, u32[]{:S(2)}, u32[]{:S(2)}) collective-permute-start(f32[32,128]{1,0:T(8,128)S(1)} %get-tuple-element.95.own_ref), channel_id=1, source_target_pairs={{0,9},{1,8},{2,11},{3,10},{4,13},{5,12},{6,15},{7,14},{8,1},{9,0},... | collective-permute-start | bytes 49160 | tf_op jit(solution)/shard_map/ppermute | solution.py:464
  78.9 4.5 %collective-permute-start.20 = (f32[32,128]{1,0:T(8,128)S(1)}, f32[32,128]{1,0:T(8,128)S(1)}, u32[]{:S(2)}, u32[]{:S(2)}) collective-permute-start(f32[32,128]{1,0:T(8,128)S(1)} %get-tuple-element.95.own_ref), channel_id=1, source_target_pairs={{0,8},{8,0},{16,24},{24,16},{1,9},{9,1},{17,25},{25,17},{2,10},{10... | collective-permute-start | bytes 49160 | tf_op jit(solution)/shard_map/ppermute | solution.py:454
  79.3 4.1 %collective-permute-start.16 = (f32[32,128]{1,0:T(8,128)S(1)}, f32[32,128]{1,0:T(8,128)S(1)}, u32[]{:S(2)}, u32[]{:S(2)}) collective-permute-start(f32[32,128]{1,0:T(8,128)S(1)} %get-tuple-element.95.own_ref), channel_id=1, source_target_pairs={{0,1},{1,0},{2,3},{3,2},{4,5},{5,4},{6,7},{7,6},{8,9},{9,8},{10,11... | collective-permute-start | bytes 49160 | tf_op jit(solution)/shard_map/ppermute | solution.py:457
  83.5 9.3 %collective-permute-start.22 = (bf16[320,2048]{1,0:T(8,128)(2,1)}, bf16[320,2048]{1,0:T(8,128)(2,1)S(1)}, u32[]{:S(2)}, u32[]{:S(2)}) collective-permute-start(bf16[320,2048]{1,0:T(8,128)(2,1)} %get-tuple-element.97.refs_6_), channel_id=1, source_target_pairs={{0,8},{8,0},{16,24},{24,16},{1,9},{9,1},{17,25},{25,17},{2,10},{10... | collective-permute-start | bytes 3932168 | tf_op jit(solution)/shard_map/ppermute | solution.py:454
  85.0 6.1 %collective-permute-start.17 = (bf16[896,640]{1,0:T(8,128)(2,1)S(1)}, bf16[896,640]{1,0:T(8,128)(2,1)S(1)}, u32[]{:S(2)}, u32[]{:S(2)}) collective-permute-start(bf16[896,640]{1,0:T(8,128)(2,1)S(1)} %get-tuple-element.90), channel_id=1, source_target_pairs={{0,8},{8,0},{16,24},{24,16},{1,9},{9,1},{17,25},{25,17},{2,10},{10... | collective-permute-start | bytes 3440648 | tf_op jit(solution)/shard_map/ppermute | solution.py:454
  85.4 5.8 %collective-permute-start.25 = (f32[64,128]{1,0:T(8,128)S(1)}, f32[64,128]{1,0:T(8,128)S(1)}, u32[]{:S(2)}, u32[]{:S(2)}) collective-permute-start(f32[64,128]{1,0:T(8,128)S(1)} %get-tuple-element.96.refs_10_), channel_id=1, source_target_pairs={{0,2},{1,3},{2,4},{3,5},{4,6},{5,7},{6,0},{7,1},{8,10},{9,11},{10,... | collective-permute-start | bytes 98312 | tf_op jit(solution)/shard_map/ppermute | solution.py:467
  87.6 5.0 %collective-permute-start.24 = (f32[64,128]{1,0:T(8,128)S(1)}, f32[64,128]{1,0:T(8,128)S(1)}, u32[]{:S(2)}, u32[]{:S(2)}) collective-permute-start(f32[64,128]{1,0:T(8,128)S(1)} %get-tuple-element.96.refs_10_), channel_id=1, source_target_pairs={{0,4},{1,5},{2,6},{3,7},{4,0},{5,1},{6,2},{7,3},{8,12},{9,13},{10,... | collective-permute-start | bytes 98312 | tf_op jit(solution)/shard_map/ppermute | solution.py:467
  88.5 4.3 %collective-permute-start.23 = (f32[64,128]{1,0:T(8,128)S(1)}, f32[64,128]{1,0:T(8,128)S(1)}, u32[]{:S(2)}, u32[]{:S(2)}) collective-permute-start(f32[64,128]{1,0:T(8,128)S(1)} %get-tuple-element.96.refs_10_), channel_id=1, source_target_pairs={{0,6},{1,7},{2,0},{3,1},{4,2},{5,3},{6,4},{7,5},{8,14},{9,15},{10,... | collective-permute-start | bytes 98312 | tf_op jit(solution)/shard_map/ppermute | solution.py:467

commit v15 on v14

--- a/solution.py
+++ b/solution.py
@@ -573,7 +573,7 @@
     late = turned_features(rep_scalar, late, rows)
     late = [late[0], to_core(late[1])]
     merged, first = merged_stats(
-        after(stats, *other_exps), across_stats, core_stats, both_stats
+        after(stats, other_exps[0]), across_stats, core_stats, both_stats
     )
     all_stats = [merged] + [to_z(merged, -along) for along in range(1, lines)]
     other_exps.append(to_core(after(last_exp, merged)))

time: 113 us -> 113 us (level)
    ppermute x6, waiting for transfers between devices: 2.66 us -> 1.05 us  [to_core(): return lax.ppermute(values, 'rep', swap_pairs(reps, 1))]
where the time goes in v15:
time: 113 us; the launch traced here: 112 us
  Pallas kernels  70.1 us (62%)
  starting transfers between devices  27.3 us (24%)
  waiting for transfers between devices  7.26 us (6%)
  other arithmetic  3.62 us (3%)
  local copies, waits for them, and re-layouts  3.16 us (3%)
    pallas_call x6, Pallas kernels, round_logits(): pl.pallas_call(functools.partial(logits_kernel, stat_rows, first_row, len...  32.5 us
    pallas_call x1, Pallas kernels, refresh_states(): pl.pallas_call(functools.partial(refresh_kernel, lines, length, block_row...  20 us
    ppermute x7, starting transfers between devices, to_z(): return lax.ppermute(values, 'shard', shift_pairs(lines, along, 0))  11.4 us
    ppermute x7, starting transfers between devices, to_y(): return lax.ppermute(values, 'shard', swap_pairs(shards, 1))  8.68 us
    pallas_call x1, Pallas kernels, one_hot_sums(): pl.pallas_call(functools.partial(one_hot_kernel, len(features)), grid=(co...  8.66 us
    ppermute x5, starting transfers between devices, to_x(): return lax.ppermute(values, 'rep', swap_pairs(reps, 2))  5.58 us
    pallas_call x1, Pallas kernels, prepared(): pl.pallas_call(prepare_kernel, in_specs=[pl.BlockSpec(memory_space=pltpu....  5.52 us
    ppermute x7, waiting for transfers between devices, to_z(): return lax.ppermute(values, 'shard', shift_pairs(lines, along, 0))  5.12 us
  transfers between devices with their start and end apart: 26, of which 6 were waited for; matrix products, arithmetic and copies ran while one was open for 6% of the time, Pallas kernels for 39%

profile of v15, /device:TPU:0, one launch (start us, length us, event | category | flops | bytes accessed | tf_op | source)
XLA Modules:
  0.0 112.3 jit_solution(12269870427429443478)
XLA Ops:
  0.6 1.2 %normalized.1.refs_0_ = bf16[64,3584]{1,0:T(8,128)(2,1)S(1)} custom-call(bf16[64,3584]{1,0:T(8,128)(2,1)} %hidden_ref.1, f32[3584]{0:T(1024)} %gain_ref.1), custom_call_target="tpu_custom_call" | custom-call | flops 1024 | bytes 1024 | tf_op jit(solution)/shard_map/normalized/pallas_call | solution.py:93
  1.9 3.1 %collective-permute-start.2 = (bf16[64,3584]{1,0:T(8,128)(2,1)S(1)}, bf16[64,3584]{1,0:T(8,128)(2,1)S(1)}, u32[]{:S(2)}, u32[]{:S(2)}) collective-permute-start(bf16[64,3584]{1,0:T(8,128)(2,1)S(1)} %normalized.1.refs_0_), channel_id=1, source_target_pairs={{0,2},{1,3},{2,4},{3,5},{4,6},{5,7},{6,0},{7,1},{8,10},{9,11},{10,... | collective-permute-start | bytes 1376264 | tf_op jit(solution)/shard_map/ppermute | solution.py:467
  4.9 1.5 %collective-permute-start.1 = (bf16[64,3584]{1,0:T(8,128)(2,1)S(1)}, bf16[64,3584]{1,0:T(8,128)(2,1)S(1)}, u32[]{:S(2)}, u32[]{:S(2)}) collective-permute-start(bf16[64,3584]{1,0:T(8,128)(2,1)S(1)} %normalized.1.refs_0_), channel_id=1, source_target_pairs={{0,1},{1,0},{2,3},{3,2},{4,5},{5,4},{6,7},{7,6},{8,9},{9,8},{10,11... | collective-permute-start | bytes 1376264 | tf_op jit(solution)/shard_map/ppermute | solution.py:457
  6.5 1.5 %collective-permute-start = (bf16[64,3584]{1,0:T(8,128)(2,1)S(1)}, bf16[64,3584]{1,0:T(8,128)(2,1)S(1)}, u32[]{:S(2)}, u32[]{:S(2)}) collective-permute-start(bf16[64,3584]{1,0:T(8,128)(2,1)S(1)} %normalized.1.refs_0_), channel_id=1, source_target_pairs={{0,16},{8,24},{16,0},{24,8},{1,17},{9,25},{17,1},{25,9},{2,18},{10... | collective-permute-start | bytes 1376264 | tf_op jit(solution)/shard_map/ppermute | solution.py:451
  7.9 0.7 fusion.4
  8.6 0.7 compare_and_fusion
  9.3 0.7 multiply_add_fusion
  10.0 1.2 %slice.31 = s32[1]{0:T(128)} slice(s32[2048]{0:T(1024)} %param.12), slice={[0:1]} | slice | bytes 8 | tf_op jit(solution)/shard_map/jit(_roll_static)/slice | solution.py:486
  11.2 0.8 slice.30
  12.1 0.7 broadcast_subtract_fusion
  12.9 0.7 fusion.1
  13.6 0.1 sub.38
  13.7 0.6 gather_fusion
  14.7 2.7 %collective-permute-done.2.refs_0_.refs_3_ = bf16[64,3584]{1,0:T(8,128)(2,1)S(1)} collective-permute-done((bf16[64,3584]{1,0:T(8,128)(2,1)S(1)}, bf16[64,3584]{1,0:T(8,128)(2,1)S(1)}, u32[]{:S(2)}, u32[]{:S(2)}) %collective-permute-start.2) | collective-permute-done | bytes 458784 | tf_op jit(solution)/shard_map/ppermute | solution.py:467
  17.5 1.5 %collective-permute-start.5 = (bf16[64,3584]{1,0:T(8,128)(2,1)S(1)}, bf16[64,3584]{1,0:T(8,128)(2,1)S(1)}, u32[]{:S(2)}, u32[]{:S(2)}) collective-permute-start(bf16[64,3584]{1,0:T(8,128)(2,1)S(1)} %collective-permute-done.2.refs_0_.refs_3_), channel_id=1, source_target_pairs={{0,1},{1,0},{2,3},{3,2},{4,5},{5,4},{6,7},{7,6},{8,9},{9,8},{10,11... | collective-permute-start | bytes 1376264 | tf_op jit(solution)/shard_map/ppermute | solution.py:457
  19.0 1.5 %collective-permute-start.4 = (bf16[64,3584]{1,0:T(8,128)(2,1)S(1)}, bf16[64,3584]{1,0:T(8,128)(2,1)S(1)}, u32[]{:S(2)}, u32[]{:S(2)}) collective-permute-start(bf16[64,3584]{1,0:T(8,128)(2,1)S(1)} %collective-permute-done.2.refs_0_.refs_3_), channel_id=1, source_target_pairs={{0,16},{8,24},{16,0},{24,8},{1,17},{9,25},{17,1},{25,9},{2,18},{10... | collective-permute-start | bytes 1376264 | tf_op jit(solution)/shard_map/ppermute | solution.py:451
  20.5 5.5 %prepared.1 = (bf16[3584,2048]{1,0:T(8,128)(2,1)S(1)}, s32[1280,128]{1,0:T(8,128)S(1)}, s32[1280,128]{1,0:T(8,128)S(1)}) custom-call(bf16[3584,2048]{1,0:T(8,128)(2,1)} %weight_ref.1, s32[1,1280]{1,0:T(1,128)S(1)} %squeeze.14.true_ids, s32[1,1280]{1,0:T(1,128)S(1)} %squeeze.15.sample_ids, f32[32,128]{1,0:T(8,128)S(1)} %broadcast_in_dim.20.refs_0_.refs_4_), custom_call_target="tpu_custom_call" | custom-call | flops 1024 | bytes 1024 | tf_op jit(solution)/shard_map/prepared/pallas_call | solution.py:127
  26.0 0.6 collective-permute-start.8
  26.6 5.8 %round_logits.6 = (bf16[384,2048]{1,0:T(8,128)(2,1)}, f32[32,128]{1,0:T(8,128)S(1)}) custom-call(bf16[64,3584]{1,0:T(8,128)(2,1)S(1)} %normalized.1.refs_0_, bf16[64,3584]{1,0:T(8,128)(2,1)S(1)} %collective-permute-done.refs_1_, bf16[64,3584]{1,0:T(8,128)(2,1)S(1)} %collective-permute-done.1.refs_2_, ...), custom_call_target="tpu_custom_call" | custom-call | flops 1024 | bytes 1024 | tf_op jit(solution)/shard_map/round_logits/pallas_call | solution.py:206
  32.4 0.8 collective-permute-done.3.refs_0_
  33.2 0.5 collective-permute-start.7
  33.7 0.6 collective-permute-start.6
  34.3 1.5 %collective-permute-start.11 = (bf16[64,3584]{1,0:T(8,128)(2,1)S(1)}, bf16[64,3584]{1,0:T(8,128)(2,1)S(1)}, u32[]{:S(2)}, u32[]{:S(2)}) collective-permute-start(bf16[64,3584]{1,0:T(8,128)(2,1)S(1)} %collective-permute-done.3.refs_0_), channel_id=1, source_target_pairs={{0,1},{1,0},{2,3},{3,2},{4,5},{5,4},{6,7},{7,6},{8,9},{9,8},{10,11... | collective-permute-start | bytes 1376264 | tf_op jit(solution)/shard_map/ppermute | solution.py:457
  35.8 5.8 %round_logits.7 = (bf16[384,2048]{1,0:T(8,128)(2,1)}, f32[32,128]{1,0:T(8,128)S(1)}) custom-call(bf16[64,3584]{1,0:T(8,128)(2,1)S(1)} %collective-permute-done.2.refs_0_.refs_3_, bf16[64,3584]{1,0:T(8,128)(2,1)S(1)} %collective-permute-done.4.refs_1_.refs_4_, ...), custom_call_target="tpu_custom_call", output_to_operand_aliasing={{0}: (5, {})} | custom-call | flops 1024 | bytes 1024 | tf_op jit(solution)/shard_map/round_logits/pallas_call | solution.py:206
  41.6 4.7 %round_logits.8 = (bf16[320,2048]{1,0:T(8,128)(2,1)}, f32[32,128]{1,0:T(8,128)S(1)}) custom-call(bf16[64,3584]{1,0:T(8,128)(2,1)S(1)} %collective-permute-done.3.refs_0_, bf16[64,3584]{1,0:T(8,128)(2,1)S(1)} %collective-permute-done.8.refs_1_, bf16[3584,2048]{1,0:T(8,128)(2,1)S(1)} %get-tuple-element.57.refs_3_.refs_2_, f32[32,128]{1,0:T(8,128)S(1)} %get-tuple-element.66.refs_3_), custom_call_target="tpu_custom_call" | custom-call | flops 1024 | bytes 1024 | tf_op jit(solution)/shard_map/round_logits/pallas_call | solution.py:206
  46.4 1.6 %collective-permute-start.10 = (bf16[64,3584]{1,0:T(8,128)(2,1)S(1)}, bf16[64,3584]{1,0:T(8,128)(2,1)S(1)}, u32[]{:S(2)}, u32[]{:S(2)}) collective-permute-start(bf16[64,3584]{1,0:T(8,128)(2,1)S(1)} %collective-permute-done.6.refs_2_.refs_4_), channel_id=1, source_target_pairs={{0,16},{8,24},{16,0},{24,8},{1,17},{9,25},{17,1},{25,9},{2,18},{10... | collective-permute-start | bytes 1376264 | tf_op jit(solution)/shard_map/ppermute | solution.py:451
  48.0 0.9 turned_features.2
  48.9 1.6 %collective-permute-start.15 = (bf16[64,3584]{1,0:T(8,128)(2,1)S(1)}, bf16[64,3584]{1,0:T(8,128)(2,1)S(1)}, u32[]{:S(2)}, u32[]{:S(2)}) collective-permute-start(bf16[64,3584]{1,0:T(8,128)(2,1)S(1)} %collective-permute-done.8.refs_1_), channel_id=1, source_target_pairs={{0,2},{1,3},{2,4},{3,5},{4,6},{5,7},{6,0},{7,1},{8,10},{9,11},{10,... | collective-permute-start | bytes 1376264 | tf_op jit(solution)/shard_map/ppermute | solution.py:467
  50.5 0.5 collective-permute-start.14
  51.1 5.8 %round_logits.9 = (bf16[320,2048]{1,0:T(8,128)(2,1)}, f32[32,128]{1,0:T(8,128)S(1)}) custom-call(bf16[64,3584]{1,0:T(8,128)(2,1)S(1)} %collective-permute-done.7.refs_0_.refs_2_, bf16[64,3584]{1,0:T(8,128)(2,1)S(1)} %collective-permute-done.11.refs_1_.refs_3_, ...), custom_call_target="tpu_custom_call", output_to_operand_aliasing={{0}: (5, {})} | custom-call | flops 1024 | bytes 1024 | tf_op jit(solution)/shard_map/round_logits/pallas_call | solution.py:206
  56.8 1.6 %collective-permute-start.12 = (bf16[64,3584]{1,0:T(8,128)(2,1)S(1)}, bf16[64,3584]{1,0:T(8,128)(2,1)S(1)}, u32[]{:S(2)}, u32[]{:S(2)}) collective-permute-start(bf16[64,3584]{1,0:T(8,128)(2,1)S(1)} %collective-permute-done.10.refs_0_.refs_5_), channel_id=1, source_target_pairs={{0,1},{1,0},{2,3},{3,2},{4,5},{5,4},{6,7},{7,6},{8,9},{9,8},{10,11... | collective-permute-start | bytes 1376264 | tf_op jit(solution)/shard_map/ppermute | solution.py:457
  58.4 0.5 collective-permute-start.13
  58.9 8.7 %one_hot_sums.1 = (bf16[896,2048]{1,0:T(8,128)(2,1)}, bf16[896,2048]{1,0:T(8,128)(2,1)}) custom-call(bf16[896,384]{1,0:T(8,128)(2,1)S(1)} %get-tuple-element.70.refs_0_, bf16[896,384]{1,0:T(8,128)(2,1)S(1)} %collective-permute-done.9.refs_1_, s32[1,768]{1,0:T(1,128)S(1)} %squeeze.12.refs_2_, s32[1,768]{1,0:T(1,128)S(1)} %squeeze.13.refs_3_), custom_call_target="tpu_custom_call" | custom-call | flops 1024 | bytes 1024 | tf_op jit(solution)/shard_map/one_hot_sums/pallas_call | solution.py:285
  67.6 5.7 %round_logits.10 = (bf16[320,2048]{1,0:T(8,128)(2,1)}, f32[32,128]{1,0:T(8,128)S(1)}) custom-call(bf16[64,3584]{1,0:T(8,128)(2,1)S(1)} %collective-permute-done.10.refs_0_.refs_5_, bf16[64,3584]{1,0:T(8,128)(2,1)S(1)} %collective-permute-done.14.refs_1_.refs_6_, bf16[64,3584]{1,0:T(8,128)(2,1)S(1)} %collective-permute-done.15.refs_2_.refs_7_, ...), custom_call_target="tpu_custom_call" | custom-call | flops 1024 | bytes 1024 | tf_op jit(solution)/shard_map/round_logits/pallas_call | solution.py:206
  73.3 4.7 %round_logits.11 = (bf16[320,2048]{1,0:T(8,128)(2,1)}, f32[32,128]{1,0:T(8,128)S(1)}) custom-call(bf16[64,3584]{1,0:T(8,128)(2,1)S(1)} %collective-permute-done.12.refs_0_.refs_8_, bf16[64,3584]{1,0:T(8,128)(2,1)S(1)} %collective-permute-done.13.refs_1_.refs_9_, ...), custom_call_target="tpu_custom_call", output_to_operand_aliasing={{0}: (4, {})} | custom-call | flops 1024 | bytes 1024 | tf_op jit(solution)/shard_map/round_logits/pallas_call | solution.py:206
  78.2 0.7 collective-permute-start.21
  78.9 1.5 %collective-permute-start.16 = (f32[32,128]{1,0:T(8,128)S(1)}, f32[32,128]{1,0:T(8,128)S(1)}, u32[]{:S(2)}, u32[]{:S(2)}) collective-permute-start(f32[32,128]{1,0:T(8,128)S(1)} %get-tuple-element.95.own_ref), channel_id=1, source_target_pairs={{0,1},{1,0},{2,3},{3,2},{4,5},{5,4},{6,7},{7,6},{8,9},{9,8},{10,11... | collective-permute-start | bytes 49160 | tf_op jit(solution)/shard_map/ppermute | solution.py:457
  80.4 0.2 collective-permute-start.19
  80.5 1.0 collective-permute-done.18.refs_7_
  81.6 1.1 collective-permute-done.16.across_ref
  82.7 1.4 %turned_features.3 = (bf16[896,640]{1,0:T(8,128)(2,1)S(1)}, bf16[896,640]{1,0:T(8,128)(2,1)S(1)}) custom-call(s32[1]{0:T(128)} %bitcast.rep_ref, bf16[64,3584]{1,0:T(8,128)(2,1)S(1)} %collective-permute-done.3.refs_0_, bf16[64,3584]{1,0:T(8,128)(2,1)S(1)} %collective-permute-done.8.refs_1_, bf16[64,3584]{1,0:T(8,128)(2,1)S(1)} %collective-permute-done.7.refs_0_.refs_2_, ...), custom_call_target="tpu_custom_call" | custom-call | flops 1024 | bytes 1024 | tf_op jit(solution)/shard_map/turned_features/pallas_call | solution.py:248
  84.1 0.5 collective-permute-start.17
  84.6 2.1 %collective-permute-start.25 = (f32[64,128]{1,0:T(8,128)S(1)}, f32[64,128]{1,0:T(8,128)S(1)}, u32[]{:S(2)}, u32[]{:S(2)}) collective-permute-start(f32[64,128]{1,0:T(8,128)S(1)} %get-tuple-element.96.refs_10_), channel_id=1, source_target_pairs={{0,2},{1,3},{2,4},{3,5},{4,6},{5,7},{6,0},{7,1},{8,10},{9,11},{10,... | collective-permute-start | bytes 98312 | tf_op jit(solution)/shard_map/ppermute | solution.py:467
  86.7 1.3 %collective-permute-start.24 = (f32[64,128]{1,0:T(8,128)S(1)}, f32[64,128]{1,0:T(8,128)S(1)}, u32[]{:S(2)}, u32[]{:S(2)}) collective-permute-start(f32[64,128]{1,0:T(8,128)S(1)} %get-tuple-element.96.refs_10_), channel_id=1, source_target_pairs={{0,4},{1,5},{2,6},{3,7},{4,0},{5,1},{6,2},{7,3},{8,12},{9,13},{10,... | collective-permute-start | bytes 98312 | tf_op jit(solution)/shard_map/ppermute | solution.py:467
  88.0 2.6 %collective-permute-start.23 = (f32[64,128]{1,0:T(8,128)S(1)}, f32[64,128]{1,0:T(8,128)S(1)}, u32[]{:S(2)}, u32[]{:S(2)}) collective-permute-start(f32[64,128]{1,0:T(8,128)S(1)} %get-tuple-element.96.refs_10_), channel_id=1, source_target_pairs={{0,6},{1,7},{2,0},{3,1},{4,2},{5,3},{6,4},{7,5},{8,14},{9,15},{10,... | collective-permute-start | bytes 98312 | tf_op jit(solution)/shard_map/ppermute | solution.py:467
  90.7 1.1 %collective-permute-done.24.refs_12_ = f32[64,128]{1,0:T(8,128)S(1)} collective-permute-done((f32[64,128]{1,0:T(8,128)S(1)}, f32[64,128]{1,0:T(8,128)S(1)}, u32[]{:S(2)}, u32[]{:S(2)}) %collective-permute-start.24) | collective-permute-done | bytes 32800 | tf_op jit(solution)/shard_map/ppermute | solution.py:467
  91.8 0.4 collective-permute-done.23.refs_11_
  92.3 20.0 %refresh_states.1 = (bf16[896,2048]{1,0:T(8,128)(2,1)}, bf16[896,2048]{1,0:T(8,128)(2,1)}, bf16[896,2048]{1,0:T(8,128)(2,1)}) custom-call(bf16[896,384]{1,0:T(8,128)(2,1)S(1)} %get-tuple-element.70.refs_0_, bf16[896,384]{1,0:T(8,128)(2,1)S(1)} %collective-permute-done.9.refs_1_, bf16[896,640]{1,0:T(8,128)(2,1)S(1)} %get-tuple-element.89.refs_2_, ...), custom_call_target="tpu_custom_call" | custom-call | flops 1024 | bytes 1024 | tf_op jit(solution)/shard_map/refresh_states/pallas_call | solution.py:414
  (44 shorter events, 1.0 us)
Async XLA Ops:
  1.9 15.6 %collective-permute-start.2 = (bf16[64,3584]{1,0:T(8,128)(2,1)S(1)}, bf16[64,3584]{1,0:T(8,128)(2,1)S(1)}, u32[]{:S(2)}, u32[]{:S(2)}) collective-permute-start(bf16[64,3584]{1,0:T(8,128)(2,1)S(1)} %normalized.1.refs_0_), channel_id=1, source_target_pairs={{0,2},{1,3},{2,4},{3,5},{4,6},{5,7},{6,0},{7,1},{8,10},{9,11},{10,... | collective-permute-start | bytes 1376264 | tf_op jit(solution)/shard_map/ppermute | solution.py:467
  4.9 21.1 %collective-permute-start.1 = (bf16[64,3584]{1,0:T(8,128)(2,1)S(1)}, bf16[64,3584]{1,0:T(8,128)(2,1)S(1)}, u32[]{:S(2)}, u32[]{:S(2)}) collective-permute-start(bf16[64,3584]{1,0:T(8,128)(2,1)S(1)} %normalized.1.refs_0_), channel_id=1, source_target_pairs={{0,1},{1,0},{2,3},{3,2},{4,5},{5,4},{6,7},{7,6},{8,9},{9,8},{10,11... | collective-permute-start | bytes 1376264 | tf_op jit(solution)/shard_map/ppermute | solution.py:457
  6.5 19.6 %collective-permute-start = (bf16[64,3584]{1,0:T(8,128)(2,1)S(1)}, bf16[64,3584]{1,0:T(8,128)(2,1)S(1)}, u32[]{:S(2)}, u32[]{:S(2)}) collective-permute-start(bf16[64,3584]{1,0:T(8,128)(2,1)S(1)} %normalized.1.refs_0_), channel_id=1, source_target_pairs={{0,16},{8,24},{16,0},{24,8},{1,17},{9,25},{17,1},{25,9},{2,18},{10... | collective-permute-start | bytes 1376264 | tf_op jit(solution)/shard_map/ppermute | solution.py:451
  17.5 14.9 %collective-permute-start.5 = (bf16[64,3584]{1,0:T(8,128)(2,1)S(1)}, bf16[64,3584]{1,0:T(8,128)(2,1)S(1)}, u32[]{:S(2)}, u32[]{:S(2)}) collective-permute-start(bf16[64,3584]{1,0:T(8,128)(2,1)S(1)} %collective-permute-done.2.refs_0_.refs_3_), channel_id=1, source_target_pairs={{0,1},{1,0},{2,3},{3,2},{4,5},{5,4},{6,7},{7,6},{8,9},{9,8},{10,11... | collective-permute-start | bytes 1376264 | tf_op jit(solution)/shard_map/ppermute | solution.py:457
  19.0 13.4 %collective-permute-start.4 = (bf16[64,3584]{1,0:T(8,128)(2,1)S(1)}, bf16[64,3584]{1,0:T(8,128)(2,1)S(1)}, u32[]{:S(2)}, u32[]{:S(2)}) collective-permute-start(bf16[64,3584]{1,0:T(8,128)(2,1)S(1)} %collective-permute-done.2.refs_0_.refs_3_), channel_id=1, source_target_pairs={{0,16},{8,24},{16,0},{24,8},{1,17},{9,25},{17,1},{25,9},{2,18},{10... | collective-permute-start | bytes 1376264 | tf_op jit(solution)/shard_map/ppermute | solution.py:451
  20.5 12.7 %collective-permute-start.3 = (bf16[64,3584]{1,0:T(8,128)(2,1)S(1)}, bf16[64,3584]{1,0:T(8,128)(2,1)S(1)}, u32[]{:S(2)}, u32[]{:S(2)}) collective-permute-start(bf16[64,3584]{1,0:T(8,128)(2,1)S(1)} %collective-permute-done.2.refs_0_.refs_3_), channel_id=1, source_target_pairs={{0,2},{1,3},{2,4},{3,5},{4,6},{5,7},{6,0},{7,1},{8,10},{9,11},{10,... | collective-permute-start | bytes 1376264 | tf_op jit(solution)/shard_map/ppermute | solution.py:467
  26.0 15.6 %collective-permute-start.8 = (bf16[64,3584]{1,0:T(8,128)(2,1)S(1)}, bf16[64,3584]{1,0:T(8,128)(2,1)S(1)}, u32[]{:S(2)}, u32[]{:S(2)}) collective-permute-start(bf16[64,3584]{1,0:T(8,128)(2,1)S(1)} %collective-permute-done.refs_1_), channel_id=1, source_target_pairs={{0,1},{1,0},{2,3},{3,2},{4,5},{5,4},{6,7},{7,6},{8,9},{9,8},{10,11... | collective-permute-start | bytes 1376264 | tf_op jit(solution)/shard_map/ppermute | solution.py:457
  33.2 13.2 %collective-permute-start.7 = (bf16[64,3584]{1,0:T(8,128)(2,1)S(1)}, bf16[64,3584]{1,0:T(8,128)(2,1)S(1)}, u32[]{:S(2)}, u32[]{:S(2)}) collective-permute-start(bf16[64,3584]{1,0:T(8,128)(2,1)S(1)} %collective-permute-done.3.refs_0_), channel_id=1, source_target_pairs={{0,16},{8,24},{16,0},{24,8},{1,17},{9,25},{17,1},{25,9},{2,18},{10... | collective-permute-start | bytes 1376264 | tf_op jit(solution)/shard_map/ppermute | solution.py:451
  33.7 12.7 %collective-permute-start.6 = (bf16[64,3584]{1,0:T(8,128)(2,1)S(1)}, bf16[64,3584]{1,0:T(8,128)(2,1)S(1)}, u32[]{:S(2)}, u32[]{:S(2)}) collective-permute-start(bf16[64,3584]{1,0:T(8,128)(2,1)S(1)} %collective-permute-done.3.refs_0_), channel_id=1, source_target_pairs={{0,2},{1,3},{2,4},{3,5},{4,6},{5,7},{6,0},{7,1},{8,10},{9,11},{10,... | collective-permute-start | bytes 1376264 | tf_op jit(solution)/shard_map/ppermute | solution.py:467
  34.3 16.7 %collective-permute-start.11 = (bf16[64,3584]{1,0:T(8,128)(2,1)S(1)}, bf16[64,3584]{1,0:T(8,128)(2,1)S(1)}, u32[]{:S(2)}, u32[]{:S(2)}) collective-permute-start(bf16[64,3584]{1,0:T(8,128)(2,1)S(1)} %collective-permute-done.3.refs_0_), channel_id=1, source_target_pairs={{0,1},{1,0},{2,3},{3,2},{4,5},{5,4},{6,7},{7,6},{8,9},{9,8},{10,11... | collective-permute-start | bytes 1376264 | tf_op jit(solution)/shard_map/ppermute | solution.py:457
  46.4 10.4 %collective-permute-start.10 = (bf16[64,3584]{1,0:T(8,128)(2,1)S(1)}, bf16[64,3584]{1,0:T(8,128)(2,1)S(1)}, u32[]{:S(2)}, u32[]{:S(2)}) collective-permute-start(bf16[64,3584]{1,0:T(8,128)(2,1)S(1)} %collective-permute-done.6.refs_2_.refs_4_), channel_id=1, source_target_pairs={{0,16},{8,24},{16,0},{24,8},{1,17},{9,25},{17,1},{25,9},{2,18},{10... | collective-permute-start | bytes 1376264 | tf_op jit(solution)/shard_map/ppermute | solution.py:451
  48.8 10.1 %collective-permute-start.9 = (bf16[896,384]{1,0:T(8,128)(2,1)S(1)}, bf16[896,384]{1,0:T(8,128)(2,1)S(1)}, u32[]{:S(2)}, u32[]{:S(2)}) collective-permute-start(bf16[896,384]{1,0:T(8,128)(2,1)S(1)} %get-tuple-element.71), channel_id=1, source_target_pairs={{0,8},{8,0},{16,24},{24,16},{1,9},{9,1},{17,25},{25,17},{2,10},{10... | collective-permute-start | bytes 2064392 | tf_op jit(solution)/shard_map/ppermute | solution.py:454
  48.9 18.7 %collective-permute-start.15 = (bf16[64,3584]{1,0:T(8,128)(2,1)S(1)}, bf16[64,3584]{1,0:T(8,128)(2,1)S(1)}, u32[]{:S(2)}, u32[]{:S(2)}) collective-permute-start(bf16[64,3584]{1,0:T(8,128)(2,1)S(1)} %collective-permute-done.8.refs_1_), channel_id=1, source_target_pairs={{0,2},{1,3},{2,4},{3,5},{4,6},{5,7},{6,0},{7,1},{8,10},{9,11},{10,... | collective-permute-start | bytes 1376264 | tf_op jit(solution)/shard_map/ppermute | solution.py:467
  50.5 17.0 %collective-permute-start.14 = (bf16[64,3584]{1,0:T(8,128)(2,1)S(1)}, bf16[64,3584]{1,0:T(8,128)(2,1)S(1)}, u32[]{:S(2)}, u32[]{:S(2)}) collective-permute-start(bf16[64,3584]{1,0:T(8,128)(2,1)S(1)} %collective-permute-done.6.refs_2_.refs_4_), channel_id=1, source_target_pairs={{0,1},{1,0},{2,3},{3,2},{4,5},{5,4},{6,7},{7,6},{8,9},{9,8},{10,11... | collective-permute-start | bytes 1376264 | tf_op jit(solution)/shard_map/ppermute | solution.py:457
  56.8 16.5 %collective-permute-start.12 = (bf16[64,3584]{1,0:T(8,128)(2,1)S(1)}, bf16[64,3584]{1,0:T(8,128)(2,1)S(1)}, u32[]{:S(2)}, u32[]{:S(2)}) collective-permute-start(bf16[64,3584]{1,0:T(8,128)(2,1)S(1)} %collective-permute-done.10.refs_0_.refs_5_), channel_id=1, source_target_pairs={{0,1},{1,0},{2,3},{3,2},{4,5},{5,4},{6,7},{7,6},{8,9},{9,8},{10,11... | collective-permute-start | bytes 1376264 | tf_op jit(solution)/shard_map/ppermute | solution.py:457
  58.4 14.9 %collective-permute-start.13 = (bf16[64,3584]{1,0:T(8,128)(2,1)S(1)}, bf16[64,3584]{1,0:T(8,128)(2,1)S(1)}, u32[]{:S(2)}, u32[]{:S(2)}) collective-permute-start(bf16[64,3584]{1,0:T(8,128)(2,1)S(1)} %collective-permute-done.11.refs_1_.refs_3_), channel_id=1, source_target_pairs={{0,16},{8,24},{16,0},{24,8},{1,17},{9,25},{17,1},{25,9},{2,18},{10... | collective-permute-start | bytes 1376264 | tf_op jit(solution)/shard_map/ppermute | solution.py:451
  73.3 4.8 %copy-start = (bf16[384,2048]{1,0:T(8,128)(2,1)S(1)}, bf16[384,2048]{1,0:T(8,128)(2,1)}, u32[]{:S(2)}) copy-start(bf16[384,2048]{1,0:T(8,128)(2,1)} %get-tuple-element.93.refs_4_) | copy-start | bytes 4718596
  73.3 7.0 %copy-start.1 = (bf16[320,2048]{1,0:T(8,128)(2,1)S(1)}, bf16[320,2048]{1,0:T(8,128)(2,1)}, u32[]{:S(2)}) copy-start(bf16[320,2048]{1,0:T(8,128)(2,1)} %get-tuple-element.94.refs_5_) | copy-start | bytes 3932164
  78.1 3.5 %collective-permute-start.18 = (bf16[384,2048]{1,0:T(8,128)(2,1)S(1)}, bf16[384,2048]{1,0:T(8,128)(2,1)S(1)}, u32[]{:S(2)}, u32[]{:S(2)}) collective-permute-start(bf16[384,2048]{1,0:T(8,128)(2,1)S(1)} %copy-done), channel_id=1, source_target_pairs={{0,8},{8,0},{16,24},{24,16},{1,9},{9,1},{17,25},{25,17},{2,10},{10... | collective-permute-start | bytes 4718600 | tf_op jit(solution)/shard_map/ppermute | solution.py:454
  78.2 3.4 %collective-permute-start.21 = (f32[32,128]{1,0:T(8,128)S(1)}, f32[32,128]{1,0:T(8,128)S(1)}, u32[]{:S(2)}, u32[]{:S(2)}) collective-permute-start(f32[32,128]{1,0:T(8,128)S(1)} %get-tuple-element.95.own_ref), channel_id=1, source_target_pairs={{0,9},{1,8},{2,11},{3,10},{4,13},{5,12},{6,15},{7,14},{8,1},{9,0},... | collective-permute-start | bytes 49160 | tf_op jit(solution)/shard_map/ppermute | solution.py:464
  78.8 2.7 %collective-permute-start.20 = (f32[32,128]{1,0:T(8,128)S(1)}, f32[32,128]{1,0:T(8,128)S(1)}, u32[]{:S(2)}, u32[]{:S(2)}) collective-permute-start(f32[32,128]{1,0:T(8,128)S(1)} %get-tuple-element.95.own_ref), channel_id=1, source_target_pairs={{0,8},{8,0},{16,24},{24,16},{1,9},{9,1},{17,25},{25,17},{2,10},{10... | collective-permute-start | bytes 49160 | tf_op jit(solution)/shard_map/ppermute | solution.py:454
  78.9 3.7 %collective-permute-start.16 = (f32[32,128]{1,0:T(8,128)S(1)}, f32[32,128]{1,0:T(8,128)S(1)}, u32[]{:S(2)}, u32[]{:S(2)}) collective-permute-start(f32[32,128]{1,0:T(8,128)S(1)} %get-tuple-element.95.own_ref), channel_id=1, source_target_pairs={{0,1},{1,0},{2,3},{3,2},{4,5},{5,4},{6,7},{7,6},{8,9},{9,8},{10,11... | collective-permute-start | bytes 49160 | tf_op jit(solution)/shard_map/ppermute | solution.py:457
  80.4 10.3 %collective-permute-start.19 = (bf16[320,2048]{1,0:T(8,128)(2,1)S(1)}, bf16[320,2048]{1,0:T(8,128)(2,1)S(1)}, u32[]{:S(2)}, u32[]{:S(2)}) collective-permute-start(bf16[320,2048]{1,0:T(8,128)(2,1)S(1)} %copy-done.1), channel_id=1, source_target_pairs={{0,8},{8,0},{16,24},{24,16},{1,9},{9,1},{17,25},{25,17},{2,10},{10... | collective-permute-start | bytes 3932168 | tf_op jit(solution)/shard_map/ppermute | solution.py:454
  82.7 9.6 %collective-permute-start.22 = (bf16[320,2048]{1,0:T(8,128)(2,1)}, bf16[320,2048]{1,0:T(8,128)(2,1)S(1)}, u32[]{:S(2)}, u32[]{:S(2)}) collective-permute-start(bf16[320,2048]{1,0:T(8,128)(2,1)} %get-tuple-element.97.refs_6_), channel_id=1, source_target_pairs={{0,8},{8,0},{16,24},{24,16},{1,9},{9,1},{17,25},{25,17},{2,10},{10... | collective-permute-start | bytes 3932168 | tf_op jit(solution)/shard_map/ppermute | solution.py:454
  84.1 3.9 %collective-permute-start.17 = (bf16[896,640]{1,0:T(8,128)(2,1)S(1)}, bf16[896,640]{1,0:T(8,128)(2,1)S(1)}, u32[]{:S(2)}, u32[]{:S(2)}) collective-permute-start(bf16[896,640]{1,0:T(8,128)(2,1)S(1)} %get-tuple-element.90), channel_id=1, source_target_pairs={{0,8},{8,0},{16,24},{24,16},{1,9},{9,1},{17,25},{25,17},{2,10},{10... | collective-permute-start | bytes 3440648 | tf_op jit(solution)/shard_map/ppermute | solution.py:454
  84.6 6.1 %collective-permute-start.25 = (f32[64,128]{1,0:T(8,128)S(1)}, f32[64,128]{1,0:T(8,128)S(1)}, u32[]{:S(2)}, u32[]{:S(2)}) collective-permute-start(f32[64,128]{1,0:T(8,128)S(1)} %get-tuple-element.96.refs_10_), channel_id=1, source_target_pairs={{0,2},{1,3},{2,4},{3,5},{4,6},{5,7},{6,0},{7,1},{8,10},{9,11},{10,... | collective-permute-start | bytes 98312 | tf_op jit(solution)/shard_map/ppermute | solution.py:467
  86.7 5.1 %collective-permute-start.24 = (f32[64,128]{1,0:T(8,128)S(1)}, f32[64,128]{1,0:T(8,128)S(1)}, u32[]{:S(2)}, u32[]{:S(2)}) collective-permute-start(f32[64,128]{1,0:T(8,128)S(1)} %get-tuple-element.96.refs_10_), channel_id=1, source_target_pairs={{0,4},{1,5},{2,6},{3,7},{4,0},{5,1},{6,2},{7,3},{8,12},{9,13},{10,... | collective-permute-start | bytes 98312 | tf_op jit(solution)/shard_map/ppermute | solution.py:467
  88.0 4.2 %collective-permute-start.23 = (f32[64,128]{1,0:T(8,128)S(1)}, f32[64,128]{1,0:T(8,128)S(1)}, u32[]{:S(2)}, u32[]{:S(2)}) collective-permute-start(f32[64,128]{1,0:T(8,128)S(1)} %get-tuple-element.96.refs_10_), channel_id=1, source_target_pairs={{0,6},{1,7},{2,0},{3,1},{4,2},{5,3},{6,4},{7,5},{8,14},{9,15},{10,... | collective-permute-start | bytes 98312 | tf_op jit(solution)/shard_map/ppermute | solution.py:467
